TPU v7x, 32 devices: a whole 2x2x4 slice. The times are simulated.
32 devices in a mesh: row: 8 (over z, x), col: 4 (over y, core).
Axes of the slice: x: 2, y: 2, z: 4, core: 2. Of those that a mesh axis runs over, the one named last changes fastest.
Arguments:
- objective: float32 [128, 8192], P('row', 'col'), may hold values from -6 to 6
- center: bfloat16 [128, 8192], P('row', 'col'), may hold values from -5 to 5
- radius: bfloat16 [128, 8192], P('row', 'col'), may hold values from 0.049804688 to 1
- lower_gap: bfloat16 [3, 128, 8192], P(None, 'row', 'col'), may hold values from 0.19921875 to 3
- upper_gap: bfloat16 [3, 128, 8192], P(None, 'row', 'col'), may hold values from 0.19921875 to 3
- kernels: float32 [4, 3, 3, 64, 64], replicated, may hold values from -0.25 to 0.25
- biases: float32 [4, 64], replicated, may hold values from -3 to 3
- step_sizes: float32 [3], replicated, may hold values from 0.2 to 1
Outputs:
- bounds: float32 [3], replicated
- final_duals: float32 [3, 128, 8192], P(None, 'row', 'col')
- final_multipliers: float32 [3, 128, 8192], P(None, 'row', 'col')
All inputs are finite; a program needn't handle non-finite values.
Results may differ from a plain program's by a relative error of at most 0.0003.
Values sent between devices are 32-bit elements; how exact they have to be, the bound alone decides.
No kernel may reach another device: no remote copies, remote signals or barrier semaphores. Data moves between devices by JAX's collectives and lax.ppermute only.
A program may use at most 128 MiB of HBM per device.

v0:
```python
import jax
import jax.numpy as jnp
from jax import lax
from jax.sharding import PartitionSpec as P

CH = 64
LAYERS = 4
ITERS = 3


TEMP = 0.5
EPS = 1e-06


def extended(cells, sides, width):
    for axis, dim in sides:
        count = lax.axis_size(axis)
        ends = count - 1
        head = lax.slice_in_dim(cells, 0, width, axis=dim)
        tail = lax.slice_in_dim(cells, cells.shape[dim] - width, cells.shape[dim], axis=dim)
        cells = jnp.concatenate(
            [
                lax.ppermute(tail, axis, [(i, (i + 1) % count) for i in range(ends)]),
                cells,
                lax.ppermute(head, axis, [((i + 1) % count, i) for i in range(ends)]),
            ],
            axis=dim,
        )
    return cells


def soft_value(coef, low, high):
    return coef * low - TEMP * jax.nn.softplus(coef * (low - high) / TEMP)


def soft_point(coef, low, high):
    return low + (high - low) * jax.nn.sigmoid(coef * (low - high) / TEMP)


def flipped(kernel):
    return jnp.transpose(kernel[::-1, ::-1], (0, 1, 3, 2))


def conv_valid(padded, kernel):
    out_rows = padded.shape[0] - 2
    out_cols = padded.shape[1] - 2
    in_chan = padded.shape[2]
    result = jnp.zeros((out_rows * out_cols, kernel.shape[3]), jnp.float32)
    for offset_row in range(3):
        for offset_col in range(3):
            window = padded[
                offset_row : offset_row + out_rows, offset_col : offset_col + out_cols
            ].reshape(out_rows * out_cols, in_chan)
            result = result + jnp.dot(
                window,
                kernel[offset_row, offset_col],
                precision=lax.Precision.HIGHEST,
                preferred_element_type=jnp.float32,
            )
    return result.reshape(out_rows, out_cols, kernel.shape[3])


def shards(objective, center, radius, lower_gap, upper_gap, kernels, biases, step_sizes):
    depth = LAYERS - 1
    tile_rows = objective.shape[0]
    tile_cols = objective.shape[1] // CH

    def cube(plane):
        return plane.reshape(plane.shape[:-1] + (tile_cols, CH))

    target = cube(objective)
    target_rim = extended(target, (("row", 0), ("col", 1)), 1)
    target_back = conv_valid(target_rim, flipped(kernels[LAYERS - 1]))
    fixed_part = jnp.sum(target * biases[LAYERS - 1])
    middle = cube(center.astype(jnp.float32))
    half = cube(radius.astype(jnp.float32))
    below = cube(lower_gap.astype(jnp.float32))
    above = cube(upper_gap.astype(jnp.float32))
    zero_map = jnp.zeros_like(middle)
    lows = [middle - half] + [zero_map] * depth
    highs = [middle + half] + [above[j] for j in range(depth)]
    duals = jnp.zeros((depth, tile_rows, tile_cols, CH), jnp.float32)
    multipliers = jnp.zeros_like(duals)
    total_cells = tile_rows * tile_cols * CH * lax.axis_size("row") * lax.axis_size("col")
    bounds = []
    for step in range(ITERS):
        coefs = []
        dual_rim = extended(duals, (("row", 1), ("col", 2)), 1)
        for layer in range(depth):
            coef = -conv_valid(dual_rim[layer], flipped(kernels[layer]))
            if layer > 0:
                coef = coef + multipliers[layer - 1]
            coefs.append(coef)
        points = [soft_point(coefs[layer], lows[layer], highs[layer]) for layer in range(depth)]
        primal = extended(jnp.stack(points), (("row", 1), ("col", 2)), 1)
        input_rims = [primal[layer] for layer in range(depth)]
        coefs.append(target_back + multipliers[depth - 1])
        points.append(soft_point(coefs[depth], lows[depth], highs[depth]))
        value = fixed_part
        for layer in range(LAYERS):
            value = value + jnp.sum(soft_value(coefs[layer], lows[layer], highs[layer]))
        slope_duals = []
        slope_mults = []
        squares = jnp.zeros((), jnp.float32)
        for j in range(depth):
            pos_coef = duals[j] - multipliers[j]
            neg_coef = -duals[j]
            value = value + jnp.sum(soft_value(pos_coef, zero_map, above[j]))
            value = value + jnp.sum(soft_value(neg_coef, zero_map, below[j]))
            value = value - jnp.sum(duals[j] * biases[j])
            positive = soft_point(pos_coef, zero_map, above[j])
            negative = soft_point(neg_coef, zero_map, below[j])
            slope_dual = positive - negative - conv_valid(input_rims[j], kernels[j]) - biases[j]
            slope_mult = points[j + 1] - positive
            squares = squares + jnp.sum(slope_dual * slope_dual) + jnp.sum(slope_mult * slope_mult)
            slope_duals.append(slope_dual)
            slope_mults.append(slope_mult)
        total_squares, total_value = lax.psum((squares, value), ("row", "col"))
        bounds.append(total_value / total_cells)
        scale = step_sizes[step] / jnp.sqrt(total_squares / (2 * depth * total_cells) + EPS)
        duals = duals + scale * jnp.stack(slope_duals)
        multipliers = multipliers + scale * jnp.stack(slope_mults)
    bound_array = jnp.stack(bounds)
    final_duals = duals.reshape(depth, tile_rows, tile_cols * CH)
    final_multipliers = multipliers.reshape(depth, tile_rows, tile_cols * CH)
    return (bound_array, final_duals, final_multipliers)


def solution(mesh):
    placed = (
        P("row", "col"),
        P("row", "col"),
        P("row", "col"),
        P(None, "row", "col"),
        P(None, "row", "col"),
        P(),
        P(),
        P(),
    )
    return jax.shard_map(
        shards,
        mesh=mesh,
        in_specs=placed,
        out_specs=(P(), P(None, "row", "col"), P(None, "row", "col")),
        check_vma=False,
    )
```

profile of v0, /device:TPU:0, one launch (start us, length us, event | category | flops | bytes accessed | tf_op | source)
XLA Modules:
  0.0 541.6 jit_solution(1517671033400070243)
XLA Ops:
  1.3 5.4 %collective-permute-start = (f32[3,1,32,64]{3,2,1,0:T(8,128)}, f32[3,1,32,64]{3,2,1,0:T(8,128)}, u32[]{:S(2)}, u32[]{:S(2)}) collective-permute-start(f32[3,1,32,64]{3,2,1,0:T(8,128)} %broadcast.870), channel_id=1, source_target_pairs={{0,4},{4,8},{8,12},{12,16},{16,20},{20,24},{24,28},{1,5},{5,9},{9,... | collective-permute-start | bytes 73736 | tf_op jit(solution)/shard_map/ppermute | solution.py:23
  9.0 4.5 collective-permute-start.4
  51.7 4.3 collective-permute-start.2
  83.2 4.5 collective-permute-start.8
  95.3 3.0 collective-permute-start.10
  99.9 2.3 multiply_reduce_fusion.14
  124.6 2.6 subtract_subtract_fusion.11
  131.0 43.8 %psum.43 = f32[]{:T(128)} all-reduce(f32[]{:T(128)S(6)} %add.1337), channel_id=1, replica_groups=mesh['row'=8,'col'=4] {'row','col'}, use_global_device_ids=true, to_apply=%region_21.22 | all-reduce | flops 1 | bytes 8 | tf_op jit(solution)/shard_map/psum | solution.py:118
  178.2 4.3 collective-permute-start.12
  185.4 3.1 collective-permute-done.13
  191.7 2.4 collective-permute-done.15
  214.2 2.4 fusion.140
  217.3 4.5 collective-permute-start.16
  224.3 3.7 collective-permute-done.17
  229.4 3.6 collective-permute-start.18
  265.6 2.7 multiply_subtract_fusion.1
  294.3 41.5 %psum.45 = f32[]{:T(128)} all-reduce(f32[]{:T(128)S(6)} %add.1442), channel_id=1, replica_groups=mesh['row'=8,'col'=4] {'row','col'}, use_global_device_ids=true, to_apply=%region_42.43 | all-reduce | flops 1 | bytes 8 | tf_op jit(solution)/shard_map/psum | solution.py:118
  340.2 4.8 collective-permute-start.20
  389.9 2.5 fusion.142
  393.2 5.1 collective-permute-start.24
  409.7 4.8 collective-permute-start.26
  416.0 4.4 fusion.41
  453.5 2.5 multiply_subtract_fusion
  493.9 41.3 %all-reduce = (f32[]{:T(128)}, f32[]{:T(128)}, f32[]{:T(128)}, f32[]{:T(128)}) all-reduce(f32[]{:T(128)S(6)} %sub.1093, f32[]{:T(128)S(6)} %sub.1044, f32[]{:T(128)S(6)} %sub.986, f32[]{:T(128)S(6)} %add.1554), channel_id=1, replica_groups=mesh['row'=8,'col'=4] {'row','col'}, use_global_device_ids=true, to_apply=%region_56.57 | all-reduce | flops 4 | bytes 32 | tf_op jit(solution)/shard_map/psum | solution.py:118
  (789 shorter events, 289.7 us)
Async XLA Ops:
  1.3 49.6 %collective-permute-start = (f32[3,1,32,64]{3,2,1,0:T(8,128)}, f32[3,1,32,64]{3,2,1,0:T(8,128)}, u32[]{:S(2)}, u32[]{:S(2)}) collective-permute-start(f32[3,1,32,64]{3,2,1,0:T(8,128)} %broadcast.870), channel_id=1, source_target_pairs={{0,4},{4,8},{8,12},{12,16},{16,20},{20,24},{24,28},{1,5},{5,9},{9,... | collective-permute-start | bytes 73736 | tf_op jit(solution)/shard_map/ppermute | solution.py:23
  6.7 44.1 %collective-permute-start.1 = (f32[3,1,32,64]{3,2,1,0:T(8,128)}, f32[3,1,32,64]{3,2,1,0:T(8,128)}, u32[]{:S(2)}, u32[]{:S(2)}) collective-permute-start(f32[3,1,32,64]{3,2,1,0:T(8,128)} %broadcast.870), channel_id=1, source_target_pairs={{4,0},{8,4},{12,8},{16,12},{20,16},{24,20},{28,24},{5,1},{9,5},{13... | collective-permute-start | bytes 73736 | tf_op jit(solution)/shard_map/ppermute | solution.py:25
  9.0 30.7 %collective-permute-start.4 = (f32[1,32,64]{2,1,0:T(8,128)S(1)}, f32[1,32,64]{2,1,0:T(8,128)S(1)}, u32[]{:S(2)}, u32[]{:S(2)}) collective-permute-start(f32[1,32,64]{2,1,0:T(8,128)S(1)} %slice.1193), channel_id=1, source_target_pairs={{0,4},{4,8},{8,12},{12,16},{16,20},{20,24},{24,28},{1,5},{5,9},{9,... | collective-permute-start | bytes 24584 | tf_op jit(solution)/shard_map/ppermute | solution.py:23
  14.2 25.5 %collective-permute-start.5 = (f32[1,32,64]{2,1,0:T(8,128)}, f32[1,32,64]{2,1,0:T(8,128)S(1)}, u32[]{:S(2)}, u32[]{:S(2)}) collective-permute-start(f32[1,32,64]{2,1,0:T(8,128)} %slice.1195), channel_id=1, source_target_pairs={{4,0},{8,4},{12,8},{16,12},{20,16},{24,20},{28,24},{5,1},{9,5},{13... | collective-permute-start | bytes 24584 | tf_op jit(solution)/shard_map/ppermute | solution.py:25
  41.0 4.1 collective-permute-start.6
  42.3 4.8 collective-permute-start.7
  51.7 6.9 %collective-permute-start.2 = (f32[3,18,1,64]{3,2,1,0:T(1,128)S(1)}, f32[3,18,1,64]{3,2,1,0:T(1,128)S(1)}, u32[]{:S(2)}, u32[]{:S(2)}) collective-permute-start(f32[3,18,1,64]{3,2,1,0:T(1,128)S(1)} %get-tuple-element.123), channel_id=1, source_target_pairs={{0,1},{1,2},{2,3},{4,5},{5,6},{6,7},{8,9},{9,10},{10,11},{12,13},{... | collective-permute-start | bytes 41480 | tf_op jit(solution)/shard_map/ppermute | solution.py:23
  83.2 9.7 %collective-permute-start.8 = (f32[3,1,32,64]{3,2,1,0:T(8,128)}, f32[3,1,32,64]{3,2,1,0:T(8,128)S(1)}, u32[]{:S(2)}, u32[]{:S(2)}) collective-permute-start(f32[3,1,32,64]{3,2,1,0:T(8,128)} %get-tuple-element.160), channel_id=1, source_target_pairs={{0,4},{4,8},{8,12},{12,16},{16,20},{20,24},{24,28},{1,5},{5,9},{9,... | collective-permute-start | bytes 73736 | tf_op jit(solution)/shard_map/ppermute | solution.py:23
  87.7 6.9 %collective-permute-start.9 = (f32[3,1,32,64]{3,2,1,0:T(8,128)}, f32[3,1,32,64]{3,2,1,0:T(8,128)S(1)}, u32[]{:S(2)}, u32[]{:S(2)}) collective-permute-start(f32[3,1,32,64]{3,2,1,0:T(8,128)} %get-tuple-element.161), channel_id=1, source_target_pairs={{4,0},{8,4},{12,8},{16,12},{20,16},{24,20},{28,24},{5,1},{9,5},{13... | collective-permute-start | bytes 73736 | tf_op jit(solution)/shard_map/ppermute | solution.py:25
  95.3 8.6 %collective-permute-start.10 = (f32[3,18,1,64]{3,2,1,0:T(1,128)}, f32[3,18,1,64]{3,2,1,0:T(1,128)S(1)}, u32[]{:S(2)}, u32[]{:S(2)}) collective-permute-start(f32[3,18,1,64]{3,2,1,0:T(1,128)} %get-tuple-element.121), channel_id=1, source_target_pairs={{0,1},{1,2},{2,3},{4,5},{5,6},{6,7},{8,9},{9,10},{10,11},{12,13},{... | collective-permute-start | bytes 41480 | tf_op jit(solution)/shard_map/ppermute | solution.py:23
  98.3 5.6 %collective-permute-start.11 = (f32[3,18,1,64]{3,2,1,0:T(1,128)}, f32[3,18,1,64]{3,2,1,0:T(1,128)}, u32[]{:S(2)}, u32[]{:S(2)}) collective-permute-start(f32[3,18,1,64]{3,2,1,0:T(1,128)} %get-tuple-element.122), channel_id=1, source_target_pairs={{1,0},{2,1},{3,2},{5,4},{6,5},{7,6},{9,8},{10,9},{11,10},{13,12},{... | collective-permute-start | bytes 41480 | tf_op jit(solution)/shard_map/ppermute | solution.py:25
  178.2 7.3 %collective-permute-start.12 = (f32[3,1,32,64]{3,2,1,0:T(8,128)S(1)}, f32[3,1,32,64]{3,2,1,0:T(8,128)S(1)}, u32[]{:S(2)}, u32[]{:S(2)}) collective-permute-start(f32[3,1,32,64]{3,2,1,0:T(8,128)S(1)} %get-tuple-element.158), channel_id=1, source_target_pairs={{0,4},{4,8},{8,12},{12,16},{16,20},{20,24},{24,28},{1,5},{5,9},{9,... | collective-permute-start | bytes 73736 | tf_op jit(solution)/shard_map/ppermute | solution.py:23
  182.5 6.0 %collective-permute-start.13 = (f32[3,1,32,64]{3,2,1,0:T(8,128)S(1)}, f32[3,1,32,64]{3,2,1,0:T(8,128)S(1)}, u32[]{:S(2)}, u32[]{:S(2)}) collective-permute-start(f32[3,1,32,64]{3,2,1,0:T(8,128)S(1)} %get-tuple-element.159), channel_id=1, source_target_pairs={{4,0},{8,4},{12,8},{16,12},{20,16},{24,20},{28,24},{5,1},{9,5},{13... | collective-permute-start | bytes 73736 | tf_op jit(solution)/shard_map/ppermute | solution.py:25
  189.8 4.2 collective-permute-start.15
  217.3 7.0 %collective-permute-start.16 = (f32[3,1,32,64]{3,2,1,0:T(8,128)}, f32[3,1,32,64]{3,2,1,0:T(8,128)}, u32[]{:S(2)}, u32[]{:S(2)}) collective-permute-start(f32[3,1,32,64]{3,2,1,0:T(8,128)} %get-tuple-element.156), channel_id=1, source_target_pairs={{0,4},{4,8},{8,12},{12,16},{16,20},{20,24},{24,28},{1,5},{5,9},{9,... | collective-permute-start | bytes 73736 | tf_op jit(solution)/shard_map/ppermute | solution.py:23
  221.7 6.3 %collective-permute-start.17 = (f32[3,1,32,64]{3,2,1,0:T(8,128)}, f32[3,1,32,64]{3,2,1,0:T(8,128)}, u32[]{:S(2)}, u32[]{:S(2)}) collective-permute-start(f32[3,1,32,64]{3,2,1,0:T(8,128)} %get-tuple-element.157), channel_id=1, source_target_pairs={{4,0},{8,4},{12,8},{16,12},{20,16},{24,20},{28,24},{5,1},{9,5},{13... | collective-permute-start | bytes 73736 | tf_op jit(solution)/shard_map/ppermute | solution.py:25
  229.4 22.1 %collective-permute-start.18 = (f32[3,18,1,64]{3,2,1,0:T(1,128)}, f32[3,18,1,64]{3,2,1,0:T(1,128)}, u32[]{:S(2)}, u32[]{:S(2)}) collective-permute-start(f32[3,18,1,64]{3,2,1,0:T(1,128)} %get-tuple-element.117), channel_id=1, source_target_pairs={{0,1},{1,2},{2,3},{4,5},{5,6},{6,7},{8,9},{9,10},{10,11},{12,13},{... | collective-permute-start | bytes 41480 | tf_op jit(solution)/shard_map/ppermute | solution.py:23
  233.1 18.5 %collective-permute-start.19 = (f32[3,18,1,64]{3,2,1,0:T(1,128)}, f32[3,18,1,64]{3,2,1,0:T(1,128)}, u32[]{:S(2)}, u32[]{:S(2)}) collective-permute-start(f32[3,18,1,64]{3,2,1,0:T(1,128)} %get-tuple-element.118), channel_id=1, source_target_pairs={{1,0},{2,1},{3,2},{5,4},{6,5},{7,6},{9,8},{10,9},{11,10},{13,12},{... | collective-permute-start | bytes 41480 | tf_op jit(solution)/shard_map/ppermute | solution.py:25
  340.2 19.2 %collective-permute-start.20 = (f32[3,1,32,64]{3,2,1,0:T(8,128)}, f32[3,1,32,64]{3,2,1,0:T(8,128)}, u32[]{:S(2)}, u32[]{:S(2)}) collective-permute-start(f32[3,1,32,64]{3,2,1,0:T(8,128)} %get-tuple-element.150), channel_id=1, source_target_pairs={{0,4},{4,8},{8,12},{12,16},{16,20},{20,24},{24,28},{1,5},{5,9},{9,... | collective-permute-start | bytes 73736 | tf_op jit(solution)/shard_map/ppermute | solution.py:23
  345.0 14.4 %collective-permute-start.21 = (f32[3,1,32,64]{3,2,1,0:T(8,128)}, f32[3,1,32,64]{3,2,1,0:T(8,128)}, u32[]{:S(2)}, u32[]{:S(2)}) collective-permute-start(f32[3,1,32,64]{3,2,1,0:T(8,128)} %get-tuple-element.151), channel_id=1, source_target_pairs={{4,0},{8,4},{12,8},{16,12},{20,16},{24,20},{28,24},{5,1},{9,5},{13... | collective-permute-start | bytes 73736 | tf_op jit(solution)/shard_map/ppermute | solution.py:25
  393.2 14.7 %collective-permute-start.24 = (f32[3,1,32,64]{3,2,1,0:T(8,128)}, f32[3,1,32,64]{3,2,1,0:T(8,128)}, u32[]{:S(2)}, u32[]{:S(2)}) collective-permute-start(f32[3,1,32,64]{3,2,1,0:T(8,128)} %get-tuple-element.143), channel_id=1, source_target_pairs={{0,4},{4,8},{8,12},{12,16},{16,20},{20,24},{24,28},{1,5},{5,9},{9,... | collective-permute-start | bytes 73736 | tf_op jit(solution)/shard_map/ppermute | solution.py:23
  398.3 9.5 %collective-permute-start.25 = (f32[3,1,32,64]{3,2,1,0:T(8,128)}, f32[3,1,32,64]{3,2,1,0:T(8,128)}, u32[]{:S(2)}, u32[]{:S(2)}) collective-permute-start(f32[3,1,32,64]{3,2,1,0:T(8,128)} %get-tuple-element.144), channel_id=1, source_target_pairs={{4,0},{8,4},{12,8},{16,12},{20,16},{24,20},{28,24},{5,1},{9,5},{13... | collective-permute-start | bytes 73736 | tf_op jit(solution)/shard_map/ppermute | solution.py:25
  409.7 28.8 %collective-permute-start.26 = (f32[3,18,1,64]{3,2,1,0:T(1,128)}, f32[3,18,1,64]{3,2,1,0:T(1,128)}, u32[]{:S(2)}, u32[]{:S(2)}) collective-permute-start(f32[3,18,1,64]{3,2,1,0:T(1,128)} %get-tuple-element.113), channel_id=1, source_target_pairs={{0,1},{1,2},{2,3},{4,5},{5,6},{6,7},{8,9},{9,10},{10,11},{12,13},{... | collective-permute-start | bytes 41480 | tf_op jit(solution)/shard_map/ppermute | solution.py:23
  414.5 24.0 %collective-permute-start.27 = (f32[3,18,1,64]{3,2,1,0:T(1,128)}, f32[3,18,1,64]{3,2,1,0:T(1,128)}, u32[]{:S(2)}, u32[]{:S(2)}) collective-permute-start(f32[3,18,1,64]{3,2,1,0:T(1,128)} %get-tuple-element.114), channel_id=1, source_target_pairs={{1,0},{2,1},{3,2},{5,4},{6,5},{7,6},{9,8},{10,9},{11,10},{13,12},{... | collective-permute-start | bytes 41480 | tf_op jit(solution)/shard_map/ppermute | solution.py:25
  (194 other events, 2852.0 us)
where the time goes:
time: 550 us; the launch traced here: 542 us
  blocking collectives  127 us (23%)
  local copies, waits for them, and re-layouts  125 us (23%)
  matrix products  87.9 us (16%)
  starting transfers between devices  72.7 us (13%)
  other arithmetic  66.3 us (12%)
  between operations  47.8 us (9%)
  waiting for transfers between devices  15.1 us (3%)
    psum x3, blocking collectives, shards(): total_squares, total_value = lax.psum((squares, value), ('row', 'col'))  127 us
    dot_general x171, matrix products, conv_valid(): jnp.dot(window, kernel[offset_row, offset_col], precision=lax.Precision.H...  87.9 us
    ppermute x14, starting transfers between devices, extended(): lax.ppermute(tail, axis, [(i, (i + 1) % count) for i in range(ends)])  52.9 us
    neg x15, local copies, waits for them, and re-layouts, shards(): coef = -conv_valid(dual_rim[layer], flipped(kernels[layer]))  21.6 us
    ppermute x14, starting transfers between devices, extended(): lax.ppermute(head, axis, [((i + 1) % count, i) for i in range(ends)])  19.8 us
    ppermute x14, waiting for transfers between devices, extended(): lax.ppermute(head, axis, [((i + 1) % count, i) for i in range(ends)])  15.1 us
    sub x7, other arithmetic, shards(): slope_mult = points[j + 1] - positive  13.1 us
  transfers between devices with their start and end apart: 28, of which 7 were waited for; matrix products, arithmetic and copies ran while one was open for 18% of the time, Pallas kernels for 0%

commit v1 on v0

v1 whole, which is shorter than its diff:
```python
import functools
import math

import jax
import jax.numpy as jnp
from jax import lax
from jax.experimental import pallas as pl
from jax.experimental.pallas import tpu as pltpu
from jax.sharding import PartitionSpec as P

CH = 64
LAYERS = 4
ITERS = 3
EPS = 1e-06
LANES = 2 * CH
HALO_PAIRS = 3
WIDE = 5
EDGE = 4
F32 = jnp.float32
BF16 = jnp.bfloat16

ROWS_SENT = (5, 5, 5, 4, 4, 4, 4, 3, 3)
ROW_START = tuple(sum(ROWS_SENT[:m]) for m in range(9))
SENT = 40

VMEM = pl.BlockSpec(memory_space=pltpu.VMEM)
SMEM = pl.BlockSpec(memory_space=pltpu.SMEM)


def call(body, outs, scratch, operands, flops, mem=24, scalars=()):
    return pl.pallas_call(
        body,
        out_shape=outs,
        in_specs=[SMEM if j in scalars else VMEM for j in range(len(operands))],
        out_specs=jax.tree.map(lambda _: VMEM, outs),
        scratch_shapes=scratch,
        compiler_params=pltpu.CompilerParams(vmem_limit_bytes=mem << 20),
        cost_estimate=pl.CostEstimate(flops=flops, bytes_accessed=4 << 20, transcendentals=0),
    )(*operands)


def shape(*dims, dtype=F32):
    return jax.ShapeDtypeStruct(dims, dtype)


def split(value):
    high = value.astype(BF16)
    return high, (value - high.astype(F32)).astype(BF16)


def weights_body(kernels, biases, fwd_hi, fwd_lo, bwd_hi, bwd_lo, bias2):
    zero = jnp.zeros((CH, CH), F32)

    def put(hi, lo, k, j, dh, first, second):
        block = jnp.concatenate([first, second], axis=1)
        high, low = split(block)
        where = (k, pl.ds(CH * j, CH), pl.ds(LANES * dh, LANES))
        hi[where] = high
        lo[where] = low

    for k in range(LAYERS):
        for dh in range(3):
            taps = [kernels[k * 9 + dh * 3 + dw] for dw in range(3)]
            if k < LAYERS - 1:
                for j in range(4):
                    put(fwd_hi, fwd_lo, k, j, dh, taps[j] if j < 3 else zero, taps[j - 1] if j > 0 else zero)
            flips = [tap.T for tap in taps]
            for j in range(4):
                put(bwd_hi, bwd_lo, k, j, 2 - dh, flips[2 - j] if j < 3 else zero, flips[3 - j] if j > 0 else zero)
    for k in range(LAYERS):
        row = biases[k : k + 1, :]
        bias2[k : k + 1, :] = jnp.concatenate([row, row], axis=1)


def weights(kernels, biases):
    n = 4 * CH
    outs = (
        shape(LAYERS - 1, n, 3 * LANES, dtype=BF16),
        shape(LAYERS - 1, n, 3 * LANES, dtype=BF16),
        shape(LAYERS, n, 3 * LANES, dtype=BF16),
        shape(LAYERS, n, 3 * LANES, dtype=BF16),
        shape(8, LANES),
    )
    return call(weights_body, outs, [], (kernels.reshape(LAYERS * 9, CH, CH), biases), 1 << 22)


def sources(objective, center, radius, lower, upper):
    return [
        lambda cols: center[:, cols].astype(F32),
        lambda cols: upper[0, :, cols].astype(F32),
        lambda cols: upper[1, :, cols].astype(F32),
        lambda cols: upper[2, :, cols].astype(F32),
        lambda cols: lower[0, :, cols].astype(F32),
        lambda cols: lower[1, :, cols].astype(F32),
        lambda cols: lower[2, :, cols].astype(F32),
        lambda cols: radius[:, cols].astype(F32),
        lambda cols: objective[:, cols],
    ]


def sides_body(objective, center, radius, lower, upper, head, tail):
    rows, cols = objective.shape
    strip = HALO_PAIRS * LANES
    for m, read in enumerate(sources(objective, center, radius, lower, upper)):
        here = pl.ds(m * rows, rows)
        head[here, :] = read(pl.ds(0, strip))
        tail[here, :] = read(pl.ds(cols - strip, strip))


def column(reads, left, right, rows, pairs, m, q):
    if q < HALO_PAIRS:
        return left[m * rows : (m + 1) * rows, q * LANES : (q + 1) * LANES]
    if q >= HALO_PAIRS + pairs:
        q -= HALO_PAIRS + pairs
        return right[m * rows : (m + 1) * rows, q * LANES : (q + 1) * LANES]
    return reads[m](pl.ds((q - HALO_PAIRS) * LANES, LANES))


def ends_body(objective, center, radius, lower, upper, left, right, top, bottom):
    rows, cols = objective.shape
    pairs = cols // LANES
    reads = sources(objective, center, radius, lower, upper)
    for m in range(9):
        sent = ROWS_SENT[m]
        here = slice(ROW_START[m], ROW_START[m] + sent)
        for q in range(pairs + 2 * HALO_PAIRS):
            value = column(reads, left, right, rows, pairs, m, q)
            top[q, here, :] = value[:sent]
            bottom[q, here, :] = value[rows - sent :]
    spare = slice(sum(ROWS_SENT), SENT)
    top[:, spare, :] = jnp.zeros((pairs + 2 * HALO_PAIRS, SENT - sum(ROWS_SENT), LANES), F32)
    bottom[:, spare, :] = jnp.zeros((pairs + 2 * HALO_PAIRS, SENT - sum(ROWS_SENT), LANES), F32)


def neighbours(head, tail, axis):
    count = lax.axis_size(axis)
    before = lax.ppermute(tail, axis, [(i, i + 1) for i in range(count - 1)])
    after = lax.ppermute(head, axis, [(i + 1, i) for i in range(count - 1)])
    return before, after


def roll_rows(value, shift):
    return pltpu.roll(value, shift % value.shape[0], 0)


def slide(maps, count, store, produce):
    rows = store.shape[2]
    early = lax.broadcasted_iota(jnp.int32, (rows, LANES), 1) < CH
    zero = jnp.zeros((rows, LANES), F32)

    def step(q, carry):
        fresh = [pltpu.roll(value, CH, 1) for value in produce(q)]
        for k in range(maps):
            store[k, q] = jnp.where(early, carry[k], fresh[k])
        return tuple(fresh)

    last = lax.fori_loop(0, count, step, (zero,) * maps)
    for k in range(maps):
        store[k, count] = jnp.where(early, last[k], zero)


def multiply(store, k, first, count, hi, lo, layer, sums, exact=False):
    rows = store.shape[2]
    left = store[k, pl.ds(first, count)].reshape(count * rows, LANES)
    right = store[k, pl.ds(first + 1, count)].reshape(count * rows, LANES)
    window = jnp.concatenate([left, right], axis=1)
    dot = functools.partial(jnp.dot, preferred_element_type=F32)
    if exact:
        high = window.astype(BF16)
        result = dot(high, hi[layer]) + dot(high, lo[layer])
    else:
        high, low = split(window)
        result = dot(high, hi[layer]) + dot(high, lo[layer]) + dot(low, hi[layer])
    for d in range(3):
        sums[k, d, pl.ds(0, count)] = result[:, d * LANES : (d + 1) * LANES].reshape(count, rows, LANES)


def gathered(sums, k, q):
    return roll_rows(sums[k, 0, q], 1) + sums[k, 1, q] + roll_rows(sums[k, 2, q], -1)


def scale_of(total, step, cells):
    squares = jnp.sum(total[0:1, :], axis=1, keepdims=True)
    return step / jnp.sqrt(squares / (2 * (LAYERS - 1) * cells) + EPS)


def soft(top, t):
    return 0.5 * top * (1.0 - jnp.tanh(t))


class Bound:
    def __init__(self, start):
        self.linear = start
        self.factor = None

    def add(self, t):
        self.linear = self.linear - jnp.maximum(-t, 0.0)
        factor = 1.0 + jnp.exp(-2.0 * jnp.abs(t))
        self.factor = factor if self.factor is None else self.factor * factor

    def total(self):
        return self.linear - 0.5 * jnp.log(self.factor)


def own_rows(value):
    rows = value.shape[0]
    row = lax.broadcasted_iota(jnp.int32, value.shape, 0)
    kept = jnp.where((row >= EDGE) & (row < rows - EDGE), value, 0.0)
    return jnp.sum(kept, axis=0, keepdims=True)


def stats(rows):
    blank = [jnp.zeros((1, LANES), F32)] * (8 - len(rows))
    return jnp.concatenate(list(rows) + blank, axis=0)


def first_body(
    objective, center, radius, lower, upper, left, right, above, below,
    fwd_hi, fwd_lo, bwd_hi, bwd_lo, bias,
    box, back, slope, mult, stat, value,
    raw, target, store, sums,
):
    rows, cols = objective.shape
    pairs = cols // LANES
    frame = rows + 2 * EDGE
    wide = pairs + 4
    reads = sources(objective, center, radius, lower, upper)
    for m in range(9):
        sent = ROWS_SENT[m]
        here = slice(ROW_START[m], ROW_START[m] + sent)
        for q in range(pairs + 2 * HALO_PAIRS):
            if m >= 3 and not 1 <= q < wide + 1:
                continue
            own = column(reads, left, right, rows, pairs, m, q)
            if m < 3:
                dest, at, edge = raw.at[m, q], 0, WIDE
            else:
                dest, at, edge = (target.at[q - 1] if m == 8 else box.at[m, q - 1]), EDGE - sent, EDGE
                if at:
                    dest[0:EDGE, :] = jnp.zeros((EDGE, LANES), F32)
                    dest[EDGE + rows : frame, :] = jnp.zeros((EDGE, LANES), F32)
            dest[at : at + sent, :] = above[q, here, :]
            dest[edge : edge + rows, :] = own
            dest[edge + rows : edge + rows + sent, :] = below[q, here, :]
    raw[:, :, rows + 2 * WIDE :, :] = jnp.zeros((3, wide + 2, raw.shape[2] - rows - 2 * WIDE, LANES), F32)
    for m in range(3):
        for q in range(wide):
            box[m, q] = raw[m, q + 1, 1 : 1 + frame, :]

    tall = raw.shape[2]
    early = lax.broadcasted_iota(jnp.int32, (tall, LANES), 1) < CH

    def middle(q):
        return [raw[0, q], 0.5 * raw[1, q], 0.5 * raw[2, q]]

    slide(3, wide + 2, store, middle)
    for k in range(3):
        multiply(store, k, 1, wide, fwd_hi, fwd_lo, k, sums, exact=True)

    def slopes(q, carry):
        for k in range(3):
            conv = (
                sums[k, 0, q][:frame]
                + roll_rows(sums[k, 1, q], -1)[:frame]
                + roll_rows(sums[k, 2, q], -2)[:frame]
            )
            gap = box[1 + k, q]
            dl = 0.5 * (gap - box[4 + k, q]) - conv - bias[k : k + 1, :]
            slope[k, q] = jnp.where(gap > 0.0, dl, 0.0)
        return carry

    lax.fori_loop(0, wide, slopes, 0)

    early = lax.broadcasted_iota(jnp.int32, (frame, LANES), 1) < CH
    zero = jnp.zeros((frame, LANES), F32)

    def shift(q, carry):
        fresh = pltpu.roll(target[q], CH, 1)
        store[0, q, 0:frame, :] = jnp.where(early, carry, fresh)
        return fresh

    last = lax.fori_loop(0, wide, shift, zero)
    store[0, wide, 0:frame, :] = jnp.where(early, last, zero)
    lhs = jnp.concatenate(
        [
            store[0, 0:wide, 0:frame, :].reshape(wide * frame, LANES),
            store[0, 1 : wide + 1, 0:frame, :].reshape(wide * frame, LANES),
        ],
        axis=1,
    )
    high, low = split(lhs)
    dot = functools.partial(jnp.dot, preferred_element_type=F32)
    k = LAYERS - 1
    result = dot(high, bwd_hi[k]) + dot(high, bwd_lo[k]) + dot(low, bwd_hi[k])
    for d in range(3):
        sums[0, d, 0:wide, 0:frame, :] = result[:, d * LANES : (d + 1) * LANES].reshape(wide, frame, LANES)

    def pulls(q, carry):
        squares, worth, fixed = carry
        pull = (
            roll_rows(sums[0, 0, q][:frame], 1)
            + sums[0, 1, q][:frame]
            + roll_rows(sums[0, 2, q][:frame], -1)
        )
        back[q] = pull
        gap = box[3, q]
        t = pull * gap
        dm = -0.5 * gap * jnp.tanh(t)
        mult[q] = dm
        new = dm * dm
        for k in range(3):
            dl = slope[k, q]
            new = new + dl * dl
        bound = Bound(jnp.full((frame, LANES), -4.5 * math.log(2.0), F32))
        bound.add(t)
        own = (q >= 2) & (q < wide - 2)
        squares = squares + jnp.where(own, new, 0.0)
        worth = worth + jnp.where(own, bound.total(), 0.0)
        fixed = fixed + jnp.where(own, target[q] * bias[3:4, :], 0.0)
        return squares, worth, fixed

    squares, worth, fixed = lax.fori_loop(0, wide, pulls, (zero, zero, zero))
    fixed = own_rows(fixed)
    stat[...] = stats([own_rows(squares)])
    value[...] = stats([own_rows(worth) + fixed, fixed])


def second_pull_body(slope, bwd_hi, bwd_lo, back, store, sums):
    count = slope.shape[1]
    slide(3, count, store, lambda q: [slope[k, q] for k in range(3)])
    for k in range(3):
        multiply(store, k, 0, count, bwd_hi, bwd_lo, k, sums)

    def step(q, carry):
        for k in range(3):
            back[k, q] = gathered(sums, k, q)
        return carry

    lax.fori_loop(0, count, step, 0)


def second_body(
    total, steps, box, back, slope, mult, pull, fwd_hi, fwd_lo, bias,
    slope_out, mult_out, stat, value,
    points, store, sums, *, cells,
):
    wide = box.shape[1]
    frame = box.shape[2]
    scale = jnp.broadcast_to(scale_of(total, steps[0], cells), (frame, LANES))
    zero = jnp.zeros((frame, LANES), F32)

    def produce(q):
        radius = box[7, q]
        outs = [box[0, q] - radius * jnp.tanh(-2.0 * radius * (scale * pull[0, q]))]
        for k in (1, 2):
            gap = box[k, q]
            x = soft(gap, -(scale * pull[k, q]) * gap)
            points[k - 1, q] = x
            outs.append(x)
        return outs

    slide(3, wide, store, produce)
    for k in range(3):
        multiply(store, k, 1, wide - 2, fwd_hi, fwd_lo, k, sums)

    def step(j, carry):
        squares, worth = carry
        q = j + 1
        new = zero
        g = -(scale * pull[0, q])
        radius = box[7, q]
        bound = Bound(g * (box[0, q] - radius))
        bound.add(2.0 * g * radius)
        for k in range(3):
            gap = box[1 + k, q]
            low = box[4 + k, q]
            lam = scale * slope[k, q]
            if k < 2:
                x = points[k, q]
                bound.add(-(scale * pull[k + 1, q]) * gap)
                tp = lam * gap
            else:
                mu = scale * mult[q]
                t = (back[q] + mu) * gap
                x = soft(gap, t)
                bound.add(t)
                tp = (lam - mu) * gap
            tn = -lam * low
            bound.add(tp)
            bound.add(tn)
            bound.linear = bound.linear - lam * bias[k : k + 1, :]
            positive = soft(gap, tp)
            dl = positive - soft(low, tn) - gathered(sums, k, j) - bias[k : k + 1, :]
            dl = jnp.where(gap > 0.0, dl, 0.0)
            dm = x - positive
            slope_out[k, j] = dl
            mult_out[k, j] = dm
            new = new + dl * dl + dm * dm
        own = (q >= 2) & (q < wide - 2)
        return squares + jnp.where(own, new, 0.0), worth + jnp.where(own, bound.total(), 0.0)

    squares, worth = lax.fori_loop(0, wide - 2, step, (zero, zero))
    stat[...] = stats([own_rows(squares)])
    value[...] = stats([own_rows(worth)])


def third_body(
    total0, total1, steps, box, back, slope0, mult0, pull0, slope1, mult1, pull1, fwd_hi, fwd_lo, bias,
    value0, value1,
    duals, multipliers, slope_out, mult_out, stat,
    points, store, sums, *, cells,
):
    wide = box.shape[1]
    frame = box.shape[2]
    rows = frame - 2 * EDGE
    s0 = jnp.broadcast_to(scale_of(total0, steps[0], cells), (frame, LANES))
    s1 = jnp.broadcast_to(scale_of(total1, steps[1], cells), (frame, LANES))
    zero = jnp.zeros((frame, LANES), F32)

    def pull_of(k, j):
        g = -(s0 * pull0[k, j + 1] + s1 * pull1[k, j])
        return g if k == 0 else g + s1 * mult1[k - 1, j]

    def produce(j):
        q = j + 1
        radius = box[7, q]
        outs = [box[0, q] - radius * jnp.tanh(2.0 * radius * pull_of(0, j))]
        for k in (1, 2):
            gap = box[k, q]
            x = soft(gap, pull_of(k, j) * gap)
            points[k - 1, j] = x
            outs.append(x)
        return outs

    slide(3, wide - 2, store, produce)
    for k in range(3):
        multiply(store, k, 1, wide - 4, fwd_hi, fwd_lo, k, sums)

    def step(i, carry):
        squares, worth = carry
        j = i + 1
        q = i + 2
        new = zero
        g = pull_of(0, j)
        radius = box[7, q]
        bound = Bound(g * (box[0, q] - radius))
        bound.add(2.0 * g * radius)
        here = pl.ds(pl.multiple_of(i * LANES, LANES), LANES)
        for k in range(3):
            gap = box[1 + k, q]
            low = box[4 + k, q]
            lam = s0 * slope0[k, q] + s1 * slope1[k, j]
            mu = s1 * mult1[k, j]
            if k < 2:
                x = points[k, j]
                bound.add(pull_of(k + 1, j) * gap)
            else:
                mu = mu + s0 * mult0[q]
                t = (back[q] + mu) * gap
                x = soft(gap, t)
                bound.add(t)
            tp = (lam - mu) * gap
            tn = -lam * low
            bound.add(tp)
            bound.add(tn)
            bound.linear = bound.linear - lam * bias[k : k + 1, :]
            positive = soft(gap, tp)
            dl = positive - soft(low, tn) - gathered(sums, k, i) - bias[k : k + 1, :]
            dm = x - positive
            duals[k, :, here] = lam[EDGE : EDGE + rows]
            multipliers[k, :, here] = mu[EDGE : EDGE + rows]
            slope_out[k, :, here] = dl[EDGE : EDGE + rows]
            mult_out[k, :, here] = dm[EDGE : EDGE + rows]
            new = new + dl * dl + dm * dm
        return squares + new, worth + bound.total()

    squares, worth = lax.fori_loop(0, wide - 4, step, (zero, zero))
    fixed = value0[1:2, :]
    stat[...] = stats([own_rows(squares), value0[0:1, :], value1[0:1, :] + fixed, own_rows(worth) + fixed])


def last_body(total, steps, duals, multipliers, slope, mult, bounds, duals_out, mult_out, *, cells):
    scale = jnp.broadcast_to(scale_of(total, steps[2], cells), (duals.shape[1], duals.shape[2]))
    for k in range(LAYERS - 1):
        duals_out[k] = duals[k] + scale * slope[k]
        mult_out[k] = multipliers[k] + scale * mult[k]
    sums = jnp.sum(total[...], axis=1, keepdims=True) / cells
    bounds[...] = jnp.broadcast_to(sums, bounds.shape)


def everyone(partial):
    return lax.psum(partial, ("row", "col"))


def shards(objective, center, radius, lower, upper, kernels, biases, steps):
    rows, cols = objective.shape
    pairs = cols // LANES
    wide = pairs + 4
    frame = rows + 2 * EDGE
    tall = -(-(rows + 2 * WIDE) // 8) * 8
    cells = rows * cols * lax.axis_size("row") * lax.axis_size("col")
    inputs = (objective, center, radius, lower, upper)
    flops = 3 * 2 * 3 * wide * frame * 4 * CH * 3 * LANES

    strip = shape(9 * rows, HALO_PAIRS * LANES)
    head, tail = call(sides_body, (strip, strip), [], inputs, 1 << 20)
    left, right = neighbours(head, tail, "col")
    fwd_hi, fwd_lo, bwd_hi, bwd_lo, bias = weights(kernels, biases)
    strip = shape(pairs + 2 * HALO_PAIRS, SENT, LANES)
    top, bottom = call(ends_body, (strip, strip), [], inputs + (left, right), 1 << 20)
    above, below = neighbours(top, bottom, "row")

    stat_shape = shape(8, LANES)
    box, back, slope0, mult0, stat0, value0 = call(
        first_body,
        (
            shape(8, wide, frame, LANES),
            shape(wide, frame, LANES),
            shape(3, wide, frame, LANES),
            shape(wide, frame, LANES),
            stat_shape,
            stat_shape,
        ),
        [
            pltpu.VMEM((3, wide + 2, tall, LANES), F32),
            pltpu.VMEM((wide, frame, LANES), F32),
            pltpu.VMEM((3, wide + 3, tall, LANES), F32),
            pltpu.VMEM((3, 3, wide, tall, LANES), F32),
        ],
        inputs + (left, right, above, below, fwd_hi, fwd_lo, bwd_hi, bwd_lo, bias),
        2 * flops,
    )

    def pulled(slope):
        count = slope.shape[1]
        return call(
            second_pull_body,
            shape(3, count, frame, LANES),
            [
                pltpu.VMEM((3, count + 1, frame, LANES), F32),
                pltpu.VMEM((3, 3, count, frame, LANES), F32),
            ],
            (slope, bwd_hi, bwd_lo),
            flops,
        )

    total0 = everyone(stat0)
    pull0 = pulled(slope0)
    slope1, mult1, stat1, value1 = call(
        functools.partial(second_body, cells=cells),
        (shape(3, wide - 2, frame, LANES), shape(3, wide - 2, frame, LANES), stat_shape, stat_shape),
        [
            pltpu.VMEM((2, wide, frame, LANES), F32),
            pltpu.VMEM((3, wide + 1, frame, LANES), F32),
            pltpu.VMEM((3, 3, wide - 2, frame, LANES), F32),
        ],
        (total0, steps, box, back, slope0, mult0, pull0, fwd_hi, fwd_lo, bias),
        flops,
        scalars=(1,),
    )
    total1 = everyone(stat1)
    pull1 = pulled(slope1)
    out = shape(3, rows, cols)
    duals, multipliers, slope2, mult2, stat2 = call(
        functools.partial(third_body, cells=cells),
        (out, out, out, out, stat_shape),
        [
            pltpu.VMEM((2, wide - 2, frame, LANES), F32),
            pltpu.VMEM((3, wide - 1, frame, LANES), F32),
            pltpu.VMEM((3, 3, wide - 4, frame, LANES), F32),
        ],
        (
            total0, total1, steps, box, back, slope0, mult0, pull0, slope1, mult1, pull1,
            fwd_hi, fwd_lo, bias, value0, value1,
        ),
        flops,
        scalars=(2,),
    )
    total2 = everyone(stat2)
    bounds, final_duals, final_multipliers = call(
        functools.partial(last_body, cells=cells),
        (stat_shape, out, out),
        [],
        (total2, steps, duals, multipliers, slope2, mult2),
        1 << 20,
        scalars=(1,),
    )
    return bounds[1 : 1 + ITERS, 0], final_duals, final_multipliers


def solution(mesh):
    placed = (
        P("row", "col"),
        P("row", "col"),
        P("row", "col"),
        P(None, "row", "col"),
        P(None, "row", "col"),
        P(),
        P(),
        P(),
    )
    return jax.shard_map(
        shards,
        mesh=mesh,
        in_specs=placed,
        out_specs=(P(), P(None, "row", "col"), P(None, "row", "col")),
        check_vma=False,
    )
```

time: 550 us -> 204 us (0.37); the launches traced: 542 us -> 203 us
  local copies, waits for them, and re-layouts: 125 us -> 25.6 us
  matrix products: 87.9 us -> 0 us
  other arithmetic: 66.3 us -> 0 us
  starting transfers between devices: 72.7 us -> 8.38 us
  between operations: 47.8 us -> 0.94 us
  Pallas kernels: 0 us -> 25.2 us
    dot_general x171 -> x0, matrix products: 87.9 us -> none  [conv_valid(): jnp.dot(window, kernel[offset_row, offset_col], precision=lax.Precision.H...]
    ppermute x28 -> x4, starting transfers between devices: 72.7 us -> 8.38 us  [the longest x2 5.79 us: neighbours(): before = lax.ppermute(tail, axis, [(i, i + 1) for i in range(count - 1)])]
    squeeze x41 -> x0, local copies, waits for them, and re-layouts: 37.1 us -> none  [the longest x8 9.27 us: shards(): pos_coef = duals[j] - multipliers[j]]
    neg x19 -> x0, local copies, waits for them, and re-layouts: 25.3 us -> none  [the longest x15 21.6 us: shards(): coef = -conv_valid(dual_rim[layer], flipped(kernels[layer]))]
    pallas_call x0 -> x9, Pallas kernels: none -> 25.2 us  [call(): pl.pallas_call(body, out_shape=outs, in_specs=[SMEM if j in scalars else...]
    reduce_sum x13 -> x0, other arithmetic: 23.2 us -> none  [the longest x3 6.8 us: shards(): jnp.sum(slope_mult * slope_mult)]
    sub x11 -> x0, other arithmetic: 18 us -> none  [the longest x7 13.1 us: shards(): slope_mult = points[j + 1] - positive]
    sub x13 -> x0, local copies, waits for them, and re-layouts: 15.6 us -> none  [the longest x6 8.64 us: soft_value(): return coef * low - TEMP * jax.nn.softplus(coef * (low - high) / TEMP)]
  transfers between devices with their start and end apart: 28 -> 4, of which waited for: 7 -> 2; matrix products, arithmetic and copies ran while one was open for 18% -> 0% of each run, Pallas kernels for 0% -> 0%
where the time goes in v1:
time: 204 us; the launch traced here: 203 us
  blocking collectives  125 us (61%)
  local copies, waits for them, and re-layouts  25.6 us (13%)
  Pallas kernels  25.2 us (12%)
  waiting for transfers between devices  18.1 us (9%)
  starting transfers between devices  8.38 us (4%)
    psum x3, blocking collectives, everyone(): return lax.psum(partial, ('row', 'col'))  125 us
    pallas_call x9, Pallas kernels, call(): pl.pallas_call(body, out_shape=outs, in_specs=[SMEM if j in scalars else...  25.2 us
    unnamed x76, local copies, waits for them, and re-layouts  24.9 us
    ppermute x2, waiting for transfers between devices, neighbours(): before = lax.ppermute(tail, axis, [(i, i + 1) for i in range(count - 1)])  13.9 us
    ppermute x2, starting transfers between devices, neighbours(): before = lax.ppermute(tail, axis, [(i, i + 1) for i in range(count - 1)])  5.79 us
    ppermute x2, waiting for transfers between devices, neighbours(): after = lax.ppermute(head, axis, [(i + 1, i) for i in range(count - 1)])  4.19 us
  transfers between devices with their start and end apart: 4, of which 2 were waited for; matrix products, arithmetic and copies ran while one was open for 0% of the time, Pallas kernels for 0%

profile of v1, /device:TPU:0, one launch (start us, length us, event | category | flops | bytes accessed | tf_op | source)
XLA Modules:
  0.0 203.0 jit_solution(5282234550711857701)
XLA Ops:
  0.7 1.0 copy-done.13
  5.2 2.4 %collective-permute-start = (f32[144,384]{1,0:T(8,128)S(1)}, f32[144,384]{1,0:T(8,128)S(1)}, u32[]{:S(2)}, u32[]{:S(2)}) collective-permute-start(f32[144,384]{1,0:T(8,128)S(1)} %get-tuple-element.30), channel_id=1, source_target_pairs={{0,1},{1,2},{2,3},{4,5},{5,6},{6,7},{8,9},{9,10},{10,11},{12,13},{... | collective-permute-start | bytes 663560 | tf_op jit(solution)/shard_map/ppermute | solution.py:137
  7.6 1.3 collective-permute-start.1
  8.9 4.2 %collective-permute-done.1.right = f32[144,384]{1,0:T(8,128)S(1)} collective-permute-done((f32[144,384]{1,0:T(8,128)S(1)}, f32[144,384]{1,0:T(8,128)S(1)}, u32[]{:S(2)}, u32[]{:S(2)}) %collective-permute-start.1) | collective-permute-done | bytes 221216 | tf_op jit(solution)/shard_map/ppermute | solution.py:138
  13.2 3.4 %collective-permute-start.2 = (f32[22,40,128]{2,1,0:T(8,128)S(1)}, f32[22,40,128]{2,1,0:T(8,128)S(1)}, u32[]{:S(2)}, u32[]{:S(2)}) collective-permute-start(f32[22,40,128]{2,1,0:T(8,128)S(1)} %get-tuple-element.32), channel_id=1, source_target_pairs={{0,4},{4,8},{8,12},{12,16},{16,20},{20,24},{24,28},{1,5},{5,9},{9,... | collective-permute-start | bytes 1351688 | tf_op jit(solution)/shard_map/ppermute | solution.py:137
  16.6 1.3 collective-permute-start.3
  19.6 13.9 %collective-permute-done.2.above = f32[22,40,128]{2,1,0:T(8,128)S(1)} collective-permute-done((f32[22,40,128]{2,1,0:T(8,128)S(1)}, f32[22,40,128]{2,1,0:T(8,128)S(1)}, u32[]{:S(2)}, u32[]{:S(2)}) %collective-permute-start.2) | collective-permute-done | bytes 450592 | tf_op jit(solution)/shard_map/ppermute | solution.py:137
  33.5 6.3 %shard_map.106 = (f32[8,20,24,128]{3,2,1,0:T(8,128)S(1)}, f32[20,24,128]{2,1,0:T(8,128)S(1)}, f32[3,20,24,128]{3,2,1,0:T(8,128)S(1)}, f32[20,24,128]{2,1,0:T(8,1...) custom-call(f32[16,2048]{1,0:T(8,128)S(1)} %copy-done.21, bf16[16,2048]{1,0:T(8,128)(2,1)S(1)} %copy-done.30, ...), custom_call_target="tpu_custom_call" | custom-call | flops 1698693120 | bytes 4194304 | tf_op jit(solution)/shard_map/pallas_call | solution.py:31
  41.2 44.8 %psum.21.total.total0 = f32[8,128]{1,0:T(8,128)S(1)} all-reduce(f32[8,128]{1,0:T(8,128)S(1)} %get-tuple-element.39), channel_id=1, replica_groups=mesh['row'=8,'col'=4] {'row','col'}, use_global_device_ids=true, to_apply=%region_0.0 | all-reduce | flops 1024 | bytes 8192 | tf_op jit(solution)/shard_map/psum | solution.py:492
  86.0 1.2 copy-done.35
  87.3 1.1 copy-done.37
  88.4 3.1 %shard_map.107.pull.pull0 = f32[3,20,24,128]{3,2,1,0:T(8,128)S(1)} custom-call(f32[3,20,24,128]{3,2,1,0:T(8,128)S(1)} %get-tuple-element.42.slope.slope0, bf16[4,256,384]{2,1,0:T(8,128)(2,1)S(1)} %copy-done.35, bf16[4,256,384]{2,1,0:T(8,128)(2,1)S(1)} %copy-done.37), custom_call_target="tpu_custom_call" | custom-call | flops 849346560 | bytes 4194304 | tf_op jit(solution)/shard_map/pallas_call | solution.py:31
  91.6 5.3 %shard_map.108 = (f32[3,18,24,128]{3,2,1,0:T(8,128)S(1)}, f32[3,18,24,128]{3,2,1,0:T(8,128)S(1)}, f32[8,128]{1,0:T(8,128)S(1)}, f32[8,128]{1,0:T(8,128)S(1)}) custom-call(f32[8,128]{1,0:T(8,128)S(1)} %psum.21.total.total0, f32[3]{0:T(128)S(1)} %copy-done.32, f32[8,20,24,128]{3,2,1,0:T(8,128)S(1)} %get-tuple-element.40.box, f32[20,24,128]{2,1,0:T(8,128)S(1)} %copy-done.8, ...), custom_call_target="tpu_custom_call" | custom-call | flops 849346560 | bytes 4194304 | tf_op jit(solution)/shard_map/pallas_call | solution.py:31
  96.9 2.8 %shard_map.109.pull1 = f32[3,18,24,128]{3,2,1,0:T(8,128)S(1)} custom-call(f32[3,18,24,128]{3,2,1,0:T(8,128)S(1)} %get-tuple-element.45.slope.slope1, bf16[4,256,384]{2,1,0:T(8,128)(2,1)S(1)} %copy-done.35, bf16[4,256,384]{2,1,0:T(8,128)(2,1)S(1)} %copy-done.37), custom_call_target="tpu_custom_call" | custom-call | flops 849346560 | bytes 4194304 | tf_op jit(solution)/shard_map/pallas_call | solution.py:31
  101.4 39.7 %psum.22.total1 = f32[8,128]{1,0:T(8,128)S(1)} all-reduce(f32[8,128]{1,0:T(8,128)S(1)} %get-tuple-element.44), channel_id=1, replica_groups=mesh['row'=8,'col'=4] {'row','col'}, use_global_device_ids=true, to_apply=%region_1.0 | all-reduce | flops 1024 | bytes 8192 | tf_op jit(solution)/shard_map/psum | solution.py:492
  141.1 1.1 copy-done.2
  142.1 1.1 copy-done.5
  145.1 1.1 copy-done.16
  146.2 1.1 copy-done.18
  147.3 1.1 copy-done.20
  148.4 5.1 %shard_map.110 = (f32[3,16,2048]{2,1,0:T(8,128)S(1)}, f32[3,16,2048]{2,1,0:T(8,128)S(1)}, f32[3,16,2048]{2,1,0:T(8,128)S(1)}, f32[3,16,2048]{2,1,0:T(8,128)S(1)}, f32[8,128]{1,0:T(8,128)S(1)}) custom-call(f32[8,128]{1,0:T(8,128)S(1)} %psum.21.total.total0, f32[8,128]{1,0:T(8,128)S(1)} %psum.22.total1, f32[3]{0:T(128)S(1)} %copy-done.32, ...), custom_call_target="tpu_custom_call" | custom-call | flops 849346560 | bytes 4194304 | tf_op jit(solution)/shard_map/pallas_call | solution.py:31
  156.5 40.3 %psum.23.total = f32[8,128]{1,0:T(8,128)S(1)} all-reduce(f32[8,128]{1,0:T(8,128)S(1)} %get-tuple-element.49), channel_id=1, replica_groups=mesh['row'=8,'col'=4] {'row','col'}, use_global_device_ids=true, to_apply=%region_2.0 | all-reduce | flops 1024 | bytes 8192 | tf_op jit(solution)/shard_map/psum | solution.py:492
  196.8 1.0 copy-done.23
  200.8 1.6 shard_map.111
  (73 shorter events, 16.9 us)
Async XLA Ops:
  0.6 17.3 %copy-start.6 = (f32[4,3,3,64,64]{4,3,2,1,0:T(8,128)S(1)}, f32[4,3,3,64,64]{4,3,2,1,0:T(8,128)}, u32[]{:S(2)}) copy-start(f32[4,3,3,64,64]{4,3,2,1,0:T(8,128)} %param.13) | copy-start | bytes 1769476
  0.6 1.0 copy-start.13
  5.2 3.7 %collective-permute-start = (f32[144,384]{1,0:T(8,128)S(1)}, f32[144,384]{1,0:T(8,128)S(1)}, u32[]{:S(2)}, u32[]{:S(2)}) collective-permute-start(f32[144,384]{1,0:T(8,128)S(1)} %get-tuple-element.30), channel_id=1, source_target_pairs={{0,1},{1,2},{2,3},{4,5},{5,6},{6,7},{8,9},{9,10},{10,11},{12,13},{... | collective-permute-start | bytes 663560 | tf_op jit(solution)/shard_map/ppermute | solution.py:137
  7.6 5.5 %collective-permute-start.1 = (f32[144,384]{1,0:T(8,128)S(1)}, f32[144,384]{1,0:T(8,128)S(1)}, u32[]{:S(2)}, u32[]{:S(2)}) collective-permute-start(f32[144,384]{1,0:T(8,128)S(1)} %get-tuple-element.31), channel_id=1, source_target_pairs={{1,0},{2,1},{3,2},{5,4},{6,5},{7,6},{9,8},{10,9},{11,10},{13,12},{... | collective-permute-start | bytes 663560 | tf_op jit(solution)/shard_map/ppermute | solution.py:138
  13.2 20.3 %collective-permute-start.2 = (f32[22,40,128]{2,1,0:T(8,128)S(1)}, f32[22,40,128]{2,1,0:T(8,128)S(1)}, u32[]{:S(2)}, u32[]{:S(2)}) collective-permute-start(f32[22,40,128]{2,1,0:T(8,128)S(1)} %get-tuple-element.32), channel_id=1, source_target_pairs={{0,4},{4,8},{8,12},{12,16},{16,20},{20,24},{24,28},{1,5},{5,9},{9,... | collective-permute-start | bytes 1351688 | tf_op jit(solution)/shard_map/ppermute | solution.py:137
  16.6 16.9 %collective-permute-start.3 = (f32[22,40,128]{2,1,0:T(8,128)S(1)}, f32[22,40,128]{2,1,0:T(8,128)S(1)}, u32[]{:S(2)}, u32[]{:S(2)}) collective-permute-start(f32[22,40,128]{2,1,0:T(8,128)S(1)} %get-tuple-element.33), channel_id=1, source_target_pairs={{4,0},{8,4},{12,8},{16,12},{20,16},{24,20},{28,24},{5,1},{9,5},{13... | collective-permute-start | bytes 1351688 | tf_op jit(solution)/shard_map/ppermute | solution.py:138
  19.6 20.2 %copy-start = (bf16[3,256,384]{2,1,0:T(8,128)(2,1)}, bf16[3,256,384]{2,1,0:T(8,128)(2,1)S(1)}, u32[]{:S(2)}) copy-start(bf16[3,256,384]{2,1,0:T(8,128)(2,1)S(1)} %get-tuple-element.34.fwd_hi) | copy-start | bytes 1769476
  19.6 20.2 %copy-start.3 = (bf16[3,256,384]{2,1,0:T(8,128)(2,1)}, bf16[3,256,384]{2,1,0:T(8,128)(2,1)S(1)}, u32[]{:S(2)}) copy-start(bf16[3,256,384]{2,1,0:T(8,128)(2,1)S(1)} %get-tuple-element.35.fwd_lo) | copy-start | bytes 1769476
  19.6 20.2 %copy-start.34 = (bf16[4,256,384]{2,1,0:T(8,128)(2,1)}, bf16[4,256,384]{2,1,0:T(8,128)(2,1)S(1)}, u32[]{:S(2)}) copy-start(bf16[4,256,384]{2,1,0:T(8,128)(2,1)S(1)} %get-tuple-element.36.bwd_hi) | copy-start | bytes 2359300
  19.6 20.2 %copy-start.36 = (bf16[4,256,384]{2,1,0:T(8,128)(2,1)}, bf16[4,256,384]{2,1,0:T(8,128)(2,1)S(1)}, u32[]{:S(2)}) copy-start(bf16[4,256,384]{2,1,0:T(8,128)(2,1)S(1)} %get-tuple-element.37.bwd_lo) | copy-start | bytes 2359300
  41.2 50.3 %copy-start.32 = (f32[3]{0:T(128)S(1)}, f32[3]{0:T(128)}, u32[]{:S(2)}) copy-start(f32[3]{0:T(128)} %steps.5) | copy-start | bytes 40
  86.0 5.5 %copy-start.1 = (bf16[3,256,384]{2,1,0:T(8,128)(2,1)S(1)}, bf16[3,256,384]{2,1,0:T(8,128)(2,1)}, u32[]{:S(2)}) copy-start(bf16[3,256,384]{2,1,0:T(8,128)(2,1)} %copy-done) | copy-start | bytes 1769476
  86.0 5.5 %copy-start.4 = (bf16[3,256,384]{2,1,0:T(8,128)(2,1)S(1)}, bf16[3,256,384]{2,1,0:T(8,128)(2,1)}, u32[]{:S(2)}) copy-start(bf16[3,256,384]{2,1,0:T(8,128)(2,1)} %copy-done.3) | copy-start | bytes 1769476
  86.0 5.5 %copy-start.8 = (f32[20,24,128]{2,1,0:T(8,128)S(1)}, f32[20,24,128]{2,1,0:T(8,128)}, u32[]{:S(2)}) copy-start(f32[20,24,128]{2,1,0:T(8,128)} %copy-done.7) | copy-start | bytes 737284
  86.0 5.5 %copy-start.11 = (f32[20,24,128]{2,1,0:T(8,128)S(1)}, f32[20,24,128]{2,1,0:T(8,128)}, u32[]{:S(2)}) copy-start(f32[20,24,128]{2,1,0:T(8,128)} %copy-done.10) | copy-start | bytes 737284
  86.0 1.3 copy-start.35
  87.3 1.1 copy-start.37
  96.9 2.8 %copy-start.17 = (f32[3,18,24,128]{3,2,1,0:T(8,128)}, f32[3,18,24,128]{3,2,1,0:T(8,128)S(1)}, u32[]{:S(2)}) copy-start(f32[3,18,24,128]{3,2,1,0:T(8,128)S(1)} %get-tuple-element.46.mult1) | copy-start | bytes 1990660
  141.1 1.1 copy-start.2
  142.1 1.1 copy-start.5
  145.1 1.1 copy-start.16
  146.2 1.1 copy-start.18
  147.3 1.1 copy-start.20
  196.8 1.0 copy-start.23
  (18 other events, 15.2 us)

commit v2 on v1

--- a/solution.py
+++ b/solution.py
@@ -179,8 +179,12 @@
     return roll_rows(sums[k, 0, q], 1) + sums[k, 1, q] + roll_rows(sums[k, 2, q], -1)
 
 
+def summed(total):
+    return jnp.sum(total[...], axis=0, keepdims=True)
+
+
 def scale_of(total, step, cells):
-    squares = jnp.sum(total[0:1, :], axis=1, keepdims=True)
+    squares = summed(total)[:, 0:1]
     return step / jnp.sqrt(squares / (2 * (LAYERS - 1) * cells) + EPS)
 
 
@@ -209,9 +213,12 @@
     return jnp.sum(kept, axis=0, keepdims=True)
 
 
-def stats(rows):
-    blank = [jnp.zeros((1, LANES), F32)] * (8 - len(rows))
-    return jnp.concatenate(list(rows) + blank, axis=0)
+def stats(out, rows):
+    lane = lax.broadcasted_iota(jnp.int32, (1, LANES), 1)
+    packed = jnp.zeros((1, LANES), F32)
+    for j, row in enumerate(rows):
+        packed = jnp.where(lane == j, jnp.sum(row, axis=1, keepdims=True), packed)
+    out[...] = jnp.broadcast_to(packed, out.shape)
 
 
 def first_body(
@@ -321,8 +328,8 @@
 
     squares, worth, fixed = lax.fori_loop(0, wide, pulls, (zero, zero, zero))
     fixed = own_rows(fixed)
-    stat[...] = stats([own_rows(squares)])
-    value[...] = stats([own_rows(worth) + fixed, fixed])
+    stats(stat, [own_rows(squares)])
+    stats(value, [own_rows(worth) + fixed, fixed])
 
 
 def second_pull_body(slope, bwd_hi, bwd_lo, back, store, sums):
@@ -400,8 +407,8 @@
         return squares + jnp.where(own, new, 0.0), worth + jnp.where(own, bound.total(), 0.0)
 
     squares, worth = lax.fori_loop(0, wide - 2, step, (zero, zero))
-    stat[...] = stats([own_rows(squares)])
-    value[...] = stats([own_rows(worth)])
+    stats(stat, [own_rows(squares)])
+    stats(value, [own_rows(worth)])
 
 
 def third_body(
@@ -475,8 +482,10 @@
         return squares + new, worth + bound.total()
 
     squares, worth = lax.fori_loop(0, wide - 4, step, (zero, zero))
-    fixed = value0[1:2, :]
-    stat[...] = stats([own_rows(squares), value0[0:1, :], value1[0:1, :] + fixed, own_rows(worth) + fixed])
+    lane = lax.broadcasted_iota(jnp.int32, (1, LANES), 1)
+    first, fixed = (jnp.where(lane == j, value0[0:1, :], 0.0) for j in range(2))
+    second = jnp.where(lane == 0, value1[0:1, :], 0.0)
+    stats(stat, [own_rows(squares), first, second + fixed, own_rows(worth) + fixed])
 
 
 def last_body(total, steps, duals, multipliers, slope, mult, bounds, duals_out, mult_out, *, cells):
@@ -484,12 +493,11 @@
     for k in range(LAYERS - 1):
         duals_out[k] = duals[k] + scale * slope[k]
         mult_out[k] = multipliers[k] + scale * mult[k]
-    sums = jnp.sum(total[...], axis=1, keepdims=True) / cells
-    bounds[...] = jnp.broadcast_to(sums, bounds.shape)
+    bounds[...] = jnp.broadcast_to(summed(total) / cells, bounds.shape)
 
 
 def everyone(partial):
-    return lax.psum(partial, ("row", "col"))
+    return lax.all_to_all(partial, ("row", "col"), 0, 0, tiled=True)
 
 
 def shards(objective, center, radius, lower, upper, kernels, biases, steps):
@@ -511,6 +519,7 @@
     above, below = neighbours(top, bottom, "row")
 
     stat_shape = shape(8, LANES)
+    spread = shape(lax.axis_size("row") * lax.axis_size("col"), LANES)
     box, back, slope0, mult0, stat0, value0 = call(
         first_body,
         (
@@ -518,7 +527,7 @@
             shape(wide, frame, LANES),
             shape(3, wide, frame, LANES),
             shape(wide, frame, LANES),
-            stat_shape,
+            spread,
             stat_shape,
         ),
         [
@@ -548,7 +557,7 @@
     pull0 = pulled(slope0)
     slope1, mult1, stat1, value1 = call(
         functools.partial(second_body, cells=cells),
-        (shape(3, wide - 2, frame, LANES), shape(3, wide - 2, frame, LANES), stat_shape, stat_shape),
+        (shape(3, wide - 2, frame, LANES), shape(3, wide - 2, frame, LANES), spread, stat_shape),
         [
             pltpu.VMEM((2, wide, frame, LANES), F32),
             pltpu.VMEM((3, wide + 1, frame, LANES), F32),
@@ -563,7 +572,7 @@
     out = shape(3, rows, cols)
     duals, multipliers, slope2, mult2, stat2 = call(
         functools.partial(third_body, cells=cells),
-        (out, out, out, out, stat_shape),
+        (out, out, out, out, spread),
         [
             pltpu.VMEM((2, wide - 2, frame, LANES), F32),
             pltpu.VMEM((3, wide - 1, frame, LANES), F32),
@@ -585,7 +594,7 @@
         1 << 20,
         scalars=(1,),
     )
-    return bounds[1 : 1 + ITERS, 0], final_duals, final_multipliers
+    return bounds[0, 1 : 1 + ITERS], final_duals, final_multipliers
 
 
 def solution(mesh):

time: 204 us -> 109 us (0.53)
  blocking collectives: 125 us -> 12.6 us
  starting transfers between devices: 8.38 us -> 21.7 us
    psum x3 -> x0, blocking collectives: 125 us -> none  [everyone(): return lax.psum(partial, ('row', 'col'))]
    all_to_all x0 -> x2, starting transfers between devices: none -> 13.3 us  [everyone(): return lax.all_to_all(partial, ('row', 'col'), 0, 0, tiled=True)]
    all_to_all x0 -> x1, blocking collectives: none -> 12.6 us  [everyone(): return lax.all_to_all(partial, ('row', 'col'), 0, 0, tiled=True)]
    unnamed x76 -> x66, local copies, waits for them, and re-layouts: 24.9 us -> 26 us
  transfers between devices with their start and end apart: 4 -> 6, of which waited for: 2 -> 4; matrix products, arithmetic and copies ran while one was open for 0% -> 0% of each run, Pallas kernels for 0% -> 6%
where the time goes in v2:
time: 109 us; the launch traced here: 108 us
  local copies, waits for them, and re-layouts  26.6 us (24%)
  Pallas kernels  26.6 us (24%)
  starting transfers between devices  21.7 us (20%)
  waiting for transfers between devices  20 us (18%)
  blocking collectives  12.6 us (12%)
    pallas_call x9, Pallas kernels, call(): pl.pallas_call(body, out_shape=outs, in_specs=[SMEM if j in scalars else...  26.6 us
    unnamed x66, local copies, waits for them, and re-layouts  26 us
    ppermute x2, waiting for transfers between devices, neighbours(): before = lax.ppermute(tail, axis, [(i, i + 1) for i in range(count - 1)])  13.9 us
    all_to_all x2, starting transfers between devices, everyone(): return lax.all_to_all(partial, ('row', 'col'), 0, 0, tiled=True)  13.3 us
    all_to_all x1, blocking collectives, everyone(): return lax.all_to_all(partial, ('row', 'col'), 0, 0, tiled=True)  12.6 us
    ppermute x2, starting transfers between devices, neighbours(): before = lax.ppermute(tail, axis, [(i, i + 1) for i in range(count - 1)])  5.79 us
    ppermute x2, waiting for transfers between devices, neighbours(): after = lax.ppermute(head, axis, [(i + 1, i) for i in range(count - 1)])  4.19 us
    ppermute x2, starting transfers between devices, neighbours(): after = lax.ppermute(head, axis, [(i + 1, i) for i in range(count - 1)])  2.58 us
  transfers between devices with their start and end apart: 6, of which 4 were waited for; matrix products, arithmetic and copies ran while one was open for 0% of the time, Pallas kernels for 6%

profile of v2, /device:TPU:0, one launch (start us, length us, event | category | flops | bytes accessed | tf_op | source)
XLA Modules:
  0.0 108.4 jit_solution(2475280625398036640)
XLA Ops:
  5.2 2.4 %collective-permute-start = (f32[144,384]{1,0:T(8,128)S(1)}, f32[144,384]{1,0:T(8,128)S(1)}, u32[]{:S(2)}, u32[]{:S(2)}) collective-permute-start(f32[144,384]{1,0:T(8,128)S(1)} %get-tuple-element.30), channel_id=1, source_target_pairs={{0,1},{1,2},{2,3},{4,5},{5,6},{6,7},{8,9},{9,10},{10,11},{12,13},{... | collective-permute-start | bytes 663560 | tf_op jit(solution)/shard_map/ppermute | solution.py:137
  7.6 1.3 %collective-permute-start.1 = (f32[144,384]{1,0:T(8,128)S(1)}, f32[144,384]{1,0:T(8,128)S(1)}, u32[]{:S(2)}, u32[]{:S(2)}) collective-permute-start(f32[144,384]{1,0:T(8,128)S(1)} %get-tuple-element.31), channel_id=1, source_target_pairs={{1,0},{2,1},{3,2},{5,4},{6,5},{7,6},{9,8},{10,9},{11,10},{13,12},{... | collective-permute-start | bytes 663560 | tf_op jit(solution)/shard_map/ppermute | solution.py:138
  8.9 4.2 %collective-permute-done.1.right = f32[144,384]{1,0:T(8,128)S(1)} collective-permute-done((f32[144,384]{1,0:T(8,128)S(1)}, f32[144,384]{1,0:T(8,128)S(1)}, u32[]{:S(2)}, u32[]{:S(2)}) %collective-permute-start.1) | collective-permute-done | bytes 221216 | tf_op jit(solution)/shard_map/ppermute | solution.py:138
  13.2 3.4 %collective-permute-start.2 = (f32[22,40,128]{2,1,0:T(8,128)S(1)}, f32[22,40,128]{2,1,0:T(8,128)S(1)}, u32[]{:S(2)}, u32[]{:S(2)}) collective-permute-start(f32[22,40,128]{2,1,0:T(8,128)S(1)} %get-tuple-element.32), channel_id=1, source_target_pairs={{0,4},{4,8},{8,12},{12,16},{16,20},{20,24},{24,28},{1,5},{5,9},{9,... | collective-permute-start | bytes 1351688 | tf_op jit(solution)/shard_map/ppermute | solution.py:137
  16.6 1.3 %collective-permute-start.3 = (f32[22,40,128]{2,1,0:T(8,128)S(1)}, f32[22,40,128]{2,1,0:T(8,128)S(1)}, u32[]{:S(2)}, u32[]{:S(2)}) collective-permute-start(f32[22,40,128]{2,1,0:T(8,128)S(1)} %get-tuple-element.33), channel_id=1, source_target_pairs={{4,0},{8,4},{12,8},{16,12},{20,16},{24,20},{28,24},{5,1},{9,5},{13... | collective-permute-start | bytes 1351688 | tf_op jit(solution)/shard_map/ppermute | solution.py:138
  19.6 13.9 %collective-permute-done.2.above = f32[22,40,128]{2,1,0:T(8,128)S(1)} collective-permute-done((f32[22,40,128]{2,1,0:T(8,128)S(1)}, f32[22,40,128]{2,1,0:T(8,128)S(1)}, u32[]{:S(2)}, u32[]{:S(2)}) %collective-permute-start.2) | collective-permute-done | bytes 450592 | tf_op jit(solution)/shard_map/ppermute | solution.py:137
  33.5 6.9 %shard_map.106 = (f32[8,20,24,128]{3,2,1,0:T(8,128)S(1)}, f32[20,24,128]{2,1,0:T(8,128)S(1)}, f32[3,20,24,128]{3,2,1,0:T(8,128)S(1)}, f32[20,24,128]{2,1,0:T(8,1...) custom-call(f32[16,2048]{1,0:T(8,128)S(1)} %copy-done.22, bf16[16,2048]{1,0:T(8,128)(2,1)S(1)} %copy-done.23, ...), custom_call_target="tpu_custom_call" | custom-call | flops 1698693120 | bytes 4194304 | tf_op jit(solution)/shard_map/pallas_call | solution.py:31
  41.8 9.2 %all-to-all-start = ((f32[32,1,128]{2,1,0:T(1,128)}), f32[32,1,128]{2,1,0:T(1,128)S(1)}, u32[]{:S(2)}, u32[]{:S(2)}) async-start(f32[32,1,128]{2,1,0:T(1,128)} %bitcast.2), calls=%async_computation | async-start | bytes 32768 | tf_op jit(solution)/shard_map/all_to_all | solution.py:500
  51.1 1.1 %copy-done.28 = bf16[4,256,384]{2,1,0:T(8,128)(2,1)S(1)} copy-done((bf16[4,256,384]{2,1,0:T(8,128)(2,1)S(1)}, bf16[4,256,384]{2,1,0:T(8,128)(2,1)}, u32[]{:S(2)}) %copy-start.28) | copy-done | bytes 786456
  52.2 1.1 %copy-done.31 = bf16[4,256,384]{2,1,0:T(8,128)(2,1)S(1)} copy-done((bf16[4,256,384]{2,1,0:T(8,128)(2,1)S(1)}, bf16[4,256,384]{2,1,0:T(8,128)(2,1)}, u32[]{:S(2)}) %copy-start.31) | copy-done | bytes 786456
  53.4 3.1 %shard_map.107.pull.pull0 = f32[3,20,24,128]{3,2,1,0:T(8,128)S(1)} custom-call(f32[3,20,24,128]{3,2,1,0:T(8,128)S(1)} %get-tuple-element.42.slope.slope0, bf16[4,256,384]{2,1,0:T(8,128)(2,1)S(1)} %copy-done.28, bf16[4,256,384]{2,1,0:T(8,128)(2,1)S(1)} %copy-done.31), custom_call_target="tpu_custom_call" | custom-call | flops 849346560 | bytes 4194304 | tf_op jit(solution)/shard_map/pallas_call | solution.py:31
  56.4 1.8 %all-to-all-done = f32[32,1,128]{2,1,0:T(1,128)S(1)} async-done(((f32[32,1,128]{2,1,0:T(1,128)}), f32[32,1,128]{2,1,0:T(1,128)S(1)}, u32[]{:S(2)}, u32[]{:S(2)}) %all-to-all-start) | async-done | bytes 16416 | tf_op jit(solution)/shard_map/all_to_all | solution.py:500
  62.3 6.0 %shard_map.108 = (f32[3,18,24,128]{3,2,1,0:T(8,128)S(1)}, f32[3,18,24,128]{3,2,1,0:T(8,128)S(1)}, f32[32,128]{1,0:T(8,128)}, f32[8,128]{1,0:T(8,128)S(1)}) custom-call(f32[32,128]{1,0:T(8,128)S(1)} %bitcast.16, f32[3]{0:T(128)S(1)} %copy-done.25, f32[8,20,24,128]{3,2,1,0:T(8,128)S(1)} %get-tuple-element.40.box, f32[20,24,128]{2,1,0:T(8,128)S(1)} %copy-done.8, ...), custom_call_target="tpu_custom_call" | custom-call | flops 849346560 | bytes 4194304 | tf_op jit(solution)/shard_map/pallas_call | solution.py:31
  69.9 4.1 %all-to-all-start.1 = ((f32[32,1,128]{2,1,0:T(1,128)}), f32[32,1,128]{2,1,0:T(1,128)S(1)}, u32[]{:S(2)}, u32[]{:S(2)}) async-start(f32[32,1,128]{2,1,0:T(1,128)} %bitcast.5), calls=%async_computation.1 | async-start | bytes 32768 | tf_op jit(solution)/shard_map/all_to_all | solution.py:500
  74.0 1.1 copy-done.16
  75.1 1.1 %copy-done.29 = bf16[4,256,384]{2,1,0:T(8,128)(2,1)S(1)} copy-done((bf16[4,256,384]{2,1,0:T(8,128)(2,1)S(1)}, bf16[4,256,384]{2,1,0:T(8,128)(2,1)}, u32[]{:S(2)}) %copy-start.29) | copy-done | bytes 786456
  76.2 1.1 %copy-done.32 = bf16[4,256,384]{2,1,0:T(8,128)(2,1)S(1)} copy-done((bf16[4,256,384]{2,1,0:T(8,128)(2,1)S(1)}, bf16[4,256,384]{2,1,0:T(8,128)(2,1)}, u32[]{:S(2)}) %copy-start.32) | copy-done | bytes 786456
  77.4 2.8 %shard_map.109.pull1 = f32[3,18,24,128]{3,2,1,0:T(8,128)S(1)} custom-call(f32[3,18,24,128]{3,2,1,0:T(8,128)S(1)} %copy-done.16, bf16[4,256,384]{2,1,0:T(8,128)(2,1)S(1)} %copy-done.29, bf16[4,256,384]{2,1,0:T(8,128)(2,1)S(1)} %copy-done.32), custom_call_target="tpu_custom_call" | custom-call | flops 849346560 | bytes 4194304 | tf_op jit(solution)/shard_map/pallas_call | solution.py:31
  85.2 1.1 %copy-done.17 = f32[3,18,24,128]{3,2,1,0:T(8,128)S(1)} copy-done((f32[3,18,24,128]{3,2,1,0:T(8,128)S(1)}, f32[3,18,24,128]{3,2,1,0:T(8,128)}, u32[]{:S(2)}) %copy-start.17) | copy-done | bytes 663576
  86.3 1.1 %copy-done.19 = f32[3,18,24,128]{3,2,1,0:T(8,128)S(1)} copy-done((f32[3,18,24,128]{3,2,1,0:T(8,128)S(1)}, f32[3,18,24,128]{3,2,1,0:T(8,128)}, u32[]{:S(2)}) %copy-start.19) | copy-done | bytes 663576
  87.4 1.1 %copy-done.21 = f32[3,18,24,128]{3,2,1,0:T(8,128)S(1)} copy-done((f32[3,18,24,128]{3,2,1,0:T(8,128)S(1)}, f32[3,18,24,128]{3,2,1,0:T(8,128)}, u32[]{:S(2)}) %copy-start.21) | copy-done | bytes 663576
  88.4 5.1 %shard_map.110 = (f32[3,16,2048]{2,1,0:T(8,128)S(1)}, f32[3,16,2048]{2,1,0:T(8,128)S(1)}, f32[3,16,2048]{2,1,0:T(8,128)S(1)}, f32[3,16,2048]{2,1,0:T(8,128)S(1)}, f32[32,128]{1,0:T(8,128)S(1)}) custom-call(f32[32,128]{1,0:T(8,128)S(1)} %bitcast.17, f32[32,128]{1,0:T(8,128)S(1)} %bitcast.18, f32[3]{0:T(128)S(1)} %copy-done.25, ...), custom_call_target="tpu_custom_call" | custom-call | flops 849346560 | bytes 4194304 | tf_op jit(solution)/shard_map/pallas_call | solution.py:31
  93.6 12.6 %all_to_all.33 = f32[32,1,128]{2,1,0:T(1,128)S(1)} all-to-all(f32[32,1,128]{2,1,0:T(1,128)S(1)} %bitcast.20), channel_id=1, replica_groups=mesh['row'=8,'col'=4] {'row','col'}, dimensions={0} | all-to-all | bytes 32768 | tf_op jit(solution)/shard_map/all_to_all | solution.py:500
  106.2 1.6 %shard_map.111 = (f32[8,128]{1,0:T(8,128)S(1)}, f32[3,16,2048]{2,1,0:T(8,128)}, f32[3,16,2048]{2,1,0:T(8,128)}) custom-call(f32[32,128]{1,0:T(8,128)S(1)} %bitcast.19, f32[3]{0:T(128)S(1)} %copy-done.25, f32[3,16,2048]{2,1,0:T(8,128)S(1)} %get-tuple-element.50.duals, f32[3,16,2048]{2,1,0:T(8,128)S(1)} %get-tuple-element.51.multipliers, ...), custom_call_target="tpu_custom_call" | custom-call | flops 1048576 | bytes 4194304 | tf_op jit(solution)/shard_map/pallas_call | solution.py:31
  (65 shorter events, 19.0 us)
Async XLA Ops:
  0.6 17.3 %copy-start.6 = (f32[4,3,3,64,64]{4,3,2,1,0:T(8,128)S(1)}, f32[4,3,3,64,64]{4,3,2,1,0:T(8,128)}, u32[]{:S(2)}) copy-start(f32[4,3,3,64,64]{4,3,2,1,0:T(8,128)} %param.13) | copy-start | bytes 1769476
  5.2 3.7 %collective-permute-start = (f32[144,384]{1,0:T(8,128)S(1)}, f32[144,384]{1,0:T(8,128)S(1)}, u32[]{:S(2)}, u32[]{:S(2)}) collective-permute-start(f32[144,384]{1,0:T(8,128)S(1)} %get-tuple-element.30), channel_id=1, source_target_pairs={{0,1},{1,2},{2,3},{4,5},{5,6},{6,7},{8,9},{9,10},{10,11},{12,13},{... | collective-permute-start | bytes 663560 | tf_op jit(solution)/shard_map/ppermute | solution.py:137
  7.6 5.5 %collective-permute-start.1 = (f32[144,384]{1,0:T(8,128)S(1)}, f32[144,384]{1,0:T(8,128)S(1)}, u32[]{:S(2)}, u32[]{:S(2)}) collective-permute-start(f32[144,384]{1,0:T(8,128)S(1)} %get-tuple-element.31), channel_id=1, source_target_pairs={{1,0},{2,1},{3,2},{5,4},{6,5},{7,6},{9,8},{10,9},{11,10},{13,12},{... | collective-permute-start | bytes 663560 | tf_op jit(solution)/shard_map/ppermute | solution.py:138
  13.2 20.3 %collective-permute-start.2 = (f32[22,40,128]{2,1,0:T(8,128)S(1)}, f32[22,40,128]{2,1,0:T(8,128)S(1)}, u32[]{:S(2)}, u32[]{:S(2)}) collective-permute-start(f32[22,40,128]{2,1,0:T(8,128)S(1)} %get-tuple-element.32), channel_id=1, source_target_pairs={{0,4},{4,8},{8,12},{12,16},{16,20},{20,24},{24,28},{1,5},{5,9},{9,... | collective-permute-start | bytes 1351688 | tf_op jit(solution)/shard_map/ppermute | solution.py:137
  16.6 16.9 %collective-permute-start.3 = (f32[22,40,128]{2,1,0:T(8,128)S(1)}, f32[22,40,128]{2,1,0:T(8,128)S(1)}, u32[]{:S(2)}, u32[]{:S(2)}) collective-permute-start(f32[22,40,128]{2,1,0:T(8,128)S(1)} %get-tuple-element.33), channel_id=1, source_target_pairs={{4,0},{8,4},{12,8},{16,12},{20,16},{24,20},{28,24},{5,1},{9,5},{13... | collective-permute-start | bytes 1351688 | tf_op jit(solution)/shard_map/ppermute | solution.py:138
  19.6 20.9 %copy-start = (bf16[3,256,384]{2,1,0:T(8,128)(2,1)}, bf16[3,256,384]{2,1,0:T(8,128)(2,1)S(1)}, u32[]{:S(2)}) copy-start(bf16[3,256,384]{2,1,0:T(8,128)(2,1)S(1)} %get-tuple-element.34.fwd_hi) | copy-start | bytes 1769476
  19.6 20.9 %copy-start.3 = (bf16[3,256,384]{2,1,0:T(8,128)(2,1)}, bf16[3,256,384]{2,1,0:T(8,128)(2,1)S(1)}, u32[]{:S(2)}) copy-start(bf16[3,256,384]{2,1,0:T(8,128)(2,1)S(1)} %get-tuple-element.35.fwd_lo) | copy-start | bytes 1769476
  19.6 20.9 %copy-start.27 = (bf16[4,256,384]{2,1,0:T(8,128)(2,1)}, bf16[4,256,384]{2,1,0:T(8,128)(2,1)S(1)}, u32[]{:S(2)}) copy-start(bf16[4,256,384]{2,1,0:T(8,128)(2,1)S(1)} %get-tuple-element.36.bwd_hi) | copy-start | bytes 2359300
  19.6 20.8 %copy-start.30 = (bf16[4,256,384]{2,1,0:T(8,128)(2,1)}, bf16[4,256,384]{2,1,0:T(8,128)(2,1)S(1)}, u32[]{:S(2)}) copy-start(bf16[4,256,384]{2,1,0:T(8,128)(2,1)S(1)} %get-tuple-element.37.bwd_lo) | copy-start | bytes 2359300
  41.8 16.4 %copy-start.25 = (f32[3]{0:T(128)S(1)}, f32[3]{0:T(128)}, u32[]{:S(2)}) copy-start(f32[3]{0:T(128)} %steps.5) | copy-start | bytes 40
  41.8 16.4 %all-to-all-start = ((f32[32,1,128]{2,1,0:T(1,128)}), f32[32,1,128]{2,1,0:T(1,128)S(1)}, u32[]{:S(2)}, u32[]{:S(2)}) async-start(f32[32,1,128]{2,1,0:T(1,128)} %bitcast.2), calls=%async_computation | async-start | bytes 32768 | tf_op jit(solution)/shard_map/all_to_all | solution.py:500
  51.1 1.1 %copy-start.28 = (bf16[4,256,384]{2,1,0:T(8,128)(2,1)S(1)}, bf16[4,256,384]{2,1,0:T(8,128)(2,1)}, u32[]{:S(2)}) copy-start(bf16[4,256,384]{2,1,0:T(8,128)(2,1)} %copy-done.27) | copy-start | bytes 2359300
  52.2 1.1 %copy-start.31 = (bf16[4,256,384]{2,1,0:T(8,128)(2,1)S(1)}, bf16[4,256,384]{2,1,0:T(8,128)(2,1)}, u32[]{:S(2)}) copy-start(bf16[4,256,384]{2,1,0:T(8,128)(2,1)} %copy-done.30) | copy-start | bytes 2359300
  58.2 1.1 copy-start.1
  59.3 1.1 copy-start.4
  69.9 11.2 %all-to-all-start.1 = ((f32[32,1,128]{2,1,0:T(1,128)}), f32[32,1,128]{2,1,0:T(1,128)S(1)}, u32[]{:S(2)}, u32[]{:S(2)}) async-start(f32[32,1,128]{2,1,0:T(1,128)} %bitcast.5), calls=%async_computation.1 | async-start | bytes 32768 | tf_op jit(solution)/shard_map/all_to_all | solution.py:500
  74.0 1.1 %copy-start.16 = (f32[3,18,24,128]{3,2,1,0:T(8,128)S(1)}, f32[3,18,24,128]{3,2,1,0:T(8,128)}, u32[]{:S(2)}) copy-start(f32[3,18,24,128]{3,2,1,0:T(8,128)} %copy-done.15) | copy-start | bytes 1990660
  75.1 1.1 %copy-start.29 = (bf16[4,256,384]{2,1,0:T(8,128)(2,1)S(1)}, bf16[4,256,384]{2,1,0:T(8,128)(2,1)}, u32[]{:S(2)}) copy-start(bf16[4,256,384]{2,1,0:T(8,128)(2,1)} %copy-done.27) | copy-start | bytes 2359300
  76.2 1.1 %copy-start.32 = (bf16[4,256,384]{2,1,0:T(8,128)(2,1)S(1)}, bf16[4,256,384]{2,1,0:T(8,128)(2,1)}, u32[]{:S(2)}) copy-start(bf16[4,256,384]{2,1,0:T(8,128)(2,1)} %copy-done.30) | copy-start | bytes 2359300
  81.2 1.1 copy-start.2
  82.2 1.1 copy-start.5
  85.2 1.1 %copy-start.17 = (f32[3,18,24,128]{3,2,1,0:T(8,128)S(1)}, f32[3,18,24,128]{3,2,1,0:T(8,128)}, u32[]{:S(2)}) copy-start(f32[3,18,24,128]{3,2,1,0:T(8,128)} %copy-done.15) | copy-start | bytes 1990660
  86.3 1.1 %copy-start.19 = (f32[3,18,24,128]{3,2,1,0:T(8,128)S(1)}, f32[3,18,24,128]{3,2,1,0:T(8,128)}, u32[]{:S(2)}) copy-start(f32[3,18,24,128]{3,2,1,0:T(8,128)} %copy-done.18) | copy-start | bytes 1990660
  87.4 1.1 %copy-start.21 = (f32[3,18,24,128]{3,2,1,0:T(8,128)S(1)}, f32[3,18,24,128]{3,2,1,0:T(8,128)}, u32[]{:S(2)}) copy-start(f32[3,18,24,128]{3,2,1,0:T(8,128)} %copy-done.20) | copy-start | bytes 1990660
  (15 other events, 12.9 us)

commit v3 on v2

v3 whole, which is shorter than its diff:
```python
import functools
import math

import jax
import jax.numpy as jnp
from jax import lax
from jax.experimental import pallas as pl
from jax.experimental.pallas import tpu as pltpu
from jax.sharding import PartitionSpec as P

CH = 64
LAYERS = 4
ITERS = 3
EPS = 1e-06
LANES = 2 * CH
HALO_PAIRS = 3
WIDE = 5
EDGE = 4
F32 = jnp.float32
BF16 = jnp.bfloat16

ROWS_SENT = (5, 5, 5, 4, 4, 4, 4, 3, 3)
ROW_START = tuple(sum(ROWS_SENT[:m]) for m in range(9))
SENT = 40
NEAR = (0, 1, 2, 8)

VMEM = pl.BlockSpec(memory_space=pltpu.VMEM)
SMEM = pl.BlockSpec(memory_space=pltpu.SMEM)
HBM = pl.BlockSpec(memory_space=pltpu.HBM)


def call(body, outs, scratch, operands, flops, mem=20, scalars=(), far=(), far_outs=()):
    specs = [SMEM if j in scalars else HBM if j in far else VMEM for j in range(len(operands))]
    out_specs = tuple(HBM if j in far_outs else VMEM for j in range(len(outs)))
    return pl.pallas_call(
        body,
        out_shape=outs,
        in_specs=specs,
        out_specs=out_specs,
        scratch_shapes=scratch,
        compiler_params=pltpu.CompilerParams(vmem_limit_bytes=mem << 20),
        cost_estimate=pl.CostEstimate(flops=flops, bytes_accessed=4 << 20, transcendentals=0),
    )(*operands)


def shape(*dims, dtype=F32):
    return jax.ShapeDtypeStruct(dims, dtype)


def copies(pairs, sem):
    made = [pltpu.make_async_copy(src, dst, sem.at[j]) for j, (src, dst) in enumerate(pairs)]
    for one in made:
        one.start()
    return made


def finish(made):
    for one in made:
        one.wait()


def split(value):
    high = value.astype(BF16)
    return high, (value - high.astype(F32)).astype(BF16)


def weights_body(kernels, biases, fwd_out, bwd_out, bias2, fwd, bwd, sem):
    zero = jnp.zeros((CH, CH), F32)

    def put(dest, k, j, dh, first, second):
        block = jnp.concatenate([first, second], axis=1)
        for part, value in enumerate(split(block)):
            dest[part, k, pl.ds(CH * j, CH), pl.ds(LANES * dh, LANES)] = value

    for k in range(LAYERS):
        for dh in range(3):
            taps = [kernels[k * 9 + dh * 3 + dw] for dw in range(3)]
            if k < LAYERS - 1:
                for j in range(4):
                    put(fwd, k, j, dh, taps[j] if j < 3 else zero, taps[j - 1] if j > 0 else zero)
            flips = [tap.T for tap in taps]
            for j in range(4):
                put(bwd, k, j, 2 - dh, flips[2 - j] if j < 3 else zero, flips[3 - j] if j > 0 else zero)
    for k in range(LAYERS):
        row = biases[k : k + 1, :]
        bias2[k : k + 1, :] = jnp.concatenate([row, row], axis=1)
    finish(copies([(fwd, fwd_out), (bwd, bwd_out)], sem))


FWD = (2, LAYERS - 1, 4 * CH, 3 * LANES)
BWD = (2, LAYERS, 4 * CH, 3 * LANES)


def weights(kernels, biases):
    return call(
        weights_body,
        (shape(*FWD, dtype=BF16), shape(*BWD, dtype=BF16), shape(8, LANES)),
        [pltpu.VMEM(FWD, BF16), pltpu.VMEM(BWD, BF16), pltpu.SemaphoreType.DMA((2,))],
        (kernels.reshape(LAYERS * 9, CH, CH), biases),
        1 << 22,
        far_outs=(0, 1),
    )


def sources(objective, center, radius, lower, upper):
    return [
        lambda cols: center[:, cols].astype(F32),
        lambda cols: upper[0, :, cols].astype(F32),
        lambda cols: upper[1, :, cols].astype(F32),
        lambda cols: upper[2, :, cols].astype(F32),
        lambda cols: lower[0, :, cols].astype(F32),
        lambda cols: lower[1, :, cols].astype(F32),
        lambda cols: lower[2, :, cols].astype(F32),
        lambda cols: radius[:, cols].astype(F32),
        lambda cols: objective[:, cols],
    ]


def sides_body(objective, center, radius, lower, upper, head, tail, *rest):
    rows, cols = objective.shape
    strip = HALO_PAIRS * LANES
    ends, sem = rest[:-1], rest[-1]
    moves = []
    for side, at in enumerate((0, cols - strip)):
        here = pl.ds(at, strip)
        five = ends[5 * side : 5 * side + 5]
        moves += [
            (objective.at[:, here], five[0]),
            (center.at[:, here], five[1]),
            (radius.at[:, here], five[2]),
            (lower.at[:, :, here], five[3]),
            (upper.at[:, :, here], five[4]),
        ]
    finish(copies(moves, sem))
    for side, out in enumerate((head, tail)):
        for m, read in enumerate(sources(*ends[5 * side : 5 * side + 5])):
            out[pl.ds(m * rows, rows), :] = read(slice(None))


def column(reads, left, right, rows, pairs, m, q):
    if q < HALO_PAIRS:
        return left[m * rows : (m + 1) * rows, q * LANES : (q + 1) * LANES]
    if q >= HALO_PAIRS + pairs:
        q -= HALO_PAIRS + pairs
        return right[m * rows : (m + 1) * rows, q * LANES : (q + 1) * LANES]
    return reads[m](pl.ds((q - HALO_PAIRS) * LANES, LANES))


def ends_body(objective, center, radius, lower, upper, left, right, near_top, near_bottom, top, bottom):
    rows, cols = objective.shape
    pairs = cols // LANES
    reads = sources(objective, center, radius, lower, upper)
    for m in range(9):
        sent = ROWS_SENT[m]
        here = slice(ROW_START[m], ROW_START[m] + sent)
        for q in range(pairs + 2 * HALO_PAIRS):
            value = column(reads, left, right, rows, pairs, m, q)
            top[q, here, :] = value[:sent]
            bottom[q, here, :] = value[rows - sent :]
            if m in NEAR and HALO_PAIRS - 1 <= q <= HALO_PAIRS + pairs:
                row = NEAR.index(m)
                near_top[q - HALO_PAIRS + 1, row : row + 1, :] = value[:1]
                near_bottom[q - HALO_PAIRS + 1, row : row + 1, :] = value[rows - 1 :]
    spare = slice(sum(ROWS_SENT), SENT)
    blank = jnp.zeros((pairs + 2 * HALO_PAIRS, SENT - sum(ROWS_SENT), LANES), F32)
    top[:, spare, :] = blank
    bottom[:, spare, :] = blank


def neighbours(head, tail, axis):
    count = lax.axis_size(axis)
    before = lax.ppermute(tail, axis, [(i, i + 1) for i in range(count - 1)])
    after = lax.ppermute(head, axis, [(i + 1, i) for i in range(count - 1)])
    return before, after


def roll_rows(value, shift):
    return pltpu.roll(value, shift % value.shape[0], 0)


def slide(maps, count, store, produce):
    rows = store.shape[2]
    early = lax.broadcasted_iota(jnp.int32, (rows, LANES), 1) < CH
    zero = jnp.zeros((rows, LANES), F32)

    def step(q, carry):
        fresh = [pltpu.roll(value, CH, 1) for value in produce(q)]
        for k in range(maps):
            store[k, q] = jnp.where(early, carry[k], fresh[k])
        return tuple(fresh)

    last = lax.fori_loop(0, count, step, (zero,) * maps)
    for k in range(maps):
        store[k, count] = jnp.where(early, last[k], zero)


def multiply(store, k, first, count, weight, layer, sums, exact=False):
    rows = store.shape[2]
    left = store[k, pl.ds(first, count)].reshape(count * rows, LANES)
    right = store[k, pl.ds(first + 1, count)].reshape(count * rows, LANES)
    window = jnp.concatenate([left, right], axis=1)
    dot = functools.partial(jnp.dot, preferred_element_type=F32)
    high, low = split(window)
    result = dot(high, weight[0, layer]) + dot(high, weight[1, layer])
    if not exact:
        result = result + dot(low, weight[0, layer])
    for d in range(3):
        sums[k, d, pl.ds(0, count)] = result[:, d * LANES : (d + 1) * LANES].reshape(count, rows, LANES)


def gathered(sums, k, q):
    return roll_rows(sums[k, 0, q], 1) + sums[k, 1, q] + roll_rows(sums[k, 2, q], -1)


def inner(sums, k, q, first, rows):
    parts = [roll_rows(sums[k, d, q], 1 - d - first)[:rows] for d in range(3)]
    return parts[0] + parts[1] + parts[2]


def summed(total):
    return jnp.sum(total[...], axis=0, keepdims=True)


def scale_of(total, step, cells, dims):
    squares = summed(total)[:, 0:1]
    return jnp.broadcast_to(step / jnp.sqrt(squares / (2 * (LAYERS - 1) * cells) + EPS), dims)


def soft(top, t):
    return 0.5 * top * (1.0 - jnp.tanh(t))


class Bound:
    def __init__(self, start):
        self.linear = start
        self.factor = None

    def add(self, t):
        self.linear = self.linear - jnp.maximum(-t, 0.0)
        factor = 1.0 + jnp.exp(-2.0 * jnp.abs(t))
        self.factor = factor if self.factor is None else self.factor * factor

    def total(self):
        return self.linear - 0.5 * jnp.log(self.factor)


def folded(value):
    return jnp.sum(value, axis=0, keepdims=True)


def own_rows(value):
    rows = value.shape[0]
    row = lax.broadcasted_iota(jnp.int32, value.shape, 0)
    return folded(jnp.where((row >= EDGE) & (row < rows - EDGE), value, 0.0))


def stats(out, rows):
    lane = lax.broadcasted_iota(jnp.int32, (1, LANES), 1)
    packed = jnp.zeros((1, LANES), F32)
    for j, row in enumerate(rows):
        packed = jnp.where(lane == j, jnp.sum(row, axis=1, keepdims=True), packed)
    out[...] = jnp.broadcast_to(packed, out.shape)


def own_body(
    objective, center, radius, lower, upper, left, right, above, below, fwd_far, bwd_far, bias,
    stat,
    raw, store, sums, fwd, bwd, sem,
):
    arrivals = copies([(fwd_far, fwd), (bwd_far.at[:, LAYERS - 1], bwd.at[:, 0])], sem)
    rows, cols = objective.shape
    pairs = cols // LANES
    frame = raw.shape[2]
    reads = sources(objective, center, radius, lower, upper)
    for row, m in enumerate(NEAR):
        for q in range(pairs + 2):
            raw[row, q, 0:1, :] = above[q, row : row + 1, :]
            raw[row, q, 1 : rows + 1, :] = column(reads, left, right, rows, pairs, m, q + HALO_PAIRS - 1)
            raw[row, q, rows + 1 : rows + 2, :] = below[q, row : row + 1, :]
    raw[:, :, rows + 2 :, :] = jnp.zeros((4, pairs + 2, frame - rows - 2, LANES), F32)
    slide(4, pairs + 2, store, lambda q: [raw[0, q], 0.5 * raw[1, q], 0.5 * raw[2, q], raw[3, q]])
    finish(arrivals)
    for k in range(3):
        multiply(store, k, 1, pairs, fwd, k, sums, exact=True)
    multiply(store, 3, 1, pairs, bwd, 0, sums)

    def step(q, squares):
        here = pl.ds(pl.multiple_of(q * LANES, LANES), LANES)
        for k in range(3):
            gap = upper[k, :, here].astype(F32)
            low = lower[k, :, here].astype(F32)
            dl = 0.5 * (gap - low) - inner(sums, k, q, 1, rows) - bias[k : k + 1, :]
            squares = squares + dl * dl
        dm = 0.5 * gap * jnp.tanh(inner(sums, 3, q, 1, rows) * gap)
        return squares + dm * dm

    squares = lax.fori_loop(0, pairs, step, jnp.zeros((rows, LANES), F32))
    stats(stat, [folded(squares)])


def wide_body(
    objective, center, radius, lower, upper, left, right, above, below, fwd_far, bwd_far, bias, after,
    near_box, far_box, back, slope_out, mult, pull, value,
    raw, gaps, target, slope, store, sums, fwd, bwd, sem,
):
    del after
    arrivals = copies([(fwd_far, fwd), (bwd_far, bwd)], sem)
    rows, cols = objective.shape
    pairs = cols // LANES
    frame = rows + 2 * EDGE
    wide = pairs + 4
    reads = sources(objective, center, radius, lower, upper)
    for m in range(9):
        sent = ROWS_SENT[m]
        here = slice(ROW_START[m], ROW_START[m] + sent)
        for q in range(pairs + 2 * HALO_PAIRS):
            if m >= 3 and not 1 <= q < wide + 1:
                continue
            own = column(reads, left, right, rows, pairs, m, q)
            if m < 3:
                dest, at, edge = raw.at[m, q], 0, WIDE
            else:
                dest, at, edge = (target.at[q - 1] if m == 8 else gaps.at[m - 3, q - 1]), EDGE - sent, EDGE
                if at:
                    dest[0:EDGE, :] = jnp.zeros((EDGE, LANES), F32)
                    dest[EDGE + rows : frame, :] = jnp.zeros((EDGE, LANES), F32)
            dest[at : at + sent, :] = above[q, here, :]
            dest[edge : edge + rows, :] = own
            dest[edge + rows : edge + rows + sent, :] = below[q, here, :]
    raw[:, :, rows + 2 * WIDE :, :] = jnp.zeros((3, wide + 2, raw.shape[2] - rows - 2 * WIDE, LANES), F32)

    slide(3, wide + 2, store, lambda q: [raw[0, q], 0.5 * raw[1, q], 0.5 * raw[2, q]])
    finish(arrivals)
    for k in range(3):
        multiply(store, k, 1, wide, fwd, k, sums, exact=True)

    def slopes(q, carry):
        near = [raw[m, q + 1][1 : 1 + frame] for m in range(3)] + [gaps[4, q]]
        far = [gaps[m, q] for m in range(4)]
        for m in range(4):
            near_box[m, q] = near[m].astype(BF16)
            far_box[m, q] = far[m].astype(BF16)
        for k in range(3):
            gap = near[1 + k] if k < 2 else far[0]
            dl = 0.5 * (gap - far[1 + k]) - inner(sums, k, q, 1, frame) - bias[k : k + 1, :]
            slope[k, q] = jnp.where(gap > 0.0, dl, 0.0)
        return carry

    lax.fori_loop(0, wide, slopes, 0)
    slope_out[...] = slope[:, 1 : wide - 1]

    def produce(q):
        return [slope[k, q] for k in range(3)] + [target[q]]

    window = store.at[:, :, 0:frame, :]
    slide(4, wide, window, produce)
    short = sums.at[:, :, :, 0:frame, :]
    for k in range(4):
        multiply(window, k, 0, wide, bwd, k, short)

    zero = jnp.zeros((frame, LANES), F32)

    def pulls(q, carry):
        worth, fixed = carry
        for k in range(3):
            pull[k, q] = gathered(short, k, q)
        tug = gathered(short, 3, q)
        back[q] = tug
        gap = gaps[0, q]
        t = tug * gap
        mult[q] = -0.5 * gap * jnp.tanh(t)
        bound = Bound(jnp.full((frame, LANES), -4.5 * math.log(2.0), F32))
        bound.add(t)
        own = (q >= 2) & (q < wide - 2)
        worth = worth + jnp.where(own, bound.total(), 0.0)
        fixed = fixed + jnp.where(own, target[q] * bias[3:4, :], 0.0)
        return worth, fixed

    worth, fixed = lax.fori_loop(0, wide, pulls, (zero, zero))
    fixed = own_rows(fixed)
    stats(value, [own_rows(worth) + fixed, fixed])


def second_body(
    total, steps, near_box, far_box, back, slope, mult, pull, fwd_far, bias,
    base, slope_out, mult_out, duals, last_mult, last_slope, last_pull, stat,
    points, store, sums, fwd, sem, *, cells,
):
    arrivals = copies([(fwd_far, fwd)], sem)
    wide, frame = near_box.shape[1:3]
    inside = slice(EDGE, frame - EDGE)
    scale = scale_of(total, steps[0], cells, (frame, LANES))
    zero = jnp.zeros((frame, LANES), F32)

    def produce(q):
        center, radius = near_box[0, q].astype(F32), near_box[3, q].astype(F32)
        g = -(scale * pull[0, q])
        base[0, q] = g
        outs = [center - radius * jnp.tanh(2.0 * radius * g)]
        for k in (1, 2):
            gap = near_box[k, q].astype(F32)
            g = -(scale * pull[k, q])
            base[k, q] = g
            x = soft(gap, g * gap)
            points[k - 1, q] = x
            outs.append(x)
        return outs

    slide(3, wide, store, produce)
    finish(arrivals)
    for k in range(3):
        multiply(store, k, 1, wide - 2, fwd, k, sums)

    def step(j, squares):
        q = j + 1
        new = zero
        for k in range(3):
            gap = (near_box[1 + k, q] if k < 2 else far_box[0, q]).astype(F32)
            low = far_box[1 + k, q].astype(F32)
            lam = scale * slope[k, j]
            if k < 2:
                x = points[k, q]
                positive = soft(gap, lam * gap)
            else:
                mu = scale * mult[q]
                g = back[q] + mu
                x = soft(gap, g * gap)
                positive = soft(gap, (lam - mu) * gap)
            dl = positive - soft(low, -lam * low) - gathered(sums, k, j) - bias[k : k + 1, :]
            dl = jnp.where(gap > 0.0, dl, 0.0)
            dm = x - positive
            slope_out[k, j] = dl
            duals[k, j] = lam[inside]
            if k < 2:
                mult_out[k, j] = dm
            else:
                last_mult[j] = mu[inside]
                last_slope[j] = dm[inside]
                last_pull[j] = g[inside]
            new = new + dl * dl + dm * dm
        own = (q >= 2) & (q < wide - 2)
        return squares + jnp.where(own, new, 0.0)

    squares = lax.fori_loop(0, wide - 2, step, zero)
    stats(stat, [own_rows(squares)])


def pulled_body(
    slope, bwd_far, center_far, radius_far, lower_far, upper_far, base, duals, last_mult, last_pull, bias,
    pull, value,
    store, sums, bwd, center, radius, lower, upper, sem,
):
    arrivals = copies(
        [
            (bwd_far.at[:, 0 : LAYERS - 1], bwd),
            (center_far, center),
            (radius_far, radius),
            (lower_far, lower),
            (upper_far, upper),
        ],
        sem,
    )
    count, frame = slope.shape[1:3]
    rows = frame - 2 * EDGE
    inside = slice(EDGE, frame - EDGE)
    slide(3, count, store, lambda q: [slope[k, q] for k in range(3)])
    finish(arrivals)
    for k in range(3):
        multiply(store, k, 0, count, bwd, k, sums)

    def step(q, carry):
        for k in range(3):
            pull[k, q] = gathered(sums, k, q)
        return carry

    lax.fori_loop(0, count, step, 0)

    def worth_of(i, worth):
        j, q = i + 1, i + 2
        here = pl.ds(pl.multiple_of(i * LANES, LANES), LANES)
        spread = radius[:, here].astype(F32)
        g = base[0, q, inside, :]
        bound = Bound(g * (center[:, here].astype(F32) - spread))
        bound.add(2.0 * g * spread)
        for k in range(3):
            gap = upper[k, :, here].astype(F32)
            lam = duals[k, j]
            if k < 2:
                bound.add(base[k + 1, q, inside, :] * gap)
                bound.add(lam * gap)
            else:
                bound.add(last_pull[j] * gap)
                bound.add((lam - last_mult[j]) * gap)
            bound.add(-lam * lower[k, :, here].astype(F32))
            bound.linear = bound.linear - lam * bias[k : k + 1, :]
        return worth + bound.total()

    worth = lax.fori_loop(0, count - 2, worth_of, jnp.zeros((rows, LANES), F32))
    stats(value, [folded(worth)])


def third_body(
    total, steps, near_box, base, pull, mult, slope, duals1, last_mult, last_slope, last_pull,
    fwd_far, lower_far, upper_far, bias, value0, value1,
    duals, multipliers, slope_out, mult_out, stat,
    points, store, sums, fwd, lower, upper, sem, *, cells,
):
    arrivals = copies([(fwd_far, fwd), (lower_far, lower), (upper_far, upper)], sem)
    wide, frame = near_box.shape[1:3]
    rows = frame - 2 * EDGE
    inside = slice(EDGE, frame - EDGE)
    scale = scale_of(total, steps[1], cells, (frame, LANES))
    zero = jnp.zeros((frame, LANES), F32)

    def body(j, worth):
        q = j + 1
        center, radius = near_box[0, q].astype(F32), near_box[3, q].astype(F32)
        g = base[0, q] - scale * pull[0, j]
        bound = Bound(g * (center - radius))
        t = 2.0 * radius * g
        bound.add(t)
        outs = [center - radius * jnp.tanh(t)]
        for k in (1, 2):
            gap = near_box[k, q].astype(F32)
            t = (base[k, q] + scale * (mult[k - 1, j] - pull[k, j])) * gap
            bound.add(t)
            x = soft(gap, t)
            points[k - 1, j] = x
            outs.append(x)
        own = (q >= 2) & (q < wide - 2)
        return outs, worth + jnp.where(own, bound.total(), 0.0)

    early = lax.broadcasted_iota(jnp.int32, (frame, LANES), 1) < CH

    def first(j, carry):
        outs, worth = body(j, carry[3])
        fresh = [pltpu.roll(value, CH, 1) for value in outs]
        for k in range(3):
            store[k, j] = jnp.where(early, carry[k], fresh[k])
        return tuple(fresh) + (worth,)

    framed = lax.fori_loop(0, wide - 2, first, (zero,) * 4)[3]
    finish(arrivals)
    for k in range(3):
        multiply(store, k, 1, wide - 4, fwd, k, sums)

    scale = scale[:rows]

    def step(i, carry):
        squares, worth = carry
        j = i + 1
        here = pl.ds(pl.multiple_of(i * LANES, LANES), LANES)
        bound = None
        for k in range(3):
            gap = upper[k, :, here].astype(F32)
            low = lower[k, :, here].astype(F32)
            lam = duals1[k, j] + scale * slope[k, j, inside, :]
            if bound is None:
                bound = Bound(-lam * bias[k : k + 1, :])
            else:
                bound.linear = bound.linear - lam * bias[k : k + 1, :]
            if k < 2:
                x = points[k, j, inside, :]
                mu = scale * mult[k, j, inside, :]
            else:
                change = scale * last_slope[j]
                mu = last_mult[j] + change
                t = (last_pull[j] + change) * gap
                x = soft(gap, t)
                bound.add(t)
            tp = (lam - mu) * gap
            tn = -lam * low
            bound.add(tp)
            bound.add(tn)
            positive = soft(gap, tp)
            dl = positive - soft(low, tn) - inner(sums, k, i, EDGE, rows) - bias[k : k + 1, :]
            dm = x - positive
            duals[k, :, here] = lam
            multipliers[k, :, here] = mu
            slope_out[k, :, here] = dl
            mult_out[k, :, here] = dm
            squares = squares + dl * dl + dm * dm
        return squares, worth + bound.total()

    zero = jnp.zeros((rows, LANES), F32)
    squares, worth = lax.fori_loop(0, wide - 4, step, (zero, zero))
    lane = lax.broadcasted_iota(jnp.int32, (1, LANES), 1)
    start, fixed = (jnp.where(lane == j, value0[0:1, :], 0.0) for j in range(2))
    middle = jnp.where(lane == 0, value1[0:1, :], 0.0)
    stats(stat, [folded(squares), start, middle + fixed, folded(worth) + own_rows(framed) + fixed])


def last_body(total, steps, duals, multipliers, slope, mult, bounds, duals_out, mult_out, *, cells):
    scale = scale_of(total, steps[2], cells, duals.shape[1:])
    for k in range(LAYERS - 1):
        duals_out[k] = duals[k] + scale * slope[k]
        mult_out[k] = multipliers[k] + scale * mult[k]
    bounds[...] = jnp.broadcast_to(summed(total) / cells, bounds.shape)


def everyone(partial):
    return lax.all_to_all(partial, ("row", "col"), 0, 0, tiled=True)


def shards(objective, center, radius, lower, upper, kernels, biases, steps):
    rows, cols = objective.shape
    pairs = cols // LANES
    wide = pairs + 4
    frame = rows + 2 * EDGE
    tall = -(-(rows + 2 * WIDE) // 8) * 8
    low = -(-(rows + 2) // 8) * 8
    cells = rows * cols * lax.axis_size("row") * lax.axis_size("col")
    inputs = (objective, center, radius, lower, upper)
    flops = 3 * 2 * 3 * wide * frame * 4 * CH * 3 * LANES
    dma = pltpu.SemaphoreType.DMA
    spread = shape(lax.axis_size("row") * lax.axis_size("col"), LANES)
    small = shape(8, LANES)

    strip = HALO_PAIRS * LANES
    five = [
        pltpu.VMEM((rows, strip), F32),
        pltpu.VMEM((rows, strip), BF16),
        pltpu.VMEM((rows, strip), BF16),
        pltpu.VMEM((3, rows, strip), BF16),
        pltpu.VMEM((3, rows, strip), BF16),
    ]
    head, tail = call(
        sides_body,
        (shape(9 * rows, strip), shape(9 * rows, strip)),
        five + five + [dma((10,))],
        inputs,
        1 << 20,
        far=range(5),
    )
    left, right = neighbours(head, tail, "col")
    fwd, bwd, bias = weights(kernels, biases)
    near = shape(pairs + 2, len(NEAR), LANES)
    strip = shape(pairs + 2 * HALO_PAIRS, SENT, LANES)
    near_top, near_bottom, top, bottom = call(
        ends_body, (near, near, strip, strip), [], inputs + (left, right), 1 << 20
    )
    near_above, near_below = neighbours(near_top, near_bottom, "row")
    above, below = neighbours(top, bottom, "row")

    (stat0,) = call(
        own_body,
        (spread,),
        [
            pltpu.VMEM((4, pairs + 2, low, LANES), F32),
            pltpu.VMEM((4, pairs + 3, low, LANES), F32),
            pltpu.VMEM((4, 3, pairs, low, LANES), F32),
            pltpu.VMEM(FWD, BF16),
            pltpu.VMEM((2, 1) + BWD[2:], BF16),
            dma((2,)),
        ],
        inputs + (left, right, near_above, near_below, fwd, bwd, bias),
        flops,
        far=(9, 10),
    )
    total0 = everyone(stat0)
    near_box, far_box, back, slope0, mult0, pull0, value0 = call(
        wide_body,
        (
            shape(4, wide, frame, LANES, dtype=BF16),
            shape(4, wide, frame, LANES, dtype=BF16),
            shape(wide, frame, LANES),
            shape(3, wide - 2, frame, LANES),
            shape(wide, frame, LANES),
            shape(3, wide, frame, LANES),
            small,
        ),
        [
            pltpu.VMEM((3, wide + 2, tall, LANES), F32),
            pltpu.VMEM((5, wide, frame, LANES), F32),
            pltpu.VMEM((wide, frame, LANES), F32),
            pltpu.VMEM((3, wide, frame, LANES), F32),
            pltpu.VMEM((4, wide + 3, tall, LANES), F32),
            pltpu.VMEM((4, 3, wide, tall, LANES), F32),
            pltpu.VMEM(FWD, BF16),
            pltpu.VMEM(BWD, BF16),
            dma((2,)),
        ],
        inputs + (left, right, above, below, fwd, bwd, bias, stat0),
        2 * flops,
        mem=30,
        far=(9, 10),
    )

    tile = shape(wide - 2, rows, LANES)
    base, slope1, mult1, duals1, last_mult, last_slope, last_pull, stat1 = call(
        functools.partial(second_body, cells=cells),
        (
            shape(3, wide, frame, LANES),
            shape(3, wide - 2, frame, LANES),
            shape(2, wide - 2, frame, LANES),
            shape(3, wide - 2, rows, LANES),
            tile,
            tile,
            tile,
            spread,
        ),
        [
            pltpu.VMEM((2, wide, frame, LANES), F32),
            pltpu.VMEM((3, wide + 1, frame, LANES), F32),
            pltpu.VMEM((3, 3, wide - 2, frame, LANES), F32),
            pltpu.VMEM(FWD, BF16),
            dma((1,)),
        ],
        (total0, steps, near_box, far_box, back, slope0, mult0, pull0, fwd, bias),
        flops,
        scalars=(1,),
        far=(8,),
    )
    total1 = everyone(stat1)
    gaps = pltpu.VMEM((3, rows, cols), BF16)
    pull1, value1 = call(
        pulled_body,
        (shape(3, wide - 2, frame, LANES), small),
        [
            pltpu.VMEM((3, wide - 1, frame, LANES), F32),
            pltpu.VMEM((3, 3, wide - 2, frame, LANES), F32),
            pltpu.VMEM(FWD, BF16),
            pltpu.VMEM((rows, cols), BF16),
            pltpu.VMEM((rows, cols), BF16),
            gaps,
            gaps,
            dma((5,)),
        ],
        (slope1, bwd, center, radius, lower, upper, base, duals1, last_mult, last_pull, bias),
        flops,
        far=(1, 2, 3, 4, 5),
    )
    out = shape(3, rows, cols)
    duals, multipliers, slope2, mult2, stat2 = call(
        functools.partial(third_body, cells=cells),
        (out, out, out, out, spread),
        [
            pltpu.VMEM((2, wide - 2, frame, LANES), F32),
            pltpu.VMEM((3, wide - 1, frame, LANES), F32),
            pltpu.VMEM((3, 3, wide - 4, frame, LANES), F32),
            pltpu.VMEM(FWD, BF16),
            gaps,
            gaps,
            dma((3,)),
        ],
        (
            total1, steps, near_box, base, pull1, mult1, slope1, duals1, last_mult, last_slope, last_pull,
            fwd, lower, upper, bias, value0, value1,
        ),
        flops,
        scalars=(1,),
        far=(11, 12, 13),
    )
    total2 = everyone(stat2)
    bounds, final_duals, final_multipliers = call(
        functools.partial(last_body, cells=cells),
        (small, out, out),
        [],
        (total2, steps, duals, multipliers, slope2, mult2),
        1 << 20,
        scalars=(1,),
    )
    return bounds[0, 1 : 1 + ITERS], final_duals, final_multipliers


def solution(mesh):
    placed = (
        P("row", "col"),
        P("row", "col"),
        P("row", "col"),
        P(None, "row", "col"),
        P(None, "row", "col"),
        P(),
        P(),
        P(),
    )
    return jax.shard_map(
        shards,
        mesh=mesh,
        in_specs=placed,
        out_specs=(P(), P(None, "row", "col"), P(None, "row", "col")),
        check_vma=False,
    )
```

time: 109 us -> 136 us (1.25)
  local copies, waits for them, and re-layouts: 26.6 us -> 43.4 us
  starting transfers between devices: 21.7 us -> 30.1 us
  Pallas kernels: 26.6 us -> 33.2 us
  waiting for transfers between devices: 20 us -> 13.6 us
    unnamed x66 -> x120, local copies, waits for them, and re-layouts: 26 us -> 42.8 us
    pallas_call x9, Pallas kernels: 26.6 us -> 33.2 us  [call(): pl.pallas_call(body, out_shape=outs, in_specs=specs, out_specs=out_specs,...]
    ppermute x2 -> x3, starting transfers between devices: 5.79 us -> 11.2 us  [neighbours(): before = lax.ppermute(tail, axis, [(i, i + 1) for i in range(count - 1)])]
    ppermute x2 -> x3, waiting for transfers between devices: 13.9 us -> 9.44 us  [neighbours(): before = lax.ppermute(tail, axis, [(i, i + 1) for i in range(count - 1)])]
    all_to_all x2, waiting for transfers between devices: 1.94 us -> 0.01 us  [everyone(): return lax.all_to_all(partial, ('row', 'col'), 0, 0, tiled=True)]
    all_to_all x2, starting transfers between devices: 13.3 us -> 15.1 us  [everyone(): return lax.all_to_all(partial, ('row', 'col'), 0, 0, tiled=True)]
    ppermute x2 -> x3, starting transfers between devices: 2.58 us -> 3.86 us  [neighbours(): after = lax.ppermute(head, axis, [(i + 1, i) for i in range(count - 1)])]
    ppermute x2 -> x3, waiting for transfers between devices: 4.19 us -> 4.18 us  [neighbours(): after = lax.ppermute(head, axis, [(i + 1, i) for i in range(count - 1)])]
  transfers between devices with their start and end apart: 6 -> 8, of which waited for: 4 -> 2; matrix products, arithmetic and copies ran while one was open for 0% -> 0% of each run, Pallas kernels for 6% -> 15%
where the time goes in v3:
time: 136 us; the launch traced here: 134 us
  local copies, waits for them, and re-layouts  43.4 us (32%)
  Pallas kernels  33.2 us (24%)
  starting transfers between devices  30.1 us (22%)
  waiting for transfers between devices  13.6 us (10%)
  blocking collectives  12.8 us (9%)
    unnamed x120, local copies, waits for them, and re-layouts  42.8 us
    pallas_call x9, Pallas kernels, call(): pl.pallas_call(body, out_shape=outs, in_specs=specs, out_specs=out_specs,...  33.2 us
    all_to_all x2, starting transfers between devices, everyone(): return lax.all_to_all(partial, ('row', 'col'), 0, 0, tiled=True)  15.1 us
    all_to_all x1, blocking collectives, everyone(): return lax.all_to_all(partial, ('row', 'col'), 0, 0, tiled=True)  12.8 us
    ppermute x3, starting transfers between devices, neighbours(): before = lax.ppermute(tail, axis, [(i, i + 1) for i in range(count - 1)])  11.2 us
    ppermute x3, waiting for transfers between devices, neighbours(): before = lax.ppermute(tail, axis, [(i, i + 1) for i in range(count - 1)])  9.44 us
    ppermute x3, waiting for transfers between devices, neighbours(): after = lax.ppermute(head, axis, [(i + 1, i) for i in range(count - 1)])  4.18 us
    ppermute x3, starting transfers between devices, neighbours(): after = lax.ppermute(head, axis, [(i + 1, i) for i in range(count - 1)])  3.86 us
  transfers between devices with their start and end apart: 8, of which 2 were waited for; matrix products, arithmetic and copies ran while one was open for 0% of the time, Pallas kernels for 15%

profile of v3, /device:TPU:0, one launch (start us, length us, event | category | flops | bytes accessed | tf_op | source)
XLA Modules:
  0.0 134.1 jit_solution(7860089001182880306)
XLA Ops:
  5.3 2.5 %collective-permute-start = (f32[144,384]{1,0:T(8,128)S(1)}, f32[144,384]{1,0:T(8,128)S(1)}, u32[]{:S(2)}, u32[]{:S(2)}) collective-permute-start(f32[144,384]{1,0:T(8,128)S(1)} %get-tuple-element.37), channel_id=1, source_target_pairs={{0,1},{1,2},{2,3},{4,5},{5,6},{6,7},{8,9},{9,10},{10,11},{12,13},{... | collective-permute-start | bytes 663560 | tf_op jit(solution)/shard_map/ppermute | solution.py:172
  7.8 1.3 collective-permute-start.1
  9.2 4.2 %collective-permute-done.1.right = f32[144,384]{1,0:T(8,128)S(1)} collective-permute-done((f32[144,384]{1,0:T(8,128)S(1)}, f32[144,384]{1,0:T(8,128)S(1)}, u32[]{:S(2)}, u32[]{:S(2)}) %collective-permute-start.1) | collective-permute-done | bytes 221216 | tf_op jit(solution)/shard_map/ppermute | solution.py:173
  13.3 1.1 shard_map.104
  14.4 4.2 %collective-permute-start.4 = (f32[22,40,128]{2,1,0:T(8,128)}, f32[22,40,128]{2,1,0:T(8,128)}, u32[]{:S(2)}, u32[]{:S(2)}) collective-permute-start(f32[22,40,128]{2,1,0:T(8,128)} %get-tuple-element.44), channel_id=1, source_target_pairs={{0,4},{4,8},{8,12},{12,16},{16,20},{20,24},{24,28},{1,5},{5,9},{9,... | collective-permute-start | bytes 1351688 | tf_op jit(solution)/shard_map/ppermute | solution.py:172
  18.6 1.3 collective-permute-start.5
  19.9 4.5 %collective-permute-start.2 = (f32[18,4,128]{2,1,0:T(4,128)S(1)}, f32[18,4,128]{2,1,0:T(4,128)S(1)}, u32[]{:S(2)}, u32[]{:S(2)}) collective-permute-start(f32[18,4,128]{2,1,0:T(4,128)S(1)} %get-tuple-element.39), channel_id=1, source_target_pairs={{0,4},{4,8},{8,12},{12,16},{16,20},{20,24},{24,28},{1,5},{5,9},{9,... | collective-permute-start | bytes 110600 | tf_op jit(solution)/shard_map/ppermute | solution.py:172
  24.4 1.3 collective-permute-start.3
  25.8 1.3 shard_map.105
  27.1 9.4 %collective-permute-done.2.above = f32[18,4,128]{2,1,0:T(4,128)S(1)} collective-permute-done((f32[18,4,128]{2,1,0:T(4,128)S(1)}, f32[18,4,128]{2,1,0:T(4,128)S(1)}, u32[]{:S(2)}, u32[]{:S(2)}) %collective-permute-start.2) | collective-permute-done | bytes 36896 | tf_op jit(solution)/shard_map/ppermute | solution.py:172
  36.5 4.1 %shard_map.106.after = f32[32,128]{1,0:T(8,128)} custom-call(f32[16,2048]{1,0:T(8,128)S(1)} %copy-done.17, bf16[16,2048]{1,0:T(8,128)(2,1)S(1)} %copy-done.19, bf16[16,2048]{1,0:T(8,128)(2,1)S(1)} %copy-done.21, bf16[3,16,2048]{2,1,0:T(8,128)(2,1)S(1)} %copy-done.1, bf16[3,16,2048]{2,1,0:T(8,128)(2,1)S(1)} %copy-done.3, ...), custom_call_target="tpu_custom_call" | custom-call | flops 849346560 | bytes 4194304 | tf_op jit(solution)/shard_map/pallas_call | solution.py:35
  40.7 9.2 %all-to-all-start = ((f32[32,1,128]{2,1,0:T(1,128)}), f32[32,1,128]{2,1,0:T(1,128)S(1)}, u32[]{:S(2)}, u32[]{:S(2)}) async-start(f32[32,1,128]{2,1,0:T(1,128)} %bitcast.2), calls=%async_computation | async-start | bytes 32768 | tf_op jit(solution)/shard_map/all_to_all | solution.py:602
  51.9 9.6 %shard_map.107 = (bf16[4,20,24,128]{3,2,1,0:T(8,128)(2,1)S(1)}, bf16[4,20,24,128]{3,2,1,0:T(8,128)(2,1)S(1)}, f32[20,24,128]{2,1,0:T(8,128)S(1)}, f32[3,18,24,12...) custom-call(f32[16,2048]{1,0:T(8,128)S(1)} %copy-done.17, ...), custom_call_target="tpu_custom_call" | custom-call | flops 1698693120 | bytes 4194304 | tf_op jit(solution)/shard_map/pallas_call | solution.py:35
  68.4 1.1 copy-done.28
  69.6 1.1 copy-done.32
  75.6 5.4 %shard_map.108 = (f32[3,20,24,128]{3,2,1,0:T(8,128)S(1)}, f32[3,18,24,128]{3,2,1,0:T(8,128)S(1)}, f32[2,18,24,128]{3,2,1,0:T(8,128)S(1)}, f32[3,18,16,128]{3,2,1...) custom-call(f32[32,128]{1,0:T(8,128)S(1)} %bitcast.16, ...), custom_call_target="tpu_custom_call" | custom-call | flops 849346560 | bytes 4194304 | tf_op jit(solution)/shard_map/pallas_call | solution.py:35
  85.7 5.8 %all-to-all-start.1 = ((f32[32,1,128]{2,1,0:T(1,128)}), f32[32,1,128]{2,1,0:T(1,128)S(1)}, u32[]{:S(2)}, u32[]{:S(2)}) async-start(f32[32,1,128]{2,1,0:T(1,128)} %bitcast.5), calls=%async_computation.1 | async-start | bytes 32768 | tf_op jit(solution)/shard_map/all_to_all | solution.py:602
  91.5 1.1 copy-done.5
  92.6 1.1 copy-done.8
  95.6 4.5 %shard_map.109 = (f32[3,18,24,128]{3,2,1,0:T(8,128)S(1)}, f32[8,128]{1,0:T(8,128)S(1)}) custom-call(f32[3,18,24,128]{3,2,1,0:T(8,128)S(1)} %copy-done.8, bf16[2,4,256,384]{3,2,1,0:T(8,128)(2,1)S(1)} %get-tuple-element.42.bwd_far, bf16[16,2048]{1,0:T(8,128)(2,1)S(1)} %copy-done.20, bf16[16,2048]{1,0:T(8,128)(2,1)S(1)} %copy-done.22, ...), custom_call_target="tpu_custom_call" | custom-call | flops 849346560 | bytes 4194304 | tf_op jit(solution)/shard_map/pallas_call | solution.py:35
  102.2 1.1 copy-done.6
  113.8 5.3 %shard_map.110 = (f32[3,16,2048]{2,1,0:T(8,128)S(1)}, f32[3,16,2048]{2,1,0:T(8,128)S(1)}, f32[3,16,2048]{2,1,0:T(8,128)S(1)}, f32[3,16,2048]{2,1,0:T(8,128)S(1)}, f32[32,128]{1,0:T(8,128)S(1)}) custom-call(f32[32,128]{1,0:T(8,128)S(1)} %bitcast.17, f32[3]{0:T(128)S(1)} %copy-done.54, bf16[4,20,24,128]{3,2,1,0:T(8,128)(2,1)S(1)} %copy-done.12, ...), custom_call_target="tpu_custom_call" | custom-call | flops 849346560 | bytes 4194304 | tf_op jit(solution)/shard_map/pallas_call | solution.py:35
  119.1 12.8 %all_to_all.33 = f32[32,1,128]{2,1,0:T(1,128)S(1)} all-to-all(f32[32,1,128]{2,1,0:T(1,128)S(1)} %bitcast.19), channel_id=1, replica_groups=mesh['row'=8,'col'=4] {'row','col'}, dimensions={0} | all-to-all | bytes 32768 | tf_op jit(solution)/shard_map/all_to_all | solution.py:602
  131.9 1.6 %shard_map.111 = (f32[8,128]{1,0:T(8,128)S(1)}, f32[3,16,2048]{2,1,0:T(8,128)}, f32[3,16,2048]{2,1,0:T(8,128)}) custom-call(f32[32,128]{1,0:T(8,128)S(1)} %bitcast.18, f32[3]{0:T(128)S(1)} %copy-done.54, f32[3,16,2048]{2,1,0:T(8,128)S(1)} %get-tuple-element.64.duals, f32[3,16,2048]{2,1,0:T(8,128)S(1)} %get-tuple-element.65.multipliers, ...), custom_call_target="tpu_custom_call" | custom-call | flops 1048576 | bytes 4194304 | tf_op jit(solution)/shard_map/pallas_call | solution.py:35
  (123 shorter events, 38.1 us)
Async XLA Ops:
  5.1 20.7 %copy-start.18 = (f32[4,3,3,64,64]{4,3,2,1,0:T(8,128)S(1)}, f32[4,3,3,64,64]{4,3,2,1,0:T(8,128)}, u32[]{:S(2)}) copy-start(f32[4,3,3,64,64]{4,3,2,1,0:T(8,128)} %param.13) | copy-start | bytes 1769476
  5.1 20.7 %copy-start.59 = (f32[4,64]{1,0:T(4,128)S(1)}, f32[4,64]{1,0:T(4,128)}, u32[]{:S(2)}) copy-start(f32[4,64]{1,0:T(4,128)} %biases.1) | copy-start | bytes 3076
  5.3 31.2 %copy-start.1 = (bf16[3,16,2048]{2,1,0:T(8,128)(2,1)S(1)}, bf16[3,16,2048]{2,1,0:T(8,128)(2,1)}, u32[]{:S(2)}) copy-start(bf16[3,16,2048]{2,1,0:T(8,128)(2,1)} %lower_far.3) | copy-start | bytes 589828
  5.3 31.2 %copy-start.3 = (bf16[3,16,2048]{2,1,0:T(8,128)(2,1)S(1)}, bf16[3,16,2048]{2,1,0:T(8,128)(2,1)}, u32[]{:S(2)}) copy-start(bf16[3,16,2048]{2,1,0:T(8,128)(2,1)} %upper_far.3) | copy-start | bytes 589828
  5.3 31.2 %copy-start.17 = (f32[16,2048]{1,0:T(8,128)S(1)}, f32[16,2048]{1,0:T(8,128)}, u32[]{:S(2)}) copy-start(f32[16,2048]{1,0:T(8,128)} %objective.7) | copy-start | bytes 393220
  5.3 3.8 %collective-permute-start = (f32[144,384]{1,0:T(8,128)S(1)}, f32[144,384]{1,0:T(8,128)S(1)}, u32[]{:S(2)}, u32[]{:S(2)}) collective-permute-start(f32[144,384]{1,0:T(8,128)S(1)} %get-tuple-element.37), channel_id=1, source_target_pairs={{0,1},{1,2},{2,3},{4,5},{5,6},{6,7},{8,9},{9,10},{10,11},{12,13},{... | collective-permute-start | bytes 663560 | tf_op jit(solution)/shard_map/ppermute | solution.py:172
  7.8 5.5 %collective-permute-start.1 = (f32[144,384]{1,0:T(8,128)S(1)}, f32[144,384]{1,0:T(8,128)S(1)}, u32[]{:S(2)}, u32[]{:S(2)}) collective-permute-start(f32[144,384]{1,0:T(8,128)S(1)} %get-tuple-element.38), channel_id=1, source_target_pairs={{1,0},{2,1},{3,2},{5,4},{6,5},{7,6},{9,8},{10,9},{11,10},{13,12},{... | collective-permute-start | bytes 663560 | tf_op jit(solution)/shard_map/ppermute | solution.py:173
  9.1 31.5 %copy-start.23 = (f32[144,384]{1,0:T(8,128)}, f32[144,384]{1,0:T(8,128)S(1)}, u32[]{:S(2)}) copy-start(f32[144,384]{1,0:T(8,128)S(1)} %collective-permute-done.left) | copy-start | bytes 663556
  13.3 27.3 %copy-start.25 = (f32[144,384]{1,0:T(8,128)}, f32[144,384]{1,0:T(8,128)S(1)}, u32[]{:S(2)}) copy-start(f32[144,384]{1,0:T(8,128)S(1)} %collective-permute-done.1.right) | copy-start | bytes 663556
  14.4 35.5 %collective-permute-start.4 = (f32[22,40,128]{2,1,0:T(8,128)}, f32[22,40,128]{2,1,0:T(8,128)}, u32[]{:S(2)}, u32[]{:S(2)}) collective-permute-start(f32[22,40,128]{2,1,0:T(8,128)} %get-tuple-element.44), channel_id=1, source_target_pairs={{0,4},{4,8},{8,12},{12,16},{16,20},{20,24},{24,28},{1,5},{5,9},{9,... | collective-permute-start | bytes 1351688 | tf_op jit(solution)/shard_map/ppermute | solution.py:172
  18.6 31.4 %collective-permute-start.5 = (f32[22,40,128]{2,1,0:T(8,128)}, f32[22,40,128]{2,1,0:T(8,128)}, u32[]{:S(2)}, u32[]{:S(2)}) collective-permute-start(f32[22,40,128]{2,1,0:T(8,128)} %get-tuple-element.45), channel_id=1, source_target_pairs={{4,0},{8,4},{12,8},{16,12},{20,16},{24,20},{28,24},{5,1},{9,5},{13... | collective-permute-start | bytes 1351688 | tf_op jit(solution)/shard_map/ppermute | solution.py:173
  19.9 16.6 %collective-permute-start.2 = (f32[18,4,128]{2,1,0:T(4,128)S(1)}, f32[18,4,128]{2,1,0:T(4,128)S(1)}, u32[]{:S(2)}, u32[]{:S(2)}) collective-permute-start(f32[18,4,128]{2,1,0:T(4,128)S(1)} %get-tuple-element.39), channel_id=1, source_target_pairs={{0,4},{4,8},{8,12},{12,16},{16,20},{20,24},{24,28},{1,5},{5,9},{9,... | collective-permute-start | bytes 110600 | tf_op jit(solution)/shard_map/ppermute | solution.py:172
  24.4 12.1 %collective-permute-start.3 = (f32[18,4,128]{2,1,0:T(4,128)S(1)}, f32[18,4,128]{2,1,0:T(4,128)S(1)}, u32[]{:S(2)}, u32[]{:S(2)}) collective-permute-start(f32[18,4,128]{2,1,0:T(4,128)S(1)} %get-tuple-element.40), channel_id=1, source_target_pairs={{4,0},{8,4},{12,8},{16,12},{20,16},{24,20},{28,24},{5,1},{9,5},{13... | collective-permute-start | bytes 110600 | tf_op jit(solution)/shard_map/ppermute | solution.py:173
  27.1 22.9 %copy-start.46 = (f32[8,128]{1,0:T(8,128)}, f32[8,128]{1,0:T(8,128)S(1)}, u32[]{:S(2)}) copy-start(f32[8,128]{1,0:T(8,128)S(1)} %get-tuple-element.43.bias) | copy-start | bytes 12292
  36.5 13.4 %copy-start.20 = (bf16[16,2048]{1,0:T(8,128)(2,1)S(1)}, bf16[16,2048]{1,0:T(8,128)(2,1)}, u32[]{:S(2)}) copy-start(bf16[16,2048]{1,0:T(8,128)(2,1)} %center_far.1) | copy-start | bytes 196612
  36.5 13.4 %copy-start.22 = (bf16[16,2048]{1,0:T(8,128)(2,1)S(1)}, bf16[16,2048]{1,0:T(8,128)(2,1)}, u32[]{:S(2)}) copy-start(bf16[16,2048]{1,0:T(8,128)(2,1)} %radius_far.1) | copy-start | bytes 196612
  40.7 26.1 %all-to-all-start = ((f32[32,1,128]{2,1,0:T(1,128)}), f32[32,1,128]{2,1,0:T(1,128)S(1)}, u32[]{:S(2)}, u32[]{:S(2)}) async-start(f32[32,1,128]{2,1,0:T(1,128)} %bitcast.2), calls=%async_computation | async-start | bytes 32768 | tf_op jit(solution)/shard_map/all_to_all | solution.py:602
  68.4 1.1 copy-start.28
  69.6 1.1 copy-start.32
  85.7 15.9 %all-to-all-start.1 = ((f32[32,1,128]{2,1,0:T(1,128)}), f32[32,1,128]{2,1,0:T(1,128)S(1)}, u32[]{:S(2)}, u32[]{:S(2)}) async-start(f32[32,1,128]{2,1,0:T(1,128)} %bitcast.5), calls=%async_computation.1 | async-start | bytes 32768 | tf_op jit(solution)/shard_map/all_to_all | solution.py:602
  91.5 1.1 copy-start.5
  92.6 1.1 copy-start.8
  102.2 1.1 copy-start.6
  103.3 1.1 copy-start.9
  (44 other events, 36.2 us)

commit v4 on v2

--- a/solution.py
+++ b/solution.py
@@ -497,7 +497,7 @@
 
 
 def everyone(partial):
-    return lax.all_to_all(partial, ("row", "col"), 0, 0, tiled=True)
+    return lax.all_gather(partial, ("row", "col"), axis=0, tiled=True)
 
 
 def shards(objective, center, radius, lower, upper, kernels, biases, steps):
@@ -519,7 +519,7 @@
     above, below = neighbours(top, bottom, "row")
 
     stat_shape = shape(8, LANES)
-    spread = shape(lax.axis_size("row") * lax.axis_size("col"), LANES)
+    spread = shape(1, LANES)
     box, back, slope0, mult0, stat0, value0 = call(
         first_body,
         (

time: 109 us -> 176 us (1.61)
  blocking collectives: 12.6 us -> 117 us
  local copies, waits for them, and re-layouts: 26.6 us -> 5.79 us
  starting transfers between devices: 21.7 us -> 8.38 us
  waiting for transfers between devices: 20 us -> 18.1 us
    all_gather x0 -> x3, blocking collectives: none -> 117 us  [everyone(): return lax.all_gather(partial, ('row', 'col'), axis=0, tiled=True)]
    unnamed x66 -> x16, local copies, waits for them, and re-layouts: 26 us -> 5.21 us
    all_to_all x2 -> x0, starting transfers between devices: 13.3 us -> none  [everyone(): return lax.all_to_all(partial, ('row', 'col'), 0, 0, tiled=True)]
    all_to_all x1 -> x0, blocking collectives: 12.6 us -> none  [everyone(): return lax.all_to_all(partial, ('row', 'col'), 0, 0, tiled=True)]
    all_to_all x2 -> x0, waiting for transfers between devices: 1.94 us -> none  [everyone(): return lax.all_to_all(partial, ('row', 'col'), 0, 0, tiled=True)]
  transfers between devices with their start and end apart: 6 -> 4, of which waited for: 4 -> 2; matrix products, arithmetic and copies ran while one was open for 0% -> 0% of each run, Pallas kernels for 6% -> 1%
where the time goes in v4:
time: 176 us
  blocking collectives  117 us (66%)
  Pallas kernels  25.5 us (14%)
  waiting for transfers between devices  18.1 us (10%)
  starting transfers between devices  8.38 us (5%)
  local copies, waits for them, and re-layouts  5.79 us (3%)
    all_gather x3, blocking collectives, everyone(): return lax.all_gather(partial, ('row', 'col'), axis=0, tiled=True)  117 us
    pallas_call x9, Pallas kernels, call(): pl.pallas_call(body, out_shape=outs, in_specs=[SMEM if j in scalars else...  25.5 us
    ppermute x2, waiting for transfers between devices, neighbours(): before = lax.ppermute(tail, axis, [(i, i + 1) for i in range(count - 1)])  13.9 us
    ppermute x2, starting transfers between devices, neighbours(): before = lax.ppermute(tail, axis, [(i, i + 1) for i in range(count - 1)])  5.79 us
    unnamed x16, local copies, waits for them, and re-layouts  5.21 us
    ppermute x2, waiting for transfers between devices, neighbours(): after = lax.ppermute(head, axis, [(i + 1, i) for i in range(count - 1)])  4.19 us
  transfers between devices with their start and end apart: 4, of which 2 were waited for; matrix products, arithmetic and copies ran while one was open for 0% of the time, Pallas kernels for 1%

profile of v4, /device:TPU:0, one launch (start us, length us, event | category | flops | bytes accessed | tf_op | source)
XLA Modules:
  0.0 175.9 jit_solution(3568038843587944459)
XLA Ops:
  0.7 1.0 copy-done.1
  1.7 0.9 copy-done.2
  2.6 0.9 copy-done.3
  3.5 0.8 copy-done.4
  4.3 0.8 copy-done.5
  5.2 2.4 %collective-permute-start = (f32[144,384]{1,0:T(8,128)S(1)}, f32[144,384]{1,0:T(8,128)S(1)}, u32[]{:S(2)}, u32[]{:S(2)}) collective-permute-start(f32[144,384]{1,0:T(8,128)S(1)} %get-tuple-element.30), channel_id=1, source_target_pairs={{0,1},{1,2},{2,3},{4,5},{5,6},{6,7},{8,9},{9,10},{10,11},{12,13},{... | collective-permute-start | bytes 663560 | tf_op jit(solution)/shard_map/ppermute | solution.py:137
  7.6 1.3 collective-permute-start.1
  8.9 4.2 %collective-permute-done.1.right = f32[144,384]{1,0:T(8,128)S(1)} collective-permute-done((f32[144,384]{1,0:T(8,128)S(1)}, f32[144,384]{1,0:T(8,128)S(1)}, u32[]{:S(2)}, u32[]{:S(2)}) %collective-permute-start.1) | collective-permute-done | bytes 221216 | tf_op jit(solution)/shard_map/ppermute | solution.py:138
  13.1 0.1 shard_map.104
  13.2 3.4 %collective-permute-start.2 = (f32[22,40,128]{2,1,0:T(8,128)S(1)}, f32[22,40,128]{2,1,0:T(8,128)S(1)}, u32[]{:S(2)}, u32[]{:S(2)}) collective-permute-start(f32[22,40,128]{2,1,0:T(8,128)S(1)} %get-tuple-element.32), channel_id=1, source_target_pairs={{0,4},{4,8},{8,12},{12,16},{16,20},{20,24},{24,28},{1,5},{5,9},{9,... | collective-permute-start | bytes 1351688 | tf_op jit(solution)/shard_map/ppermute | solution.py:137
  16.6 1.3 collective-permute-start.3
  18.0 0.7 copy-done.7
  18.6 0.9 shard_map.105
  19.6 13.9 %collective-permute-done.2.above = f32[22,40,128]{2,1,0:T(8,128)S(1)} collective-permute-done((f32[22,40,128]{2,1,0:T(8,128)S(1)}, f32[22,40,128]{2,1,0:T(8,128)S(1)}, u32[]{:S(2)}, u32[]{:S(2)}) %collective-permute-start.2) | collective-permute-done | bytes 450592 | tf_op jit(solution)/shard_map/ppermute | solution.py:137
  33.5 6.3 %shard_map.106 = (f32[8,20,24,128]{3,2,1,0:T(8,128)S(1)}, f32[20,24,128]{2,1,0:T(8,128)S(1)}, f32[3,20,24,128]{3,2,1,0:T(8,128)S(1)}, f32[20,24,128]{2,1,0:T(8,1...) custom-call(f32[16,2048]{1,0:T(8,128)S(1)} %copy-done.3, bf16[16,2048]{1,0:T(8,128)(2,1)S(1)} %copy-done.4, ...), custom_call_target="tpu_custom_call" | custom-call | flops 1698693120 | bytes 4194304 | tf_op jit(solution)/shard_map/pallas_call | solution.py:31
  39.9 43.2 %all-gather = f32[32,1,128]{2,1,0:T(1,128)S(1)} all-gather(f32[1,1,128]{2,1,0:T(1,128)S(1)} %bitcast.15), channel_id=1, replica_groups=mesh['row'=8,'col'=4] {'row','col'}, dimensions={0}, use_global_device_ids=true | all-gather | bytes 16896 | tf_op jit(solution)/shard_map/all_gather | solution.py:500
  83.0 3.1 %shard_map.107.pull.pull0 = f32[3,20,24,128]{3,2,1,0:T(8,128)S(1)} custom-call(f32[3,20,24,128]{3,2,1,0:T(8,128)S(1)} %get-tuple-element.42.slope.slope0, bf16[4,256,384]{2,1,0:T(8,128)(2,1)S(1)} %get-tuple-element.36.bwd_hi, bf16[4,256,384]{2,1,0:T(8,128)(2,1)S(1)} %get-tuple-element.37.bwd_lo), custom_call_target="tpu_custom_call" | custom-call | flops 849346560 | bytes 4194304 | tf_op jit(solution)/shard_map/pallas_call | solution.py:31
  86.1 5.4 %shard_map.108 = (f32[3,18,24,128]{3,2,1,0:T(8,128)S(1)}, f32[3,18,24,128]{3,2,1,0:T(8,128)S(1)}, f32[1,128]{1,0:T(1,128)S(1)}, f32[8,128]{1,0:T(8,128)S(1)}) custom-call(f32[32,128]{1,0:T(8,128)S(1)} %bitcast.10, f32[3]{0:T(128)S(1)} %copy-done.6, f32[8,20,24,128]{3,2,1,0:T(8,128)S(1)} %get-tuple-element.40.box, f32[20,24,128]{2,1,0:T(8,128)S(1)} %get-tuple-element.41.back, ...), custom_call_target="tpu_custom_call" | custom-call | flops 849346560 | bytes 4194304 | tf_op jit(solution)/shard_map/pallas_call | solution.py:31
  91.5 2.8 %shard_map.109.pull1 = f32[3,18,24,128]{3,2,1,0:T(8,128)S(1)} custom-call(f32[3,18,24,128]{3,2,1,0:T(8,128)S(1)} %get-tuple-element.45.slope.slope1, bf16[4,256,384]{2,1,0:T(8,128)(2,1)S(1)} %get-tuple-element.36.bwd_hi, bf16[4,256,384]{2,1,0:T(8,128)(2,1)S(1)} %get-tuple-element.37.bwd_lo), custom_call_target="tpu_custom_call" | custom-call | flops 849346560 | bytes 4194304 | tf_op jit(solution)/shard_map/pallas_call | solution.py:31
  94.3 36.4 %all-gather.1 = f32[32,1,128]{2,1,0:T(1,128)S(1)} all-gather(f32[1,1,128]{2,1,0:T(1,128)S(1)} %bitcast.16), channel_id=1, replica_groups=mesh['row'=8,'col'=4] {'row','col'}, dimensions={0}, use_global_device_ids=true | all-gather | bytes 16896 | tf_op jit(solution)/shard_map/all_gather | solution.py:500
  130.7 5.2 %shard_map.110 = (f32[3,16,2048]{2,1,0:T(8,128)S(1)}, f32[3,16,2048]{2,1,0:T(8,128)S(1)}, f32[3,16,2048]{2,1,0:T(8,128)S(1)}, f32[3,16,2048]{2,1,0:T(8,128)S(1)}, f32[1,128]{1,0:T(1,128)S(1)}) custom-call(f32[32,128]{1,0:T(8,128)S(1)} %bitcast.11, f32[32,128]{1,0:T(8,128)S(1)} %bitcast.12, f32[3]{0:T(128)S(1)} %copy-done.6, ...), custom_call_target="tpu_custom_call" | custom-call | flops 849346560 | bytes 4194304 | tf_op jit(solution)/shard_map/pallas_call | solution.py:31
  135.9 37.8 %all-gather.2 = f32[32,1,128]{2,1,0:T(1,128)S(1)} all-gather(f32[1,1,128]{2,1,0:T(1,128)S(1)} %bitcast.14), channel_id=1, replica_groups=mesh['row'=8,'col'=4] {'row','col'}, dimensions={0}, use_global_device_ids=true | all-gather | bytes 16896 | tf_op jit(solution)/shard_map/all_gather | solution.py:500
  173.7 1.6 shard_map.111
  175.3 0.6 slice_bitcast_fusion
  (13 shorter events, 0.1 us)
Async XLA Ops:
  0.6 17.3 %copy-start = (f32[4,3,3,64,64]{4,3,2,1,0:T(8,128)S(1)}, f32[4,3,3,64,64]{4,3,2,1,0:T(8,128)}, u32[]{:S(2)}) copy-start(f32[4,3,3,64,64]{4,3,2,1,0:T(8,128)} %param.13) | copy-start | bytes 1769476
  0.6 1.0 copy-start.1
  1.7 0.9 copy-start.2
  2.6 0.9 copy-start.3
  3.5 0.8 copy-start.4
  4.3 0.8 copy-start.5
  5.2 3.7 %collective-permute-start = (f32[144,384]{1,0:T(8,128)S(1)}, f32[144,384]{1,0:T(8,128)S(1)}, u32[]{:S(2)}, u32[]{:S(2)}) collective-permute-start(f32[144,384]{1,0:T(8,128)S(1)} %get-tuple-element.30), channel_id=1, source_target_pairs={{0,1},{1,2},{2,3},{4,5},{5,6},{6,7},{8,9},{9,10},{10,11},{12,13},{... | collective-permute-start | bytes 663560 | tf_op jit(solution)/shard_map/ppermute | solution.py:137
  7.6 5.5 %collective-permute-start.1 = (f32[144,384]{1,0:T(8,128)S(1)}, f32[144,384]{1,0:T(8,128)S(1)}, u32[]{:S(2)}, u32[]{:S(2)}) collective-permute-start(f32[144,384]{1,0:T(8,128)S(1)} %get-tuple-element.31), channel_id=1, source_target_pairs={{1,0},{2,1},{3,2},{5,4},{6,5},{7,6},{9,8},{10,9},{11,10},{13,12},{... | collective-permute-start | bytes 663560 | tf_op jit(solution)/shard_map/ppermute | solution.py:138
  13.2 20.3 %collective-permute-start.2 = (f32[22,40,128]{2,1,0:T(8,128)S(1)}, f32[22,40,128]{2,1,0:T(8,128)S(1)}, u32[]{:S(2)}, u32[]{:S(2)}) collective-permute-start(f32[22,40,128]{2,1,0:T(8,128)S(1)} %get-tuple-element.32), channel_id=1, source_target_pairs={{0,4},{4,8},{8,12},{12,16},{16,20},{20,24},{24,28},{1,5},{5,9},{9,... | collective-permute-start | bytes 1351688 | tf_op jit(solution)/shard_map/ppermute | solution.py:137
  16.6 16.9 %collective-permute-start.3 = (f32[22,40,128]{2,1,0:T(8,128)S(1)}, f32[22,40,128]{2,1,0:T(8,128)S(1)}, u32[]{:S(2)}, u32[]{:S(2)}) collective-permute-start(f32[22,40,128]{2,1,0:T(8,128)S(1)} %get-tuple-element.33), channel_id=1, source_target_pairs={{4,0},{8,4},{12,8},{16,12},{20,16},{24,20},{28,24},{5,1},{9,5},{13... | collective-permute-start | bytes 1351688 | tf_op jit(solution)/shard_map/ppermute | solution.py:138
  17.9 0.7 copy-start.7
  39.9 46.3 %copy-start.6 = (f32[3]{0:T(128)S(1)}, f32[3]{0:T(128)}, u32[]{:S(2)}) copy-start(f32[3]{0:T(128)} %steps.5) | copy-start | bytes 40

commit v5 on v3

v5 whole, which is shorter than its diff:
```python
import functools
import math

import jax
import jax.numpy as jnp
from jax import lax
from jax.experimental import pallas as pl
from jax.experimental.pallas import tpu as pltpu
from jax.sharding import PartitionSpec as P

CH = 64
LAYERS = 4
ITERS = 3
EPS = 1e-06
LANES = 2 * CH
HALO_PAIRS = 3
WIDE = 5
EDGE = 4
F32 = jnp.float32
BF16 = jnp.bfloat16

ROWS_SENT = (5, 5, 5, 4, 4, 4, 4, 3, 3)
ROW_START = tuple(sum(ROWS_SENT[:m]) for m in range(9))
SENT = 40
WINDOW = 4 * CH

VMEM = pl.BlockSpec(memory_space=pltpu.VMEM)
SMEM = pl.BlockSpec(memory_space=pltpu.SMEM)
HBM = pl.BlockSpec(memory_space=pltpu.HBM)


def call(body, outs, scratch, operands, flops, mem=20, scalars=(), far=(), scalar_outs=()):
    specs = [SMEM if j in scalars else HBM if j in far else VMEM for j in range(len(operands))]
    out_specs = tuple(SMEM if j in scalar_outs else VMEM for j in range(len(outs)))
    return pl.pallas_call(
        body,
        out_shape=outs,
        in_specs=specs,
        out_specs=out_specs,
        scratch_shapes=scratch,
        compiler_params=pltpu.CompilerParams(vmem_limit_bytes=mem << 20),
        cost_estimate=pl.CostEstimate(flops=flops, bytes_accessed=4 << 20, transcendentals=0),
    )(*operands)


def shape(*dims, dtype=F32):
    return jax.ShapeDtypeStruct(dims, dtype)


def copies(pairs, sem):
    made = [pltpu.make_async_copy(src, dst, sem.at[j]) for j, (src, dst) in enumerate(pairs)]
    for one in made:
        one.start()
    return made


def finish(made):
    for one in made:
        one.wait()


def split(value):
    high = value.astype(BF16)
    return high, (value - high.astype(F32)).astype(BF16)


def weights_body(kernels, biases, fwd, bwd, bias2):
    zero = jnp.zeros((CH, CH), F32)

    def put(dest, k, j, dh, first, second):
        high, low = split(jnp.concatenate([first, second], axis=1))
        for part, value in enumerate((low, high, high)):
            dest[k, pl.ds(WINDOW * part + CH * j, CH), pl.ds(LANES * dh, LANES)] = value

    for k in range(LAYERS):
        for dh in range(3):
            taps = [kernels[k * 9 + dh * 3 + dw] for dw in range(3)]
            if k < LAYERS - 1:
                for j in range(4):
                    put(fwd, k, j, dh, taps[j] if j < 3 else zero, taps[j - 1] if j > 0 else zero)
            flips = [tap.T for tap in taps]
            for j in range(4):
                put(bwd, k, j, 2 - dh, flips[2 - j] if j < 3 else zero, flips[3 - j] if j > 0 else zero)
    for k in range(LAYERS):
        row = biases[k : k + 1, :]
        bias2[k : k + 1, :] = jnp.concatenate([row, row], axis=1)


def weights(kernels, biases):
    size = (3 * WINDOW, 3 * LANES)
    return call(
        weights_body,
        (shape(LAYERS - 1, *size, dtype=BF16), shape(LAYERS, *size, dtype=BF16), shape(8, LANES)),
        [],
        (kernels.reshape(LAYERS * 9, CH, CH), biases),
        1 << 22,
    )


def sources(objective, center, radius, lower, upper):
    return [
        lambda cols: center[:, cols].astype(F32),
        lambda cols: upper[0, :, cols].astype(F32),
        lambda cols: upper[1, :, cols].astype(F32),
        lambda cols: upper[2, :, cols].astype(F32),
        lambda cols: lower[0, :, cols].astype(F32),
        lambda cols: lower[1, :, cols].astype(F32),
        lambda cols: lower[2, :, cols].astype(F32),
        lambda cols: radius[:, cols].astype(F32),
        lambda cols: objective[:, cols],
    ]


def sides_body(
    objective, center, radius, lower, upper, head, tail, top, bottom, *rest
):
    rows, cols = objective.shape
    pairs = cols // LANES
    strip = HALO_PAIRS * LANES
    held, sem = rest[:5], rest[5]
    finish(copies(list(zip((objective, center, radius, lower, upper), held)), sem))
    for m, read in enumerate(sources(*held)):
        head[pl.ds(m * rows, rows), :] = read(pl.ds(0, strip))
        tail[pl.ds(m * rows, rows), :] = read(pl.ds(cols - strip, strip))
    for q in range(pairs):
        ends_of([read(pl.ds(q * LANES, LANES)) for read in sources(*held)], top.at[q], bottom.at[q])


def ends_of(values, top, bottom):
    for m, value in enumerate(values):
        here = slice(ROW_START[m], ROW_START[m] + ROWS_SENT[m])
        top[here, :] = value[: ROWS_SENT[m]]
        bottom[here, :] = value[value.shape[0] - ROWS_SENT[m] :]
    spare = slice(sum(ROWS_SENT), SENT)
    blank = jnp.zeros((SENT - sum(ROWS_SENT), LANES), F32)
    top[spare, :] = blank
    bottom[spare, :] = blank


def corners_body(left, right, top, bottom):
    rows = left.shape[0] // 9
    for side, strip in enumerate((left, right)):
        for q in range(HALO_PAIRS):
            values = [strip[pl.ds(m * rows, rows), pl.ds(q * LANES, LANES)] for m in range(9)]
            at = side * HALO_PAIRS + q
            ends_of(values, top.at[at], bottom.at[at])


def column(reads, left, right, rows, pairs, m, q):
    if q < HALO_PAIRS:
        return left[m * rows : (m + 1) * rows, q * LANES : (q + 1) * LANES]
    if q >= HALO_PAIRS + pairs:
        q -= HALO_PAIRS + pairs
        return right[m * rows : (m + 1) * rows, q * LANES : (q + 1) * LANES]
    return reads[m](pl.ds((q - HALO_PAIRS) * LANES, LANES))


def halo(middle, corner, pairs, q, here):
    if q < HALO_PAIRS:
        return corner[q, here, :]
    if q >= HALO_PAIRS + pairs:
        return corner[q - pairs, here, :]
    return middle[q - HALO_PAIRS, here, :]


def neighbours(head, tail, axis):
    count = lax.axis_size(axis)
    before = lax.ppermute(tail, axis, [(i, i + 1) for i in range(count - 1)])
    after = lax.ppermute(head, axis, [(i + 1, i) for i in range(count - 1)])
    return before, after


def roll_rows(value, shift):
    return pltpu.roll(value, shift % value.shape[0], 0)


def slide(maps, count, store, produce):
    rows = store.shape[2]
    early = lax.broadcasted_iota(jnp.int32, (rows, LANES), 1) < CH
    zero = jnp.zeros((rows, LANES), F32)

    def step(q, carry):
        fresh = [pltpu.roll(value, CH, 1) for value in produce(q)]
        for k in range(maps):
            store[k, q] = jnp.where(early, carry[k], fresh[k])
        return tuple(fresh)

    last = lax.fori_loop(0, count, step, (zero,) * maps, unroll=2)
    for k in range(maps):
        store[k, count] = jnp.where(early, last[k], zero)


def multiply(store, k, first, count, weight, layer, sums, exact=False):
    rows = store.shape[2]
    left = store[k, pl.ds(first, count)].reshape(count * rows, LANES)
    right = store[k, pl.ds(first + 1, count)].reshape(count * rows, LANES)
    high, low = split(jnp.concatenate([left, right], axis=1))
    terms = [high, high] if exact else [high, high, low]
    result = jnp.dot(
        jnp.concatenate(terms, axis=1),
        weight[layer, 0 : WINDOW * len(terms), :],
        preferred_element_type=F32,
    )
    for d in range(3):
        sums[k, d, pl.ds(0, count)] = result[:, d * LANES : (d + 1) * LANES].reshape(count, rows, LANES)


def gathered(sums, k, q):
    return roll_rows(sums[k, 0, q], 1) + sums[k, 1, q] + roll_rows(sums[k, 2, q], -1)


def inner(sums, k, q, first, rows):
    parts = [roll_rows(sums[k, d, q], 1 - d - first)[:rows] for d in range(3)]
    return parts[0] + parts[1] + parts[2]


def summed(total):
    return jnp.sum(total[...], axis=0, keepdims=True)


def scale_of(total, step, cells, dims):
    squares = summed(total)[:, 0:1]
    return jnp.broadcast_to(step / jnp.sqrt(squares / (2 * (LAYERS - 1) * cells) + EPS), dims)


def soft(top, t):
    return 0.5 * top * (1.0 - jnp.tanh(t))


class Bound:
    def __init__(self, start):
        self.linear = start
        self.factor = None

    def add(self, t):
        self.linear = self.linear - jnp.maximum(-t, 0.0)
        factor = 1.0 + jnp.exp(-2.0 * jnp.abs(t))
        self.factor = factor if self.factor is None else self.factor * factor

    def total(self):
        return self.linear - 0.5 * jnp.log(self.factor)


def folded(value):
    return jnp.sum(value, axis=0, keepdims=True)


def own_rows(value):
    rows = value.shape[0]
    row = lax.broadcasted_iota(jnp.int32, value.shape, 0)
    return folded(jnp.where((row >= EDGE) & (row < rows - EDGE), value, 0.0))


def stats(out, rows):
    lane = lax.broadcasted_iota(jnp.int32, (1, LANES), 1)
    packed = jnp.zeros((1, LANES), F32)
    for j, row in enumerate(rows):
        packed = jnp.where(lane == j, jnp.sum(row, axis=1, keepdims=True), packed)
    out[...] = jnp.broadcast_to(packed, out.shape)


def first_body(
    objective, center, radius, lower, upper, left, right, above, below, above_corner, below_corner, fwd, bwd, bias,
    near_box, far_box, back, slope, mult, stat, value,
    raw, gaps, target, store, sums,
):
    rows, cols = objective.shape
    pairs = cols // LANES
    frame = rows + 2 * EDGE
    wide = pairs + 4
    reads = sources(objective, center, radius, lower, upper)
    for m in range(9):
        sent = ROWS_SENT[m]
        here = slice(ROW_START[m], ROW_START[m] + sent)
        for q in range(pairs + 2 * HALO_PAIRS):
            if m >= 3 and not 1 <= q < wide + 1:
                continue
            own = column(reads, left, right, rows, pairs, m, q)
            if m < 3:
                dest, at, edge = raw.at[m, q], 0, WIDE
            else:
                dest, at, edge = (target.at[q - 1] if m == 8 else gaps.at[m - 3, q - 1]), EDGE - sent, EDGE
                if at:
                    dest[0:EDGE, :] = jnp.zeros((EDGE, LANES), F32)
                    dest[EDGE + rows : frame, :] = jnp.zeros((EDGE, LANES), F32)
            dest[at : at + sent, :] = halo(above, above_corner, pairs, q, here)
            dest[edge : edge + rows, :] = own
            dest[edge + rows : edge + rows + sent, :] = halo(below, below_corner, pairs, q, here)
    raw[:, :, rows + 2 * WIDE :, :] = jnp.zeros((3, wide + 2, raw.shape[2] - rows - 2 * WIDE, LANES), F32)

    slide(3, wide + 2, store, lambda q: [raw[0, q], 0.5 * raw[1, q], 0.5 * raw[2, q]])
    tugged = store.at[3:4, :, 0:frame, :]
    slide(1, wide, tugged, lambda q: [target[q]])
    for k in range(3):
        multiply(store, k, 1, wide, fwd, k, sums, exact=True)
    short = sums.at[3:4, :, :, 0:frame, :]
    multiply(tugged, 0, 0, wide, bwd, LAYERS - 1, short)
    zero = jnp.zeros((frame, LANES), F32)

    def step(q, carry):
        squares, worth, fixed = carry
        near = [raw[m, q + 1][1 : 1 + frame] for m in range(3)] + [gaps[4, q]]
        far = [gaps[m, q] for m in range(4)]
        for m in range(4):
            near_box[m, q] = near[m].astype(BF16)
            far_box[m, q] = far[m].astype(BF16)
        new = zero
        for k in range(3):
            gap = near[1 + k] if k < 2 else far[0]
            dl = 0.5 * (gap - far[1 + k]) - inner(sums, k, q, 1, frame) - bias[k : k + 1, :]
            dl = jnp.where(gap > 0.0, dl, 0.0)
            slope[k, q] = dl
            new = new + dl * dl
        tug = gathered(short, 0, q)
        back[q] = tug
        t = tug * gap
        dm = -0.5 * gap * jnp.tanh(t)
        mult[q] = dm
        new = new + dm * dm
        bound = Bound(jnp.full((frame, LANES), -4.5 * math.log(2.0), F32))
        bound.add(t)
        own = (q >= 2) & (q < wide - 2)
        squares = squares + jnp.where(own, new, 0.0)
        worth = worth + jnp.where(own, bound.total(), 0.0)
        fixed = fixed + jnp.where(own, target[q] * bias[3:4, :], 0.0)
        return squares, worth, fixed

    squares, worth, fixed = lax.fori_loop(0, wide, step, (zero, zero, zero), unroll=2)
    fixed = own_rows(fixed)
    stats(stat, [own_rows(squares)])
    stats(value, [own_rows(worth) + fixed, fixed])


def second_body(
    total, steps, near_box, far_box, back, slope, mult, fwd, bwd, bias,
    base, slope_out, mult_out, duals, last_mult, last_slope, last_pull, stat, value,
    points, store, sums, *, cells,
):
    wide, frame = near_box.shape[1:3]
    inside = slice(EDGE, frame - EDGE)
    scale = scale_of(total, steps[0], cells, (frame, LANES))
    zero = jnp.zeros((frame, LANES), F32)
    slide(3, wide, store, lambda q: [slope[k, q] for k in range(3)])
    for k in range(3):
        multiply(store, k, 0, wide, bwd, k, sums)

    def produce(q):
        center, radius = near_box[0, q].astype(F32), near_box[3, q].astype(F32)
        g = -(scale * gathered(sums, 0, q))
        base[0, q] = g
        outs = [center - radius * jnp.tanh(2.0 * radius * g)]
        for k in (1, 2):
            gap = near_box[k, q].astype(F32)
            g = -(scale * gathered(sums, k, q))
            base[k, q] = g
            x = soft(gap, g * gap)
            points[k - 1, q] = x
            outs.append(x)
        return outs

    slide(3, wide, store, produce)
    for k in range(3):
        multiply(store, k, 1, wide - 2, fwd, k, sums)

    def step(j, carry):
        squares, worth = carry
        q = j + 1
        new = zero
        center, radius = near_box[0, q].astype(F32), near_box[3, q].astype(F32)
        g = base[0, q]
        bound = Bound(g * (center - radius))
        bound.add(2.0 * g * radius)
        for k in range(3):
            gap = (near_box[1 + k, q] if k < 2 else far_box[0, q]).astype(F32)
            low = far_box[1 + k, q].astype(F32)
            lam = scale * slope[k, q]
            if k < 2:
                bound.add(base[k + 1, q] * gap)
                x = points[k, q]
                tp = lam * gap
            else:
                mu = scale * mult[q]
                g = back[q] + mu
                t = g * gap
                bound.add(t)
                x = soft(gap, t)
                tp = (lam - mu) * gap
            tn = -lam * low
            bound.add(tp)
            bound.add(tn)
            bound.linear = bound.linear - lam * bias[k : k + 1, :]
            positive = soft(gap, tp)
            dl = positive - soft(low, tn) - gathered(sums, k, j) - bias[k : k + 1, :]
            dl = jnp.where(gap > 0.0, dl, 0.0)
            dm = x - positive
            slope_out[k, j] = dl
            duals[k, j] = lam[inside]
            if k < 2:
                mult_out[k, j] = dm
            else:
                last_mult[j] = mu[inside]
                last_slope[j] = dm[inside]
                last_pull[j] = g[inside]
            new = new + dl * dl + dm * dm
        own = (q >= 2) & (q < wide - 2)
        return squares + jnp.where(own, new, 0.0), worth + jnp.where(own, bound.total(), 0.0)

    squares, worth = lax.fori_loop(0, wide - 2, step, (zero, zero))
    stats(stat, [own_rows(squares)])
    stats(value, [own_rows(worth)])


def third_body(
    total, steps, near_box, base, mult, slope, duals1, last_mult, last_slope, last_pull,
    fwd, bwd, lower, upper, bias, value0, value1,
    duals, multipliers, slope_out, mult_out, stat,
    points, store, sums, *, cells,
):
    wide, frame = near_box.shape[1:3]
    rows = frame - 2 * EDGE
    inside = slice(EDGE, frame - EDGE)
    scale = scale_of(total, steps[1], cells, (frame, LANES))
    zero = jnp.zeros((frame, LANES), F32)
    slide(3, wide - 2, store, lambda j: [slope[k, j] for k in range(3)])
    for k in range(3):
        multiply(store, k, 0, wide - 2, bwd, k, sums)
    early = lax.broadcasted_iota(jnp.int32, (frame, LANES), 1) < CH

    def point(j, carry):
        q = j + 1
        center, radius = near_box[0, q].astype(F32), near_box[3, q].astype(F32)
        g = base[0, q] - scale * gathered(sums, 0, j)
        bound = Bound(g * (center - radius))
        t = 2.0 * radius * g
        bound.add(t)
        outs = [center - radius * jnp.tanh(t)]
        for k in (1, 2):
            gap = near_box[k, q].astype(F32)
            t = (base[k, q] + scale * (mult[k - 1, j] - gathered(sums, k, j))) * gap
            bound.add(t)
            x = soft(gap, t)
            points[k - 1, j] = x
            outs.append(x)
        own = (q >= 2) & (q < wide - 2)
        fresh = [pltpu.roll(value, CH, 1) for value in outs]
        for k in range(3):
            store[k, j] = jnp.where(early, carry[k], fresh[k])
        return tuple(fresh) + (carry[3] + jnp.where(own, bound.total(), 0.0),)

    framed = lax.fori_loop(0, wide - 2, point, (zero,) * 4)[3]
    for k in range(3):
        multiply(store, k, 1, wide - 4, fwd, k, sums)

    scale = scale[:rows]

    def step(i, carry):
        squares, worth = carry
        j = i + 1
        here = pl.ds(pl.multiple_of(i * LANES, LANES), LANES)
        bound = Bound(jnp.zeros((rows, LANES), F32))
        for k in range(3):
            gap = upper[k, :, here].astype(F32)
            low = lower[k, :, here].astype(F32)
            lam = duals1[k, j] + scale * slope[k, j, inside, :]
            bound.linear = bound.linear - lam * bias[k : k + 1, :]
            if k < 2:
                x = points[k, j, inside, :]
                mu = scale * mult[k, j, inside, :]
            else:
                change = scale * last_slope[j]
                mu = last_mult[j] + change
                t = (last_pull[j] + change) * gap
                x = soft(gap, t)
                bound.add(t)
            tp = (lam - mu) * gap
            tn = -lam * low
            bound.add(tp)
            bound.add(tn)
            positive = soft(gap, tp)
            dl = positive - soft(low, tn) - inner(sums, k, i, EDGE, rows) - bias[k : k + 1, :]
            dm = x - positive
            duals[k, :, here] = lam
            multipliers[k, :, here] = mu
            slope_out[k, :, here] = dl
            mult_out[k, :, here] = dm
            squares = squares + dl * dl + dm * dm
        return squares, worth + bound.total()

    zero = jnp.zeros((rows, LANES), F32)
    squares, worth = lax.fori_loop(0, wide - 4, step, (zero, zero), unroll=2)
    lane = lax.broadcasted_iota(jnp.int32, (1, LANES), 1)
    start, fixed = (jnp.where(lane == j, value0[0:1, :], 0.0) for j in range(2))
    middle = jnp.where(lane == 0, value1[0:1, :], 0.0)
    stats(stat, [folded(squares), start, middle + fixed, folded(worth) + own_rows(framed) + fixed])


def last_body(total, steps, duals, multipliers, slope, mult, duals_out, mult_out, bounds, *, cells):
    scale = scale_of(total, steps[2], cells, duals.shape[1:])
    for k in range(LAYERS - 1):
        duals_out[k] = duals[k] + scale * slope[k]
        mult_out[k] = multipliers[k] + scale * mult[k]
    values = summed(total) / cells
    lane = lax.broadcasted_iota(jnp.int32, (1, LANES), 1)
    for j in range(ITERS):
        bounds[j] = jnp.sum(jnp.where(lane == j + 1, values, 0.0))


def everyone(partial):
    return lax.all_to_all(partial, ("row", "col"), 0, 0, tiled=True)


def shards(objective, center, radius, lower, upper, kernels, biases, steps):
    rows, cols = objective.shape
    pairs = cols // LANES
    wide = pairs + 4
    frame = rows + 2 * EDGE
    tall = -(-(rows + 2 * WIDE) // 8) * 8
    cells = rows * cols * lax.axis_size("row") * lax.axis_size("col")
    inputs = (objective, center, radius, lower, upper)
    flops = 3 * 2 * 3 * wide * frame * 4 * CH * 3 * LANES
    spread = shape(lax.axis_size("row") * lax.axis_size("col"), LANES)
    small = shape(8, LANES)

    strip = shape(9 * rows, HALO_PAIRS * LANES)
    ends = shape(pairs, SENT, LANES)
    head, tail, top, bottom = call(
        sides_body,
        (strip, strip, ends, ends),
        [pltpu.VMEM(one.shape, one.dtype) for one in inputs] + [pltpu.SemaphoreType.DMA((5,))],
        inputs,
        1 << 20,
        mem=58,
        far=range(5),
    )
    left, right = neighbours(head, tail, "col")
    above, below = neighbours(top, bottom, "row")
    fwd, bwd, bias = weights(kernels, biases)
    corner = shape(2 * HALO_PAIRS, SENT, LANES)
    corner_top, corner_bottom = call(corners_body, (corner, corner), [], (left, right), 1 << 20)
    above_corner, below_corner = neighbours(corner_top, corner_bottom, "row")

    box = shape(4, wide, frame, LANES, dtype=BF16)
    full = shape(wide, frame, LANES)
    near_box, far_box, back, slope0, mult0, stat0, value0 = call(
        first_body,
        (box, box, full, shape(3, wide, frame, LANES), full, spread, small),
        [
            pltpu.VMEM((3, wide + 2, tall, LANES), F32),
            pltpu.VMEM((5, wide, frame, LANES), F32),
            pltpu.VMEM((wide, frame, LANES), F32),
            pltpu.VMEM((4, wide + 3, tall, LANES), F32),
            pltpu.VMEM((4, 3, wide, tall, LANES), F32),
        ],
        inputs + (left, right, above, below, above_corner, below_corner, fwd, bwd, bias),
        2 * flops,
    )

    total0 = everyone(stat0)
    tile = shape(wide - 2, rows, LANES)
    base, slope1, mult1, duals1, last_mult, last_slope, last_pull, stat1, value1 = call(
        functools.partial(second_body, cells=cells),
        (
            shape(3, wide, frame, LANES),
            shape(3, wide - 2, frame, LANES),
            shape(2, wide - 2, frame, LANES),
            shape(3, wide - 2, rows, LANES),
            tile,
            tile,
            tile,
            spread,
            small,
        ),
        [
            pltpu.VMEM((2, wide, frame, LANES), F32),
            pltpu.VMEM((3, wide + 1, frame, LANES), F32),
            pltpu.VMEM((3, 3, wide, frame, LANES), F32),
        ],
        (total0, steps, near_box, far_box, back, slope0, mult0, fwd, bwd, bias),
        2 * flops,
        scalars=(1,),
    )
    total1 = everyone(stat1)
    out = shape(3, rows, cols)
    duals, multipliers, slope2, mult2, stat2 = call(
        functools.partial(third_body, cells=cells),
        (out, out, out, out, spread),
        [
            pltpu.VMEM((2, wide - 2, frame, LANES), F32),
            pltpu.VMEM((3, wide - 1, frame, LANES), F32),
            pltpu.VMEM((3, 3, wide - 2, frame, LANES), F32),
        ],
        (
            total1, steps, near_box, base, mult1, slope1, duals1, last_mult, last_slope, last_pull,
            fwd, bwd, lower, upper, bias, value0, value1,
        ),
        2 * flops,
        scalars=(1,),
    )
    total2 = everyone(stat2)
    final_duals, final_multipliers, bounds = call(
        functools.partial(last_body, cells=cells),
        (out, out, shape(ITERS)),
        [],
        (total2, steps, duals, multipliers, slope2, mult2),
        1 << 20,
        scalar_outs=(2,),
        scalars=(1,),
    )
    return bounds, final_duals, final_multipliers


def solution(mesh):
    placed = (
        P("row", "col"),
        P("row", "col"),
        P("row", "col"),
        P(None, "row", "col"),
        P(None, "row", "col"),
        P(),
        P(),
        P(),
    )
    return jax.shard_map(
        shards,
        mesh=mesh,
        in_specs=placed,
        out_specs=(P(), P(None, "row", "col"), P(None, "row", "col")),
        check_vma=False,
    )
```

time: 136 us -> 83.7 us (0.62); the launches traced: 134 us -> 83.3 us
  local copies, waits for them, and re-layouts: 43.4 us -> 1.97 us
  blocking collectives: 12.8 us -> 33.3 us
  starting transfers between devices: 30.1 us -> 15 us
  Pallas kernels: 33.2 us -> 23.3 us
  waiting for transfers between devices: 13.6 us -> 8.94 us
    unnamed x120 -> x16, local copies, waits for them, and re-layouts: 42.8 us -> 1.97 us
    all_to_all x1 -> x3, blocking collectives: 12.8 us -> 33.3 us  [everyone(): return lax.all_to_all(partial, ('row', 'col'), 0, 0, tiled=True)]
    all_to_all x2 -> x0, starting transfers between devices: 15.1 us -> none  [everyone(): return lax.all_to_all(partial, ('row', 'col'), 0, 0, tiled=True)]
    pallas_call x9 -> x7, Pallas kernels: 33.2 us -> 23.3 us  [call(): pl.pallas_call(body, out_shape=outs, in_specs=specs, out_specs=out_specs,...]
    ppermute x3, waiting for transfers between devices: 4.18 us -> 0.01 us  [neighbours(): after = lax.ppermute(head, axis, [(i + 1, i) for i in range(count - 1)])]
  transfers between devices with their start and end apart: 8 -> 6, of which waited for: 2 -> 2; matrix products, arithmetic and copies ran while one was open for 0% -> 0% of each run, Pallas kernels for 15% -> 1%
where the time goes in v5:
time: 83.7 us; the launch traced here: 83.3 us
  blocking collectives  33.3 us (40%)
  Pallas kernels  23.3 us (28%)
  starting transfers between devices  15 us (18%)
  waiting for transfers between devices  8.94 us (11%)
  local copies, waits for them, and re-layouts  1.97 us (2%)
    all_to_all x3, blocking collectives, everyone(): return lax.all_to_all(partial, ('row', 'col'), 0, 0, tiled=True)  33.3 us
    pallas_call x7, Pallas kernels, call(): pl.pallas_call(body, out_shape=outs, in_specs=specs, out_specs=out_specs,...  23.3 us
    ppermute x3, starting transfers between devices, neighbours(): before = lax.ppermute(tail, axis, [(i, i + 1) for i in range(count - 1)])  11.2 us
    ppermute x3, waiting for transfers between devices, neighbours(): before = lax.ppermute(tail, axis, [(i, i + 1) for i in range(count - 1)])  8.94 us
    ppermute x3, starting transfers between devices, neighbours(): after = lax.ppermute(head, axis, [(i + 1, i) for i in range(count - 1)])  3.88 us
    unnamed x16, local copies, waits for them, and re-layouts  1.97 us
  transfers between devices with their start and end apart: 6, of which 2 were waited for; matrix products, arithmetic and copies ran while one was open for 0% of the time, Pallas kernels for 1%

profile of v5, /device:TPU:0, one launch (start us, length us, event | category | flops | bytes accessed | tf_op | source)
XLA Modules:
  0.0 83.3 jit_solution(1594090118756024354)
XLA Ops:
  0.7 2.3 %shard_map.103 = (f32[144,384]{1,0:T(8,128)}, f32[144,384]{1,0:T(8,128)}, f32[16,40,128]{2,1,0:T(8,128)}, f32[16,40,128]{2,1,0:T(8,128)}) custom-call(f32[16,2048]{1,0:T(8,128)} %objective.3, bf16[16,2048]{1,0:T(8,128)(2,1)} %center.3, bf16[16,2048]{1,0:T(8,128)(2,1)} %radius.3, bf16[3,16,2048]{2,1,0:T(8,128)(2,1)} %lower.5, bf16[3,16,2048]{2,1,0:T(8,128)(2,1)} %upper.5), custom_call_target="tpu_custom_call" | custom-call | flops 1048576 | bytes 4194304 | tf_op jit(solution)/shard_map/pallas_call | solution.py:35
  3.0 2.4 %collective-permute-start = (f32[144,384]{1,0:T(8,128)}, f32[144,384]{1,0:T(8,128)S(1)}, u32[]{:S(2)}, u32[]{:S(2)}) collective-permute-start(f32[144,384]{1,0:T(8,128)} %get-tuple-element.36), channel_id=1, source_target_pairs={{0,1},{1,2},{2,3},{4,5},{5,6},{6,7},{8,9},{9,10},{10,11},{12,13},{... | collective-permute-start | bytes 663560 | tf_op jit(solution)/shard_map/ppermute | solution.py:168
  5.3 1.3 %collective-permute-start.1 = (f32[144,384]{1,0:T(8,128)}, f32[144,384]{1,0:T(8,128)S(1)}, u32[]{:S(2)}, u32[]{:S(2)}) collective-permute-start(f32[144,384]{1,0:T(8,128)} %get-tuple-element.37), channel_id=1, source_target_pairs={{1,0},{2,1},{3,2},{5,4},{6,5},{7,6},{9,8},{10,9},{11,10},{13,12},{... | collective-permute-start | bytes 663560 | tf_op jit(solution)/shard_map/ppermute | solution.py:169
  6.6 4.2 %collective-permute-start.2 = (f32[16,40,128]{2,1,0:T(8,128)}, f32[16,40,128]{2,1,0:T(8,128)S(1)}, u32[]{:S(2)}, u32[]{:S(2)}) collective-permute-start(f32[16,40,128]{2,1,0:T(8,128)} %get-tuple-element.38), channel_id=1, source_target_pairs={{0,4},{4,8},{8,12},{12,16},{16,20},{20,24},{24,28},{1,5},{5,9},{9,... | collective-permute-start | bytes 983048 | tf_op jit(solution)/shard_map/ppermute | solution.py:168
  10.9 1.3 %collective-permute-start.3 = (f32[16,40,128]{2,1,0:T(8,128)}, f32[16,40,128]{2,1,0:T(8,128)S(1)}, u32[]{:S(2)}, u32[]{:S(2)}) collective-permute-start(f32[16,40,128]{2,1,0:T(8,128)} %get-tuple-element.39), channel_id=1, source_target_pairs={{4,0},{8,4},{12,8},{16,12},{20,16},{24,20},{28,24},{5,1},{9,5},{13... | collective-permute-start | bytes 983048 | tf_op jit(solution)/shard_map/ppermute | solution.py:169
  12.2 0.0 collective-permute-done.left
  12.2 0.0 collective-permute-done.1.right
  12.2 4.6 %collective-permute-start.4 = (f32[6,40,128]{2,1,0:T(8,128)S(1)}, f32[6,40,128]{2,1,0:T(8,128)S(1)}, u32[]{:S(2)}, u32[]{:S(2)}) collective-permute-start(f32[6,40,128]{2,1,0:T(8,128)S(1)} %get-tuple-element.40), channel_id=1, source_target_pairs={{0,4},{4,8},{8,12},{12,16},{16,20},{20,24},{24,28},{1,5},{5,9},{9,... | collective-permute-start | bytes 368648 | tf_op jit(solution)/shard_map/ppermute | solution.py:168
  16.8 1.3 %collective-permute-start.5 = (f32[6,40,128]{2,1,0:T(8,128)S(1)}, f32[6,40,128]{2,1,0:T(8,128)S(1)}, u32[]{:S(2)}, u32[]{:S(2)}) collective-permute-start(f32[6,40,128]{2,1,0:T(8,128)S(1)} %get-tuple-element.41), channel_id=1, source_target_pairs={{4,0},{8,4},{12,8},{16,12},{20,16},{24,20},{28,24},{5,1},{9,5},{13... | collective-permute-start | bytes 368648 | tf_op jit(solution)/shard_map/ppermute | solution.py:169
  18.1 0.0 copy-start
  18.1 1.3 %copy-done = f32[4,3,3,64,64]{4,3,2,1,0:T(8,128)S(1)} copy-done((f32[4,3,3,64,64]{4,3,2,1,0:T(8,128)S(1)}, f32[4,3,3,64,64]{4,3,2,1,0:T(8,128)}, u32[]{:S(2)}) %copy-start) | copy-done | bytes 589848
  19.4 0.7 copy-done.7
  20.1 0.9 %shard_map.105 = (bf16[3,768,384]{2,1,0:T(8,128)(2,1)S(1)}, bf16[4,768,384]{2,1,0:T(8,128)(2,1)S(1)}, f32[8,128]{1,0:T(8,128)S(1)}) custom-call(f32[36,64,64]{2,1,0:T(8,128)S(1)} %bitcast.13, f32[4,64]{1,0:T(4,128)S(1)} %copy-done.7), custom_call_target="tpu_custom_call" | custom-call | flops 4194304 | bytes 4194304 | tf_op jit(solution)/shard_map/pallas_call | solution.py:35
  21.0 6.4 %collective-permute-done.2.above = f32[16,40,128]{2,1,0:T(8,128)S(1)} collective-permute-done((f32[16,40,128]{2,1,0:T(8,128)}, f32[16,40,128]{2,1,0:T(8,128)S(1)}, u32[]{:S(2)}, u32[]{:S(2)}) %collective-permute-start.2) | collective-permute-done | bytes 327712 | tf_op jit(solution)/shard_map/ppermute | solution.py:168
  27.4 0.0 collective-permute-done.3.below
  27.4 2.5 %collective-permute-done.4.above_corner = f32[6,40,128]{2,1,0:T(8,128)S(1)} collective-permute-done((f32[6,40,128]{2,1,0:T(8,128)S(1)}, f32[6,40,128]{2,1,0:T(8,128)S(1)}, u32[]{:S(2)}, u32[]{:S(2)}) %collective-permute-start.4) | collective-permute-done | bytes 122912 | tf_op jit(solution)/shard_map/ppermute | solution.py:168
  30.0 0.0 copy-start.6
  30.0 4.8 %shard_map.106 = (bf16[4,20,24,128]{3,2,1,0:T(8,128)(2,1)S(1)}, bf16[4,20,24,128]{3,2,1,0:T(8,128)(2,1)S(1)}, f32[20,24,128]{2,1,0:T(8,128)S(1)}, f32[3,20,24,12...) custom-call(f32[16,2048]{1,0:T(8,128)S(1)} %copy-done.3, ...), custom_call_target="tpu_custom_call" | custom-call | flops 1698693120 | bytes 4194304 | tf_op jit(solution)/shard_map/pallas_call | solution.py:35
  34.8 15.6 %all_to_all.33 = f32[32,1,128]{2,1,0:T(1,128)S(1)} all-to-all(f32[32,1,128]{2,1,0:T(1,128)S(1)} %bitcast.19), channel_id=1, replica_groups=mesh['row'=8,'col'=4] {'row','col'}, dimensions={0} | all-to-all | bytes 32768 | tf_op jit(solution)/shard_map/all_to_all | solution.py:509
  50.4 7.0 %shard_map.107 = (f32[3,20,24,128]{3,2,1,0:T(8,128)S(1)}, f32[3,18,24,128]{3,2,1,0:T(8,128)S(1)}, f32[2,18,24,128]{3,2,1,0:T(8,128)S(1)}, f32[3,18,16,128]{3,2,1...) custom-call(f32[32,128]{1,0:T(8,128)S(1)} %bitcast.15, ...), custom_call_target="tpu_custom_call" | custom-call | flops 1698693120 | bytes 4194304 | tf_op jit(solution)/shard_map/pallas_call | solution.py:35
  57.4 8.8 %all_to_all.34 = f32[32,1,128]{2,1,0:T(1,128)S(1)} all-to-all(f32[32,1,128]{2,1,0:T(1,128)S(1)} %bitcast.18), channel_id=1, replica_groups=mesh['row'=8,'col'=4] {'row','col'}, dimensions={0} | all-to-all | bytes 32768 | tf_op jit(solution)/shard_map/all_to_all | solution.py:509
  66.2 6.6 %shard_map.108 = (f32[3,16,2048]{2,1,0:T(8,128)S(1)}, f32[3,16,2048]{2,1,0:T(8,128)S(1)}, f32[3,16,2048]{2,1,0:T(8,128)S(1)}, f32[3,16,2048]{2,1,0:T(8,128)S(1)}, f32[32,128]{1,0:T(8,128)S(1)}) custom-call(f32[32,128]{1,0:T(8,128)S(1)} %bitcast.14, f32[3]{0:T(128)S(1)} %copy-done.6, bf16[4,20,24,128]{3,2,1,0:T(8,128)(2,1)S(1)} %get-tuple-element.46.near_box, ...), custom_call_target="tpu_custom_call" | custom-call | flops 1698693120 | bytes 4194304 | tf_op jit(solution)/shard_map/pallas_call | solution.py:35
  72.9 8.8 %all_to_all.35 = f32[32,1,128]{2,1,0:T(1,128)S(1)} all-to-all(f32[32,1,128]{2,1,0:T(1,128)S(1)} %bitcast.17), channel_id=1, replica_groups=mesh['row'=8,'col'=4] {'row','col'}, dimensions={0} | all-to-all | bytes 32768 | tf_op jit(solution)/shard_map/all_to_all | solution.py:509
  81.7 1.6 %shard_map.109 = (f32[3,16,2048]{2,1,0:T(8,128)}, f32[3,16,2048]{2,1,0:T(8,128)}, f32[3]{0:T(128)}) custom-call(f32[32,128]{1,0:T(8,128)S(1)} %bitcast.16, f32[3]{0:T(128)S(1)} %copy-done.6, f32[3,16,2048]{2,1,0:T(8,128)S(1)} %get-tuple-element.62.duals, f32[3,16,2048]{2,1,0:T(8,128)S(1)} %get-tuple-element.63.multipliers, ...), custom_call_target="tpu_custom_call" | custom-call | flops 1048576 | bytes 4194304 | tf_op jit(solution)/shard_map/pallas_call | solution.py:35
  (14 shorter events, 0.1 us)
Async XLA Ops:
  0.6 29.3 %copy-start.2 = (bf16[3,16,2048]{2,1,0:T(8,128)(2,1)S(1)}, bf16[3,16,2048]{2,1,0:T(8,128)(2,1)}, u32[]{:S(2)}) copy-start(bf16[3,16,2048]{2,1,0:T(8,128)(2,1)} %upper.5) | copy-start | bytes 589828
  0.6 29.3 %copy-start.1 = (bf16[3,16,2048]{2,1,0:T(8,128)(2,1)S(1)}, bf16[3,16,2048]{2,1,0:T(8,128)(2,1)}, u32[]{:S(2)}) copy-start(bf16[3,16,2048]{2,1,0:T(8,128)(2,1)} %lower.5) | copy-start | bytes 589828
  0.7 29.3 %copy-start.5 = (bf16[16,2048]{1,0:T(8,128)(2,1)S(1)}, bf16[16,2048]{1,0:T(8,128)(2,1)}, u32[]{:S(2)}) copy-start(bf16[16,2048]{1,0:T(8,128)(2,1)} %radius.3) | copy-start | bytes 196612
  0.7 29.3 %copy-start.4 = (bf16[16,2048]{1,0:T(8,128)(2,1)S(1)}, bf16[16,2048]{1,0:T(8,128)(2,1)}, u32[]{:S(2)}) copy-start(bf16[16,2048]{1,0:T(8,128)(2,1)} %center.3) | copy-start | bytes 196612
  0.7 29.3 %copy-start.3 = (f32[16,2048]{1,0:T(8,128)S(1)}, f32[16,2048]{1,0:T(8,128)}, u32[]{:S(2)}) copy-start(f32[16,2048]{1,0:T(8,128)} %objective.3) | copy-start | bytes 393220
  3.0 9.2 %collective-permute-start = (f32[144,384]{1,0:T(8,128)}, f32[144,384]{1,0:T(8,128)S(1)}, u32[]{:S(2)}, u32[]{:S(2)}) collective-permute-start(f32[144,384]{1,0:T(8,128)} %get-tuple-element.36), channel_id=1, source_target_pairs={{0,1},{1,2},{2,3},{4,5},{5,6},{6,7},{8,9},{9,10},{10,11},{12,13},{... | collective-permute-start | bytes 663560 | tf_op jit(solution)/shard_map/ppermute | solution.py:168
  5.3 6.9 %collective-permute-start.1 = (f32[144,384]{1,0:T(8,128)}, f32[144,384]{1,0:T(8,128)S(1)}, u32[]{:S(2)}, u32[]{:S(2)}) collective-permute-start(f32[144,384]{1,0:T(8,128)} %get-tuple-element.37), channel_id=1, source_target_pairs={{1,0},{2,1},{3,2},{5,4},{6,5},{7,6},{9,8},{10,9},{11,10},{13,12},{... | collective-permute-start | bytes 663560 | tf_op jit(solution)/shard_map/ppermute | solution.py:169
  6.6 20.8 %collective-permute-start.2 = (f32[16,40,128]{2,1,0:T(8,128)}, f32[16,40,128]{2,1,0:T(8,128)S(1)}, u32[]{:S(2)}, u32[]{:S(2)}) collective-permute-start(f32[16,40,128]{2,1,0:T(8,128)} %get-tuple-element.38), channel_id=1, source_target_pairs={{0,4},{4,8},{8,12},{12,16},{16,20},{20,24},{24,28},{1,5},{5,9},{9,... | collective-permute-start | bytes 983048 | tf_op jit(solution)/shard_map/ppermute | solution.py:168
  10.9 16.5 %collective-permute-start.3 = (f32[16,40,128]{2,1,0:T(8,128)}, f32[16,40,128]{2,1,0:T(8,128)S(1)}, u32[]{:S(2)}, u32[]{:S(2)}) collective-permute-start(f32[16,40,128]{2,1,0:T(8,128)} %get-tuple-element.39), channel_id=1, source_target_pairs={{4,0},{8,4},{12,8},{16,12},{20,16},{24,20},{28,24},{5,1},{9,5},{13... | collective-permute-start | bytes 983048 | tf_op jit(solution)/shard_map/ppermute | solution.py:169
  12.2 17.7 %collective-permute-start.4 = (f32[6,40,128]{2,1,0:T(8,128)S(1)}, f32[6,40,128]{2,1,0:T(8,128)S(1)}, u32[]{:S(2)}, u32[]{:S(2)}) collective-permute-start(f32[6,40,128]{2,1,0:T(8,128)S(1)} %get-tuple-element.40), channel_id=1, source_target_pairs={{0,4},{4,8},{8,12},{12,16},{16,20},{20,24},{24,28},{1,5},{5,9},{9,... | collective-permute-start | bytes 368648 | tf_op jit(solution)/shard_map/ppermute | solution.py:168
  16.8 13.1 %collective-permute-start.5 = (f32[6,40,128]{2,1,0:T(8,128)S(1)}, f32[6,40,128]{2,1,0:T(8,128)S(1)}, u32[]{:S(2)}, u32[]{:S(2)}) collective-permute-start(f32[6,40,128]{2,1,0:T(8,128)S(1)} %get-tuple-element.41), channel_id=1, source_target_pairs={{4,0},{8,4},{12,8},{16,12},{20,16},{24,20},{28,24},{5,1},{9,5},{13... | collective-permute-start | bytes 368648 | tf_op jit(solution)/shard_map/ppermute | solution.py:169
  18.1 1.3 %copy-start = (f32[4,3,3,64,64]{4,3,2,1,0:T(8,128)S(1)}, f32[4,3,3,64,64]{4,3,2,1,0:T(8,128)}, u32[]{:S(2)}) copy-start(f32[4,3,3,64,64]{4,3,2,1,0:T(8,128)} %param.13) | copy-start | bytes 1769476
  19.4 0.7 copy-start.7
  30.0 20.4 %copy-start.6 = (f32[3]{0:T(128)S(1)}, f32[3]{0:T(128)}, u32[]{:S(2)}) copy-start(f32[3]{0:T(128)} %steps.5) | copy-start | bytes 40

commit v6 on v5

--- a/solution.py
+++ b/solution.py
@@ -19,9 +19,9 @@
 F32 = jnp.float32
 BF16 = jnp.bfloat16
 
-ROWS_SENT = (5, 5, 5, 4, 4, 4, 4, 3, 3)
+ROWS_SENT = (5, 5, 5, 4, 4, 4, 2, 3, 3)
 ROW_START = tuple(sum(ROWS_SENT[:m]) for m in range(9))
-SENT = 40
+SENT = sum(ROWS_SENT)
 WINDOW = 4 * CH
 
 VMEM = pl.BlockSpec(memory_space=pltpu.VMEM)
@@ -111,39 +111,36 @@
     ]
 
 
-def sides_body(
-    objective, center, radius, lower, upper, head, tail, top, bottom, *rest
-):
+def sides_body(objective, center, radius, lower, upper, head, tail):
     rows, cols = objective.shape
-    pairs = cols // LANES
     strip = HALO_PAIRS * LANES
+    for m, read in enumerate(sources(objective, center, radius, lower, upper)):
+        head[pl.ds(m * rows, rows), :] = read(pl.ds(0, strip))
+        tail[pl.ds(m * rows, rows), :] = read(pl.ds(cols - strip, strip))
+
+
+def ends_body(objective, center, radius, lower, upper, top, bottom, *rest):
+    rows, cols = objective.shape
     held, sem = rest[:5], rest[5]
     finish(copies(list(zip((objective, center, radius, lower, upper), held)), sem))
-    for m, read in enumerate(sources(*held)):
-        head[pl.ds(m * rows, rows), :] = read(pl.ds(0, strip))
-        tail[pl.ds(m * rows, rows), :] = read(pl.ds(cols - strip, strip))
-    for q in range(pairs):
-        ends_of([read(pl.ds(q * LANES, LANES)) for read in sources(*held)], top.at[q], bottom.at[q])
-
-
-def ends_of(values, top, bottom):
-    for m, value in enumerate(values):
-        here = slice(ROW_START[m], ROW_START[m] + ROWS_SENT[m])
-        top[here, :] = value[: ROWS_SENT[m]]
-        bottom[here, :] = value[value.shape[0] - ROWS_SENT[m] :]
-    spare = slice(sum(ROWS_SENT), SENT)
-    blank = jnp.zeros((SENT - sum(ROWS_SENT), LANES), F32)
-    top[spare, :] = blank
-    bottom[spare, :] = blank
-
-
-def corners_body(left, right, top, bottom):
-    rows = left.shape[0] // 9
-    for side, strip in enumerate((left, right)):
-        for q in range(HALO_PAIRS):
-            values = [strip[pl.ds(m * rows, rows), pl.ds(q * LANES, LANES)] for m in range(9)]
-            at = side * HALO_PAIRS + q
-            ends_of(values, top.at[at], bottom.at[at])
+    row = lax.broadcasted_iota(jnp.int32, (rows, LANES), 0)
+    outer = (row >= 2) & (row < rows - 2)
+    for q in range(cols // LANES):
+        values = [read(pl.ds(q * LANES, LANES)) for read in sources(*held)]
+        values[3] = jnp.where(outer, values[3] - values[6], values[3])
+        for m, value in enumerate(values):
+            here = pl.ds(q * SENT + ROW_START[m], ROWS_SENT[m])
+            top[here, :] = value[: ROWS_SENT[m]]
+            bottom[here, :] = value[rows - ROWS_SENT[m] :]
+
+
+def corners_body(above, below, head, tail):
+    count = HALO_PAIRS * SENT
+    size = above.shape[0]
+    for part, source in enumerate((above, below)):
+        here = pl.ds(part * count, count)
+        head[here, :] = source[0:count, :]
+        tail[here, :] = source[size - count : size, :]
 
 
 def column(reads, left, right, rows, pairs, m, q):
@@ -155,12 +152,14 @@
     return reads[m](pl.ds((q - HALO_PAIRS) * LANES, LANES))
 
 
-def halo(middle, corner, pairs, q, here):
+def halo(middle, left, right, part, pairs, q, m):
     if q < HALO_PAIRS:
-        return corner[q, here, :]
-    if q >= HALO_PAIRS + pairs:
-        return corner[q - pairs, here, :]
-    return middle[q - HALO_PAIRS, here, :]
+        source, at = left, part * HALO_PAIRS + q
+    elif q >= HALO_PAIRS + pairs:
+        source, at = right, part * HALO_PAIRS + q - HALO_PAIRS - pairs
+    else:
+        source, at = middle, q - HALO_PAIRS
+    return source[pl.ds(at * SENT + ROW_START[m], ROWS_SENT[m]), :]
 
 
 def neighbours(head, tail, axis):
@@ -260,7 +259,7 @@
 
 
 def first_body(
-    objective, center, radius, lower, upper, left, right, above, below, above_corner, below_corner, fwd, bwd, bias,
+    objective, center, radius, lower, upper, left, right, above, below, left_corner, right_corner, fwd, bwd, bias,
     near_box, far_box, back, slope, mult, stat, value,
     raw, gaps, target, store, sums,
 ):
@@ -271,7 +270,6 @@
     reads = sources(objective, center, radius, lower, upper)
     for m in range(9):
         sent = ROWS_SENT[m]
-        here = slice(ROW_START[m], ROW_START[m] + sent)
         for q in range(pairs + 2 * HALO_PAIRS):
             if m >= 3 and not 1 <= q < wide + 1:
                 continue
@@ -283,9 +281,9 @@
                 if at:
                     dest[0:EDGE, :] = jnp.zeros((EDGE, LANES), F32)
                     dest[EDGE + rows : frame, :] = jnp.zeros((EDGE, LANES), F32)
-            dest[at : at + sent, :] = halo(above, above_corner, pairs, q, here)
+            dest[at : at + sent, :] = halo(above, left_corner, right_corner, 0, pairs, q, m)
             dest[edge : edge + rows, :] = own
-            dest[edge + rows : edge + rows + sent, :] = halo(below, below_corner, pairs, q, here)
+            dest[edge + rows : edge + rows + sent, :] = halo(below, left_corner, right_corner, 1, pairs, q, m)
     raw[:, :, rows + 2 * WIDE :, :] = jnp.zeros((3, wide + 2, raw.shape[2] - rows - 2 * WIDE, LANES), F32)
 
     slide(3, wide + 2, store, lambda q: [raw[0, q], 0.5 * raw[1, q], 0.5 * raw[2, q]])
@@ -308,7 +306,7 @@
         for k in range(3):
             gap = near[1 + k] if k < 2 else far[0]
             dl = 0.5 * (gap - far[1 + k]) - inner(sums, k, q, 1, frame) - bias[k : k + 1, :]
-            dl = jnp.where(gap > 0.0, dl, 0.0)
+            dl = jnp.where(near[1] > 0.0, dl, 0.0)
             slope[k, q] = dl
             new = new + dl * dl
         tug = gathered(short, 0, q)
@@ -521,23 +519,24 @@
     spread = shape(lax.axis_size("row") * lax.axis_size("col"), LANES)
     small = shape(8, LANES)
 
-    strip = shape(9 * rows, HALO_PAIRS * LANES)
-    ends = shape(pairs, SENT, LANES)
-    head, tail, top, bottom = call(
-        sides_body,
-        (strip, strip, ends, ends),
+    ends = shape(pairs * SENT, LANES)
+    top, bottom = call(
+        ends_body,
+        (ends, ends),
         [pltpu.VMEM(one.shape, one.dtype) for one in inputs] + [pltpu.SemaphoreType.DMA((5,))],
         inputs,
         1 << 20,
         mem=58,
         far=range(5),
     )
+    above, below = neighbours(top, bottom, "row")
+    strip = shape(9 * rows, HALO_PAIRS * LANES)
+    head, tail = call(sides_body, (strip, strip), [], inputs, 1 << 20)
     left, right = neighbours(head, tail, "col")
-    above, below = neighbours(top, bottom, "row")
     fwd, bwd, bias = weights(kernels, biases)
-    corner = shape(2 * HALO_PAIRS, SENT, LANES)
-    corner_top, corner_bottom = call(corners_body, (corner, corner), [], (left, right), 1 << 20)
-    above_corner, below_corner = neighbours(corner_top, corner_bottom, "row")
+    corner = shape(2 * HALO_PAIRS * SENT, LANES)
+    corner_head, corner_tail = call(corners_body, (corner, corner), [], (above, below), 1 << 20)
+    left_corner, right_corner = neighbours(corner_head, corner_tail, "col")
 
     box = shape(4, wide, frame, LANES, dtype=BF16)
     full = shape(wide, frame, LANES)
@@ -551,7 +550,7 @@
             pltpu.VMEM((4, wide + 3, tall, LANES), F32),
             pltpu.VMEM((4, 3, wide, tall, LANES), F32),
         ],
-        inputs + (left, right, above, below, above_corner, below_corner, fwd, bwd, bias),
+        inputs + (left, right, above, below, left_corner, right_corner, fwd, bwd, bias),
         2 * flops,
     )
 

time: 83.7 us -> 80.4 us (0.961)
  starting transfers between devices: 15 us -> 11.6 us
  local copies, waits for them, and re-layouts: 1.97 us -> 4.46 us
  waiting for transfers between devices: 8.94 us -> 6.51 us
    ppermute x3, waiting for transfers between devices: 8.94 us -> 3.83 us  [neighbours(): before = lax.ppermute(tail, axis, [(i, i + 1) for i in range(count - 1)])]
    ppermute x3, starting transfers between devices: 11.2 us -> 7.76 us  [neighbours(): before = lax.ppermute(tail, axis, [(i, i + 1) for i in range(count - 1)])]
    ppermute x3, waiting for transfers between devices: 0.01 us -> 2.68 us  [neighbours(): after = lax.ppermute(head, axis, [(i + 1, i) for i in range(count - 1)])]
    unnamed x16 -> x22, local copies, waits for them, and re-layouts: 1.97 us -> 4.46 us
    pallas_call x7 -> x8, Pallas kernels: 23.3 us -> 23.2 us  [call(): pl.pallas_call(body, out_shape=outs, in_specs=specs, out_specs=out_specs,...]
where the time goes in v6:
time: 80.4 us; the launch traced here: 79.9 us
  blocking collectives  33.3 us (41%)
  Pallas kernels  23.2 us (29%)
  starting transfers between devices  11.6 us (14%)
  waiting for transfers between devices  6.51 us (8%)
  local copies, waits for them, and re-layouts  4.46 us (6%)
    all_to_all x3, blocking collectives, everyone(): return lax.all_to_all(partial, ('row', 'col'), 0, 0, tiled=True)  33.3 us
    pallas_call x8, Pallas kernels, call(): pl.pallas_call(body, out_shape=outs, in_specs=specs, out_specs=out_specs,...  23.2 us
    ppermute x3, starting transfers between devices, neighbours(): before = lax.ppermute(tail, axis, [(i, i + 1) for i in range(count - 1)])  7.76 us
    unnamed x22, local copies, waits for them, and re-layouts  4.46 us
    ppermute x3, starting transfers between devices, neighbours(): after = lax.ppermute(head, axis, [(i + 1, i) for i in range(count - 1)])  3.88 us
    ppermute x3, waiting for transfers between devices, neighbours(): before = lax.ppermute(tail, axis, [(i, i + 1) for i in range(count - 1)])  3.83 us
    ppermute x3, waiting for transfers between devices, neighbours(): after = lax.ppermute(head, axis, [(i + 1, i) for i in range(count - 1)])  2.68 us
  transfers between devices with their start and end apart: 6, of which 2 were waited for; matrix products, arithmetic and copies ran while one was open for 0% of the time, Pallas kernels for 1%

profile of v6, /device:TPU:0, one launch (start us, length us, event | category | flops | bytes accessed | tf_op | source)
XLA Modules:
  0.0 79.9 jit_solution(5521249043869384520)
XLA Ops:
  0.7 0.0 copy-start.6
  0.7 2.1 %shard_map.104 = (f32[560,128]{1,0:T(8,128)}, f32[560,128]{1,0:T(8,128)}) custom-call(f32[16,2048]{1,0:T(8,128)} %objective.5, bf16[16,2048]{1,0:T(8,128)(2,1)} %center.5, bf16[16,2048]{1,0:T(8,128)(2,1)} %radius.5, bf16[3,16,2048]{2,1,0:T(8,128)(2,1)} %lower.7, bf16[3,16,2048]{2,1,0:T(8,128)(2,1)} %upper.7), custom_call_target="tpu_custom_call" | custom-call | flops 1048576 | bytes 4194304 | tf_op jit(solution)/shard_map/pallas_call | solution.py:35
  2.8 4.9 %collective-permute-start.2 = (f32[560,128]{1,0:T(8,128)}, f32[560,128]{1,0:T(8,128)S(1)}, u32[]{:S(2)}, u32[]{:S(2)}) collective-permute-start(f32[560,128]{1,0:T(8,128)} %get-tuple-element.38), channel_id=1, source_target_pairs={{0,4},{4,8},{8,12},{12,16},{16,20},{20,24},{24,28},{1,5},{5,9},{9,... | collective-permute-start | bytes 860168 | tf_op jit(solution)/shard_map/ppermute | solution.py:167
  7.7 1.3 %collective-permute-start.3 = (f32[560,128]{1,0:T(8,128)}, f32[560,128]{1,0:T(8,128)S(1)}, u32[]{:S(2)}, u32[]{:S(2)}) collective-permute-start(f32[560,128]{1,0:T(8,128)} %get-tuple-element.39), channel_id=1, source_target_pairs={{4,0},{8,4},{12,8},{16,12},{20,16},{24,20},{28,24},{5,1},{9,5},{13... | collective-permute-start | bytes 860168 | tf_op jit(solution)/shard_map/ppermute | solution.py:168
  9.0 0.0 copy-start
  9.0 0.9 %copy-done = bf16[3,16,2048]{2,1,0:T(8,128)(2,1)S(1)} copy-done((bf16[3,16,2048]{2,1,0:T(8,128)(2,1)S(1)}, bf16[3,16,2048]{2,1,0:T(8,128)(2,1)}, u32[]{:S(2)}) %copy-start) | copy-done | bytes 196632
  9.9 0.9 %copy-done.2 = bf16[3,16,2048]{2,1,0:T(8,128)(2,1)S(1)} copy-done((bf16[3,16,2048]{2,1,0:T(8,128)(2,1)S(1)}, bf16[3,16,2048]{2,1,0:T(8,128)(2,1)}, u32[]{:S(2)}) %copy-start.2) | copy-done | bytes 196632
  10.9 0.9 %copy-done.5 = f32[16,2048]{1,0:T(8,128)S(1)} copy-done((f32[16,2048]{1,0:T(8,128)S(1)}, f32[16,2048]{1,0:T(8,128)}, u32[]{:S(2)}) %copy-start.5) | copy-done | bytes 131096
  11.8 0.8 %copy-done.7 = bf16[16,2048]{1,0:T(8,128)(2,1)S(1)} copy-done((bf16[16,2048]{1,0:T(8,128)(2,1)S(1)}, bf16[16,2048]{1,0:T(8,128)(2,1)}, u32[]{:S(2)}) %copy-start.7) | copy-done | bytes 65560
  12.6 0.8 %copy-done.8 = bf16[16,2048]{1,0:T(8,128)(2,1)S(1)} copy-done((bf16[16,2048]{1,0:T(8,128)(2,1)S(1)}, bf16[16,2048]{1,0:T(8,128)(2,1)}, u32[]{:S(2)}) %copy-start.8) | copy-done | bytes 65560
  13.5 1.6 %collective-permute-start = (f32[144,384]{1,0:T(8,128)S(1)}, f32[144,384]{1,0:T(8,128)S(1)}, u32[]{:S(2)}, u32[]{:S(2)}) collective-permute-start(f32[144,384]{1,0:T(8,128)S(1)} %get-tuple-element.36), channel_id=1, source_target_pairs={{0,1},{1,2},{2,3},{4,5},{5,6},{6,7},{8,9},{9,10},{10,11},{12,13},{... | collective-permute-start | bytes 663560 | tf_op jit(solution)/shard_map/ppermute | solution.py:167
  15.1 1.3 %collective-permute-start.1 = (f32[144,384]{1,0:T(8,128)S(1)}, f32[144,384]{1,0:T(8,128)S(1)}, u32[]{:S(2)}, u32[]{:S(2)}) collective-permute-start(f32[144,384]{1,0:T(8,128)S(1)} %get-tuple-element.37), channel_id=1, source_target_pairs={{1,0},{2,1},{3,2},{5,4},{6,5},{7,6},{9,8},{10,9},{11,10},{13,12},{... | collective-permute-start | bytes 663560 | tf_op jit(solution)/shard_map/ppermute | solution.py:168
  16.4 3.8 %collective-permute-done.2.above = f32[560,128]{1,0:T(8,128)S(1)} collective-permute-done((f32[560,128]{1,0:T(8,128)}, f32[560,128]{1,0:T(8,128)S(1)}, u32[]{:S(2)}, u32[]{:S(2)}) %collective-permute-start.2) | collective-permute-done | bytes 286752 | tf_op jit(solution)/shard_map/ppermute | solution.py:167
  20.2 1.3 %collective-permute-start.4 = (f32[210,128]{1,0:T(8,128)S(1)}, f32[210,128]{1,0:T(8,128)S(1)}, u32[]{:S(2)}, u32[]{:S(2)}) collective-permute-start(f32[210,128]{1,0:T(8,128)S(1)} %get-tuple-element.40), channel_id=1, source_target_pairs={{0,1},{1,2},{2,3},{4,5},{5,6},{6,7},{8,9},{9,10},{10,11},{12,13},{... | collective-permute-start | bytes 322568 | tf_op jit(solution)/shard_map/ppermute | solution.py:167
  21.5 1.3 %collective-permute-start.5 = (f32[210,128]{1,0:T(8,128)S(1)}, f32[210,128]{1,0:T(8,128)S(1)}, u32[]{:S(2)}, u32[]{:S(2)}) collective-permute-start(f32[210,128]{1,0:T(8,128)S(1)} %get-tuple-element.41), channel_id=1, source_target_pairs={{1,0},{2,1},{3,2},{5,4},{6,5},{7,6},{9,8},{10,9},{11,10},{13,12},{... | collective-permute-start | bytes 322568 | tf_op jit(solution)/shard_map/ppermute | solution.py:168
  22.9 0.9 %shard_map.106 = (bf16[3,768,384]{2,1,0:T(8,128)(2,1)S(1)}, bf16[4,768,384]{2,1,0:T(8,128)(2,1)S(1)}, f32[8,128]{1,0:T(8,128)S(1)}) custom-call(f32[36,64,64]{2,1,0:T(8,128)S(1)} %bitcast.13, f32[4,64]{1,0:T(4,128)S(1)} %copy-done.10), custom_call_target="tpu_custom_call" | custom-call | flops 4194304 | bytes 4194304 | tf_op jit(solution)/shard_map/pallas_call | solution.py:35
  23.8 2.7 %collective-permute-done.5.right_corner = f32[210,128]{1,0:T(8,128)S(1)} collective-permute-done((f32[210,128]{1,0:T(8,128)S(1)}, f32[210,128]{1,0:T(8,128)S(1)}, u32[]{:S(2)}, u32[]{:S(2)}) %collective-permute-start.5) | collective-permute-done | bytes 107552 | tf_op jit(solution)/shard_map/ppermute | solution.py:168
  26.5 4.8 %shard_map.107 = (bf16[4,20,24,128]{3,2,1,0:T(8,128)(2,1)S(1)}, bf16[4,20,24,128]{3,2,1,0:T(8,128)(2,1)S(1)}, f32[20,24,128]{2,1,0:T(8,128)S(1)}, f32[3,20,24,12...) custom-call(f32[16,2048]{1,0:T(8,128)S(1)} %copy-done.6, ...), custom_call_target="tpu_custom_call" | custom-call | flops 1698693120 | bytes 4194304 | tf_op jit(solution)/shard_map/pallas_call | solution.py:35
  31.3 15.7 %all_to_all.33 = f32[32,1,128]{2,1,0:T(1,128)S(1)} all-to-all(f32[32,1,128]{2,1,0:T(1,128)S(1)} %bitcast.19), channel_id=1, replica_groups=mesh['row'=8,'col'=4] {'row','col'}, dimensions={0} | all-to-all | bytes 32768 | tf_op jit(solution)/shard_map/all_to_all | solution.py:507
  47.0 7.0 %shard_map.108 = (f32[3,20,24,128]{3,2,1,0:T(8,128)S(1)}, f32[3,18,24,128]{3,2,1,0:T(8,128)S(1)}, f32[2,18,24,128]{3,2,1,0:T(8,128)S(1)}, f32[3,18,16,128]{3,2,1...) custom-call(f32[32,128]{1,0:T(8,128)S(1)} %bitcast.15, ...), custom_call_target="tpu_custom_call" | custom-call | flops 1698693120 | bytes 4194304 | tf_op jit(solution)/shard_map/pallas_call | solution.py:35
  54.0 8.8 %all_to_all.34 = f32[32,1,128]{2,1,0:T(1,128)S(1)} all-to-all(f32[32,1,128]{2,1,0:T(1,128)S(1)} %bitcast.18), channel_id=1, replica_groups=mesh['row'=8,'col'=4] {'row','col'}, dimensions={0} | all-to-all | bytes 32768 | tf_op jit(solution)/shard_map/all_to_all | solution.py:507
  62.9 6.6 %shard_map.109 = (f32[3,16,2048]{2,1,0:T(8,128)S(1)}, f32[3,16,2048]{2,1,0:T(8,128)S(1)}, f32[3,16,2048]{2,1,0:T(8,128)S(1)}, f32[3,16,2048]{2,1,0:T(8,128)S(1)}, f32[32,128]{1,0:T(8,128)S(1)}) custom-call(f32[32,128]{1,0:T(8,128)S(1)} %bitcast.14, f32[3]{0:T(128)S(1)} %copy-done.9, bf16[4,20,24,128]{3,2,1,0:T(8,128)(2,1)S(1)} %get-tuple-element.46.near_box, ...), custom_call_target="tpu_custom_call" | custom-call | flops 1698693120 | bytes 4194304 | tf_op jit(solution)/shard_map/pallas_call | solution.py:35
  69.5 8.8 %all_to_all.35 = f32[32,1,128]{2,1,0:T(1,128)S(1)} all-to-all(f32[32,1,128]{2,1,0:T(1,128)S(1)} %bitcast.17), channel_id=1, replica_groups=mesh['row'=8,'col'=4] {'row','col'}, dimensions={0} | all-to-all | bytes 32768 | tf_op jit(solution)/shard_map/all_to_all | solution.py:507
  78.4 1.6 %shard_map.110 = (f32[3,16,2048]{2,1,0:T(8,128)}, f32[3,16,2048]{2,1,0:T(8,128)}, f32[3]{0:T(128)}) custom-call(f32[32,128]{1,0:T(8,128)S(1)} %bitcast.16, f32[3]{0:T(128)S(1)} %copy-done.9, f32[3,16,2048]{2,1,0:T(8,128)S(1)} %get-tuple-element.62.duals, f32[3,16,2048]{2,1,0:T(8,128)S(1)} %get-tuple-element.63.multipliers, ...), custom_call_target="tpu_custom_call" | custom-call | flops 1048576 | bytes 4194304 | tf_op jit(solution)/shard_map/pallas_call | solution.py:35
  (21 shorter events, 0.1 us)
Async XLA Ops:
  0.6 25.9 %copy-start.3 = (bf16[3,16,2048]{2,1,0:T(8,128)(2,1)S(1)}, bf16[3,16,2048]{2,1,0:T(8,128)(2,1)}, u32[]{:S(2)}) copy-start(bf16[3,16,2048]{2,1,0:T(8,128)(2,1)} %upper.7) | copy-start | bytes 589828
  0.6 25.9 %copy-start.1 = (bf16[3,16,2048]{2,1,0:T(8,128)(2,1)S(1)}, bf16[3,16,2048]{2,1,0:T(8,128)(2,1)}, u32[]{:S(2)}) copy-start(bf16[3,16,2048]{2,1,0:T(8,128)(2,1)} %lower.7) | copy-start | bytes 589828
  0.7 25.9 %copy-start.6 = (f32[16,2048]{1,0:T(8,128)S(1)}, f32[16,2048]{1,0:T(8,128)}, u32[]{:S(2)}) copy-start(f32[16,2048]{1,0:T(8,128)} %objective.5) | copy-start | bytes 393220
  0.7 22.2 %copy-start.10 = (f32[4,64]{1,0:T(4,128)S(1)}, f32[4,64]{1,0:T(4,128)}, u32[]{:S(2)}) copy-start(f32[4,64]{1,0:T(4,128)} %biases.1) | copy-start | bytes 3076
  2.8 17.4 %collective-permute-start.2 = (f32[560,128]{1,0:T(8,128)}, f32[560,128]{1,0:T(8,128)S(1)}, u32[]{:S(2)}, u32[]{:S(2)}) collective-permute-start(f32[560,128]{1,0:T(8,128)} %get-tuple-element.38), channel_id=1, source_target_pairs={{0,4},{4,8},{8,12},{12,16},{16,20},{20,24},{24,28},{1,5},{5,9},{9,... | collective-permute-start | bytes 860168 | tf_op jit(solution)/shard_map/ppermute | solution.py:167
  7.7 12.5 %collective-permute-start.3 = (f32[560,128]{1,0:T(8,128)}, f32[560,128]{1,0:T(8,128)S(1)}, u32[]{:S(2)}, u32[]{:S(2)}) collective-permute-start(f32[560,128]{1,0:T(8,128)} %get-tuple-element.39), channel_id=1, source_target_pairs={{4,0},{8,4},{12,8},{16,12},{20,16},{24,20},{28,24},{5,1},{9,5},{13... | collective-permute-start | bytes 860168 | tf_op jit(solution)/shard_map/ppermute | solution.py:168
  9.0 0.9 %copy-start = (bf16[3,16,2048]{2,1,0:T(8,128)(2,1)S(1)}, bf16[3,16,2048]{2,1,0:T(8,128)(2,1)}, u32[]{:S(2)}) copy-start(bf16[3,16,2048]{2,1,0:T(8,128)(2,1)} %lower.7) | copy-start | bytes 589828
  9.9 0.9 %copy-start.2 = (bf16[3,16,2048]{2,1,0:T(8,128)(2,1)S(1)}, bf16[3,16,2048]{2,1,0:T(8,128)(2,1)}, u32[]{:S(2)}) copy-start(bf16[3,16,2048]{2,1,0:T(8,128)(2,1)} %upper.7) | copy-start | bytes 589828
  10.9 0.9 %copy-start.5 = (f32[16,2048]{1,0:T(8,128)S(1)}, f32[16,2048]{1,0:T(8,128)}, u32[]{:S(2)}) copy-start(f32[16,2048]{1,0:T(8,128)} %objective.5) | copy-start | bytes 393220
  11.8 0.8 %copy-start.7 = (bf16[16,2048]{1,0:T(8,128)(2,1)S(1)}, bf16[16,2048]{1,0:T(8,128)(2,1)}, u32[]{:S(2)}) copy-start(bf16[16,2048]{1,0:T(8,128)(2,1)} %center.5) | copy-start | bytes 196612
  12.6 0.8 %copy-start.8 = (bf16[16,2048]{1,0:T(8,128)(2,1)S(1)}, bf16[16,2048]{1,0:T(8,128)(2,1)}, u32[]{:S(2)}) copy-start(bf16[16,2048]{1,0:T(8,128)(2,1)} %radius.5) | copy-start | bytes 196612
  13.4 9.4 %copy-start.4 = (f32[4,3,3,64,64]{4,3,2,1,0:T(8,128)S(1)}, f32[4,3,3,64,64]{4,3,2,1,0:T(8,128)}, u32[]{:S(2)}) copy-start(f32[4,3,3,64,64]{4,3,2,1,0:T(8,128)} %param.13) | copy-start | bytes 1769476
  13.5 10.3 %collective-permute-start = (f32[144,384]{1,0:T(8,128)S(1)}, f32[144,384]{1,0:T(8,128)S(1)}, u32[]{:S(2)}, u32[]{:S(2)}) collective-permute-start(f32[144,384]{1,0:T(8,128)S(1)} %get-tuple-element.36), channel_id=1, source_target_pairs={{0,1},{1,2},{2,3},{4,5},{5,6},{6,7},{8,9},{9,10},{10,11},{12,13},{... | collective-permute-start | bytes 663560 | tf_op jit(solution)/shard_map/ppermute | solution.py:167
  15.1 8.7 %collective-permute-start.1 = (f32[144,384]{1,0:T(8,128)S(1)}, f32[144,384]{1,0:T(8,128)S(1)}, u32[]{:S(2)}, u32[]{:S(2)}) collective-permute-start(f32[144,384]{1,0:T(8,128)S(1)} %get-tuple-element.37), channel_id=1, source_target_pairs={{1,0},{2,1},{3,2},{5,4},{6,5},{7,6},{9,8},{10,9},{11,10},{13,12},{... | collective-permute-start | bytes 663560 | tf_op jit(solution)/shard_map/ppermute | solution.py:168
  20.2 3.6 %collective-permute-start.4 = (f32[210,128]{1,0:T(8,128)S(1)}, f32[210,128]{1,0:T(8,128)S(1)}, u32[]{:S(2)}, u32[]{:S(2)}) collective-permute-start(f32[210,128]{1,0:T(8,128)S(1)} %get-tuple-element.40), channel_id=1, source_target_pairs={{0,1},{1,2},{2,3},{4,5},{5,6},{6,7},{8,9},{9,10},{10,11},{12,13},{... | collective-permute-start | bytes 322568 | tf_op jit(solution)/shard_map/ppermute | solution.py:167
  21.5 5.0 %collective-permute-start.5 = (f32[210,128]{1,0:T(8,128)S(1)}, f32[210,128]{1,0:T(8,128)S(1)}, u32[]{:S(2)}, u32[]{:S(2)}) collective-permute-start(f32[210,128]{1,0:T(8,128)S(1)} %get-tuple-element.41), channel_id=1, source_target_pairs={{1,0},{2,1},{3,2},{5,4},{6,5},{7,6},{9,8},{10,9},{11,10},{13,12},{... | collective-permute-start | bytes 322568 | tf_op jit(solution)/shard_map/ppermute | solution.py:168
  26.5 20.5 %copy-start.9 = (f32[3]{0:T(128)S(1)}, f32[3]{0:T(128)}, u32[]{:S(2)}) copy-start(f32[3]{0:T(128)} %steps.5) | copy-start | bytes 40

commit v7 on v6

--- a/solution.py
+++ b/solution.py
@@ -111,18 +111,14 @@
     ]
 
 
-def sides_body(objective, center, radius, lower, upper, head, tail):
-    rows, cols = objective.shape
-    strip = HALO_PAIRS * LANES
-    for m, read in enumerate(sources(objective, center, radius, lower, upper)):
-        head[pl.ds(m * rows, rows), :] = read(pl.ds(0, strip))
-        tail[pl.ds(m * rows, rows), :] = read(pl.ds(cols - strip, strip))
-
-
-def ends_body(objective, center, radius, lower, upper, top, bottom, *rest):
+def ends_body(objective, center, radius, lower, upper, top, bottom, head, tail, *rest):
     rows, cols = objective.shape
     held, sem = rest[:5], rest[5]
     finish(copies(list(zip((objective, center, radius, lower, upper), held)), sem))
+    strip = HALO_PAIRS * LANES
+    for m, read in enumerate(sources(*held)):
+        head[pl.ds(m * rows, rows), :] = read(pl.ds(0, strip))
+        tail[pl.ds(m * rows, rows), :] = read(pl.ds(cols - strip, strip))
     row = lax.broadcasted_iota(jnp.int32, (rows, LANES), 0)
     outer = (row >= 2) & (row < rows - 2)
     for q in range(cols // LANES):
@@ -222,8 +218,8 @@
     return jnp.broadcast_to(step / jnp.sqrt(squares / (2 * (LAYERS - 1) * cells) + EPS), dims)
 
 
-def soft(top, t):
-    return 0.5 * top * (1.0 - jnp.tanh(t))
+def soft(top, bend):
+    return 0.5 * top * (1.0 - bend)
 
 
 class Bound:
@@ -232,12 +228,14 @@
         self.factor = None
 
     def add(self, t):
-        self.linear = self.linear - jnp.maximum(-t, 0.0)
-        factor = 1.0 + jnp.exp(-2.0 * jnp.abs(t))
+        bend = jnp.tanh(t)
+        self.linear = self.linear + (jnp.minimum(t, 0.0) - 0.5 * math.log(2.0))
+        factor = 1.0 + jnp.abs(bend)
         self.factor = factor if self.factor is None else self.factor * factor
+        return bend
 
     def total(self):
-        return self.linear - 0.5 * jnp.log(self.factor)
+        return self.linear + 0.5 * jnp.log(self.factor)
 
 
 def folded(value):
@@ -311,12 +309,10 @@
             new = new + dl * dl
         tug = gathered(short, 0, q)
         back[q] = tug
-        t = tug * gap
-        dm = -0.5 * gap * jnp.tanh(t)
+        bound = Bound(jnp.full((frame, LANES), -4.5 * math.log(2.0), F32))
+        dm = -0.5 * gap * bound.add(tug * gap)
         mult[q] = dm
         new = new + dm * dm
-        bound = Bound(jnp.full((frame, LANES), -4.5 * math.log(2.0), F32))
-        bound.add(t)
         own = (q >= 2) & (q < wide - 2)
         squares = squares + jnp.where(own, new, 0.0)
         worth = worth + jnp.where(own, bound.total(), 0.0)
@@ -332,7 +328,7 @@
 def second_body(
     total, steps, near_box, far_box, back, slope, mult, fwd, bwd, bias,
     base, slope_out, mult_out, duals, last_mult, last_slope, last_pull, stat, value,
-    points, store, sums, *, cells,
+    points, worths, store, sums, *, cells,
 ):
     wide, frame = near_box.shape[1:3]
     inside = slice(EDGE, frame - EDGE)
@@ -346,14 +342,16 @@
         center, radius = near_box[0, q].astype(F32), near_box[3, q].astype(F32)
         g = -(scale * gathered(sums, 0, q))
         base[0, q] = g
-        outs = [center - radius * jnp.tanh(2.0 * radius * g)]
+        bound = Bound(g * (center - radius))
+        outs = [center - radius * bound.add(2.0 * radius * g)]
         for k in (1, 2):
             gap = near_box[k, q].astype(F32)
             g = -(scale * gathered(sums, k, q))
             base[k, q] = g
-            x = soft(gap, g * gap)
+            x = soft(gap, bound.add(g * gap))
             points[k - 1, q] = x
             outs.append(x)
+        worths[q] = bound.total()
         return outs
 
     slide(3, wide, store, produce)
@@ -364,31 +362,23 @@
         squares, worth = carry
         q = j + 1
         new = zero
-        center, radius = near_box[0, q].astype(F32), near_box[3, q].astype(F32)
-        g = base[0, q]
-        bound = Bound(g * (center - radius))
-        bound.add(2.0 * g * radius)
+        bound = Bound(worths[q])
         for k in range(3):
             gap = (near_box[1 + k, q] if k < 2 else far_box[0, q]).astype(F32)
             low = far_box[1 + k, q].astype(F32)
             lam = scale * slope[k, q]
             if k < 2:
-                bound.add(base[k + 1, q] * gap)
                 x = points[k, q]
                 tp = lam * gap
             else:
                 mu = scale * mult[q]
                 g = back[q] + mu
-                t = g * gap
-                bound.add(t)
-                x = soft(gap, t)
+                x = soft(gap, bound.add(g * gap))
                 tp = (lam - mu) * gap
-            tn = -lam * low
-            bound.add(tp)
-            bound.add(tn)
+            positive = soft(gap, bound.add(tp))
+            negative = soft(low, bound.add(-lam * low))
             bound.linear = bound.linear - lam * bias[k : k + 1, :]
-            positive = soft(gap, tp)
-            dl = positive - soft(low, tn) - gathered(sums, k, j) - bias[k : k + 1, :]
+            dl = positive - negative - gathered(sums, k, j) - bias[k : k + 1, :]
             dl = jnp.where(gap > 0.0, dl, 0.0)
             dm = x - positive
             slope_out[k, j] = dl
@@ -403,7 +393,7 @@
         own = (q >= 2) & (q < wide - 2)
         return squares + jnp.where(own, new, 0.0), worth + jnp.where(own, bound.total(), 0.0)
 
-    squares, worth = lax.fori_loop(0, wide - 2, step, (zero, zero))
+    squares, worth = lax.fori_loop(0, wide - 2, step, (zero, zero), unroll=2)
     stats(stat, [own_rows(squares)])
     stats(value, [own_rows(worth)])
 
@@ -429,14 +419,11 @@
         center, radius = near_box[0, q].astype(F32), near_box[3, q].astype(F32)
         g = base[0, q] - scale * gathered(sums, 0, j)
         bound = Bound(g * (center - radius))
-        t = 2.0 * radius * g
-        bound.add(t)
-        outs = [center - radius * jnp.tanh(t)]
+        outs = [center - radius * bound.add(2.0 * radius * g)]
         for k in (1, 2):
             gap = near_box[k, q].astype(F32)
             t = (base[k, q] + scale * (mult[k - 1, j] - gathered(sums, k, j))) * gap
-            bound.add(t)
-            x = soft(gap, t)
+            x = soft(gap, bound.add(t))
             points[k - 1, j] = x
             outs.append(x)
         own = (q >= 2) & (q < wide - 2)
@@ -445,7 +432,7 @@
             store[k, j] = jnp.where(early, carry[k], fresh[k])
         return tuple(fresh) + (carry[3] + jnp.where(own, bound.total(), 0.0),)
 
-    framed = lax.fori_loop(0, wide - 2, point, (zero,) * 4)[3]
+    framed = lax.fori_loop(0, wide - 2, point, (zero,) * 4, unroll=2)[3]
     for k in range(3):
         multiply(store, k, 1, wide - 4, fwd, k, sums)
 
@@ -467,15 +454,10 @@
             else:
                 change = scale * last_slope[j]
                 mu = last_mult[j] + change
-                t = (last_pull[j] + change) * gap
-                x = soft(gap, t)
-                bound.add(t)
-            tp = (lam - mu) * gap
-            tn = -lam * low
-            bound.add(tp)
-            bound.add(tn)
-            positive = soft(gap, tp)
-            dl = positive - soft(low, tn) - inner(sums, k, i, EDGE, rows) - bias[k : k + 1, :]
+                x = soft(gap, bound.add((last_pull[j] + change) * gap))
+            positive = soft(gap, bound.add((lam - mu) * gap))
+            negative = soft(low, bound.add(-lam * low))
+            dl = positive - negative - inner(sums, k, i, EDGE, rows) - bias[k : k + 1, :]
             dm = x - positive
             duals[k, :, here] = lam
             multipliers[k, :, here] = mu
@@ -520,9 +502,10 @@
     small = shape(8, LANES)
 
     ends = shape(pairs * SENT, LANES)
-    top, bottom = call(
+    strip = shape(9 * rows, HALO_PAIRS * LANES)
+    top, bottom, head, tail = call(
         ends_body,
-        (ends, ends),
+        (ends, ends, strip, strip),
         [pltpu.VMEM(one.shape, one.dtype) for one in inputs] + [pltpu.SemaphoreType.DMA((5,))],
         inputs,
         1 << 20,
@@ -530,8 +513,6 @@
         far=range(5),
     )
     above, below = neighbours(top, bottom, "row")
-    strip = shape(9 * rows, HALO_PAIRS * LANES)
-    head, tail = call(sides_body, (strip, strip), [], inputs, 1 << 20)
     left, right = neighbours(head, tail, "col")
     fwd, bwd, bias = weights(kernels, biases)
     corner = shape(2 * HALO_PAIRS * SENT, LANES)
@@ -571,6 +552,7 @@
         ),
         [
             pltpu.VMEM((2, wide, frame, LANES), F32),
+            pltpu.VMEM((wide, frame, LANES), F32),
             pltpu.VMEM((3, wide + 1, frame, LANES), F32),
             pltpu.VMEM((3, 3, wide, frame, LANES), F32),
         ],

time: 80.4 us -> 79.1 us (0.984)
  waiting for transfers between devices: 6.51 us -> 10.4 us
  local copies, waits for them, and re-layouts: 4.46 us -> 0.71 us
  Pallas kernels: 23.2 us -> 21.9 us
    ppermute x3, waiting for transfers between devices: 3.83 us -> 8.44 us  [neighbours(): before = lax.ppermute(tail, axis, [(i, i + 1) for i in range(count - 1)])]
    unnamed x22 -> x16, local copies, waits for them, and re-layouts: 4.46 us -> 0.71 us
    pallas_call x8 -> x7, Pallas kernels: 23.2 us -> 21.9 us  [call(): pl.pallas_call(body, out_shape=outs, in_specs=specs, out_specs=out_specs,...]
where the time goes in v7:
time: 79.1 us; the launch traced here: 78.7 us
  blocking collectives  33.3 us (42%)
  Pallas kernels  21.9 us (28%)
  starting transfers between devices  11.5 us (15%)
  waiting for transfers between devices  10.4 us (13%)
  between operations  0.82 us (1%)
    all_to_all x3, blocking collectives, everyone(): return lax.all_to_all(partial, ('row', 'col'), 0, 0, tiled=True)  33.3 us
    pallas_call x7, Pallas kernels, call(): pl.pallas_call(body, out_shape=outs, in_specs=specs, out_specs=out_specs,...  21.9 us
    ppermute x3, waiting for transfers between devices, neighbours(): before = lax.ppermute(tail, axis, [(i, i + 1) for i in range(count - 1)])  8.44 us
    ppermute x3, starting transfers between devices, neighbours(): before = lax.ppermute(tail, axis, [(i, i + 1) for i in range(count - 1)])  7.63 us
    ppermute x3, starting transfers between devices, neighbours(): after = lax.ppermute(head, axis, [(i + 1, i) for i in range(count - 1)])  3.88 us
    ppermute x3, waiting for transfers between devices, neighbours(): after = lax.ppermute(head, axis, [(i + 1, i) for i in range(count - 1)])  2.01 us
  transfers between devices with their start and end apart: 6, of which 2 were waited for; matrix products, arithmetic and copies ran while one was open for 0% of the time, Pallas kernels for 1%

profile of v7, /device:TPU:0, one launch (start us, length us, event | category | flops | bytes accessed | tf_op | source)
XLA Modules:
  0.0 78.7 jit_solution(10079574631950272659)
XLA Ops:
  0.7 2.3 %shard_map.103 = (f32[560,128]{1,0:T(8,128)}, f32[560,128]{1,0:T(8,128)}, f32[144,384]{1,0:T(8,128)}, f32[144,384]{1,0:T(8,128)}) custom-call(f32[16,2048]{1,0:T(8,128)} %objective.3, bf16[16,2048]{1,0:T(8,128)(2,1)} %center.3, bf16[16,2048]{1,0:T(8,128)(2,1)} %radius.3, bf16[3,16,2048]{2,1,0:T(8,128)(2,1)} %lower.5, bf16[3,16,2048]{2,1,0:T(8,128)(2,1)} %upper.5), custom_call_target="tpu_custom_call" | custom-call | flops 1048576 | bytes 4194304 | tf_op jit(solution)/shard_map/pallas_call | solution.py:35
  3.0 4.9 %collective-permute-start.2 = (f32[560,128]{1,0:T(8,128)}, f32[560,128]{1,0:T(8,128)S(1)}, u32[]{:S(2)}, u32[]{:S(2)}) collective-permute-start(f32[560,128]{1,0:T(8,128)} %get-tuple-element.38), channel_id=1, source_target_pairs={{0,4},{4,8},{8,12},{12,16},{16,20},{20,24},{24,28},{1,5},{5,9},{9,... | collective-permute-start | bytes 860168 | tf_op jit(solution)/shard_map/ppermute | solution.py:163
  7.9 1.3 %collective-permute-start.3 = (f32[560,128]{1,0:T(8,128)}, f32[560,128]{1,0:T(8,128)S(1)}, u32[]{:S(2)}, u32[]{:S(2)}) collective-permute-start(f32[560,128]{1,0:T(8,128)} %get-tuple-element.39), channel_id=1, source_target_pairs={{4,0},{8,4},{12,8},{16,12},{20,16},{24,20},{28,24},{5,1},{9,5},{13... | collective-permute-start | bytes 860168 | tf_op jit(solution)/shard_map/ppermute | solution.py:164
  9.2 1.5 %collective-permute-start = (f32[144,384]{1,0:T(8,128)}, f32[144,384]{1,0:T(8,128)S(1)}, u32[]{:S(2)}, u32[]{:S(2)}) collective-permute-start(f32[144,384]{1,0:T(8,128)} %get-tuple-element.36), channel_id=1, source_target_pairs={{0,1},{1,2},{2,3},{4,5},{5,6},{6,7},{8,9},{9,10},{10,11},{12,13},{... | collective-permute-start | bytes 663560 | tf_op jit(solution)/shard_map/ppermute | solution.py:163
  10.7 1.3 %collective-permute-start.1 = (f32[144,384]{1,0:T(8,128)}, f32[144,384]{1,0:T(8,128)S(1)}, u32[]{:S(2)}, u32[]{:S(2)}) collective-permute-start(f32[144,384]{1,0:T(8,128)} %get-tuple-element.37), channel_id=1, source_target_pairs={{1,0},{2,1},{3,2},{5,4},{6,5},{7,6},{9,8},{10,9},{11,10},{13,12},{... | collective-permute-start | bytes 663560 | tf_op jit(solution)/shard_map/ppermute | solution.py:164
  12.0 8.4 %collective-permute-done.2.above = f32[560,128]{1,0:T(8,128)S(1)} collective-permute-done((f32[560,128]{1,0:T(8,128)}, f32[560,128]{1,0:T(8,128)S(1)}, u32[]{:S(2)}, u32[]{:S(2)}) %collective-permute-start.2) | collective-permute-done | bytes 286752 | tf_op jit(solution)/shard_map/ppermute | solution.py:163
  20.4 0.0 collective-permute-done.3.below
  20.4 1.3 %collective-permute-start.4 = (f32[210,128]{1,0:T(8,128)S(1)}, f32[210,128]{1,0:T(8,128)S(1)}, u32[]{:S(2)}, u32[]{:S(2)}) collective-permute-start(f32[210,128]{1,0:T(8,128)S(1)} %get-tuple-element.40), channel_id=1, source_target_pairs={{0,1},{1,2},{2,3},{4,5},{5,6},{6,7},{8,9},{9,10},{10,11},{12,13},{... | collective-permute-start | bytes 322568 | tf_op jit(solution)/shard_map/ppermute | solution.py:163
  21.7 1.3 %collective-permute-start.5 = (f32[210,128]{1,0:T(8,128)S(1)}, f32[210,128]{1,0:T(8,128)S(1)}, u32[]{:S(2)}, u32[]{:S(2)}) collective-permute-start(f32[210,128]{1,0:T(8,128)S(1)} %get-tuple-element.41), channel_id=1, source_target_pairs={{1,0},{2,1},{3,2},{5,4},{6,5},{7,6},{9,8},{10,9},{11,10},{13,12},{... | collective-permute-start | bytes 322568 | tf_op jit(solution)/shard_map/ppermute | solution.py:164
  23.0 0.0 copy-start.7
  23.0 0.7 copy-done.7
  23.7 0.9 %shard_map.105 = (bf16[3,768,384]{2,1,0:T(8,128)(2,1)S(1)}, bf16[4,768,384]{2,1,0:T(8,128)(2,1)S(1)}, f32[8,128]{1,0:T(8,128)S(1)}) custom-call(f32[36,64,64]{2,1,0:T(8,128)S(1)} %bitcast.13, f32[4,64]{1,0:T(4,128)S(1)} %copy-done.7), custom_call_target="tpu_custom_call" | custom-call | flops 4194304 | bytes 4194304 | tf_op jit(solution)/shard_map/pallas_call | solution.py:35
  24.7 0.0 collective-permute-done.left
  24.7 0.0 collective-permute-done.1.right
  24.7 0.0 collective-permute-done.4.left_corner
  24.7 2.0 %collective-permute-done.5.right_corner = f32[210,128]{1,0:T(8,128)S(1)} collective-permute-done((f32[210,128]{1,0:T(8,128)S(1)}, f32[210,128]{1,0:T(8,128)S(1)}, u32[]{:S(2)}, u32[]{:S(2)}) %collective-permute-start.5) | collective-permute-done | bytes 107552 | tf_op jit(solution)/shard_map/ppermute | solution.py:164
  26.7 0.0 copy-start.6
  26.7 4.8 %shard_map.106 = (bf16[4,20,24,128]{3,2,1,0:T(8,128)(2,1)S(1)}, bf16[4,20,24,128]{3,2,1,0:T(8,128)(2,1)S(1)}, f32[20,24,128]{2,1,0:T(8,128)S(1)}, f32[3,20,24,12...) custom-call(f32[16,2048]{1,0:T(8,128)S(1)} %copy-done.3, ...), custom_call_target="tpu_custom_call" | custom-call | flops 1698693120 | bytes 4194304 | tf_op jit(solution)/shard_map/pallas_call | solution.py:35
  31.5 15.7 %all_to_all.33 = f32[32,1,128]{2,1,0:T(1,128)S(1)} all-to-all(f32[32,1,128]{2,1,0:T(1,128)S(1)} %bitcast.19), channel_id=1, replica_groups=mesh['row'=8,'col'=4] {'row','col'}, dimensions={0} | all-to-all | bytes 32768 | tf_op jit(solution)/shard_map/all_to_all | solution.py:489
  47.2 6.5 %shard_map.107 = (f32[3,20,24,128]{3,2,1,0:T(8,128)S(1)}, f32[3,18,24,128]{3,2,1,0:T(8,128)S(1)}, f32[2,18,24,128]{3,2,1,0:T(8,128)S(1)}, f32[3,18,16,128]{3,2,1...) custom-call(f32[32,128]{1,0:T(8,128)S(1)} %bitcast.15, ...), custom_call_target="tpu_custom_call" | custom-call | flops 1698693120 | bytes 4194304 | tf_op jit(solution)/shard_map/pallas_call | solution.py:35
  53.7 8.8 %all_to_all.34 = f32[32,1,128]{2,1,0:T(1,128)S(1)} all-to-all(f32[32,1,128]{2,1,0:T(1,128)S(1)} %bitcast.18), channel_id=1, replica_groups=mesh['row'=8,'col'=4] {'row','col'}, dimensions={0} | all-to-all | bytes 32768 | tf_op jit(solution)/shard_map/all_to_all | solution.py:489
  62.6 5.8 %shard_map.108 = (f32[3,16,2048]{2,1,0:T(8,128)S(1)}, f32[3,16,2048]{2,1,0:T(8,128)S(1)}, f32[3,16,2048]{2,1,0:T(8,128)S(1)}, f32[3,16,2048]{2,1,0:T(8,128)S(1)}, f32[32,128]{1,0:T(8,128)S(1)}) custom-call(f32[32,128]{1,0:T(8,128)S(1)} %bitcast.14, f32[3]{0:T(128)S(1)} %copy-done.6, bf16[4,20,24,128]{3,2,1,0:T(8,128)(2,1)S(1)} %get-tuple-element.46.near_box, ...), custom_call_target="tpu_custom_call" | custom-call | flops 1698693120 | bytes 4194304 | tf_op jit(solution)/shard_map/pallas_call | solution.py:35
  68.3 8.8 %all_to_all.35 = f32[32,1,128]{2,1,0:T(1,128)S(1)} all-to-all(f32[32,1,128]{2,1,0:T(1,128)S(1)} %bitcast.17), channel_id=1, replica_groups=mesh['row'=8,'col'=4] {'row','col'}, dimensions={0} | all-to-all | bytes 32768 | tf_op jit(solution)/shard_map/all_to_all | solution.py:489
  77.1 1.6 %shard_map.109 = (f32[3,16,2048]{2,1,0:T(8,128)}, f32[3,16,2048]{2,1,0:T(8,128)}, f32[3]{0:T(128)}) custom-call(f32[32,128]{1,0:T(8,128)S(1)} %bitcast.16, f32[3]{0:T(128)S(1)} %copy-done.6, f32[3,16,2048]{2,1,0:T(8,128)S(1)} %get-tuple-element.62.duals, f32[3,16,2048]{2,1,0:T(8,128)S(1)} %get-tuple-element.63.multipliers, ...), custom_call_target="tpu_custom_call" | custom-call | flops 1048576 | bytes 4194304 | tf_op jit(solution)/shard_map/pallas_call | solution.py:35
  (14 shorter events, 0.0 us)
Async XLA Ops:
  0.6 22.4 %copy-start = (f32[4,3,3,64,64]{4,3,2,1,0:T(8,128)S(1)}, f32[4,3,3,64,64]{4,3,2,1,0:T(8,128)}, u32[]{:S(2)}) copy-start(f32[4,3,3,64,64]{4,3,2,1,0:T(8,128)} %param.13) | copy-start | bytes 1769476
  0.6 26.0 %copy-start.1 = (bf16[3,16,2048]{2,1,0:T(8,128)(2,1)S(1)}, bf16[3,16,2048]{2,1,0:T(8,128)(2,1)}, u32[]{:S(2)}) copy-start(bf16[3,16,2048]{2,1,0:T(8,128)(2,1)} %lower.5) | copy-start | bytes 589828
  0.7 26.0 %copy-start.2 = (bf16[3,16,2048]{2,1,0:T(8,128)(2,1)S(1)}, bf16[3,16,2048]{2,1,0:T(8,128)(2,1)}, u32[]{:S(2)}) copy-start(bf16[3,16,2048]{2,1,0:T(8,128)(2,1)} %upper.5) | copy-start | bytes 589828
  0.7 26.0 %copy-start.3 = (f32[16,2048]{1,0:T(8,128)S(1)}, f32[16,2048]{1,0:T(8,128)}, u32[]{:S(2)}) copy-start(f32[16,2048]{1,0:T(8,128)} %objective.3) | copy-start | bytes 393220
  0.7 26.0 %copy-start.4 = (bf16[16,2048]{1,0:T(8,128)(2,1)S(1)}, bf16[16,2048]{1,0:T(8,128)(2,1)}, u32[]{:S(2)}) copy-start(bf16[16,2048]{1,0:T(8,128)(2,1)} %center.3) | copy-start | bytes 196612
  0.7 26.0 %copy-start.5 = (bf16[16,2048]{1,0:T(8,128)(2,1)S(1)}, bf16[16,2048]{1,0:T(8,128)(2,1)}, u32[]{:S(2)}) copy-start(bf16[16,2048]{1,0:T(8,128)(2,1)} %radius.3) | copy-start | bytes 196612
  3.0 17.4 %collective-permute-start.2 = (f32[560,128]{1,0:T(8,128)}, f32[560,128]{1,0:T(8,128)S(1)}, u32[]{:S(2)}, u32[]{:S(2)}) collective-permute-start(f32[560,128]{1,0:T(8,128)} %get-tuple-element.38), channel_id=1, source_target_pairs={{0,4},{4,8},{8,12},{12,16},{16,20},{20,24},{24,28},{1,5},{5,9},{9,... | collective-permute-start | bytes 860168 | tf_op jit(solution)/shard_map/ppermute | solution.py:163
  7.9 12.5 %collective-permute-start.3 = (f32[560,128]{1,0:T(8,128)}, f32[560,128]{1,0:T(8,128)S(1)}, u32[]{:S(2)}, u32[]{:S(2)}) collective-permute-start(f32[560,128]{1,0:T(8,128)} %get-tuple-element.39), channel_id=1, source_target_pairs={{4,0},{8,4},{12,8},{16,12},{20,16},{24,20},{28,24},{5,1},{9,5},{13... | collective-permute-start | bytes 860168 | tf_op jit(solution)/shard_map/ppermute | solution.py:164
  9.2 15.5 %collective-permute-start = (f32[144,384]{1,0:T(8,128)}, f32[144,384]{1,0:T(8,128)S(1)}, u32[]{:S(2)}, u32[]{:S(2)}) collective-permute-start(f32[144,384]{1,0:T(8,128)} %get-tuple-element.36), channel_id=1, source_target_pairs={{0,1},{1,2},{2,3},{4,5},{5,6},{6,7},{8,9},{9,10},{10,11},{12,13},{... | collective-permute-start | bytes 663560 | tf_op jit(solution)/shard_map/ppermute | solution.py:163
  10.7 14.0 %collective-permute-start.1 = (f32[144,384]{1,0:T(8,128)}, f32[144,384]{1,0:T(8,128)S(1)}, u32[]{:S(2)}, u32[]{:S(2)}) collective-permute-start(f32[144,384]{1,0:T(8,128)} %get-tuple-element.37), channel_id=1, source_target_pairs={{1,0},{2,1},{3,2},{5,4},{6,5},{7,6},{9,8},{10,9},{11,10},{13,12},{... | collective-permute-start | bytes 663560 | tf_op jit(solution)/shard_map/ppermute | solution.py:164
  20.4 4.3 %collective-permute-start.4 = (f32[210,128]{1,0:T(8,128)S(1)}, f32[210,128]{1,0:T(8,128)S(1)}, u32[]{:S(2)}, u32[]{:S(2)}) collective-permute-start(f32[210,128]{1,0:T(8,128)S(1)} %get-tuple-element.40), channel_id=1, source_target_pairs={{0,1},{1,2},{2,3},{4,5},{5,6},{6,7},{8,9},{9,10},{10,11},{12,13},{... | collective-permute-start | bytes 322568 | tf_op jit(solution)/shard_map/ppermute | solution.py:163
  21.7 5.0 %collective-permute-start.5 = (f32[210,128]{1,0:T(8,128)S(1)}, f32[210,128]{1,0:T(8,128)S(1)}, u32[]{:S(2)}, u32[]{:S(2)}) collective-permute-start(f32[210,128]{1,0:T(8,128)S(1)} %get-tuple-element.41), channel_id=1, source_target_pairs={{1,0},{2,1},{3,2},{5,4},{6,5},{7,6},{9,8},{10,9},{11,10},{13,12},{... | collective-permute-start | bytes 322568 | tf_op jit(solution)/shard_map/ppermute | solution.py:164
  23.0 0.7 copy-start.7
  26.7 20.5 %copy-start.6 = (f32[3]{0:T(128)S(1)}, f32[3]{0:T(128)}, u32[]{:S(2)}) copy-start(f32[3]{0:T(128)} %steps.5) | copy-start | bytes 40

commit v8 on v7

--- a/solution.py
+++ b/solution.py
@@ -130,7 +130,8 @@
             bottom[here, :] = value[rows - ROWS_SENT[m] :]
 
 
-def corners_body(above, below, head, tail):
+def corners_body(above, below, after, head, tail):
+    del after
     count = HALO_PAIRS * SENT
     size = above.shape[0]
     for part, source in enumerate((above, below)):
@@ -256,8 +257,89 @@
     out[...] = jnp.broadcast_to(packed, out.shape)
 
 
+def assemble(reads, above, below, left, right, corners, slots, rows, pairs, raw, gaps, target):
+    frame = rows + 2 * EDGE
+    blank = jnp.zeros((EDGE, LANES), F32)
+    for slot, q in enumerate(slots):
+        outside = not 1 <= q < pairs + 2 * HALO_PAIRS - 1
+        for m in range(9):
+            sent = ROWS_SENT[m]
+            if m < 3:
+                dest, at, edge = raw.at[m, slot], 0, WIDE
+            else:
+                dest, at, edge = (target.at[slot] if m == 8 else gaps.at[m - 3, slot]), EDGE - sent, EDGE
+                if outside:
+                    dest[...] = jnp.zeros((frame, LANES), F32)
+                    continue
+                if at:
+                    dest[0:EDGE, :] = blank
+                    dest[EDGE + rows : frame, :] = blank
+            dest[at : at + sent, :] = halo(above, *corners, 0, pairs, q, m)
+            dest[edge : edge + rows, :] = column(reads, left, right, rows, pairs, m, q)
+            dest[edge + rows : edge + rows + sent, :] = halo(below, *corners, 1, pairs, q, m)
+    count = len(slots)
+    spare = raw.shape[2] - rows - 2 * WIDE
+    raw[:, :, rows + 2 * WIDE :, :] = jnp.zeros((3, count, spare, LANES), F32)
+
+
+def start_convs(raw, target, store, sums, fwd, bwd, frame):
+    count = raw.shape[1]
+    slide(3, count, store, lambda q: [raw[0, q], 0.5 * raw[1, q], 0.5 * raw[2, q]])
+    tugged = store.at[3:4, :, 0:frame, :]
+    slide(1, count, tugged, lambda q: [target[q]])
+    for k in range(3):
+        multiply(store, k, 1, count - 2, fwd, k, sums, exact=True)
+    multiply(tugged, 0, 1, count - 2, bwd, LAYERS - 1, sums.at[3:4, :, :, 0:frame, :])
+
+
+def start_step(slot, out, raw, gaps, target, sums, bias, near_box, far_box, back, slope, mult):
+    frame = gaps.shape[2]
+    near = [raw[m, slot][1 : 1 + frame] for m in range(3)] + [gaps[4, slot]]
+    far = [gaps[m, slot] for m in range(4)]
+    for m in range(4):
+        near_box[m, out] = near[m].astype(BF16)
+        far_box[m, out] = far[m].astype(BF16)
+    new = jnp.zeros((frame, LANES), F32)
+    for k in range(3):
+        gap = near[1 + k] if k < 2 else far[0]
+        dl = 0.5 * (gap - far[1 + k]) - inner(sums, k, slot - 1, 1, frame) - bias[k : k + 1, :]
+        dl = jnp.where(near[1] > 0.0, dl, 0.0)
+        slope[k, out] = dl
+        new = new + dl * dl
+    tug = gathered(sums.at[3:4, :, :, 0:frame, :], 0, slot - 1)
+    back[out] = tug
+    bound = Bound(jnp.full((frame, LANES), -4.5 * math.log(2.0), F32))
+    dm = -0.5 * gap * bound.add(tug * gap)
+    mult[out] = dm
+    return new + dm * dm, bound.total(), target[slot] * bias[3:4, :]
+
+
+def middle_body(
+    objective, center, radius, lower, upper, above, below, fwd, bwd, bias,
+    near_box, far_box, back, slope, mult, totals,
+    raw, gaps, target, store, sums,
+):
+    rows, cols = objective.shape
+    pairs = cols // LANES
+    frame = rows + 2 * EDGE
+    reads = sources(objective, center, radius, lower, upper)
+    slots = range(HALO_PAIRS, HALO_PAIRS + pairs)
+    assemble(reads, above, below, None, None, (None, None), slots, rows, pairs, raw, gaps, target)
+    start_convs(raw, target, store, sums, fwd, bwd, frame)
+
+    def step(q, carry):
+        new = start_step(q + 1, q, raw, gaps, target, sums, bias, near_box, far_box, back, slope, mult)
+        return tuple(old + one for old, one in zip(carry, new))
+
+    zero = jnp.zeros((frame, LANES), F32)
+    sizes = lax.fori_loop(0, pairs - 2, step, (zero, zero, zero), unroll=2)
+    for j in range(3):
+        totals[j] = sizes[j]
+
+
 def first_body(
     objective, center, radius, lower, upper, left, right, above, below, left_corner, right_corner, fwd, bwd, bias,
+    near_in, far_in, back_in, slope_in, mult_in, totals,
     near_box, far_box, back, slope, mult, stat, value,
     raw, gaps, target, store, sums,
 ):
@@ -266,63 +348,24 @@
     frame = rows + 2 * EDGE
     wide = pairs + 4
     reads = sources(objective, center, radius, lower, upper)
-    for m in range(9):
-        sent = ROWS_SENT[m]
-        for q in range(pairs + 2 * HALO_PAIRS):
-            if m >= 3 and not 1 <= q < wide + 1:
-                continue
-            own = column(reads, left, right, rows, pairs, m, q)
-            if m < 3:
-                dest, at, edge = raw.at[m, q], 0, WIDE
-            else:
-                dest, at, edge = (target.at[q - 1] if m == 8 else gaps.at[m - 3, q - 1]), EDGE - sent, EDGE
-                if at:
-                    dest[0:EDGE, :] = jnp.zeros((EDGE, LANES), F32)
-                    dest[EDGE + rows : frame, :] = jnp.zeros((EDGE, LANES), F32)
-            dest[at : at + sent, :] = halo(above, left_corner, right_corner, 0, pairs, q, m)
-            dest[edge : edge + rows, :] = own
-            dest[edge + rows : edge + rows + sent, :] = halo(below, left_corner, right_corner, 1, pairs, q, m)
-    raw[:, :, rows + 2 * WIDE :, :] = jnp.zeros((3, wide + 2, raw.shape[2] - rows - 2 * WIDE, LANES), F32)
-
-    slide(3, wide + 2, store, lambda q: [raw[0, q], 0.5 * raw[1, q], 0.5 * raw[2, q]])
-    tugged = store.at[3:4, :, 0:frame, :]
-    slide(1, wide, tugged, lambda q: [target[q]])
-    for k in range(3):
-        multiply(store, k, 1, wide, fwd, k, sums, exact=True)
-    short = sums.at[3:4, :, :, 0:frame, :]
-    multiply(tugged, 0, 0, wide, bwd, LAYERS - 1, short)
-    zero = jnp.zeros((frame, LANES), F32)
-
-    def step(q, carry):
-        squares, worth, fixed = carry
-        near = [raw[m, q + 1][1 : 1 + frame] for m in range(3)] + [gaps[4, q]]
-        far = [gaps[m, q] for m in range(4)]
-        for m in range(4):
-            near_box[m, q] = near[m].astype(BF16)
-            far_box[m, q] = far[m].astype(BF16)
-        new = zero
-        for k in range(3):
-            gap = near[1 + k] if k < 2 else far[0]
-            dl = 0.5 * (gap - far[1 + k]) - inner(sums, k, q, 1, frame) - bias[k : k + 1, :]
-            dl = jnp.where(near[1] > 0.0, dl, 0.0)
-            slope[k, q] = dl
-            new = new + dl * dl
-        tug = gathered(short, 0, q)
-        back[q] = tug
-        bound = Bound(jnp.full((frame, LANES), -4.5 * math.log(2.0), F32))
-        dm = -0.5 * gap * bound.add(tug * gap)
-        mult[q] = dm
-        new = new + dm * dm
-        own = (q >= 2) & (q < wide - 2)
-        squares = squares + jnp.where(own, new, 0.0)
-        worth = worth + jnp.where(own, bound.total(), 0.0)
-        fixed = fixed + jnp.where(own, target[q] * bias[3:4, :], 0.0)
-        return squares, worth, fixed
-
-    squares, worth, fixed = lax.fori_loop(0, wide, step, (zero, zero, zero), unroll=2)
-    fixed = own_rows(fixed)
-    stats(stat, [own_rows(squares)])
-    stats(value, [own_rows(worth) + fixed, fixed])
+    corners = (left_corner, right_corner)
+    slots = list(range(5)) + list(range(wide - 3, wide + 2))
+    assemble(reads, above, below, left, right, corners, slots, rows, pairs, raw, gaps, target)
+    start_convs(raw, target, store, sums, fwd, bwd, frame)
+    here = slice(3, wide - 3)
+    near_box[:, here] = near_in[...]
+    far_box[:, here] = far_in[...]
+    back[here] = back_in[...]
+    slope[:, here] = slope_in[...]
+    mult[here] = mult_in[...]
+    sizes = [totals[j] for j in range(3)]
+    for slot, q in ((1, 0), (2, 1), (3, 2), (6, wide - 3), (7, wide - 2), (8, wide - 1)):
+        new = start_step(slot, q, raw, gaps, target, sums, bias, near_box, far_box, back, slope, mult)
+        if 2 <= q < wide - 2:
+            sizes = [old + one for old, one in zip(sizes, new)]
+    squares, worth, fixed = (own_rows(one) for one in sizes)
+    stats(stat, [squares])
+    stats(value, [worth + fixed, fixed])
 
 
 def second_body(
@@ -516,23 +559,36 @@
     left, right = neighbours(head, tail, "col")
     fwd, bwd, bias = weights(kernels, biases)
     corner = shape(2 * HALO_PAIRS * SENT, LANES)
-    corner_head, corner_tail = call(corners_body, (corner, corner), [], (above, below), 1 << 20)
+    corner_head, corner_tail = call(corners_body, (corner, corner), [], (above, below, bias), 1 << 20)
     left_corner, right_corner = neighbours(corner_head, corner_tail, "col")
 
-    box = shape(4, wide, frame, LANES, dtype=BF16)
-    full = shape(wide, frame, LANES)
+    def start_scratch(count):
+        return [
+            pltpu.VMEM((3, count, tall, LANES), F32),
+            pltpu.VMEM((5, count, frame, LANES), F32),
+            pltpu.VMEM((count, frame, LANES), F32),
+            pltpu.VMEM((4, count + 1, tall, LANES), F32),
+            pltpu.VMEM((4, 3, count - 2, tall, LANES), F32),
+        ]
+
+    def start_shapes(count):
+        box = shape(4, count, frame, LANES, dtype=BF16)
+        full = shape(count, frame, LANES)
+        return box, box, full, shape(3, count, frame, LANES), full
+
+    middle = call(
+        middle_body,
+        start_shapes(pairs - 2) + (shape(3, frame, LANES),),
+        start_scratch(pairs),
+        inputs + (above, below, fwd, bwd, bias),
+        flops,
+    )
     near_box, far_box, back, slope0, mult0, stat0, value0 = call(
         first_body,
-        (box, box, full, shape(3, wide, frame, LANES), full, spread, small),
-        [
-            pltpu.VMEM((3, wide + 2, tall, LANES), F32),
-            pltpu.VMEM((5, wide, frame, LANES), F32),
-            pltpu.VMEM((wide, frame, LANES), F32),
-            pltpu.VMEM((4, wide + 3, tall, LANES), F32),
-            pltpu.VMEM((4, 3, wide, tall, LANES), F32),
-        ],
-        inputs + (left, right, above, below, left_corner, right_corner, fwd, bwd, bias),
-        2 * flops,
+        start_shapes(wide) + (spread, small),
+        start_scratch(10),
+        inputs + (left, right, above, below, left_corner, right_corner, fwd, bwd, bias) + tuple(middle),
+        flops,
     )
 
     total0 = everyone(stat0)

time: 79.1 us -> 76.8 us (0.971)
  waiting for transfers between devices: 10.4 us -> 5.7 us
  local copies, waits for them, and re-layouts: 0.71 us -> 1.97 us
  blocking collectives: 33.3 us -> 34.2 us
    ppermute x3, waiting for transfers between devices: 8.44 us -> 5.55 us  [neighbours(): before = lax.ppermute(tail, axis, [(i, i + 1) for i in range(count - 1)])]
    ppermute x3, waiting for transfers between devices: 2.01 us -> 0.15 us  [neighbours(): after = lax.ppermute(head, axis, [(i + 1, i) for i in range(count - 1)])]
    unnamed x16, local copies, waits for them, and re-layouts: 0.71 us -> 1.97 us
    all_to_all x3, blocking collectives: 33.3 us -> 34.2 us  [everyone(): return lax.all_to_all(partial, ('row', 'col'), 0, 0, tiled=True)]
    pallas_call x7 -> x8, Pallas kernels: 21.9 us -> 22.3 us  [call(): pl.pallas_call(body, out_shape=outs, in_specs=specs, out_specs=out_specs,...]
  transfers between devices with their start and end apart: 6 -> 6, of which waited for: 2 -> 2; matrix products, arithmetic and copies ran while one was open for 0% -> 0% of each run, Pallas kernels for 1% -> 6%
where the time goes in v8:
time: 76.8 us; the launch traced here: 76.5 us
  blocking collectives  34.2 us (45%)
  Pallas kernels  22.3 us (29%)
  starting transfers between devices  11.5 us (15%)
  waiting for transfers between devices  5.7 us (7%)
  local copies, waits for them, and re-layouts  1.97 us (3%)
  between operations  0.83 us (1%)
    all_to_all x3, blocking collectives, everyone(): return lax.all_to_all(partial, ('row', 'col'), 0, 0, tiled=True)  34.2 us
    pallas_call x8, Pallas kernels, call(): pl.pallas_call(body, out_shape=outs, in_specs=specs, out_specs=out_specs,...  22.3 us
    ppermute x3, starting transfers between devices, neighbours(): before = lax.ppermute(tail, axis, [(i, i + 1) for i in range(count - 1)])  7.63 us
    ppermute x3, waiting for transfers between devices, neighbours(): before = lax.ppermute(tail, axis, [(i, i + 1) for i in range(count - 1)])  5.55 us
    ppermute x3, starting transfers between devices, neighbours(): after = lax.ppermute(head, axis, [(i + 1, i) for i in range(count - 1)])  3.88 us
    unnamed x16, local copies, waits for them, and re-layouts  1.97 us
  transfers between devices with their start and end apart: 6, of which 2 were waited for; matrix products, arithmetic and copies ran while one was open for 0% of the time, Pallas kernels for 6%

profile of v8, /device:TPU:0, one launch (start us, length us, event | category | flops | bytes accessed | tf_op | source)
XLA Modules:
  0.0 76.5 jit_solution(1268127202446669002)
XLA Ops:
  0.7 2.3 %shard_map.103 = (f32[560,128]{1,0:T(8,128)}, f32[560,128]{1,0:T(8,128)}, f32[144,384]{1,0:T(8,128)}, f32[144,384]{1,0:T(8,128)}) custom-call(f32[16,2048]{1,0:T(8,128)} %objective.5, bf16[16,2048]{1,0:T(8,128)(2,1)} %center.5, bf16[16,2048]{1,0:T(8,128)(2,1)} %radius.5, bf16[3,16,2048]{2,1,0:T(8,128)(2,1)} %lower.7, bf16[3,16,2048]{2,1,0:T(8,128)(2,1)} %upper.7), custom_call_target="tpu_custom_call" | custom-call | flops 1048576 | bytes 4194304 | tf_op jit(solution)/shard_map/pallas_call | solution.py:35
  3.0 4.9 %collective-permute-start.2 = (f32[560,128]{1,0:T(8,128)}, f32[560,128]{1,0:T(8,128)S(1)}, u32[]{:S(2)}, u32[]{:S(2)}) collective-permute-start(f32[560,128]{1,0:T(8,128)} %get-tuple-element.44), channel_id=1, source_target_pairs={{0,4},{4,8},{8,12},{12,16},{16,20},{20,24},{24,28},{1,5},{5,9},{9,... | collective-permute-start | bytes 860168 | tf_op jit(solution)/shard_map/ppermute | solution.py:164
  7.8 1.3 %collective-permute-start.3 = (f32[560,128]{1,0:T(8,128)}, f32[560,128]{1,0:T(8,128)S(1)}, u32[]{:S(2)}, u32[]{:S(2)}) collective-permute-start(f32[560,128]{1,0:T(8,128)} %get-tuple-element.45), channel_id=1, source_target_pairs={{4,0},{8,4},{12,8},{16,12},{20,16},{24,20},{28,24},{5,1},{9,5},{13... | collective-permute-start | bytes 860168 | tf_op jit(solution)/shard_map/ppermute | solution.py:165
  9.1 1.5 %collective-permute-start = (f32[144,384]{1,0:T(8,128)}, f32[144,384]{1,0:T(8,128)S(1)}, u32[]{:S(2)}, u32[]{:S(2)}) collective-permute-start(f32[144,384]{1,0:T(8,128)} %get-tuple-element.42), channel_id=1, source_target_pairs={{0,1},{1,2},{2,3},{4,5},{5,6},{6,7},{8,9},{9,10},{10,11},{12,13},{... | collective-permute-start | bytes 663560 | tf_op jit(solution)/shard_map/ppermute | solution.py:164
  10.6 1.3 %collective-permute-start.1 = (f32[144,384]{1,0:T(8,128)}, f32[144,384]{1,0:T(8,128)S(1)}, u32[]{:S(2)}, u32[]{:S(2)}) collective-permute-start(f32[144,384]{1,0:T(8,128)} %get-tuple-element.43), channel_id=1, source_target_pairs={{1,0},{2,1},{3,2},{5,4},{6,5},{7,6},{9,8},{10,9},{11,10},{13,12},{... | collective-permute-start | bytes 663560 | tf_op jit(solution)/shard_map/ppermute | solution.py:165
  11.9 0.0 copy-start.3
  11.9 1.3 %copy-done.3 = f32[4,3,3,64,64]{4,3,2,1,0:T(8,128)S(1)} copy-done((f32[4,3,3,64,64]{4,3,2,1,0:T(8,128)S(1)}, f32[4,3,3,64,64]{4,3,2,1,0:T(8,128)}, u32[]{:S(2)}) %copy-start.3) | copy-done | bytes 589848
  13.2 0.7 copy-done.7
  13.9 0.9 %shard_map.104 = (bf16[3,768,384]{2,1,0:T(8,128)(2,1)S(1)}, bf16[4,768,384]{2,1,0:T(8,128)(2,1)S(1)}, f32[8,128]{1,0:T(8,128)S(1)}) custom-call(f32[36,64,64]{2,1,0:T(8,128)S(1)} %bitcast.13, f32[4,64]{1,0:T(4,128)S(1)} %copy-done.7), custom_call_target="tpu_custom_call" | custom-call | flops 4194304 | bytes 4194304 | tf_op jit(solution)/shard_map/pallas_call | solution.py:35
  14.8 5.5 %collective-permute-done.2.above = f32[560,128]{1,0:T(8,128)S(1)} collective-permute-done((f32[560,128]{1,0:T(8,128)}, f32[560,128]{1,0:T(8,128)S(1)}, u32[]{:S(2)}, u32[]{:S(2)}) %collective-permute-start.2) | collective-permute-done | bytes 286752 | tf_op jit(solution)/shard_map/ppermute | solution.py:164
  20.3 0.0 collective-permute-done.3.below
  20.4 1.3 %collective-permute-start.4 = (f32[210,128]{1,0:T(8,128)S(1)}, f32[210,128]{1,0:T(8,128)S(1)}, u32[]{:S(2)}, u32[]{:S(2)}) collective-permute-start(f32[210,128]{1,0:T(8,128)S(1)} %get-tuple-element.47), channel_id=1, source_target_pairs={{0,1},{1,2},{2,3},{4,5},{5,6},{6,7},{8,9},{9,10},{10,11},{12,13},{... | collective-permute-start | bytes 322568 | tf_op jit(solution)/shard_map/ppermute | solution.py:164
  21.7 1.3 %collective-permute-start.5 = (f32[210,128]{1,0:T(8,128)S(1)}, f32[210,128]{1,0:T(8,128)S(1)}, u32[]{:S(2)}, u32[]{:S(2)}) collective-permute-start(f32[210,128]{1,0:T(8,128)S(1)} %get-tuple-element.48), channel_id=1, source_target_pairs={{1,0},{2,1},{3,2},{5,4},{6,5},{7,6},{9,8},{10,9},{11,10},{13,12},{... | collective-permute-start | bytes 322568 | tf_op jit(solution)/shard_map/ppermute | solution.py:165
  23.0 3.4 %shard_map.106 = (bf16[4,14,24,128]{3,2,1,0:T(8,128)(2,1)S(1)}, bf16[4,14,24,128]{3,2,1,0:T(8,128)(2,1)S(1)}, f32[14,24,128]{2,1,0:T(8,128)S(1)}, f32[3,14,24,12...) custom-call(f32[16,2048]{1,0:T(8,128)S(1)} %copy-done.2, bf16[16,2048]{1,0:T(8,128)(2,1)S(1)} %copy-done.4, ...), custom_call_target="tpu_custom_call" | custom-call | flops 849346560 | bytes 4194304 | tf_op jit(solution)/shard_map/pallas_call | solution.py:35
  26.5 0.0 collective-permute-done.1.right
  26.5 0.0 collective-permute-done.4.left_corner
  26.5 0.1 collective-permute-done.5.right_corner
  26.6 1.8 %shard_map.107 = (bf16[4,20,24,128]{3,2,1,0:T(8,128)(2,1)S(1)}, bf16[4,20,24,128]{3,2,1,0:T(8,128)(2,1)S(1)}, f32[20,24,128]{2,1,0:T(8,128)S(1)}, f32[3,20,24,12...) custom-call(f32[16,2048]{1,0:T(8,128)S(1)} %copy-done.2, ...), custom_call_target="tpu_custom_call" | custom-call | flops 849346560 | bytes 4194304 | tf_op jit(solution)/shard_map/pallas_call | solution.py:35
  28.4 16.5 %all_to_all.33 = f32[32,1,128]{2,1,0:T(1,128)S(1)} all-to-all(f32[32,1,128]{2,1,0:T(1,128)S(1)} %bitcast.17), channel_id=1, replica_groups=mesh['row'=8,'col'=4] {'row','col'}, dimensions={0} | all-to-all | bytes 32768 | tf_op jit(solution)/shard_map/all_to_all | solution.py:532
  44.9 6.5 %shard_map.108 = (f32[3,20,24,128]{3,2,1,0:T(8,128)S(1)}, f32[3,18,24,128]{3,2,1,0:T(8,128)S(1)}, f32[2,18,24,128]{3,2,1,0:T(8,128)S(1)}, f32[3,18,16,128]{3,2,1...) custom-call(f32[32,128]{1,0:T(8,128)S(1)} %bitcast.15, ...), custom_call_target="tpu_custom_call" | custom-call | flops 1698693120 | bytes 4194304 | tf_op jit(solution)/shard_map/pallas_call | solution.py:35
  51.5 8.8 %all_to_all.34 = f32[32,1,128]{2,1,0:T(1,128)S(1)} all-to-all(f32[32,1,128]{2,1,0:T(1,128)S(1)} %bitcast.19), channel_id=1, replica_groups=mesh['row'=8,'col'=4] {'row','col'}, dimensions={0} | all-to-all | bytes 32768 | tf_op jit(solution)/shard_map/all_to_all | solution.py:532
  60.3 5.7 %shard_map.109 = (f32[3,16,2048]{2,1,0:T(8,128)S(1)}, f32[3,16,2048]{2,1,0:T(8,128)S(1)}, f32[3,16,2048]{2,1,0:T(8,128)S(1)}, f32[3,16,2048]{2,1,0:T(8,128)S(1)}, f32[32,128]{1,0:T(8,128)S(1)}) custom-call(f32[32,128]{1,0:T(8,128)S(1)} %bitcast.14, f32[3]{0:T(128)S(1)} %copy-done.6, bf16[4,20,24,128]{3,2,1,0:T(8,128)(2,1)S(1)} %get-tuple-element.58.near_box, ...), custom_call_target="tpu_custom_call" | custom-call | flops 1698693120 | bytes 4194304 | tf_op jit(solution)/shard_map/pallas_call | solution.py:35
  66.0 8.8 %all_to_all.35 = f32[32,1,128]{2,1,0:T(1,128)S(1)} all-to-all(f32[32,1,128]{2,1,0:T(1,128)S(1)} %bitcast.18), channel_id=1, replica_groups=mesh['row'=8,'col'=4] {'row','col'}, dimensions={0} | all-to-all | bytes 32768 | tf_op jit(solution)/shard_map/all_to_all | solution.py:532
  74.9 1.6 %shard_map.110 = (f32[3,16,2048]{2,1,0:T(8,128)}, f32[3,16,2048]{2,1,0:T(8,128)}, f32[3]{0:T(128)}) custom-call(f32[32,128]{1,0:T(8,128)S(1)} %bitcast.16, f32[3]{0:T(128)S(1)} %copy-done.6, f32[3,16,2048]{2,1,0:T(8,128)S(1)} %get-tuple-element.74.duals, f32[3,16,2048]{2,1,0:T(8,128)S(1)} %get-tuple-element.75.multipliers, ...), custom_call_target="tpu_custom_call" | custom-call | flops 1048576 | bytes 4194304 | tf_op jit(solution)/shard_map/pallas_call | solution.py:35
  (15 shorter events, 0.0 us)
Async XLA Ops:
  0.6 22.3 %copy-start.1 = (bf16[3,16,2048]{2,1,0:T(8,128)(2,1)S(1)}, bf16[3,16,2048]{2,1,0:T(8,128)(2,1)}, u32[]{:S(2)}) copy-start(bf16[3,16,2048]{2,1,0:T(8,128)(2,1)} %upper.7) | copy-start | bytes 589828
  0.6 22.3 %copy-start = (bf16[3,16,2048]{2,1,0:T(8,128)(2,1)S(1)}, bf16[3,16,2048]{2,1,0:T(8,128)(2,1)}, u32[]{:S(2)}) copy-start(bf16[3,16,2048]{2,1,0:T(8,128)(2,1)} %lower.7) | copy-start | bytes 589828
  0.7 22.3 %copy-start.5 = (bf16[16,2048]{1,0:T(8,128)(2,1)S(1)}, bf16[16,2048]{1,0:T(8,128)(2,1)}, u32[]{:S(2)}) copy-start(bf16[16,2048]{1,0:T(8,128)(2,1)} %radius.5) | copy-start | bytes 196612
  0.7 22.3 %copy-start.4 = (bf16[16,2048]{1,0:T(8,128)(2,1)S(1)}, bf16[16,2048]{1,0:T(8,128)(2,1)}, u32[]{:S(2)}) copy-start(bf16[16,2048]{1,0:T(8,128)(2,1)} %center.5) | copy-start | bytes 196612
  0.7 22.3 %copy-start.2 = (f32[16,2048]{1,0:T(8,128)S(1)}, f32[16,2048]{1,0:T(8,128)}, u32[]{:S(2)}) copy-start(f32[16,2048]{1,0:T(8,128)} %objective.5) | copy-start | bytes 393220
  3.0 17.4 %collective-permute-start.2 = (f32[560,128]{1,0:T(8,128)}, f32[560,128]{1,0:T(8,128)S(1)}, u32[]{:S(2)}, u32[]{:S(2)}) collective-permute-start(f32[560,128]{1,0:T(8,128)} %get-tuple-element.44), channel_id=1, source_target_pairs={{0,4},{4,8},{8,12},{12,16},{16,20},{20,24},{24,28},{1,5},{5,9},{9,... | collective-permute-start | bytes 860168 | tf_op jit(solution)/shard_map/ppermute | solution.py:164
  7.8 12.5 %collective-permute-start.3 = (f32[560,128]{1,0:T(8,128)}, f32[560,128]{1,0:T(8,128)S(1)}, u32[]{:S(2)}, u32[]{:S(2)}) collective-permute-start(f32[560,128]{1,0:T(8,128)} %get-tuple-element.45), channel_id=1, source_target_pairs={{4,0},{8,4},{12,8},{16,12},{20,16},{24,20},{28,24},{5,1},{9,5},{13... | collective-permute-start | bytes 860168 | tf_op jit(solution)/shard_map/ppermute | solution.py:165
  9.1 17.3 %collective-permute-start = (f32[144,384]{1,0:T(8,128)}, f32[144,384]{1,0:T(8,128)S(1)}, u32[]{:S(2)}, u32[]{:S(2)}) collective-permute-start(f32[144,384]{1,0:T(8,128)} %get-tuple-element.42), channel_id=1, source_target_pairs={{0,1},{1,2},{2,3},{4,5},{5,6},{6,7},{8,9},{9,10},{10,11},{12,13},{... | collective-permute-start | bytes 663560 | tf_op jit(solution)/shard_map/ppermute | solution.py:164
  10.6 15.9 %collective-permute-start.1 = (f32[144,384]{1,0:T(8,128)}, f32[144,384]{1,0:T(8,128)S(1)}, u32[]{:S(2)}, u32[]{:S(2)}) collective-permute-start(f32[144,384]{1,0:T(8,128)} %get-tuple-element.43), channel_id=1, source_target_pairs={{1,0},{2,1},{3,2},{5,4},{6,5},{7,6},{9,8},{10,9},{11,10},{13,12},{... | collective-permute-start | bytes 663560 | tf_op jit(solution)/shard_map/ppermute | solution.py:165
  11.9 1.3 %copy-start.3 = (f32[4,3,3,64,64]{4,3,2,1,0:T(8,128)S(1)}, f32[4,3,3,64,64]{4,3,2,1,0:T(8,128)}, u32[]{:S(2)}) copy-start(f32[4,3,3,64,64]{4,3,2,1,0:T(8,128)} %param.13) | copy-start | bytes 1769476
  13.2 0.7 copy-start.7
  20.4 6.1 %collective-permute-start.4 = (f32[210,128]{1,0:T(8,128)S(1)}, f32[210,128]{1,0:T(8,128)S(1)}, u32[]{:S(2)}, u32[]{:S(2)}) collective-permute-start(f32[210,128]{1,0:T(8,128)S(1)} %get-tuple-element.47), channel_id=1, source_target_pairs={{0,1},{1,2},{2,3},{4,5},{5,6},{6,7},{8,9},{9,10},{10,11},{12,13},{... | collective-permute-start | bytes 322568 | tf_op jit(solution)/shard_map/ppermute | solution.py:164
  21.7 5.0 %collective-permute-start.5 = (f32[210,128]{1,0:T(8,128)S(1)}, f32[210,128]{1,0:T(8,128)S(1)}, u32[]{:S(2)}, u32[]{:S(2)}) collective-permute-start(f32[210,128]{1,0:T(8,128)S(1)} %get-tuple-element.48), channel_id=1, source_target_pairs={{1,0},{2,1},{3,2},{5,4},{6,5},{7,6},{9,8},{10,9},{11,10},{13,12},{... | collective-permute-start | bytes 322568 | tf_op jit(solution)/shard_map/ppermute | solution.py:165
  26.6 18.3 %copy-start.6 = (f32[3]{0:T(128)S(1)}, f32[3]{0:T(128)}, u32[]{:S(2)}) copy-start(f32[3]{0:T(128)} %steps.5) | copy-start | bytes 40

commit v9 on v8

--- a/solution.py
+++ b/solution.py
@@ -22,6 +22,8 @@
 ROWS_SENT = (5, 5, 5, 4, 4, 4, 2, 3, 3)
 ROW_START = tuple(sum(ROWS_SENT[:m]) for m in range(9))
 SENT = sum(ROWS_SENT)
+OUTER = 3 * WIDE
+CORNER = (0, OUTER, OUTER + SENT, OUTER + 2 * SENT, OUTER + 3 * SENT, OUTER + 4 * SENT, 2 * OUTER + 4 * SENT)
 WINDOW = 4 * CH
 
 VMEM = pl.BlockSpec(memory_space=pltpu.VMEM)
@@ -119,25 +121,29 @@
     for m, read in enumerate(sources(*held)):
         head[pl.ds(m * rows, rows), :] = read(pl.ds(0, strip))
         tail[pl.ds(m * rows, rows), :] = read(pl.ds(cols - strip, strip))
-    row = lax.broadcasted_iota(jnp.int32, (rows, LANES), 0)
-    outer = (row >= 2) & (row < rows - 2)
     for q in range(cols // LANES):
-        values = [read(pl.ds(q * LANES, LANES)) for read in sources(*held)]
+        ends_of([read(pl.ds(q * LANES, LANES)) for read in sources(*held)], top, bottom, q * SENT)
+
+
+def ends_of(values, top, bottom, start):
+    rows = values[0].shape[0]
+    if len(values) > 3:
+        row = lax.broadcasted_iota(jnp.int32, (rows, LANES), 0)
+        outer = (row >= 2) & (row < rows - 2)
         values[3] = jnp.where(outer, values[3] - values[6], values[3])
-        for m, value in enumerate(values):
-            here = pl.ds(q * SENT + ROW_START[m], ROWS_SENT[m])
-            top[here, :] = value[: ROWS_SENT[m]]
-            bottom[here, :] = value[rows - ROWS_SENT[m] :]
-
-
-def corners_body(above, below, after, head, tail):
-    del after
-    count = HALO_PAIRS * SENT
-    size = above.shape[0]
-    for part, source in enumerate((above, below)):
-        here = pl.ds(part * count, count)
-        head[here, :] = source[0:count, :]
-        tail[here, :] = source[size - count : size, :]
+    for m, value in enumerate(values):
+        here = pl.ds(start + ROW_START[m], ROWS_SENT[m])
+        top[here, :] = value[: ROWS_SENT[m]]
+        bottom[here, :] = value[rows - ROWS_SENT[m] :]
+
+
+def corners_body(left, right, top, bottom):
+    rows = left.shape[0] // 9
+    for j in range(2 * HALO_PAIRS):
+        strip, q = (left, j) if j < HALO_PAIRS else (right, j - HALO_PAIRS)
+        maps = 3 if j in (0, 2 * HALO_PAIRS - 1) else 9
+        values = [strip[pl.ds(m * rows, rows), pl.ds(q * LANES, LANES)] for m in range(maps)]
+        ends_of(values, top, bottom, CORNER[j])
 
 
 def column(reads, left, right, rows, pairs, m, q):
@@ -149,14 +155,12 @@
     return reads[m](pl.ds((q - HALO_PAIRS) * LANES, LANES))
 
 
-def halo(middle, left, right, part, pairs, q, m):
-    if q < HALO_PAIRS:
-        source, at = left, part * HALO_PAIRS + q
-    elif q >= HALO_PAIRS + pairs:
-        source, at = right, part * HALO_PAIRS + q - HALO_PAIRS - pairs
+def halo(middle, corner, pairs, q, m):
+    if HALO_PAIRS <= q < HALO_PAIRS + pairs:
+        source, start = middle, (q - HALO_PAIRS) * SENT
     else:
-        source, at = middle, q - HALO_PAIRS
-    return source[pl.ds(at * SENT + ROW_START[m], ROWS_SENT[m]), :]
+        source, start = corner, CORNER[q if q < HALO_PAIRS else q - pairs]
+    return source[pl.ds(start + ROW_START[m], ROWS_SENT[m]), :]
 
 
 def neighbours(head, tail, axis):
@@ -274,9 +278,9 @@
                 if at:
                     dest[0:EDGE, :] = blank
                     dest[EDGE + rows : frame, :] = blank
-            dest[at : at + sent, :] = halo(above, *corners, 0, pairs, q, m)
+            dest[at : at + sent, :] = halo(above, corners[0], pairs, q, m)
             dest[edge : edge + rows, :] = column(reads, left, right, rows, pairs, m, q)
-            dest[edge + rows : edge + rows + sent, :] = halo(below, *corners, 1, pairs, q, m)
+            dest[edge + rows : edge + rows + sent, :] = halo(below, corners[1], pairs, q, m)
     count = len(slots)
     spare = raw.shape[2] - rows - 2 * WIDE
     raw[:, :, rows + 2 * WIDE :, :] = jnp.zeros((3, count, spare, LANES), F32)
@@ -338,7 +342,7 @@
 
 
 def first_body(
-    objective, center, radius, lower, upper, left, right, above, below, left_corner, right_corner, fwd, bwd, bias,
+    objective, center, radius, lower, upper, left, right, above, below, above_corner, below_corner, fwd, bwd, bias,
     near_in, far_in, back_in, slope_in, mult_in, totals,
     near_box, far_box, back, slope, mult, stat, value,
     raw, gaps, target, store, sums,
@@ -348,7 +352,7 @@
     frame = rows + 2 * EDGE
     wide = pairs + 4
     reads = sources(objective, center, radius, lower, upper)
-    corners = (left_corner, right_corner)
+    corners = (above_corner, below_corner)
     slots = list(range(5)) + list(range(wide - 3, wide + 2))
     assemble(reads, above, below, left, right, corners, slots, rows, pairs, raw, gaps, target)
     start_convs(raw, target, store, sums, fwd, bwd, frame)
@@ -558,9 +562,9 @@
     above, below = neighbours(top, bottom, "row")
     left, right = neighbours(head, tail, "col")
     fwd, bwd, bias = weights(kernels, biases)
-    corner = shape(2 * HALO_PAIRS * SENT, LANES)
-    corner_head, corner_tail = call(corners_body, (corner, corner), [], (above, below, bias), 1 << 20)
-    left_corner, right_corner = neighbours(corner_head, corner_tail, "col")
+    corner = shape(CORNER[-1], LANES)
+    corner_top, corner_bottom = call(corners_body, (corner, corner), [], (left, right), 1 << 20)
+    above_corner, below_corner = neighbours(corner_top, corner_bottom, "row")
 
     def start_scratch(count):
         return [
@@ -587,7 +591,7 @@
         first_body,
         start_shapes(wide) + (spread, small),
         start_scratch(10),
-        inputs + (left, right, above, below, left_corner, right_corner, fwd, bwd, bias) + tuple(middle),
+        inputs + (left, right, above, below, above_corner, below_corner, fwd, bwd, bias) + tuple(middle),
         flops,
     )
 

time: 76.8 us -> 79.3 us (1.033)
  starting transfers between devices: 11.5 us -> 14.8 us
  waiting for transfers between devices: 5.7 us -> 3.86 us
  blocking collectives: 34.2 us -> 35.2 us
    ppermute x3, waiting for transfers between devices: 5.55 us -> 0.01 us  [neighbours(): before = lax.ppermute(tail, axis, [(i, i + 1) for i in range(count - 1)])]
    ppermute x3, waiting for transfers between devices: 0.15 us -> 3.85 us  [neighbours(): after = lax.ppermute(head, axis, [(i + 1, i) for i in range(count - 1)])]
    ppermute x3, starting transfers between devices: 7.63 us -> 10.9 us  [neighbours(): before = lax.ppermute(tail, axis, [(i, i + 1) for i in range(count - 1)])]
    all_to_all x3, blocking collectives: 34.2 us -> 35.2 us  [everyone(): return lax.all_to_all(partial, ('row', 'col'), 0, 0, tiled=True)]
  transfers between devices with their start and end apart: 6 -> 6, of which waited for: 2 -> 1; matrix products, arithmetic and copies ran while one was open for 0% -> 0% of each run, Pallas kernels for 6% -> 6%
where the time goes in v9:
time: 79.3 us; the launch traced here: 78.9 us
  blocking collectives  35.2 us (44%)
  Pallas kernels  22.3 us (28%)
  starting transfers between devices  14.8 us (19%)
  waiting for transfers between devices  3.86 us (5%)
  local copies, waits for them, and re-layouts  1.97 us (2%)
  between operations  0.85 us (1%)
    all_to_all x3, blocking collectives, everyone(): return lax.all_to_all(partial, ('row', 'col'), 0, 0, tiled=True)  35.2 us
    pallas_call x8, Pallas kernels, call(): pl.pallas_call(body, out_shape=outs, in_specs=specs, out_specs=out_specs,...  22.3 us
    ppermute x3, starting transfers between devices, neighbours(): before = lax.ppermute(tail, axis, [(i, i + 1) for i in range(count - 1)])  10.9 us
    ppermute x3, starting transfers between devices, neighbours(): after = lax.ppermute(head, axis, [(i + 1, i) for i in range(count - 1)])  3.88 us
    ppermute x3, waiting for transfers between devices, neighbours(): after = lax.ppermute(head, axis, [(i + 1, i) for i in range(count - 1)])  3.85 us
    unnamed x16, local copies, waits for them, and re-layouts  1.97 us
  transfers between devices with their start and end apart: 6, of which 1 were waited for; matrix products, arithmetic and copies ran while one was open for 0% of the time, Pallas kernels for 6%

profile of v9, /device:TPU:0, one launch (start us, length us, event | category | flops | bytes accessed | tf_op | source)
XLA Modules:
  0.0 78.9 jit_solution(12030427277985103328)
XLA Ops:
  0.7 2.3 %shard_map.103 = (f32[560,128]{1,0:T(8,128)}, f32[560,128]{1,0:T(8,128)}, f32[144,384]{1,0:T(8,128)}, f32[144,384]{1,0:T(8,128)}) custom-call(f32[16,2048]{1,0:T(8,128)} %objective.5, bf16[16,2048]{1,0:T(8,128)(2,1)} %center.5, bf16[16,2048]{1,0:T(8,128)(2,1)} %radius.5, bf16[3,16,2048]{2,1,0:T(8,128)(2,1)} %lower.7, bf16[3,16,2048]{2,1,0:T(8,128)(2,1)} %upper.7), custom_call_target="tpu_custom_call" | custom-call | flops 1048576 | bytes 4194304 | tf_op jit(solution)/shard_map/pallas_call | solution.py:37
  3.0 4.9 %collective-permute-start.2 = (f32[560,128]{1,0:T(8,128)}, f32[560,128]{1,0:T(8,128)S(1)}, u32[]{:S(2)}, u32[]{:S(2)}) collective-permute-start(f32[560,128]{1,0:T(8,128)} %get-tuple-element.44), channel_id=1, source_target_pairs={{0,4},{4,8},{8,12},{12,16},{16,20},{20,24},{24,28},{1,5},{5,9},{9,... | collective-permute-start | bytes 860168 | tf_op jit(solution)/shard_map/ppermute | solution.py:168
  7.8 1.3 %collective-permute-start.3 = (f32[560,128]{1,0:T(8,128)}, f32[560,128]{1,0:T(8,128)S(1)}, u32[]{:S(2)}, u32[]{:S(2)}) collective-permute-start(f32[560,128]{1,0:T(8,128)} %get-tuple-element.45), channel_id=1, source_target_pairs={{4,0},{8,4},{12,8},{16,12},{20,16},{24,20},{28,24},{5,1},{9,5},{13... | collective-permute-start | bytes 860168 | tf_op jit(solution)/shard_map/ppermute | solution.py:169
  9.1 1.5 %collective-permute-start = (f32[144,384]{1,0:T(8,128)}, f32[144,384]{1,0:T(8,128)S(1)}, u32[]{:S(2)}, u32[]{:S(2)}) collective-permute-start(f32[144,384]{1,0:T(8,128)} %get-tuple-element.42), channel_id=1, source_target_pairs={{0,1},{1,2},{2,3},{4,5},{5,6},{6,7},{8,9},{9,10},{10,11},{12,13},{... | collective-permute-start | bytes 663560 | tf_op jit(solution)/shard_map/ppermute | solution.py:168
  10.6 1.3 %collective-permute-start.1 = (f32[144,384]{1,0:T(8,128)}, f32[144,384]{1,0:T(8,128)S(1)}, u32[]{:S(2)}, u32[]{:S(2)}) collective-permute-start(f32[144,384]{1,0:T(8,128)} %get-tuple-element.43), channel_id=1, source_target_pairs={{1,0},{2,1},{3,2},{5,4},{6,5},{7,6},{9,8},{10,9},{11,10},{13,12},{... | collective-permute-start | bytes 663560 | tf_op jit(solution)/shard_map/ppermute | solution.py:169
  11.9 0.0 collective-permute-done.left
  11.9 3.8 %collective-permute-done.1.right = f32[144,384]{1,0:T(8,128)S(1)} collective-permute-done((f32[144,384]{1,0:T(8,128)}, f32[144,384]{1,0:T(8,128)S(1)}, u32[]{:S(2)}, u32[]{:S(2)}) %collective-permute-start.1) | collective-permute-done | bytes 221216 | tf_op jit(solution)/shard_map/ppermute | solution.py:169
  15.8 4.6 %collective-permute-start.4 = (f32[170,128]{1,0:T(8,128)S(1)}, f32[170,128]{1,0:T(8,128)S(1)}, u32[]{:S(2)}, u32[]{:S(2)}) collective-permute-start(f32[170,128]{1,0:T(8,128)S(1)} %get-tuple-element.46), channel_id=1, source_target_pairs={{0,4},{4,8},{8,12},{12,16},{16,20},{20,24},{24,28},{1,5},{5,9},{9,... | collective-permute-start | bytes 261128 | tf_op jit(solution)/shard_map/ppermute | solution.py:168
  20.3 1.3 %collective-permute-start.5 = (f32[170,128]{1,0:T(8,128)S(1)}, f32[170,128]{1,0:T(8,128)S(1)}, u32[]{:S(2)}, u32[]{:S(2)}) collective-permute-start(f32[170,128]{1,0:T(8,128)S(1)} %get-tuple-element.47), channel_id=1, source_target_pairs={{4,0},{8,4},{12,8},{16,12},{20,16},{24,20},{28,24},{5,1},{9,5},{13... | collective-permute-start | bytes 261128 | tf_op jit(solution)/shard_map/ppermute | solution.py:169
  21.6 0.0 copy-start.2
  21.7 1.3 %copy-done.2 = f32[4,3,3,64,64]{4,3,2,1,0:T(8,128)S(1)} copy-done((f32[4,3,3,64,64]{4,3,2,1,0:T(8,128)S(1)}, f32[4,3,3,64,64]{4,3,2,1,0:T(8,128)}, u32[]{:S(2)}) %copy-start.2) | copy-done | bytes 589848
  22.9 0.7 copy-done.7
  23.6 0.9 %shard_map.105 = (bf16[3,768,384]{2,1,0:T(8,128)(2,1)S(1)}, bf16[4,768,384]{2,1,0:T(8,128)(2,1)S(1)}, f32[8,128]{1,0:T(8,128)S(1)}) custom-call(f32[36,64,64]{2,1,0:T(8,128)S(1)} %bitcast.13, f32[4,64]{1,0:T(4,128)S(1)} %copy-done.7), custom_call_target="tpu_custom_call" | custom-call | flops 4194304 | bytes 4194304 | tf_op jit(solution)/shard_map/pallas_call | solution.py:37
  24.5 0.0 collective-permute-done.2.above
  24.5 0.0 collective-permute-done.3.below
  24.6 3.4 %shard_map.106 = (bf16[4,14,24,128]{3,2,1,0:T(8,128)(2,1)S(1)}, bf16[4,14,24,128]{3,2,1,0:T(8,128)(2,1)S(1)}, f32[14,24,128]{2,1,0:T(8,128)S(1)}, f32[3,14,24,12...) custom-call(f32[16,2048]{1,0:T(8,128)S(1)} %copy-done.3, bf16[16,2048]{1,0:T(8,128)(2,1)S(1)} %copy-done.4, ...), custom_call_target="tpu_custom_call" | custom-call | flops 849346560 | bytes 4194304 | tf_op jit(solution)/shard_map/pallas_call | solution.py:37
  28.0 0.0 copy-start.6
  28.1 1.8 %shard_map.107 = (bf16[4,20,24,128]{3,2,1,0:T(8,128)(2,1)S(1)}, bf16[4,20,24,128]{3,2,1,0:T(8,128)(2,1)S(1)}, f32[20,24,128]{2,1,0:T(8,128)S(1)}, f32[3,20,24,12...) custom-call(f32[16,2048]{1,0:T(8,128)S(1)} %copy-done.3, ...), custom_call_target="tpu_custom_call" | custom-call | flops 849346560 | bytes 4194304 | tf_op jit(solution)/shard_map/pallas_call | solution.py:37
  29.9 17.5 %all_to_all.33 = f32[32,1,128]{2,1,0:T(1,128)S(1)} all-to-all(f32[32,1,128]{2,1,0:T(1,128)S(1)} %bitcast.17), channel_id=1, replica_groups=mesh['row'=8,'col'=4] {'row','col'}, dimensions={0} | all-to-all | bytes 32768 | tf_op jit(solution)/shard_map/all_to_all | solution.py:536
  47.4 6.5 %shard_map.108 = (f32[3,20,24,128]{3,2,1,0:T(8,128)S(1)}, f32[3,18,24,128]{3,2,1,0:T(8,128)S(1)}, f32[2,18,24,128]{3,2,1,0:T(8,128)S(1)}, f32[3,18,16,128]{3,2,1...) custom-call(f32[32,128]{1,0:T(8,128)S(1)} %bitcast.15, ...), custom_call_target="tpu_custom_call" | custom-call | flops 1698693120 | bytes 4194304 | tf_op jit(solution)/shard_map/pallas_call | solution.py:37
  53.9 8.8 %all_to_all.34 = f32[32,1,128]{2,1,0:T(1,128)S(1)} all-to-all(f32[32,1,128]{2,1,0:T(1,128)S(1)} %bitcast.19), channel_id=1, replica_groups=mesh['row'=8,'col'=4] {'row','col'}, dimensions={0} | all-to-all | bytes 32768 | tf_op jit(solution)/shard_map/all_to_all | solution.py:536
  62.7 5.7 %shard_map.109 = (f32[3,16,2048]{2,1,0:T(8,128)S(1)}, f32[3,16,2048]{2,1,0:T(8,128)S(1)}, f32[3,16,2048]{2,1,0:T(8,128)S(1)}, f32[3,16,2048]{2,1,0:T(8,128)S(1)}, f32[32,128]{1,0:T(8,128)S(1)}) custom-call(f32[32,128]{1,0:T(8,128)S(1)} %bitcast.14, f32[3]{0:T(128)S(1)} %copy-done.6, bf16[4,20,24,128]{3,2,1,0:T(8,128)(2,1)S(1)} %get-tuple-element.58.near_box, ...), custom_call_target="tpu_custom_call" | custom-call | flops 1698693120 | bytes 4194304 | tf_op jit(solution)/shard_map/pallas_call | solution.py:37
  68.5 8.8 %all_to_all.35 = f32[32,1,128]{2,1,0:T(1,128)S(1)} all-to-all(f32[32,1,128]{2,1,0:T(1,128)S(1)} %bitcast.18), channel_id=1, replica_groups=mesh['row'=8,'col'=4] {'row','col'}, dimensions={0} | all-to-all | bytes 32768 | tf_op jit(solution)/shard_map/all_to_all | solution.py:536
  77.3 1.6 %shard_map.110 = (f32[3,16,2048]{2,1,0:T(8,128)}, f32[3,16,2048]{2,1,0:T(8,128)}, f32[3]{0:T(128)}) custom-call(f32[32,128]{1,0:T(8,128)S(1)} %bitcast.16, f32[3]{0:T(128)S(1)} %copy-done.6, f32[3,16,2048]{2,1,0:T(8,128)S(1)} %get-tuple-element.74.duals, f32[3,16,2048]{2,1,0:T(8,128)S(1)} %get-tuple-element.75.multipliers, ...), custom_call_target="tpu_custom_call" | custom-call | flops 1048576 | bytes 4194304 | tf_op jit(solution)/shard_map/pallas_call | solution.py:37
  (15 shorter events, 0.1 us)
Async XLA Ops:
  0.6 23.9 %copy-start.1 = (bf16[3,16,2048]{2,1,0:T(8,128)(2,1)S(1)}, bf16[3,16,2048]{2,1,0:T(8,128)(2,1)}, u32[]{:S(2)}) copy-start(bf16[3,16,2048]{2,1,0:T(8,128)(2,1)} %upper.7) | copy-start | bytes 589828
  0.6 23.9 %copy-start = (bf16[3,16,2048]{2,1,0:T(8,128)(2,1)S(1)}, bf16[3,16,2048]{2,1,0:T(8,128)(2,1)}, u32[]{:S(2)}) copy-start(bf16[3,16,2048]{2,1,0:T(8,128)(2,1)} %lower.7) | copy-start | bytes 589828
  0.7 23.9 %copy-start.5 = (bf16[16,2048]{1,0:T(8,128)(2,1)S(1)}, bf16[16,2048]{1,0:T(8,128)(2,1)}, u32[]{:S(2)}) copy-start(bf16[16,2048]{1,0:T(8,128)(2,1)} %radius.5) | copy-start | bytes 196612
  0.7 23.9 %copy-start.4 = (bf16[16,2048]{1,0:T(8,128)(2,1)S(1)}, bf16[16,2048]{1,0:T(8,128)(2,1)}, u32[]{:S(2)}) copy-start(bf16[16,2048]{1,0:T(8,128)(2,1)} %center.5) | copy-start | bytes 196612
  0.7 23.9 %copy-start.3 = (f32[16,2048]{1,0:T(8,128)S(1)}, f32[16,2048]{1,0:T(8,128)}, u32[]{:S(2)}) copy-start(f32[16,2048]{1,0:T(8,128)} %objective.5) | copy-start | bytes 393220
  3.0 21.6 %collective-permute-start.2 = (f32[560,128]{1,0:T(8,128)}, f32[560,128]{1,0:T(8,128)S(1)}, u32[]{:S(2)}, u32[]{:S(2)}) collective-permute-start(f32[560,128]{1,0:T(8,128)} %get-tuple-element.44), channel_id=1, source_target_pairs={{0,4},{4,8},{8,12},{12,16},{16,20},{20,24},{24,28},{1,5},{5,9},{9,... | collective-permute-start | bytes 860168 | tf_op jit(solution)/shard_map/ppermute | solution.py:168
  7.8 16.7 %collective-permute-start.3 = (f32[560,128]{1,0:T(8,128)}, f32[560,128]{1,0:T(8,128)S(1)}, u32[]{:S(2)}, u32[]{:S(2)}) collective-permute-start(f32[560,128]{1,0:T(8,128)} %get-tuple-element.45), channel_id=1, source_target_pairs={{4,0},{8,4},{12,8},{16,12},{20,16},{24,20},{28,24},{5,1},{9,5},{13... | collective-permute-start | bytes 860168 | tf_op jit(solution)/shard_map/ppermute | solution.py:169
  9.1 2.8 %collective-permute-start = (f32[144,384]{1,0:T(8,128)}, f32[144,384]{1,0:T(8,128)S(1)}, u32[]{:S(2)}, u32[]{:S(2)}) collective-permute-start(f32[144,384]{1,0:T(8,128)} %get-tuple-element.42), channel_id=1, source_target_pairs={{0,1},{1,2},{2,3},{4,5},{5,6},{6,7},{8,9},{9,10},{10,11},{12,13},{... | collective-permute-start | bytes 663560 | tf_op jit(solution)/shard_map/ppermute | solution.py:168
  10.6 5.2 %collective-permute-start.1 = (f32[144,384]{1,0:T(8,128)}, f32[144,384]{1,0:T(8,128)S(1)}, u32[]{:S(2)}, u32[]{:S(2)}) collective-permute-start(f32[144,384]{1,0:T(8,128)} %get-tuple-element.43), channel_id=1, source_target_pairs={{1,0},{2,1},{3,2},{5,4},{6,5},{7,6},{9,8},{10,9},{11,10},{13,12},{... | collective-permute-start | bytes 663560 | tf_op jit(solution)/shard_map/ppermute | solution.py:169
  15.8 12.2 %collective-permute-start.4 = (f32[170,128]{1,0:T(8,128)S(1)}, f32[170,128]{1,0:T(8,128)S(1)}, u32[]{:S(2)}, u32[]{:S(2)}) collective-permute-start(f32[170,128]{1,0:T(8,128)S(1)} %get-tuple-element.46), channel_id=1, source_target_pairs={{0,4},{4,8},{8,12},{12,16},{16,20},{20,24},{24,28},{1,5},{5,9},{9,... | collective-permute-start | bytes 261128 | tf_op jit(solution)/shard_map/ppermute | solution.py:168
  20.3 7.7 %collective-permute-start.5 = (f32[170,128]{1,0:T(8,128)S(1)}, f32[170,128]{1,0:T(8,128)S(1)}, u32[]{:S(2)}, u32[]{:S(2)}) collective-permute-start(f32[170,128]{1,0:T(8,128)S(1)} %get-tuple-element.47), channel_id=1, source_target_pairs={{4,0},{8,4},{12,8},{16,12},{20,16},{24,20},{28,24},{5,1},{9,5},{13... | collective-permute-start | bytes 261128 | tf_op jit(solution)/shard_map/ppermute | solution.py:169
  21.6 1.3 %copy-start.2 = (f32[4,3,3,64,64]{4,3,2,1,0:T(8,128)S(1)}, f32[4,3,3,64,64]{4,3,2,1,0:T(8,128)}, u32[]{:S(2)}) copy-start(f32[4,3,3,64,64]{4,3,2,1,0:T(8,128)} %param.13) | copy-start | bytes 1769476
  22.9 0.7 copy-start.7
  28.0 19.3 %copy-start.6 = (f32[3]{0:T(128)S(1)}, f32[3]{0:T(128)}, u32[]{:S(2)}) copy-start(f32[3]{0:T(128)} %steps.5) | copy-start | bytes 40

commit v10 on v8

--- a/solution.py
+++ b/solution.py
@@ -170,7 +170,11 @@
     return pltpu.roll(value, shift % value.shape[0], 0)
 
 
-def slide(maps, count, store, produce):
+def unrolled(count, most):
+    return max(n for n in range(1, most + 1) if count % n == 0)
+
+
+def slide(maps, count, store, produce, most=32):
     rows = store.shape[2]
     early = lax.broadcasted_iota(jnp.int32, (rows, LANES), 1) < CH
     zero = jnp.zeros((rows, LANES), F32)
@@ -181,7 +185,7 @@
             store[k, q] = jnp.where(early, carry[k], fresh[k])
         return tuple(fresh)
 
-    last = lax.fori_loop(0, count, step, (zero,) * maps, unroll=2)
+    last = lax.fori_loop(0, count, step, (zero,) * maps, unroll=unrolled(count, most))
     for k in range(maps):
         store[k, count] = jnp.where(early, last[k], zero)
 
@@ -332,7 +336,7 @@
         return tuple(old + one for old, one in zip(carry, new))
 
     zero = jnp.zeros((frame, LANES), F32)
-    sizes = lax.fori_loop(0, pairs - 2, step, (zero, zero, zero), unroll=2)
+    sizes = lax.fori_loop(0, pairs - 2, step, (zero, zero, zero), unroll=unrolled(pairs - 2, 7))
     for j in range(3):
         totals[j] = sizes[j]
 
@@ -397,7 +401,7 @@
         worths[q] = bound.total()
         return outs
 
-    slide(3, wide, store, produce)
+    slide(3, wide, store, produce, most=5)
     for k in range(3):
         multiply(store, k, 1, wide - 2, fwd, k, sums)
 
@@ -436,7 +440,7 @@
         own = (q >= 2) & (q < wide - 2)
         return squares + jnp.where(own, new, 0.0), worth + jnp.where(own, bound.total(), 0.0)
 
-    squares, worth = lax.fori_loop(0, wide - 2, step, (zero, zero), unroll=2)
+    squares, worth = lax.fori_loop(0, wide - 2, step, (zero, zero), unroll=unrolled(wide - 2, 3))
     stats(stat, [own_rows(squares)])
     stats(value, [own_rows(worth)])
 
@@ -475,7 +479,7 @@
             store[k, j] = jnp.where(early, carry[k], fresh[k])
         return tuple(fresh) + (carry[3] + jnp.where(own, bound.total(), 0.0),)
 
-    framed = lax.fori_loop(0, wide - 2, point, (zero,) * 4, unroll=2)[3]
+    framed = lax.fori_loop(0, wide - 2, point, (zero,) * 4, unroll=unrolled(wide - 2, 6))[3]
     for k in range(3):
         multiply(store, k, 1, wide - 4, fwd, k, sums)
 
@@ -510,7 +514,7 @@
         return squares, worth + bound.total()
 
     zero = jnp.zeros((rows, LANES), F32)
-    squares, worth = lax.fori_loop(0, wide - 4, step, (zero, zero), unroll=2)
+    squares, worth = lax.fori_loop(0, wide - 4, step, (zero, zero), unroll=unrolled(wide - 4, 4))
     lane = lax.broadcasted_iota(jnp.int32, (1, LANES), 1)
     start, fixed = (jnp.where(lane == j, value0[0:1, :], 0.0) for j in range(2))
     middle = jnp.where(lane == 0, value1[0:1, :], 0.0)

time: 76.8 us -> 72.6 us (0.945)
  Pallas kernels: 22.3 us -> 17.5 us
  waiting for transfers between devices: 5.7 us -> 7.05 us
  blocking collectives: 34.2 us -> 33.3 us
    pallas_call x8, Pallas kernels: 22.3 us -> 17.5 us  [call(): pl.pallas_call(body, out_shape=outs, in_specs=specs, out_specs=out_specs,...]
    ppermute x3, waiting for transfers between devices: 0.15 us -> 1.5 us  [neighbours(): after = lax.ppermute(head, axis, [(i + 1, i) for i in range(count - 1)])]
    all_to_all x3, blocking collectives: 34.2 us -> 33.3 us  [everyone(): return lax.all_to_all(partial, ('row', 'col'), 0, 0, tiled=True)]
  transfers between devices with their start and end apart: 6 -> 6, of which waited for: 2 -> 2; matrix products, arithmetic and copies ran while one was open for 0% -> 0% of each run, Pallas kernels for 6% -> 4%
where the time goes in v10:
time: 72.6 us; the launch traced here: 72.2 us
  blocking collectives  33.3 us (46%)
  Pallas kernels  17.5 us (24%)
  starting transfers between devices  11.5 us (16%)
  waiting for transfers between devices  7.05 us (10%)
  local copies, waits for them, and re-layouts  1.97 us (3%)
  between operations  0.83 us (1%)
    all_to_all x3, blocking collectives, everyone(): return lax.all_to_all(partial, ('row', 'col'), 0, 0, tiled=True)  33.3 us
    pallas_call x8, Pallas kernels, call(): pl.pallas_call(body, out_shape=outs, in_specs=specs, out_specs=out_specs,...  17.5 us
    ppermute x3, starting transfers between devices, neighbours(): before = lax.ppermute(tail, axis, [(i, i + 1) for i in range(count - 1)])  7.63 us
    ppermute x3, waiting for transfers between devices, neighbours(): before = lax.ppermute(tail, axis, [(i, i + 1) for i in range(count - 1)])  5.55 us
    ppermute x3, starting transfers between devices, neighbours(): after = lax.ppermute(head, axis, [(i + 1, i) for i in range(count - 1)])  3.88 us
    unnamed x16, local copies, waits for them, and re-layouts  1.97 us
    ppermute x3, waiting for transfers between devices, neighbours(): after = lax.ppermute(head, axis, [(i + 1, i) for i in range(count - 1)])  1.5 us
  transfers between devices with their start and end apart: 6, of which 2 were waited for; matrix products, arithmetic and copies ran while one was open for 0% of the time, Pallas kernels for 4%

profile of v10, /device:TPU:0, one launch (start us, length us, event | category | flops | bytes accessed | tf_op | source)
XLA Modules:
  0.0 72.2 jit_solution(17503322169359314264)
XLA Ops:
  0.7 2.3 %shard_map.103 = (f32[560,128]{1,0:T(8,128)}, f32[560,128]{1,0:T(8,128)}, f32[144,384]{1,0:T(8,128)}, f32[144,384]{1,0:T(8,128)}) custom-call(f32[16,2048]{1,0:T(8,128)} %objective.5, bf16[16,2048]{1,0:T(8,128)(2,1)} %center.5, bf16[16,2048]{1,0:T(8,128)(2,1)} %radius.5, bf16[3,16,2048]{2,1,0:T(8,128)(2,1)} %lower.7, bf16[3,16,2048]{2,1,0:T(8,128)(2,1)} %upper.7), custom_call_target="tpu_custom_call" | custom-call | flops 1048576 | bytes 4194304 | tf_op jit(solution)/shard_map/pallas_call | solution.py:35
  3.0 4.9 %collective-permute-start.2 = (f32[560,128]{1,0:T(8,128)}, f32[560,128]{1,0:T(8,128)S(1)}, u32[]{:S(2)}, u32[]{:S(2)}) collective-permute-start(f32[560,128]{1,0:T(8,128)} %get-tuple-element.44), channel_id=1, source_target_pairs={{0,4},{4,8},{8,12},{12,16},{16,20},{20,24},{24,28},{1,5},{5,9},{9,... | collective-permute-start | bytes 860168 | tf_op jit(solution)/shard_map/ppermute | solution.py:164
  7.8 1.3 %collective-permute-start.3 = (f32[560,128]{1,0:T(8,128)}, f32[560,128]{1,0:T(8,128)S(1)}, u32[]{:S(2)}, u32[]{:S(2)}) collective-permute-start(f32[560,128]{1,0:T(8,128)} %get-tuple-element.45), channel_id=1, source_target_pairs={{4,0},{8,4},{12,8},{16,12},{20,16},{24,20},{28,24},{5,1},{9,5},{13... | collective-permute-start | bytes 860168 | tf_op jit(solution)/shard_map/ppermute | solution.py:165
  9.1 1.5 %collective-permute-start = (f32[144,384]{1,0:T(8,128)}, f32[144,384]{1,0:T(8,128)S(1)}, u32[]{:S(2)}, u32[]{:S(2)}) collective-permute-start(f32[144,384]{1,0:T(8,128)} %get-tuple-element.42), channel_id=1, source_target_pairs={{0,1},{1,2},{2,3},{4,5},{5,6},{6,7},{8,9},{9,10},{10,11},{12,13},{... | collective-permute-start | bytes 663560 | tf_op jit(solution)/shard_map/ppermute | solution.py:164
  10.6 1.3 %collective-permute-start.1 = (f32[144,384]{1,0:T(8,128)}, f32[144,384]{1,0:T(8,128)S(1)}, u32[]{:S(2)}, u32[]{:S(2)}) collective-permute-start(f32[144,384]{1,0:T(8,128)} %get-tuple-element.43), channel_id=1, source_target_pairs={{1,0},{2,1},{3,2},{5,4},{6,5},{7,6},{9,8},{10,9},{11,10},{13,12},{... | collective-permute-start | bytes 663560 | tf_op jit(solution)/shard_map/ppermute | solution.py:165
  11.9 0.0 copy-start.3
  11.9 1.3 %copy-done.3 = f32[4,3,3,64,64]{4,3,2,1,0:T(8,128)S(1)} copy-done((f32[4,3,3,64,64]{4,3,2,1,0:T(8,128)S(1)}, f32[4,3,3,64,64]{4,3,2,1,0:T(8,128)}, u32[]{:S(2)}) %copy-start.3) | copy-done | bytes 589848
  13.2 0.7 copy-done.7
  13.9 0.9 %shard_map.104 = (bf16[3,768,384]{2,1,0:T(8,128)(2,1)S(1)}, bf16[4,768,384]{2,1,0:T(8,128)(2,1)S(1)}, f32[8,128]{1,0:T(8,128)S(1)}) custom-call(f32[36,64,64]{2,1,0:T(8,128)S(1)} %bitcast.13, f32[4,64]{1,0:T(4,128)S(1)} %copy-done.7), custom_call_target="tpu_custom_call" | custom-call | flops 4194304 | bytes 4194304 | tf_op jit(solution)/shard_map/pallas_call | solution.py:35
  14.8 5.5 %collective-permute-done.2.above = f32[560,128]{1,0:T(8,128)S(1)} collective-permute-done((f32[560,128]{1,0:T(8,128)}, f32[560,128]{1,0:T(8,128)S(1)}, u32[]{:S(2)}, u32[]{:S(2)}) %collective-permute-start.2) | collective-permute-done | bytes 286752 | tf_op jit(solution)/shard_map/ppermute | solution.py:164
  20.3 0.0 collective-permute-done.3.below
  20.4 1.3 %collective-permute-start.4 = (f32[210,128]{1,0:T(8,128)S(1)}, f32[210,128]{1,0:T(8,128)S(1)}, u32[]{:S(2)}, u32[]{:S(2)}) collective-permute-start(f32[210,128]{1,0:T(8,128)S(1)} %get-tuple-element.47), channel_id=1, source_target_pairs={{0,1},{1,2},{2,3},{4,5},{5,6},{6,7},{8,9},{9,10},{10,11},{12,13},{... | collective-permute-start | bytes 322568 | tf_op jit(solution)/shard_map/ppermute | solution.py:164
  21.7 1.3 %collective-permute-start.5 = (f32[210,128]{1,0:T(8,128)S(1)}, f32[210,128]{1,0:T(8,128)S(1)}, u32[]{:S(2)}, u32[]{:S(2)}) collective-permute-start(f32[210,128]{1,0:T(8,128)S(1)} %get-tuple-element.48), channel_id=1, source_target_pairs={{1,0},{2,1},{3,2},{5,4},{6,5},{7,6},{9,8},{10,9},{11,10},{13,12},{... | collective-permute-start | bytes 322568 | tf_op jit(solution)/shard_map/ppermute | solution.py:165
  23.0 2.1 %shard_map.106 = (bf16[4,14,24,128]{3,2,1,0:T(8,128)(2,1)S(1)}, bf16[4,14,24,128]{3,2,1,0:T(8,128)(2,1)S(1)}, f32[14,24,128]{2,1,0:T(8,128)S(1)}, f32[3,14,24,12...) custom-call(f32[16,2048]{1,0:T(8,128)S(1)} %copy-done.2, bf16[16,2048]{1,0:T(8,128)(2,1)S(1)} %copy-done.4, ...), custom_call_target="tpu_custom_call" | custom-call | flops 849346560 | bytes 4194304 | tf_op jit(solution)/shard_map/pallas_call | solution.py:35
  25.1 0.0 collective-permute-done.1.right
  25.1 0.0 collective-permute-done.4.left_corner
  25.1 1.5 %collective-permute-done.5.right_corner = f32[210,128]{1,0:T(8,128)S(1)} collective-permute-done((f32[210,128]{1,0:T(8,128)S(1)}, f32[210,128]{1,0:T(8,128)S(1)}, u32[]{:S(2)}, u32[]{:S(2)}) %collective-permute-start.5) | collective-permute-done | bytes 107552 | tf_op jit(solution)/shard_map/ppermute | solution.py:165
  26.6 1.0 %shard_map.107 = (bf16[4,20,24,128]{3,2,1,0:T(8,128)(2,1)S(1)}, bf16[4,20,24,128]{3,2,1,0:T(8,128)(2,1)S(1)}, f32[20,24,128]{2,1,0:T(8,128)S(1)}, f32[3,20,24,12...) custom-call(f32[16,2048]{1,0:T(8,128)S(1)} %copy-done.2, ...), custom_call_target="tpu_custom_call" | custom-call | flops 849346560 | bytes 4194304 | tf_op jit(solution)/shard_map/pallas_call | solution.py:35
  27.6 15.7 %all_to_all.33 = f32[32,1,128]{2,1,0:T(1,128)S(1)} all-to-all(f32[32,1,128]{2,1,0:T(1,128)S(1)} %bitcast.17), channel_id=1, replica_groups=mesh['row'=8,'col'=4] {'row','col'}, dimensions={0} | all-to-all | bytes 32768 | tf_op jit(solution)/shard_map/all_to_all | solution.py:536
  43.3 5.2 %shard_map.108 = (f32[3,20,24,128]{3,2,1,0:T(8,128)S(1)}, f32[3,18,24,128]{3,2,1,0:T(8,128)S(1)}, f32[2,18,24,128]{3,2,1,0:T(8,128)S(1)}, f32[3,18,16,128]{3,2,1...) custom-call(f32[32,128]{1,0:T(8,128)S(1)} %bitcast.15, ...), custom_call_target="tpu_custom_call" | custom-call | flops 1698693120 | bytes 4194304 | tf_op jit(solution)/shard_map/pallas_call | solution.py:35
  48.5 8.8 %all_to_all.34 = f32[32,1,128]{2,1,0:T(1,128)S(1)} all-to-all(f32[32,1,128]{2,1,0:T(1,128)S(1)} %bitcast.19), channel_id=1, replica_groups=mesh['row'=8,'col'=4] {'row','col'}, dimensions={0} | all-to-all | bytes 32768 | tf_op jit(solution)/shard_map/all_to_all | solution.py:536
  57.3 4.5 %shard_map.109 = (f32[3,16,2048]{2,1,0:T(8,128)S(1)}, f32[3,16,2048]{2,1,0:T(8,128)S(1)}, f32[3,16,2048]{2,1,0:T(8,128)S(1)}, f32[3,16,2048]{2,1,0:T(8,128)S(1)}, f32[32,128]{1,0:T(8,128)S(1)}) custom-call(f32[32,128]{1,0:T(8,128)S(1)} %bitcast.14, f32[3]{0:T(128)S(1)} %copy-done.6, bf16[4,20,24,128]{3,2,1,0:T(8,128)(2,1)S(1)} %get-tuple-element.58.near_box, ...), custom_call_target="tpu_custom_call" | custom-call | flops 1698693120 | bytes 4194304 | tf_op jit(solution)/shard_map/pallas_call | solution.py:35
  61.8 8.8 %all_to_all.35 = f32[32,1,128]{2,1,0:T(1,128)S(1)} all-to-all(f32[32,1,128]{2,1,0:T(1,128)S(1)} %bitcast.18), channel_id=1, replica_groups=mesh['row'=8,'col'=4] {'row','col'}, dimensions={0} | all-to-all | bytes 32768 | tf_op jit(solution)/shard_map/all_to_all | solution.py:536
  70.6 1.6 %shard_map.110 = (f32[3,16,2048]{2,1,0:T(8,128)}, f32[3,16,2048]{2,1,0:T(8,128)}, f32[3]{0:T(128)}) custom-call(f32[32,128]{1,0:T(8,128)S(1)} %bitcast.16, f32[3]{0:T(128)S(1)} %copy-done.6, f32[3,16,2048]{2,1,0:T(8,128)S(1)} %get-tuple-element.74.duals, f32[3,16,2048]{2,1,0:T(8,128)S(1)} %get-tuple-element.75.multipliers, ...), custom_call_target="tpu_custom_call" | custom-call | flops 1048576 | bytes 4194304 | tf_op jit(solution)/shard_map/pallas_call | solution.py:35
  (15 shorter events, 0.0 us)
Async XLA Ops:
  0.6 22.3 %copy-start.1 = (bf16[3,16,2048]{2,1,0:T(8,128)(2,1)S(1)}, bf16[3,16,2048]{2,1,0:T(8,128)(2,1)}, u32[]{:S(2)}) copy-start(bf16[3,16,2048]{2,1,0:T(8,128)(2,1)} %upper.7) | copy-start | bytes 589828
  0.6 22.3 %copy-start = (bf16[3,16,2048]{2,1,0:T(8,128)(2,1)S(1)}, bf16[3,16,2048]{2,1,0:T(8,128)(2,1)}, u32[]{:S(2)}) copy-start(bf16[3,16,2048]{2,1,0:T(8,128)(2,1)} %lower.7) | copy-start | bytes 589828
  0.7 22.3 %copy-start.5 = (bf16[16,2048]{1,0:T(8,128)(2,1)S(1)}, bf16[16,2048]{1,0:T(8,128)(2,1)}, u32[]{:S(2)}) copy-start(bf16[16,2048]{1,0:T(8,128)(2,1)} %radius.5) | copy-start | bytes 196612
  0.7 22.3 %copy-start.4 = (bf16[16,2048]{1,0:T(8,128)(2,1)S(1)}, bf16[16,2048]{1,0:T(8,128)(2,1)}, u32[]{:S(2)}) copy-start(bf16[16,2048]{1,0:T(8,128)(2,1)} %center.5) | copy-start | bytes 196612
  0.7 22.3 %copy-start.2 = (f32[16,2048]{1,0:T(8,128)S(1)}, f32[16,2048]{1,0:T(8,128)}, u32[]{:S(2)}) copy-start(f32[16,2048]{1,0:T(8,128)} %objective.5) | copy-start | bytes 393220
  3.0 17.4 %collective-permute-start.2 = (f32[560,128]{1,0:T(8,128)}, f32[560,128]{1,0:T(8,128)S(1)}, u32[]{:S(2)}, u32[]{:S(2)}) collective-permute-start(f32[560,128]{1,0:T(8,128)} %get-tuple-element.44), channel_id=1, source_target_pairs={{0,4},{4,8},{8,12},{12,16},{16,20},{20,24},{24,28},{1,5},{5,9},{9,... | collective-permute-start | bytes 860168 | tf_op jit(solution)/shard_map/ppermute | solution.py:164
  7.8 12.5 %collective-permute-start.3 = (f32[560,128]{1,0:T(8,128)}, f32[560,128]{1,0:T(8,128)S(1)}, u32[]{:S(2)}, u32[]{:S(2)}) collective-permute-start(f32[560,128]{1,0:T(8,128)} %get-tuple-element.45), channel_id=1, source_target_pairs={{4,0},{8,4},{12,8},{16,12},{20,16},{24,20},{28,24},{5,1},{9,5},{13... | collective-permute-start | bytes 860168 | tf_op jit(solution)/shard_map/ppermute | solution.py:165
  9.1 16.0 %collective-permute-start = (f32[144,384]{1,0:T(8,128)}, f32[144,384]{1,0:T(8,128)S(1)}, u32[]{:S(2)}, u32[]{:S(2)}) collective-permute-start(f32[144,384]{1,0:T(8,128)} %get-tuple-element.42), channel_id=1, source_target_pairs={{0,1},{1,2},{2,3},{4,5},{5,6},{6,7},{8,9},{9,10},{10,11},{12,13},{... | collective-permute-start | bytes 663560 | tf_op jit(solution)/shard_map/ppermute | solution.py:164
  10.6 14.5 %collective-permute-start.1 = (f32[144,384]{1,0:T(8,128)}, f32[144,384]{1,0:T(8,128)S(1)}, u32[]{:S(2)}, u32[]{:S(2)}) collective-permute-start(f32[144,384]{1,0:T(8,128)} %get-tuple-element.43), channel_id=1, source_target_pairs={{1,0},{2,1},{3,2},{5,4},{6,5},{7,6},{9,8},{10,9},{11,10},{13,12},{... | collective-permute-start | bytes 663560 | tf_op jit(solution)/shard_map/ppermute | solution.py:165
  11.9 1.3 %copy-start.3 = (f32[4,3,3,64,64]{4,3,2,1,0:T(8,128)S(1)}, f32[4,3,3,64,64]{4,3,2,1,0:T(8,128)}, u32[]{:S(2)}) copy-start(f32[4,3,3,64,64]{4,3,2,1,0:T(8,128)} %param.13) | copy-start | bytes 1769476
  13.2 0.7 copy-start.7
  20.4 4.8 %collective-permute-start.4 = (f32[210,128]{1,0:T(8,128)S(1)}, f32[210,128]{1,0:T(8,128)S(1)}, u32[]{:S(2)}, u32[]{:S(2)}) collective-permute-start(f32[210,128]{1,0:T(8,128)S(1)} %get-tuple-element.47), channel_id=1, source_target_pairs={{0,1},{1,2},{2,3},{4,5},{5,6},{6,7},{8,9},{9,10},{10,11},{12,13},{... | collective-permute-start | bytes 322568 | tf_op jit(solution)/shard_map/ppermute | solution.py:164
  21.7 5.0 %collective-permute-start.5 = (f32[210,128]{1,0:T(8,128)S(1)}, f32[210,128]{1,0:T(8,128)S(1)}, u32[]{:S(2)}, u32[]{:S(2)}) collective-permute-start(f32[210,128]{1,0:T(8,128)S(1)} %get-tuple-element.48), channel_id=1, source_target_pairs={{1,0},{2,1},{3,2},{5,4},{6,5},{7,6},{9,8},{10,9},{11,10},{13,12},{... | collective-permute-start | bytes 322568 | tf_op jit(solution)/shard_map/ppermute | solution.py:165
  26.6 16.7 %copy-start.6 = (f32[3]{0:T(128)S(1)}, f32[3]{0:T(128)}, u32[]{:S(2)}) copy-start(f32[3]{0:T(128)} %steps.5) | copy-start | bytes 40

commit v11 on v8

--- a/solution.py
+++ b/solution.py
@@ -181,7 +181,7 @@
             store[k, q] = jnp.where(early, carry[k], fresh[k])
         return tuple(fresh)
 
-    last = lax.fori_loop(0, count, step, (zero,) * maps, unroll=2)
+    last = lax.fori_loop(0, count, step, (zero,) * maps, unroll=True)
     for k in range(maps):
         store[k, count] = jnp.where(early, last[k], zero)
 
@@ -332,7 +332,7 @@
         return tuple(old + one for old, one in zip(carry, new))
 
     zero = jnp.zeros((frame, LANES), F32)
-    sizes = lax.fori_loop(0, pairs - 2, step, (zero, zero, zero), unroll=2)
+    sizes = lax.fori_loop(0, pairs - 2, step, (zero, zero, zero), unroll=True)
     for j in range(3):
         totals[j] = sizes[j]
 
@@ -436,7 +436,7 @@
         own = (q >= 2) & (q < wide - 2)
         return squares + jnp.where(own, new, 0.0), worth + jnp.where(own, bound.total(), 0.0)
 
-    squares, worth = lax.fori_loop(0, wide - 2, step, (zero, zero), unroll=2)
+    squares, worth = lax.fori_loop(0, wide - 2, step, (zero, zero), unroll=True)
     stats(stat, [own_rows(squares)])
     stats(value, [own_rows(worth)])
 
@@ -475,7 +475,7 @@
             store[k, j] = jnp.where(early, carry[k], fresh[k])
         return tuple(fresh) + (carry[3] + jnp.where(own, bound.total(), 0.0),)
 
-    framed = lax.fori_loop(0, wide - 2, point, (zero,) * 4, unroll=2)[3]
+    framed = lax.fori_loop(0, wide - 2, point, (zero,) * 4, unroll=True)[3]
     for k in range(3):
         multiply(store, k, 1, wide - 4, fwd, k, sums)
 
@@ -510,7 +510,7 @@
         return squares, worth + bound.total()
 
     zero = jnp.zeros((rows, LANES), F32)
-    squares, worth = lax.fori_loop(0, wide - 4, step, (zero, zero), unroll=2)
+    squares, worth = lax.fori_loop(0, wide - 4, step, (zero, zero), unroll=True)
     lane = lax.broadcasted_iota(jnp.int32, (1, LANES), 1)
     start, fixed = (jnp.where(lane == j, value0[0:1, :], 0.0) for j in range(2))
     middle = jnp.where(lane == 0, value1[0:1, :], 0.0)

time: 76.8 us -> 69.9 us (0.910)
  Pallas kernels: 22.3 us -> 14.3 us
  waiting for transfers between devices: 5.7 us -> 7.51 us
  blocking collectives: 34.2 us -> 33.3 us
    pallas_call x8, Pallas kernels: 22.3 us -> 14.3 us  [call(): pl.pallas_call(body, out_shape=outs, in_specs=specs, out_specs=out_specs,...]
    ppermute x3, waiting for transfers between devices: 0.15 us -> 1.96 us  [neighbours(): after = lax.ppermute(head, axis, [(i + 1, i) for i in range(count - 1)])]
    all_to_all x3, blocking collectives: 34.2 us -> 33.3 us  [everyone(): return lax.all_to_all(partial, ('row', 'col'), 0, 0, tiled=True)]
  transfers between devices with their start and end apart: 6 -> 6, of which waited for: 2 -> 2; matrix products, arithmetic and copies ran while one was open for 0% -> 0% of each run, Pallas kernels for 6% -> 4%
where the time goes in v11:
time: 69.9 us; the launch traced here: 69.5 us
  blocking collectives  33.3 us (48%)
  Pallas kernels  14.3 us (20%)
  starting transfers between devices  11.5 us (16%)
  waiting for transfers between devices  7.51 us (11%)
  local copies, waits for them, and re-layouts  1.97 us (3%)
  between operations  0.83 us (1%)
    all_to_all x3, blocking collectives, everyone(): return lax.all_to_all(partial, ('row', 'col'), 0, 0, tiled=True)  33.3 us
    pallas_call x8, Pallas kernels, call(): pl.pallas_call(body, out_shape=outs, in_specs=specs, out_specs=out_specs,...  14.3 us
    ppermute x3, starting transfers between devices, neighbours(): before = lax.ppermute(tail, axis, [(i, i + 1) for i in range(count - 1)])  7.63 us
    ppermute x3, waiting for transfers between devices, neighbours(): before = lax.ppermute(tail, axis, [(i, i + 1) for i in range(count - 1)])  5.55 us
    ppermute x3, starting transfers between devices, neighbours(): after = lax.ppermute(head, axis, [(i + 1, i) for i in range(count - 1)])  3.88 us
    unnamed x16, local copies, waits for them, and re-layouts  1.97 us
    ppermute x3, waiting for transfers between devices, neighbours(): after = lax.ppermute(head, axis, [(i + 1, i) for i in range(count - 1)])  1.96 us
  transfers between devices with their start and end apart: 6, of which 2 were waited for; matrix products, arithmetic and copies ran while one was open for 0% of the time, Pallas kernels for 4%

profile of v11, /device:TPU:0, one launch (start us, length us, event | category | flops | bytes accessed | tf_op | source)
XLA Modules:
  0.0 69.5 jit_solution(13605858137558604215)
XLA Ops:
  0.7 2.3 %shard_map.103 = (f32[560,128]{1,0:T(8,128)}, f32[560,128]{1,0:T(8,128)}, f32[144,384]{1,0:T(8,128)}, f32[144,384]{1,0:T(8,128)}) custom-call(f32[16,2048]{1,0:T(8,128)} %objective.5, bf16[16,2048]{1,0:T(8,128)(2,1)} %center.5, bf16[16,2048]{1,0:T(8,128)(2,1)} %radius.5, bf16[3,16,2048]{2,1,0:T(8,128)(2,1)} %lower.7, bf16[3,16,2048]{2,1,0:T(8,128)(2,1)} %upper.7), custom_call_target="tpu_custom_call" | custom-call | flops 1048576 | bytes 4194304 | tf_op jit(solution)/shard_map/pallas_call | solution.py:35
  3.0 4.9 %collective-permute-start.2 = (f32[560,128]{1,0:T(8,128)}, f32[560,128]{1,0:T(8,128)S(1)}, u32[]{:S(2)}, u32[]{:S(2)}) collective-permute-start(f32[560,128]{1,0:T(8,128)} %get-tuple-element.44), channel_id=1, source_target_pairs={{0,4},{4,8},{8,12},{12,16},{16,20},{20,24},{24,28},{1,5},{5,9},{9,... | collective-permute-start | bytes 860168 | tf_op jit(solution)/shard_map/ppermute | solution.py:164
  7.8 1.3 %collective-permute-start.3 = (f32[560,128]{1,0:T(8,128)}, f32[560,128]{1,0:T(8,128)S(1)}, u32[]{:S(2)}, u32[]{:S(2)}) collective-permute-start(f32[560,128]{1,0:T(8,128)} %get-tuple-element.45), channel_id=1, source_target_pairs={{4,0},{8,4},{12,8},{16,12},{20,16},{24,20},{28,24},{5,1},{9,5},{13... | collective-permute-start | bytes 860168 | tf_op jit(solution)/shard_map/ppermute | solution.py:165
  9.1 1.5 %collective-permute-start = (f32[144,384]{1,0:T(8,128)}, f32[144,384]{1,0:T(8,128)S(1)}, u32[]{:S(2)}, u32[]{:S(2)}) collective-permute-start(f32[144,384]{1,0:T(8,128)} %get-tuple-element.42), channel_id=1, source_target_pairs={{0,1},{1,2},{2,3},{4,5},{5,6},{6,7},{8,9},{9,10},{10,11},{12,13},{... | collective-permute-start | bytes 663560 | tf_op jit(solution)/shard_map/ppermute | solution.py:164
  10.6 1.3 %collective-permute-start.1 = (f32[144,384]{1,0:T(8,128)}, f32[144,384]{1,0:T(8,128)S(1)}, u32[]{:S(2)}, u32[]{:S(2)}) collective-permute-start(f32[144,384]{1,0:T(8,128)} %get-tuple-element.43), channel_id=1, source_target_pairs={{1,0},{2,1},{3,2},{5,4},{6,5},{7,6},{9,8},{10,9},{11,10},{13,12},{... | collective-permute-start | bytes 663560 | tf_op jit(solution)/shard_map/ppermute | solution.py:165
  11.9 0.0 copy-start.3
  11.9 1.3 %copy-done.3 = f32[4,3,3,64,64]{4,3,2,1,0:T(8,128)S(1)} copy-done((f32[4,3,3,64,64]{4,3,2,1,0:T(8,128)S(1)}, f32[4,3,3,64,64]{4,3,2,1,0:T(8,128)}, u32[]{:S(2)}) %copy-start.3) | copy-done | bytes 589848
  13.2 0.7 copy-done.7
  13.9 0.9 %shard_map.104 = (bf16[3,768,384]{2,1,0:T(8,128)(2,1)S(1)}, bf16[4,768,384]{2,1,0:T(8,128)(2,1)S(1)}, f32[8,128]{1,0:T(8,128)S(1)}) custom-call(f32[36,64,64]{2,1,0:T(8,128)S(1)} %bitcast.13, f32[4,64]{1,0:T(4,128)S(1)} %copy-done.7), custom_call_target="tpu_custom_call" | custom-call | flops 4194304 | bytes 4194304 | tf_op jit(solution)/shard_map/pallas_call | solution.py:35
  14.8 5.5 %collective-permute-done.2.above = f32[560,128]{1,0:T(8,128)S(1)} collective-permute-done((f32[560,128]{1,0:T(8,128)}, f32[560,128]{1,0:T(8,128)S(1)}, u32[]{:S(2)}, u32[]{:S(2)}) %collective-permute-start.2) | collective-permute-done | bytes 286752 | tf_op jit(solution)/shard_map/ppermute | solution.py:164
  20.3 0.0 collective-permute-done.3.below
  20.4 1.3 %collective-permute-start.4 = (f32[210,128]{1,0:T(8,128)S(1)}, f32[210,128]{1,0:T(8,128)S(1)}, u32[]{:S(2)}, u32[]{:S(2)}) collective-permute-start(f32[210,128]{1,0:T(8,128)S(1)} %get-tuple-element.47), channel_id=1, source_target_pairs={{0,1},{1,2},{2,3},{4,5},{5,6},{6,7},{8,9},{9,10},{10,11},{12,13},{... | collective-permute-start | bytes 322568 | tf_op jit(solution)/shard_map/ppermute | solution.py:164
  21.7 1.3 %collective-permute-start.5 = (f32[210,128]{1,0:T(8,128)S(1)}, f32[210,128]{1,0:T(8,128)S(1)}, u32[]{:S(2)}, u32[]{:S(2)}) collective-permute-start(f32[210,128]{1,0:T(8,128)S(1)} %get-tuple-element.48), channel_id=1, source_target_pairs={{1,0},{2,1},{3,2},{5,4},{6,5},{7,6},{9,8},{10,9},{11,10},{13,12},{... | collective-permute-start | bytes 322568 | tf_op jit(solution)/shard_map/ppermute | solution.py:165
  23.0 1.6 %shard_map.106 = (bf16[4,14,24,128]{3,2,1,0:T(8,128)(2,1)S(1)}, bf16[4,14,24,128]{3,2,1,0:T(8,128)(2,1)S(1)}, f32[14,24,128]{2,1,0:T(8,128)S(1)}, f32[3,14,24,12...) custom-call(f32[16,2048]{1,0:T(8,128)S(1)} %copy-done.2, bf16[16,2048]{1,0:T(8,128)(2,1)S(1)} %copy-done.4, ...), custom_call_target="tpu_custom_call" | custom-call | flops 849346560 | bytes 4194304 | tf_op jit(solution)/shard_map/pallas_call | solution.py:35
  24.6 0.0 collective-permute-done.left
  24.7 0.0 collective-permute-done.1.right
  24.7 2.0 %collective-permute-done.5.right_corner = f32[210,128]{1,0:T(8,128)S(1)} collective-permute-done((f32[210,128]{1,0:T(8,128)S(1)}, f32[210,128]{1,0:T(8,128)S(1)}, u32[]{:S(2)}, u32[]{:S(2)}) %collective-permute-start.5) | collective-permute-done | bytes 107552 | tf_op jit(solution)/shard_map/ppermute | solution.py:165
  26.6 1.0 %shard_map.107 = (bf16[4,20,24,128]{3,2,1,0:T(8,128)(2,1)S(1)}, bf16[4,20,24,128]{3,2,1,0:T(8,128)(2,1)S(1)}, f32[20,24,128]{2,1,0:T(8,128)S(1)}, f32[3,20,24,12...) custom-call(f32[16,2048]{1,0:T(8,128)S(1)} %copy-done.2, ...), custom_call_target="tpu_custom_call" | custom-call | flops 849346560 | bytes 4194304 | tf_op jit(solution)/shard_map/pallas_call | solution.py:35
  27.6 15.7 %all_to_all.33 = f32[32,1,128]{2,1,0:T(1,128)S(1)} all-to-all(f32[32,1,128]{2,1,0:T(1,128)S(1)} %bitcast.17), channel_id=1, replica_groups=mesh['row'=8,'col'=4] {'row','col'}, dimensions={0} | all-to-all | bytes 32768 | tf_op jit(solution)/shard_map/all_to_all | solution.py:532
  43.3 3.8 %shard_map.108 = (f32[3,20,24,128]{3,2,1,0:T(8,128)S(1)}, f32[3,18,24,128]{3,2,1,0:T(8,128)S(1)}, f32[2,18,24,128]{3,2,1,0:T(8,128)S(1)}, f32[3,18,16,128]{3,2,1...) custom-call(f32[32,128]{1,0:T(8,128)S(1)} %bitcast.15, ...), custom_call_target="tpu_custom_call" | custom-call | flops 1698693120 | bytes 4194304 | tf_op jit(solution)/shard_map/pallas_call | solution.py:35
  47.1 8.8 %all_to_all.34 = f32[32,1,128]{2,1,0:T(1,128)S(1)} all-to-all(f32[32,1,128]{2,1,0:T(1,128)S(1)} %bitcast.19), channel_id=1, replica_groups=mesh['row'=8,'col'=4] {'row','col'}, dimensions={0} | all-to-all | bytes 32768 | tf_op jit(solution)/shard_map/all_to_all | solution.py:532
  56.0 3.1 %shard_map.109 = (f32[3,16,2048]{2,1,0:T(8,128)S(1)}, f32[3,16,2048]{2,1,0:T(8,128)S(1)}, f32[3,16,2048]{2,1,0:T(8,128)S(1)}, f32[3,16,2048]{2,1,0:T(8,128)S(1)}, f32[32,128]{1,0:T(8,128)S(1)}) custom-call(f32[32,128]{1,0:T(8,128)S(1)} %bitcast.14, f32[3]{0:T(128)S(1)} %copy-done.6, bf16[4,20,24,128]{3,2,1,0:T(8,128)(2,1)S(1)} %get-tuple-element.58.near_box, ...), custom_call_target="tpu_custom_call" | custom-call | flops 1698693120 | bytes 4194304 | tf_op jit(solution)/shard_map/pallas_call | solution.py:35
  59.1 8.8 %all_to_all.35 = f32[32,1,128]{2,1,0:T(1,128)S(1)} all-to-all(f32[32,1,128]{2,1,0:T(1,128)S(1)} %bitcast.18), channel_id=1, replica_groups=mesh['row'=8,'col'=4] {'row','col'}, dimensions={0} | all-to-all | bytes 32768 | tf_op jit(solution)/shard_map/all_to_all | solution.py:532
  67.9 1.6 %shard_map.110 = (f32[3,16,2048]{2,1,0:T(8,128)}, f32[3,16,2048]{2,1,0:T(8,128)}, f32[3]{0:T(128)}) custom-call(f32[32,128]{1,0:T(8,128)S(1)} %bitcast.16, f32[3]{0:T(128)S(1)} %copy-done.6, f32[3,16,2048]{2,1,0:T(8,128)S(1)} %get-tuple-element.74.duals, f32[3,16,2048]{2,1,0:T(8,128)S(1)} %get-tuple-element.75.multipliers, ...), custom_call_target="tpu_custom_call" | custom-call | flops 1048576 | bytes 4194304 | tf_op jit(solution)/shard_map/pallas_call | solution.py:35
  (15 shorter events, 0.0 us)
Async XLA Ops:
  0.6 22.3 %copy-start.1 = (bf16[3,16,2048]{2,1,0:T(8,128)(2,1)S(1)}, bf16[3,16,2048]{2,1,0:T(8,128)(2,1)}, u32[]{:S(2)}) copy-start(bf16[3,16,2048]{2,1,0:T(8,128)(2,1)} %upper.7) | copy-start | bytes 589828
  0.6 22.3 %copy-start = (bf16[3,16,2048]{2,1,0:T(8,128)(2,1)S(1)}, bf16[3,16,2048]{2,1,0:T(8,128)(2,1)}, u32[]{:S(2)}) copy-start(bf16[3,16,2048]{2,1,0:T(8,128)(2,1)} %lower.7) | copy-start | bytes 589828
  0.7 22.3 %copy-start.5 = (bf16[16,2048]{1,0:T(8,128)(2,1)S(1)}, bf16[16,2048]{1,0:T(8,128)(2,1)}, u32[]{:S(2)}) copy-start(bf16[16,2048]{1,0:T(8,128)(2,1)} %radius.5) | copy-start | bytes 196612
  0.7 22.3 %copy-start.4 = (bf16[16,2048]{1,0:T(8,128)(2,1)S(1)}, bf16[16,2048]{1,0:T(8,128)(2,1)}, u32[]{:S(2)}) copy-start(bf16[16,2048]{1,0:T(8,128)(2,1)} %center.5) | copy-start | bytes 196612
  0.7 22.3 %copy-start.2 = (f32[16,2048]{1,0:T(8,128)S(1)}, f32[16,2048]{1,0:T(8,128)}, u32[]{:S(2)}) copy-start(f32[16,2048]{1,0:T(8,128)} %objective.5) | copy-start | bytes 393220
  3.0 17.4 %collective-permute-start.2 = (f32[560,128]{1,0:T(8,128)}, f32[560,128]{1,0:T(8,128)S(1)}, u32[]{:S(2)}, u32[]{:S(2)}) collective-permute-start(f32[560,128]{1,0:T(8,128)} %get-tuple-element.44), channel_id=1, source_target_pairs={{0,4},{4,8},{8,12},{12,16},{16,20},{20,24},{24,28},{1,5},{5,9},{9,... | collective-permute-start | bytes 860168 | tf_op jit(solution)/shard_map/ppermute | solution.py:164
  7.8 12.5 %collective-permute-start.3 = (f32[560,128]{1,0:T(8,128)}, f32[560,128]{1,0:T(8,128)S(1)}, u32[]{:S(2)}, u32[]{:S(2)}) collective-permute-start(f32[560,128]{1,0:T(8,128)} %get-tuple-element.45), channel_id=1, source_target_pairs={{4,0},{8,4},{12,8},{16,12},{20,16},{24,20},{28,24},{5,1},{9,5},{13... | collective-permute-start | bytes 860168 | tf_op jit(solution)/shard_map/ppermute | solution.py:165
  9.1 15.5 %collective-permute-start = (f32[144,384]{1,0:T(8,128)}, f32[144,384]{1,0:T(8,128)S(1)}, u32[]{:S(2)}, u32[]{:S(2)}) collective-permute-start(f32[144,384]{1,0:T(8,128)} %get-tuple-element.42), channel_id=1, source_target_pairs={{0,1},{1,2},{2,3},{4,5},{5,6},{6,7},{8,9},{9,10},{10,11},{12,13},{... | collective-permute-start | bytes 663560 | tf_op jit(solution)/shard_map/ppermute | solution.py:164
  10.6 14.1 %collective-permute-start.1 = (f32[144,384]{1,0:T(8,128)}, f32[144,384]{1,0:T(8,128)S(1)}, u32[]{:S(2)}, u32[]{:S(2)}) collective-permute-start(f32[144,384]{1,0:T(8,128)} %get-tuple-element.43), channel_id=1, source_target_pairs={{1,0},{2,1},{3,2},{5,4},{6,5},{7,6},{9,8},{10,9},{11,10},{13,12},{... | collective-permute-start | bytes 663560 | tf_op jit(solution)/shard_map/ppermute | solution.py:165
  11.9 1.3 %copy-start.3 = (f32[4,3,3,64,64]{4,3,2,1,0:T(8,128)S(1)}, f32[4,3,3,64,64]{4,3,2,1,0:T(8,128)}, u32[]{:S(2)}) copy-start(f32[4,3,3,64,64]{4,3,2,1,0:T(8,128)} %param.13) | copy-start | bytes 1769476
  13.2 0.7 copy-start.7
  20.4 4.3 %collective-permute-start.4 = (f32[210,128]{1,0:T(8,128)S(1)}, f32[210,128]{1,0:T(8,128)S(1)}, u32[]{:S(2)}, u32[]{:S(2)}) collective-permute-start(f32[210,128]{1,0:T(8,128)S(1)} %get-tuple-element.47), channel_id=1, source_target_pairs={{0,1},{1,2},{2,3},{4,5},{5,6},{6,7},{8,9},{9,10},{10,11},{12,13},{... | collective-permute-start | bytes 322568 | tf_op jit(solution)/shard_map/ppermute | solution.py:164
  21.7 5.0 %collective-permute-start.5 = (f32[210,128]{1,0:T(8,128)S(1)}, f32[210,128]{1,0:T(8,128)S(1)}, u32[]{:S(2)}, u32[]{:S(2)}) collective-permute-start(f32[210,128]{1,0:T(8,128)S(1)} %get-tuple-element.48), channel_id=1, source_target_pairs={{1,0},{2,1},{3,2},{5,4},{6,5},{7,6},{9,8},{10,9},{11,10},{13,12},{... | collective-permute-start | bytes 322568 | tf_op jit(solution)/shard_map/ppermute | solution.py:165
  26.6 16.7 %copy-start.6 = (f32[3]{0:T(128)S(1)}, f32[3]{0:T(128)}, u32[]{:S(2)}) copy-start(f32[3]{0:T(128)} %steps.5) | copy-start | bytes 40

commit v12 on v11

--- a/solution.py
+++ b/solution.py
@@ -111,14 +111,14 @@
     ]
 
 
-def ends_body(objective, center, radius, lower, upper, top, bottom, head, tail, *rest):
+def ends_body(objective, center, radius, lower, upper, top, bottom, far, near, *rest):
     rows, cols = objective.shape
     held, sem = rest[:5], rest[5]
     finish(copies(list(zip((objective, center, radius, lower, upper), held)), sem))
     strip = HALO_PAIRS * LANES
     for m, read in enumerate(sources(*held)):
-        head[pl.ds(m * rows, rows), :] = read(pl.ds(0, strip))
-        tail[pl.ds(m * rows, rows), :] = read(pl.ds(cols - strip, strip))
+        here = pl.ds(m * rows, rows)
+        sorted_strips(read(pl.ds(0, strip)), read(pl.ds(cols - strip, strip)), far.at[here], near.at[here])
     row = lax.broadcasted_iota(jnp.int32, (rows, LANES), 0)
     outer = (row >= 2) & (row < rows - 2)
     for q in range(cols // LANES):
@@ -130,14 +130,33 @@
             bottom[here, :] = value[rows - ROWS_SENT[m] :]
 
 
-def corners_body(above, below, after, head, tail):
+def odd_column():
+    return lax.axis_index("col") % 2 == 1
+
+
+def sorted_strips(first, last, far, near):
+    odd = odd_column()
+    far[...] = jnp.where(odd, last, first)
+    near[...] = jnp.where(odd, first, last)
+
+
+class Side:
+    def __init__(self, far, near, right):
+        self.far, self.near, self.right = far, near, right
+
+    def __getitem__(self, index):
+        odd = odd_column()
+        other = jnp.logical_not(odd) if self.right else odd
+        return jnp.where(other, self.near[index], self.far[index])
+
+
+def corners_body(above, below, after, far, near):
     del after
     count = HALO_PAIRS * SENT
     size = above.shape[0]
     for part, source in enumerate((above, below)):
         here = pl.ds(part * count, count)
-        head[here, :] = source[0:count, :]
-        tail[here, :] = source[size - count : size, :]
+        sorted_strips(source[0:count, :], source[size - count : size, :], far.at[here], near.at[here])
 
 
 def column(reads, left, right, rows, pairs, m, q):
@@ -164,6 +183,15 @@
     before = lax.ppermute(tail, axis, [(i, i + 1) for i in range(count - 1)])
     after = lax.ppermute(head, axis, [(i + 1, i) for i in range(count - 1)])
     return before, after
+
+
+def partners(far, near, axis):
+    count = lax.axis_size(axis)
+
+    def pairs(first):
+        return [(i + a, i + 1 - a) for i in range(first, count - 1, 2) for a in (0, 1)]
+
+    return lax.ppermute(far, axis, pairs(1)), lax.ppermute(near, axis, pairs(0))
 
 
 def roll_rows(value, shift):
@@ -338,7 +366,7 @@
 
 
 def first_body(
-    objective, center, radius, lower, upper, left, right, above, below, left_corner, right_corner, fwd, bwd, bias,
+    objective, center, radius, lower, upper, far, near, above, below, far_corner, near_corner, fwd, bwd, bias,
     near_in, far_in, back_in, slope_in, mult_in, totals,
     near_box, far_box, back, slope, mult, stat, value,
     raw, gaps, target, store, sums,
@@ -348,7 +376,8 @@
     frame = rows + 2 * EDGE
     wide = pairs + 4
     reads = sources(objective, center, radius, lower, upper)
-    corners = (left_corner, right_corner)
+    left, right = (Side(far, near, right) for right in (False, True))
+    corners = tuple(Side(far_corner, near_corner, right) for right in (False, True))
     slots = list(range(5)) + list(range(wide - 3, wide + 2))
     assemble(reads, above, below, left, right, corners, slots, rows, pairs, raw, gaps, target)
     start_convs(raw, target, store, sums, fwd, bwd, frame)
@@ -546,7 +575,7 @@
 
     ends = shape(pairs * SENT, LANES)
     strip = shape(9 * rows, HALO_PAIRS * LANES)
-    top, bottom, head, tail = call(
+    top, bottom, far, near = call(
         ends_body,
         (ends, ends, strip, strip),
         [pltpu.VMEM(one.shape, one.dtype) for one in inputs] + [pltpu.SemaphoreType.DMA((5,))],
@@ -556,11 +585,11 @@
         far=range(5),
     )
     above, below = neighbours(top, bottom, "row")
-    left, right = neighbours(head, tail, "col")
+    far, near = partners(far, near, "col")
     fwd, bwd, bias = weights(kernels, biases)
     corner = shape(2 * HALO_PAIRS * SENT, LANES)
-    corner_head, corner_tail = call(corners_body, (corner, corner), [], (above, below, bias), 1 << 20)
-    left_corner, right_corner = neighbours(corner_head, corner_tail, "col")
+    far_corner, near_corner = call(corners_body, (corner, corner), [], (above, below, bias), 1 << 20)
+    far_corner, near_corner = partners(far_corner, near_corner, "col")
 
     def start_scratch(count):
         return [
@@ -587,7 +616,7 @@
         first_body,
         start_shapes(wide) + (spread, small),
         start_scratch(10),
-        inputs + (left, right, above, below, left_corner, right_corner, fwd, bwd, bias) + tuple(middle),
+        inputs + (far, near, above, below, far_corner, near_corner, fwd, bwd, bias) + tuple(middle),
         flops,
     )
 

time: 69.9 us -> 67.6 us (0.967)
  waiting for transfers between devices: 7.51 us -> 4.73 us
  starting transfers between devices: 11.5 us -> 13.4 us
  blocking collectives: 33.3 us -> 32.1 us
    ppermute x0 -> x4, starting transfers between devices: none -> 7.22 us  [the longest x2 5.87 us: partners(): lax.ppermute(near, axis, pairs(0))]
    ppermute x3 -> x1, starting transfers between devices: 7.63 us -> 4.86 us  [neighbours(): before = lax.ppermute(tail, axis, [(i, i + 1) for i in range(count - 1)])]
    ppermute x3 -> x1, starting transfers between devices: 3.88 us -> 1.29 us  [neighbours(): after = lax.ppermute(head, axis, [(i + 1, i) for i in range(count - 1)])]
    ppermute x3 -> x1, waiting for transfers between devices: 1.96 us -> 0.01 us  [neighbours(): after = lax.ppermute(head, axis, [(i + 1, i) for i in range(count - 1)])]
    all_to_all x3, blocking collectives: 33.3 us -> 32.1 us  [everyone(): return lax.all_to_all(partial, ('row', 'col'), 0, 0, tiled=True)]
    ppermute x3 -> x1, waiting for transfers between devices: 5.55 us -> 4.71 us  [neighbours(): before = lax.ppermute(tail, axis, [(i, i + 1) for i in range(count - 1)])]
  transfers between devices with their start and end apart: 6 -> 6, of which waited for: 2 -> 1; matrix products, arithmetic and copies ran while one was open for 0% -> 0% of each run, Pallas kernels for 4% -> 4%
where the time goes in v12:
time: 67.6 us; the launch traced here: 67.3 us
  blocking collectives  32.1 us (47%)
  Pallas kernels  14.4 us (21%)
  starting transfers between devices  13.4 us (20%)
  waiting for transfers between devices  4.73 us (7%)
  local copies, waits for them, and re-layouts  1.98 us (3%)
  between operations  0.8 us (1%)
    all_to_all x3, blocking collectives, everyone(): return lax.all_to_all(partial, ('row', 'col'), 0, 0, tiled=True)  32.1 us
    pallas_call x8, Pallas kernels, call(): pl.pallas_call(body, out_shape=outs, in_specs=specs, out_specs=out_specs,...  14.4 us
    ppermute x2, starting transfers between devices, partners(): lax.ppermute(near, axis, pairs(0))  5.87 us
    ppermute x1, starting transfers between devices, neighbours(): before = lax.ppermute(tail, axis, [(i, i + 1) for i in range(count - 1)])  4.86 us
    ppermute x1, waiting for transfers between devices, neighbours(): before = lax.ppermute(tail, axis, [(i, i + 1) for i in range(count - 1)])  4.71 us
    unnamed x16, local copies, waits for them, and re-layouts  1.98 us
  transfers between devices with their start and end apart: 6, of which 1 were waited for; matrix products, arithmetic and copies ran while one was open for 0% of the time, Pallas kernels for 4%

profile of v12, /device:TPU:0, one launch (start us, length us, event | category | flops | bytes accessed | tf_op | source)
XLA Modules:
  0.0 67.3 jit_solution(15809572644897761008)
XLA Ops:
  0.7 2.3 %shard_map.103 = (f32[560,128]{1,0:T(8,128)}, f32[560,128]{1,0:T(8,128)}, f32[144,384]{1,0:T(8,128)}, f32[144,384]{1,0:T(8,128)}) custom-call(f32[16,2048]{1,0:T(8,128)} %objective.5, bf16[16,2048]{1,0:T(8,128)(2,1)} %center.5, bf16[16,2048]{1,0:T(8,128)(2,1)} %radius.5, bf16[3,16,2048]{2,1,0:T(8,128)(2,1)} %lower.7, bf16[3,16,2048]{2,1,0:T(8,128)(2,1)} %upper.7), custom_call_target="tpu_custom_call" | custom-call | flops 1048576 | bytes 4194304 | tf_op jit(solution)/shard_map/pallas_call | solution.py:35
  2.9 4.9 %collective-permute-start.2 = (f32[560,128]{1,0:T(8,128)}, f32[560,128]{1,0:T(8,128)S(1)}, u32[]{:S(2)}, u32[]{:S(2)}) collective-permute-start(f32[560,128]{1,0:T(8,128)} %get-tuple-element.44), channel_id=1, source_target_pairs={{0,4},{4,8},{8,12},{12,16},{16,20},{20,24},{24,28},{1,5},{5,9},{9,... | collective-permute-start | bytes 860168 | tf_op jit(solution)/shard_map/ppermute | solution.py:183
  7.8 1.3 %collective-permute-start.3 = (f32[560,128]{1,0:T(8,128)}, f32[560,128]{1,0:T(8,128)S(1)}, u32[]{:S(2)}, u32[]{:S(2)}) collective-permute-start(f32[560,128]{1,0:T(8,128)} %get-tuple-element.45), channel_id=1, source_target_pairs={{4,0},{8,4},{12,8},{16,12},{20,16},{24,20},{28,24},{5,1},{9,5},{13... | collective-permute-start | bytes 860168 | tf_op jit(solution)/shard_map/ppermute | solution.py:184
  9.1 0.7 %collective-permute-start = (f32[144,384]{1,0:T(8,128)}, f32[144,384]{1,0:T(8,128)S(1)}, u32[]{:S(2)}, u32[]{:S(2)}) collective-permute-start(f32[144,384]{1,0:T(8,128)} %get-tuple-element.42), channel_id=1, source_target_pairs={{1,2},{2,1},{5,6},{6,5},{9,10},{10,9},{13,14},{14,13},{17,18},{18,... | collective-permute-start | bytes 663560 | tf_op jit(solution)/shard_map/ppermute | solution.py:194
  9.8 2.9 %collective-permute-start.1 = (f32[144,384]{1,0:T(8,128)}, f32[144,384]{1,0:T(8,128)S(1)}, u32[]{:S(2)}, u32[]{:S(2)}) collective-permute-start(f32[144,384]{1,0:T(8,128)} %get-tuple-element.43), channel_id=1, source_target_pairs={{0,1},{1,0},{2,3},{3,2},{4,5},{5,4},{6,7},{7,6},{8,9},{9,8},{10,11... | collective-permute-start | bytes 663560 | tf_op jit(solution)/shard_map/ppermute | solution.py:194
  12.7 1.3 %copy-done.3 = f32[4,3,3,64,64]{4,3,2,1,0:T(8,128)S(1)} copy-done((f32[4,3,3,64,64]{4,3,2,1,0:T(8,128)S(1)}, f32[4,3,3,64,64]{4,3,2,1,0:T(8,128)}, u32[]{:S(2)}) %copy-start.3) | copy-done | bytes 589848
  14.0 0.7 %copy-done.7 = f32[4,64]{1,0:T(4,128)S(1)} copy-done((f32[4,64]{1,0:T(4,128)S(1)}, f32[4,64]{1,0:T(4,128)}, u32[]{:S(2)}) %copy-start.7) | copy-done | bytes 1048
  14.7 0.9 %shard_map.104 = (bf16[3,768,384]{2,1,0:T(8,128)(2,1)S(1)}, bf16[4,768,384]{2,1,0:T(8,128)(2,1)S(1)}, f32[8,128]{1,0:T(8,128)S(1)}) custom-call(f32[36,64,64]{2,1,0:T(8,128)S(1)} %bitcast.13, f32[4,64]{1,0:T(4,128)S(1)} %copy-done.7), custom_call_target="tpu_custom_call" | custom-call | flops 4194304 | bytes 4194304 | tf_op jit(solution)/shard_map/pallas_call | solution.py:35
  15.6 4.7 %collective-permute-done.2.above = f32[560,128]{1,0:T(8,128)S(1)} collective-permute-done((f32[560,128]{1,0:T(8,128)}, f32[560,128]{1,0:T(8,128)S(1)}, u32[]{:S(2)}, u32[]{:S(2)}) %collective-permute-start.2) | collective-permute-done | bytes 286752 | tf_op jit(solution)/shard_map/ppermute | solution.py:183
  20.3 0.0 collective-permute-done.3.below
  20.4 0.7 collective-permute-start.4
  21.0 2.9 %collective-permute-start.5 = (f32[210,128]{1,0:T(8,128)S(1)}, f32[210,128]{1,0:T(8,128)S(1)}, u32[]{:S(2)}, u32[]{:S(2)}) collective-permute-start(f32[210,128]{1,0:T(8,128)S(1)} %get-tuple-element.48), channel_id=1, source_target_pairs={{0,1},{1,0},{2,3},{3,2},{4,5},{5,4},{6,7},{7,6},{8,9},{9,8},{10,11... | collective-permute-start | bytes 322568 | tf_op jit(solution)/shard_map/ppermute | solution.py:194
  24.0 1.6 %shard_map.106 = (bf16[4,14,24,128]{3,2,1,0:T(8,128)(2,1)S(1)}, bf16[4,14,24,128]{3,2,1,0:T(8,128)(2,1)S(1)}, f32[14,24,128]{2,1,0:T(8,128)S(1)}, f32[3,14,24,12...) custom-call(f32[16,2048]{1,0:T(8,128)S(1)} %copy-done.2, bf16[16,2048]{1,0:T(8,128)(2,1)S(1)} %copy-done.4, ...), custom_call_target="tpu_custom_call" | custom-call | flops 849346560 | bytes 4194304 | tf_op jit(solution)/shard_map/pallas_call | solution.py:35
  25.6 0.0 collective-permute-done.far
  25.6 0.0 collective-permute-done.1.near
  25.7 0.0 collective-permute-done.4.far_corner
  25.7 0.0 copy-start.6
  25.7 1.0 %shard_map.107 = (bf16[4,20,24,128]{3,2,1,0:T(8,128)(2,1)S(1)}, bf16[4,20,24,128]{3,2,1,0:T(8,128)(2,1)S(1)}, f32[20,24,128]{2,1,0:T(8,128)S(1)}, f32[3,20,24,12...) custom-call(f32[16,2048]{1,0:T(8,128)S(1)} %copy-done.2, ...), custom_call_target="tpu_custom_call" | custom-call | flops 849346560 | bytes 4194304 | tf_op jit(solution)/shard_map/pallas_call | solution.py:35
  26.7 14.4 %all_to_all.33 = f32[32,1,128]{2,1,0:T(1,128)S(1)} all-to-all(f32[32,1,128]{2,1,0:T(1,128)S(1)} %bitcast.17), channel_id=1, replica_groups=mesh['row'=8,'col'=4] {'row','col'}, dimensions={0} | all-to-all | bytes 32768 | tf_op jit(solution)/shard_map/all_to_all | solution.py:561
  41.1 3.8 %shard_map.108 = (f32[3,20,24,128]{3,2,1,0:T(8,128)S(1)}, f32[3,18,24,128]{3,2,1,0:T(8,128)S(1)}, f32[2,18,24,128]{3,2,1,0:T(8,128)S(1)}, f32[3,18,16,128]{3,2,1...) custom-call(f32[32,128]{1,0:T(8,128)S(1)} %bitcast.15, ...), custom_call_target="tpu_custom_call" | custom-call | flops 1698693120 | bytes 4194304 | tf_op jit(solution)/shard_map/pallas_call | solution.py:35
  45.0 8.8 %all_to_all.34 = f32[32,1,128]{2,1,0:T(1,128)S(1)} all-to-all(f32[32,1,128]{2,1,0:T(1,128)S(1)} %bitcast.19), channel_id=1, replica_groups=mesh['row'=8,'col'=4] {'row','col'}, dimensions={0} | all-to-all | bytes 32768 | tf_op jit(solution)/shard_map/all_to_all | solution.py:561
  53.8 3.1 %shard_map.109 = (f32[3,16,2048]{2,1,0:T(8,128)S(1)}, f32[3,16,2048]{2,1,0:T(8,128)S(1)}, f32[3,16,2048]{2,1,0:T(8,128)S(1)}, f32[3,16,2048]{2,1,0:T(8,128)S(1)}, f32[32,128]{1,0:T(8,128)S(1)}) custom-call(f32[32,128]{1,0:T(8,128)S(1)} %bitcast.14, f32[3]{0:T(128)S(1)} %copy-done.6, bf16[4,20,24,128]{3,2,1,0:T(8,128)(2,1)S(1)} %get-tuple-element.58.near_box, ...), custom_call_target="tpu_custom_call" | custom-call | flops 1698693120 | bytes 4194304 | tf_op jit(solution)/shard_map/pallas_call | solution.py:35
  56.9 8.8 %all_to_all.35 = f32[32,1,128]{2,1,0:T(1,128)S(1)} all-to-all(f32[32,1,128]{2,1,0:T(1,128)S(1)} %bitcast.18), channel_id=1, replica_groups=mesh['row'=8,'col'=4] {'row','col'}, dimensions={0} | all-to-all | bytes 32768 | tf_op jit(solution)/shard_map/all_to_all | solution.py:561
  65.7 1.6 %shard_map.110 = (f32[3,16,2048]{2,1,0:T(8,128)}, f32[3,16,2048]{2,1,0:T(8,128)}, f32[3]{0:T(128)}) custom-call(f32[32,128]{1,0:T(8,128)S(1)} %bitcast.16, f32[3]{0:T(128)S(1)} %copy-done.6, f32[3,16,2048]{2,1,0:T(8,128)S(1)} %get-tuple-element.74.duals, f32[3,16,2048]{2,1,0:T(8,128)S(1)} %get-tuple-element.75.multipliers, ...), custom_call_target="tpu_custom_call" | custom-call | flops 1048576 | bytes 4194304 | tf_op jit(solution)/shard_map/pallas_call | solution.py:35
  (15 shorter events, 0.1 us)
Async XLA Ops:
  0.6 23.4 %copy-start.1 = (bf16[3,16,2048]{2,1,0:T(8,128)(2,1)S(1)}, bf16[3,16,2048]{2,1,0:T(8,128)(2,1)}, u32[]{:S(2)}) copy-start(bf16[3,16,2048]{2,1,0:T(8,128)(2,1)} %upper.7) | copy-start | bytes 589828
  0.6 23.3 %copy-start = (bf16[3,16,2048]{2,1,0:T(8,128)(2,1)S(1)}, bf16[3,16,2048]{2,1,0:T(8,128)(2,1)}, u32[]{:S(2)}) copy-start(bf16[3,16,2048]{2,1,0:T(8,128)(2,1)} %lower.7) | copy-start | bytes 589828
  0.7 23.3 %copy-start.5 = (bf16[16,2048]{1,0:T(8,128)(2,1)S(1)}, bf16[16,2048]{1,0:T(8,128)(2,1)}, u32[]{:S(2)}) copy-start(bf16[16,2048]{1,0:T(8,128)(2,1)} %radius.5) | copy-start | bytes 196612
  0.7 23.3 %copy-start.4 = (bf16[16,2048]{1,0:T(8,128)(2,1)S(1)}, bf16[16,2048]{1,0:T(8,128)(2,1)}, u32[]{:S(2)}) copy-start(bf16[16,2048]{1,0:T(8,128)(2,1)} %center.5) | copy-start | bytes 196612
  0.7 23.3 %copy-start.2 = (f32[16,2048]{1,0:T(8,128)S(1)}, f32[16,2048]{1,0:T(8,128)}, u32[]{:S(2)}) copy-start(f32[16,2048]{1,0:T(8,128)} %objective.5) | copy-start | bytes 393220
  2.9 17.4 %collective-permute-start.2 = (f32[560,128]{1,0:T(8,128)}, f32[560,128]{1,0:T(8,128)S(1)}, u32[]{:S(2)}, u32[]{:S(2)}) collective-permute-start(f32[560,128]{1,0:T(8,128)} %get-tuple-element.44), channel_id=1, source_target_pairs={{0,4},{4,8},{8,12},{12,16},{16,20},{20,24},{24,28},{1,5},{5,9},{9,... | collective-permute-start | bytes 860168 | tf_op jit(solution)/shard_map/ppermute | solution.py:183
  7.8 12.5 %collective-permute-start.3 = (f32[560,128]{1,0:T(8,128)}, f32[560,128]{1,0:T(8,128)S(1)}, u32[]{:S(2)}, u32[]{:S(2)}) collective-permute-start(f32[560,128]{1,0:T(8,128)} %get-tuple-element.45), channel_id=1, source_target_pairs={{4,0},{8,4},{12,8},{16,12},{20,16},{24,20},{28,24},{5,1},{9,5},{13... | collective-permute-start | bytes 860168 | tf_op jit(solution)/shard_map/ppermute | solution.py:184
  9.1 16.5 %collective-permute-start = (f32[144,384]{1,0:T(8,128)}, f32[144,384]{1,0:T(8,128)S(1)}, u32[]{:S(2)}, u32[]{:S(2)}) collective-permute-start(f32[144,384]{1,0:T(8,128)} %get-tuple-element.42), channel_id=1, source_target_pairs={{1,2},{2,1},{5,6},{6,5},{9,10},{10,9},{13,14},{14,13},{17,18},{18,... | collective-permute-start | bytes 663560 | tf_op jit(solution)/shard_map/ppermute | solution.py:194
  9.8 15.9 %collective-permute-start.1 = (f32[144,384]{1,0:T(8,128)}, f32[144,384]{1,0:T(8,128)S(1)}, u32[]{:S(2)}, u32[]{:S(2)}) collective-permute-start(f32[144,384]{1,0:T(8,128)} %get-tuple-element.43), channel_id=1, source_target_pairs={{0,1},{1,0},{2,3},{3,2},{4,5},{5,4},{6,7},{7,6},{8,9},{9,8},{10,11... | collective-permute-start | bytes 663560 | tf_op jit(solution)/shard_map/ppermute | solution.py:194
  12.7 1.3 %copy-start.3 = (f32[4,3,3,64,64]{4,3,2,1,0:T(8,128)S(1)}, f32[4,3,3,64,64]{4,3,2,1,0:T(8,128)}, u32[]{:S(2)}) copy-start(f32[4,3,3,64,64]{4,3,2,1,0:T(8,128)} %param.13) | copy-start | bytes 1769476
  14.0 0.7 %copy-start.7 = (f32[4,64]{1,0:T(4,128)S(1)}, f32[4,64]{1,0:T(4,128)}, u32[]{:S(2)}) copy-start(f32[4,64]{1,0:T(4,128)} %biases.1) | copy-start | bytes 3076
  20.4 5.3 %collective-permute-start.4 = (f32[210,128]{1,0:T(8,128)S(1)}, f32[210,128]{1,0:T(8,128)S(1)}, u32[]{:S(2)}, u32[]{:S(2)}) collective-permute-start(f32[210,128]{1,0:T(8,128)S(1)} %get-tuple-element.47), channel_id=1, source_target_pairs={{1,2},{2,1},{5,6},{6,5},{9,10},{10,9},{13,14},{14,13},{17,18},{18,... | collective-permute-start | bytes 322568 | tf_op jit(solution)/shard_map/ppermute | solution.py:194
  21.0 4.6 %collective-permute-start.5 = (f32[210,128]{1,0:T(8,128)S(1)}, f32[210,128]{1,0:T(8,128)S(1)}, u32[]{:S(2)}, u32[]{:S(2)}) collective-permute-start(f32[210,128]{1,0:T(8,128)S(1)} %get-tuple-element.48), channel_id=1, source_target_pairs={{0,1},{1,0},{2,3},{3,2},{4,5},{5,4},{6,7},{7,6},{8,9},{9,8},{10,11... | collective-permute-start | bytes 322568 | tf_op jit(solution)/shard_map/ppermute | solution.py:194
  25.7 15.5 %copy-start.6 = (f32[3]{0:T(128)S(1)}, f32[3]{0:T(128)}, u32[]{:S(2)}) copy-start(f32[3]{0:T(128)} %steps.5) | copy-start | bytes 40

commit v13 on v12

--- a/solution.py
+++ b/solution.py
@@ -29,9 +29,9 @@
 HBM = pl.BlockSpec(memory_space=pltpu.HBM)
 
 
-def call(body, outs, scratch, operands, flops, mem=20, scalars=(), far=(), scalar_outs=()):
+def call(body, outs, scratch, operands, flops, mem=20, scalars=(), far=(), scalar_outs=(), far_outs=()):
     specs = [SMEM if j in scalars else HBM if j in far else VMEM for j in range(len(operands))]
-    out_specs = tuple(SMEM if j in scalar_outs else VMEM for j in range(len(outs)))
+    out_specs = tuple(SMEM if j in scalar_outs else HBM if j in far_outs else VMEM for j in range(len(outs)))
     return pl.pallas_call(
         body,
         out_shape=outs,
@@ -111,52 +111,66 @@
     ]
 
 
-def ends_body(objective, center, radius, lower, upper, top, bottom, far, near, *rest):
+def ends_body(objective, center, radius, lower, upper, *rest):
     rows, cols = objective.shape
-    held, sem = rest[:5], rest[5]
-    finish(copies(list(zip((objective, center, radius, lower, upper), held)), sem))
+    outs, held, made, sem = rest[:4], rest[4:9], rest[9:13], rest[13]
+    arrivals = copies(list(zip((objective, center, radius, lower, upper), held)), sem)
+    finish(arrivals)
     strip = HALO_PAIRS * LANES
+    for q in range(cols // LANES):
+        values = [read(pl.ds(q * LANES, LANES)) for read in sources(*held)]
+        ends_of(values, made[0], made[1], q * SENT)
+    leaving = copies(list(zip(made[:2], outs[:2])), sem)
     for m, read in enumerate(sources(*held)):
         here = pl.ds(m * rows, rows)
-        sorted_strips(read(pl.ds(0, strip)), read(pl.ds(cols - strip, strip)), far.at[here], near.at[here])
+        sorted_strips(
+            "col", read(pl.ds(0, strip)), read(pl.ds(cols - strip, strip)), made[2].at[here], made[3].at[here]
+        )
+    finish(leaving + copies(list(zip(made[2:], outs[2:])), sem.at[2:4]))
+
+
+def ends_of(values, far, near, start):
+    rows = values[0].shape[0]
     row = lax.broadcasted_iota(jnp.int32, (rows, LANES), 0)
     outer = (row >= 2) & (row < rows - 2)
-    for q in range(cols // LANES):
-        values = [read(pl.ds(q * LANES, LANES)) for read in sources(*held)]
-        values[3] = jnp.where(outer, values[3] - values[6], values[3])
-        for m, value in enumerate(values):
-            here = pl.ds(q * SENT + ROW_START[m], ROWS_SENT[m])
-            top[here, :] = value[: ROWS_SENT[m]]
-            bottom[here, :] = value[rows - ROWS_SENT[m] :]
-
-
-def odd_column():
-    return lax.axis_index("col") % 2 == 1
-
-
-def sorted_strips(first, last, far, near):
-    odd = odd_column()
+    values[3] = jnp.where(outer, values[3] - values[6], values[3])
+    for m, value in enumerate(values):
+        here = pl.ds(start + ROW_START[m], ROWS_SENT[m])
+        sorted_strips("row", value[: ROWS_SENT[m]], value[rows - ROWS_SENT[m] :], far.at[here], near.at[here])
+
+
+def odd_index(axis):
+    return lax.axis_index(axis) % 2 == 1
+
+
+def sorted_strips(axis, first, last, far, near):
+    odd = odd_index(axis)
     far[...] = jnp.where(odd, last, first)
     near[...] = jnp.where(odd, first, last)
 
 
 class Side:
-    def __init__(self, far, near, right):
-        self.far, self.near, self.right = far, near, right
+    def __init__(self, axis, far, near, after):
+        self.axis, self.far, self.near, self.after = axis, far, near, after
+        self.shape = far.shape
 
     def __getitem__(self, index):
-        odd = odd_column()
-        other = jnp.logical_not(odd) if self.right else odd
-        return jnp.where(other, self.near[index], self.far[index])
-
-
-def corners_body(above, below, after, far, near):
+        odd = odd_index(self.axis)
+        near = jnp.logical_not(odd) if self.after else odd
+        return jnp.where(near, self.near[index], self.far[index])
+
+
+def sides(axis, far, near):
+    return Side(axis, far, near, False), Side(axis, far, near, True)
+
+
+def corners_body(far_rows, near_rows, after, far, near):
     del after
     count = HALO_PAIRS * SENT
-    size = above.shape[0]
-    for part, source in enumerate((above, below)):
+    size = far_rows.shape[0]
+    for part, source in enumerate(sides("row", far_rows, near_rows)):
         here = pl.ds(part * count, count)
-        sorted_strips(source[0:count, :], source[size - count : size, :], far.at[here], near.at[here])
+        sorted_strips("col", source[0:count, :], source[size - count : size, :], far.at[here], near.at[here])
 
 
 def column(reads, left, right, rows, pairs, m, q):
@@ -176,13 +190,6 @@
     else:
         source, at = middle, q - HALO_PAIRS
     return source[pl.ds(at * SENT + ROW_START[m], ROWS_SENT[m]), :]
-
-
-def neighbours(head, tail, axis):
-    count = lax.axis_size(axis)
-    before = lax.ppermute(tail, axis, [(i, i + 1) for i in range(count - 1)])
-    after = lax.ppermute(head, axis, [(i + 1, i) for i in range(count - 1)])
-    return before, after
 
 
 def partners(far, near, axis):
@@ -343,7 +350,7 @@
 
 
 def middle_body(
-    objective, center, radius, lower, upper, above, below, fwd, bwd, bias,
+    objective, center, radius, lower, upper, far_rows, near_rows, fwd, bwd, bias,
     near_box, far_box, back, slope, mult, totals,
     raw, gaps, target, store, sums,
 ):
@@ -351,6 +358,7 @@
     pairs = cols // LANES
     frame = rows + 2 * EDGE
     reads = sources(objective, center, radius, lower, upper)
+    above, below = sides("row", far_rows, near_rows)
     slots = range(HALO_PAIRS, HALO_PAIRS + pairs)
     assemble(reads, above, below, None, None, (None, None), slots, rows, pairs, raw, gaps, target)
     start_convs(raw, target, store, sums, fwd, bwd, frame)
@@ -366,7 +374,7 @@
 
 
 def first_body(
-    objective, center, radius, lower, upper, far, near, above, below, far_corner, near_corner, fwd, bwd, bias,
+    objective, center, radius, lower, upper, far_cols, near_cols, far_rows, near_rows, far_corner, near_corner, fwd, bwd, bias,
     near_in, far_in, back_in, slope_in, mult_in, totals,
     near_box, far_box, back, slope, mult, stat, value,
     raw, gaps, target, store, sums,
@@ -376,8 +384,9 @@
     frame = rows + 2 * EDGE
     wide = pairs + 4
     reads = sources(objective, center, radius, lower, upper)
-    left, right = (Side(far, near, right) for right in (False, True))
-    corners = tuple(Side(far_corner, near_corner, right) for right in (False, True))
+    above, below = sides("row", far_rows, near_rows)
+    left, right = sides("col", far_cols, near_cols)
+    corners = sides("col", far_corner, near_corner)
     slots = list(range(5)) + list(range(wide - 3, wide + 2))
     assemble(reads, above, below, left, right, corners, slots, rows, pairs, raw, gaps, target)
     start_convs(raw, target, store, sums, fwd, bwd, frame)
@@ -546,15 +555,22 @@
     stats(stat, [folded(squares), start, middle + fixed, folded(worth) + own_rows(framed) + fixed])
 
 
-def last_body(total, steps, duals, multipliers, slope, mult, duals_out, mult_out, bounds, *, cells):
+def last_body(
+    total, steps, duals, multipliers, slope, mult, duals_far, mult_far, bounds,
+    duals_out, mult_out, sem, *, cells,
+):
     scale = scale_of(total, steps[2], cells, duals.shape[1:])
+    leaving = []
     for k in range(LAYERS - 1):
         duals_out[k] = duals[k] + scale * slope[k]
         mult_out[k] = multipliers[k] + scale * mult[k]
+        moves = [(duals_out.at[k], duals_far.at[k]), (mult_out.at[k], mult_far.at[k])]
+        leaving += copies(moves, sem.at[2 * k : 2 * k + 2])
     values = summed(total) / cells
     lane = lax.broadcasted_iota(jnp.int32, (1, LANES), 1)
     for j in range(ITERS):
         bounds[j] = jnp.sum(jnp.where(lane == j + 1, values, 0.0))
+    finish(leaving)
 
 
 def everyone(partial):
@@ -575,20 +591,22 @@
 
     ends = shape(pairs * SENT, LANES)
     strip = shape(9 * rows, HALO_PAIRS * LANES)
-    top, bottom, far, near = call(
+    made = (ends, ends, strip, strip)
+    far_rows, near_rows, far_cols, near_cols = call(
         ends_body,
-        (ends, ends, strip, strip),
-        [pltpu.VMEM(one.shape, one.dtype) for one in inputs] + [pltpu.SemaphoreType.DMA((5,))],
+        made,
+        [pltpu.VMEM(one.shape, one.dtype) for one in inputs + made] + [pltpu.SemaphoreType.DMA((5,))],
         inputs,
         1 << 20,
         mem=58,
         far=range(5),
-    )
-    above, below = neighbours(top, bottom, "row")
-    far, near = partners(far, near, "col")
+        far_outs=range(4),
+    )
+    far_rows, near_rows = partners(far_rows, near_rows, "row")
+    far_cols, near_cols = partners(far_cols, near_cols, "col")
     fwd, bwd, bias = weights(kernels, biases)
     corner = shape(2 * HALO_PAIRS * SENT, LANES)
-    far_corner, near_corner = call(corners_body, (corner, corner), [], (above, below, bias), 1 << 20)
+    far_corner, near_corner = call(corners_body, (corner, corner), [], (far_rows, near_rows, bias), 1 << 20)
     far_corner, near_corner = partners(far_corner, near_corner, "col")
 
     def start_scratch(count):
@@ -609,14 +627,16 @@
         middle_body,
         start_shapes(pairs - 2) + (shape(3, frame, LANES),),
         start_scratch(pairs),
-        inputs + (above, below, fwd, bwd, bias),
+        inputs + (far_rows, near_rows, fwd, bwd, bias),
         flops,
     )
     near_box, far_box, back, slope0, mult0, stat0, value0 = call(
         first_body,
         start_shapes(wide) + (spread, small),
         start_scratch(10),
-        inputs + (far, near, above, below, far_corner, near_corner, fwd, bwd, bias) + tuple(middle),
+        inputs
+        + (far_cols, near_cols, far_rows, near_rows, far_corner, near_corner, fwd, bwd, bias)
+        + tuple(middle),
         flops,
     )
 
@@ -666,10 +686,11 @@
     final_duals, final_multipliers, bounds = call(
         functools.partial(last_body, cells=cells),
         (out, out, shape(ITERS)),
-        [],
+        [pltpu.VMEM(out.shape, F32), pltpu.VMEM(out.shape, F32), pltpu.SemaphoreType.DMA((6,))],
         (total2, steps, duals, multipliers, slope2, mult2),
         1 << 20,
         scalar_outs=(2,),
+        far_outs=(0, 1),
         scalars=(1,),
     )
     return bounds, final_duals, final_multipliers

time: 67.6 us -> 68.2 us (level)
  blocking collectives: 32.1 us -> 31.1 us
    ppermute x2 -> x0, starting transfers between devices: 6.15 us -> none  [the longest x1 4.86 us: neighbours(): before = lax.ppermute(tail, axis, [(i, i + 1) for i in range(count - 1)])]
    ppermute x2 -> x3, starting transfers between devices: 5.87 us -> 11.7 us  [partners(): lax.ppermute(near, axis, pairs(0))]
    ppermute x2 -> x3, waiting for transfers between devices: 0.01 us -> 5.32 us  [partners(): lax.ppermute(near, axis, pairs(0))]
    ppermute x2 -> x0, waiting for transfers between devices: 4.72 us -> none  [the longest x1 4.71 us: neighbours(): before = lax.ppermute(tail, axis, [(i, i + 1) for i in range(count - 1)])]
    all_to_all x3, blocking collectives: 32.1 us -> 31.1 us  [everyone(): return lax.all_to_all(partial, ('row', 'col'), 0, 0, tiled=True)]
    ppermute x2 -> x3, starting transfers between devices: 1.34 us -> 2.01 us  [partners(): lax.ppermute(far, axis, pairs(1))]
where the time goes in v13:
time: 68.2 us; the launch traced here: 67.9 us
  blocking collectives  31.1 us (46%)
  Pallas kernels  15 us (22%)
  starting transfers between devices  13.7 us (20%)
  waiting for transfers between devices  5.33 us (8%)
  local copies, waits for them, and re-layouts  1.98 us (3%)
  between operations  0.8 us (1%)
    all_to_all x3, blocking collectives, everyone(): return lax.all_to_all(partial, ('row', 'col'), 0, 0, tiled=True)  31.1 us
    pallas_call x8, Pallas kernels, call(): pl.pallas_call(body, out_shape=outs, in_specs=specs, out_specs=out_specs,...  15 us
    ppermute x3, starting transfers between devices, partners(): lax.ppermute(near, axis, pairs(0))  11.7 us
    ppermute x3, waiting for transfers between devices, partners(): lax.ppermute(near, axis, pairs(0))  5.32 us
    ppermute x3, starting transfers between devices, partners(): lax.ppermute(far, axis, pairs(1))  2.01 us
    unnamed x16, local copies, waits for them, and re-layouts  1.98 us
  transfers between devices with their start and end apart: 6, of which 1 were waited for; matrix products, arithmetic and copies ran while one was open for 0% of the time, Pallas kernels for 4%

profile of v13, /device:TPU:0, one launch (start us, length us, event | category | flops | bytes accessed | tf_op | source)
XLA Modules:
  0.0 67.9 jit_solution(1465732306445794281)
XLA Ops:
  0.7 2.3 %shard_map.103 = (f32[560,128]{1,0:T(8,128)}, f32[560,128]{1,0:T(8,128)}, f32[144,384]{1,0:T(8,128)}, f32[144,384]{1,0:T(8,128)}) custom-call(f32[16,2048]{1,0:T(8,128)} %objective.5, bf16[16,2048]{1,0:T(8,128)(2,1)} %center.5, bf16[16,2048]{1,0:T(8,128)(2,1)} %radius.5, bf16[3,16,2048]{2,1,0:T(8,128)(2,1)} %lower.7, bf16[3,16,2048]{2,1,0:T(8,128)(2,1)} %upper.7), custom_call_target="tpu_custom_call" | custom-call | flops 1048576 | bytes 4194304 | tf_op jit(solution)/shard_map/pallas_call | solution.py:35
  3.0 0.7 collective-permute-start.2
  3.7 5.8 %collective-permute-start.3 = (f32[560,128]{1,0:T(8,128)}, f32[560,128]{1,0:T(8,128)S(1)}, u32[]{:S(2)}, u32[]{:S(2)}) collective-permute-start(f32[560,128]{1,0:T(8,128)} %get-tuple-element.45), channel_id=1, source_target_pairs={{0,4},{4,0},{8,12},{12,8},{16,20},{20,16},{24,28},{28,24},{1,5},{5... | collective-permute-start | bytes 860168 | tf_op jit(solution)/shard_map/ppermute | solution.py:201
  9.5 0.7 collective-permute-start
  10.2 2.9 %collective-permute-start.1 = (f32[144,384]{1,0:T(8,128)}, f32[144,384]{1,0:T(8,128)S(1)}, u32[]{:S(2)}, u32[]{:S(2)}) collective-permute-start(f32[144,384]{1,0:T(8,128)} %get-tuple-element.43), channel_id=1, source_target_pairs={{0,1},{1,0},{2,3},{3,2},{4,5},{5,4},{6,7},{7,6},{8,9},{9,8},{10,11... | collective-permute-start | bytes 663560 | tf_op jit(solution)/shard_map/ppermute | solution.py:201
  13.1 1.3 %copy-done.3 = f32[4,3,3,64,64]{4,3,2,1,0:T(8,128)S(1)} copy-done((f32[4,3,3,64,64]{4,3,2,1,0:T(8,128)S(1)}, f32[4,3,3,64,64]{4,3,2,1,0:T(8,128)}, u32[]{:S(2)}) %copy-start.3) | copy-done | bytes 589848
  14.4 0.7 %copy-done.7 = f32[4,64]{1,0:T(4,128)S(1)} copy-done((f32[4,64]{1,0:T(4,128)S(1)}, f32[4,64]{1,0:T(4,128)}, u32[]{:S(2)}) %copy-start.7) | copy-done | bytes 1048
  15.0 0.9 %shard_map.104 = (bf16[3,768,384]{2,1,0:T(8,128)(2,1)S(1)}, bf16[4,768,384]{2,1,0:T(8,128)(2,1)S(1)}, f32[8,128]{1,0:T(8,128)S(1)}) custom-call(f32[36,64,64]{2,1,0:T(8,128)S(1)} %bitcast.13, f32[4,64]{1,0:T(4,128)S(1)} %copy-done.7), custom_call_target="tpu_custom_call" | custom-call | flops 4194304 | bytes 4194304 | tf_op jit(solution)/shard_map/pallas_call | solution.py:35
  16.0 0.0 collective-permute-done.2.far_rows
  16.0 5.3 %collective-permute-done.3.near_rows = f32[560,128]{1,0:T(8,128)S(1)} collective-permute-done((f32[560,128]{1,0:T(8,128)}, f32[560,128]{1,0:T(8,128)S(1)}, u32[]{:S(2)}, u32[]{:S(2)}) %collective-permute-start.3) | collective-permute-done | bytes 286752 | tf_op jit(solution)/shard_map/ppermute | solution.py:201
  21.3 0.7 collective-permute-start.4
  22.0 2.9 %collective-permute-start.5 = (f32[210,128]{1,0:T(8,128)S(1)}, f32[210,128]{1,0:T(8,128)S(1)}, u32[]{:S(2)}, u32[]{:S(2)}) collective-permute-start(f32[210,128]{1,0:T(8,128)S(1)} %get-tuple-element.48), channel_id=1, source_target_pairs={{0,1},{1,0},{2,3},{3,2},{4,5},{5,4},{6,7},{7,6},{8,9},{9,8},{10,11... | collective-permute-start | bytes 322568 | tf_op jit(solution)/shard_map/ppermute | solution.py:201
  25.0 1.7 %shard_map.106 = (bf16[4,14,24,128]{3,2,1,0:T(8,128)(2,1)S(1)}, bf16[4,14,24,128]{3,2,1,0:T(8,128)(2,1)S(1)}, f32[14,24,128]{2,1,0:T(8,128)S(1)}, f32[3,14,24,12...) custom-call(f32[16,2048]{1,0:T(8,128)S(1)} %copy-done.2, bf16[16,2048]{1,0:T(8,128)(2,1)S(1)} %copy-done.4, ...), custom_call_target="tpu_custom_call" | custom-call | flops 849346560 | bytes 4194304 | tf_op jit(solution)/shard_map/pallas_call | solution.py:35
  26.6 0.0 collective-permute-done.far_cols
  26.7 0.0 collective-permute-done.1.near_cols
  26.7 0.0 collective-permute-done.5.near_corner
  26.7 0.0 copy-start.6
  26.7 1.0 %shard_map.107 = (bf16[4,20,24,128]{3,2,1,0:T(8,128)(2,1)S(1)}, bf16[4,20,24,128]{3,2,1,0:T(8,128)(2,1)S(1)}, f32[20,24,128]{2,1,0:T(8,128)S(1)}, f32[3,20,24,12...) custom-call(f32[16,2048]{1,0:T(8,128)S(1)} %copy-done.2, ...), custom_call_target="tpu_custom_call" | custom-call | flops 849346560 | bytes 4194304 | tf_op jit(solution)/shard_map/pallas_call | solution.py:35
  27.8 13.5 %all_to_all.33 = f32[32,1,128]{2,1,0:T(1,128)S(1)} all-to-all(f32[32,1,128]{2,1,0:T(1,128)S(1)} %bitcast.17), channel_id=1, replica_groups=mesh['row'=8,'col'=4] {'row','col'}, dimensions={0} | all-to-all | bytes 32768 | tf_op jit(solution)/shard_map/all_to_all | solution.py:577
  41.2 3.8 %shard_map.108 = (f32[3,20,24,128]{3,2,1,0:T(8,128)S(1)}, f32[3,18,24,128]{3,2,1,0:T(8,128)S(1)}, f32[2,18,24,128]{3,2,1,0:T(8,128)S(1)}, f32[3,18,16,128]{3,2,1...) custom-call(f32[32,128]{1,0:T(8,128)S(1)} %bitcast.15, ...), custom_call_target="tpu_custom_call" | custom-call | flops 1698693120 | bytes 4194304 | tf_op jit(solution)/shard_map/pallas_call | solution.py:35
  45.1 8.8 %all_to_all.34 = f32[32,1,128]{2,1,0:T(1,128)S(1)} all-to-all(f32[32,1,128]{2,1,0:T(1,128)S(1)} %bitcast.19), channel_id=1, replica_groups=mesh['row'=8,'col'=4] {'row','col'}, dimensions={0} | all-to-all | bytes 32768 | tf_op jit(solution)/shard_map/all_to_all | solution.py:577
  53.9 3.1 %shard_map.109 = (f32[3,16,2048]{2,1,0:T(8,128)S(1)}, f32[3,16,2048]{2,1,0:T(8,128)S(1)}, f32[3,16,2048]{2,1,0:T(8,128)S(1)}, f32[3,16,2048]{2,1,0:T(8,128)S(1)}, f32[32,128]{1,0:T(8,128)S(1)}) custom-call(f32[32,128]{1,0:T(8,128)S(1)} %bitcast.14, f32[3]{0:T(128)S(1)} %copy-done.6, bf16[4,20,24,128]{3,2,1,0:T(8,128)(2,1)S(1)} %get-tuple-element.58.near_box, ...), custom_call_target="tpu_custom_call" | custom-call | flops 1698693120 | bytes 4194304 | tf_op jit(solution)/shard_map/pallas_call | solution.py:35
  57.0 8.8 %all_to_all.35 = f32[32,1,128]{2,1,0:T(1,128)S(1)} all-to-all(f32[32,1,128]{2,1,0:T(1,128)S(1)} %bitcast.18), channel_id=1, replica_groups=mesh['row'=8,'col'=4] {'row','col'}, dimensions={0} | all-to-all | bytes 32768 | tf_op jit(solution)/shard_map/all_to_all | solution.py:577
  65.8 2.1 %shard_map.110 = (f32[3,16,2048]{2,1,0:T(8,128)}, f32[3,16,2048]{2,1,0:T(8,128)}, f32[3]{0:T(128)}) custom-call(f32[32,128]{1,0:T(8,128)S(1)} %bitcast.16, f32[3]{0:T(128)S(1)} %copy-done.6, f32[3,16,2048]{2,1,0:T(8,128)S(1)} %get-tuple-element.74.duals, f32[3,16,2048]{2,1,0:T(8,128)S(1)} %get-tuple-element.75.multipliers, ...), custom_call_target="tpu_custom_call" | custom-call | flops 1048576 | bytes 4194304 | tf_op jit(solution)/shard_map/pallas_call | solution.py:35
  (15 shorter events, 0.1 us)
Async XLA Ops:
  0.6 24.3 %copy-start.1 = (bf16[3,16,2048]{2,1,0:T(8,128)(2,1)S(1)}, bf16[3,16,2048]{2,1,0:T(8,128)(2,1)}, u32[]{:S(2)}) copy-start(bf16[3,16,2048]{2,1,0:T(8,128)(2,1)} %upper.7) | copy-start | bytes 589828
  0.6 24.3 %copy-start = (bf16[3,16,2048]{2,1,0:T(8,128)(2,1)S(1)}, bf16[3,16,2048]{2,1,0:T(8,128)(2,1)}, u32[]{:S(2)}) copy-start(bf16[3,16,2048]{2,1,0:T(8,128)(2,1)} %lower.7) | copy-start | bytes 589828
  0.7 24.3 %copy-start.5 = (bf16[16,2048]{1,0:T(8,128)(2,1)S(1)}, bf16[16,2048]{1,0:T(8,128)(2,1)}, u32[]{:S(2)}) copy-start(bf16[16,2048]{1,0:T(8,128)(2,1)} %radius.5) | copy-start | bytes 196612
  0.7 24.3 %copy-start.4 = (bf16[16,2048]{1,0:T(8,128)(2,1)S(1)}, bf16[16,2048]{1,0:T(8,128)(2,1)}, u32[]{:S(2)}) copy-start(bf16[16,2048]{1,0:T(8,128)(2,1)} %center.5) | copy-start | bytes 196612
  0.7 24.3 %copy-start.2 = (f32[16,2048]{1,0:T(8,128)S(1)}, f32[16,2048]{1,0:T(8,128)}, u32[]{:S(2)}) copy-start(f32[16,2048]{1,0:T(8,128)} %objective.5) | copy-start | bytes 393220
  3.0 13.0 %collective-permute-start.2 = (f32[560,128]{1,0:T(8,128)}, f32[560,128]{1,0:T(8,128)S(1)}, u32[]{:S(2)}, u32[]{:S(2)}) collective-permute-start(f32[560,128]{1,0:T(8,128)} %get-tuple-element.44), channel_id=1, source_target_pairs={{4,8},{8,4},{12,16},{16,12},{20,24},{24,20},{5,9},{9,5},{13,17},{1... | collective-permute-start | bytes 860168 | tf_op jit(solution)/shard_map/ppermute | solution.py:201
  3.7 17.6 %collective-permute-start.3 = (f32[560,128]{1,0:T(8,128)}, f32[560,128]{1,0:T(8,128)S(1)}, u32[]{:S(2)}, u32[]{:S(2)}) collective-permute-start(f32[560,128]{1,0:T(8,128)} %get-tuple-element.45), channel_id=1, source_target_pairs={{0,4},{4,0},{8,12},{12,8},{16,20},{20,16},{24,28},{28,24},{1,5},{5... | collective-permute-start | bytes 860168 | tf_op jit(solution)/shard_map/ppermute | solution.py:201
  9.5 17.2 %collective-permute-start = (f32[144,384]{1,0:T(8,128)}, f32[144,384]{1,0:T(8,128)S(1)}, u32[]{:S(2)}, u32[]{:S(2)}) collective-permute-start(f32[144,384]{1,0:T(8,128)} %get-tuple-element.42), channel_id=1, source_target_pairs={{1,2},{2,1},{5,6},{6,5},{9,10},{10,9},{13,14},{14,13},{17,18},{18,... | collective-permute-start | bytes 663560 | tf_op jit(solution)/shard_map/ppermute | solution.py:201
  10.2 16.5 %collective-permute-start.1 = (f32[144,384]{1,0:T(8,128)}, f32[144,384]{1,0:T(8,128)S(1)}, u32[]{:S(2)}, u32[]{:S(2)}) collective-permute-start(f32[144,384]{1,0:T(8,128)} %get-tuple-element.43), channel_id=1, source_target_pairs={{0,1},{1,0},{2,3},{3,2},{4,5},{5,4},{6,7},{7,6},{8,9},{9,8},{10,11... | collective-permute-start | bytes 663560 | tf_op jit(solution)/shard_map/ppermute | solution.py:201
  13.1 1.3 %copy-start.3 = (f32[4,3,3,64,64]{4,3,2,1,0:T(8,128)S(1)}, f32[4,3,3,64,64]{4,3,2,1,0:T(8,128)}, u32[]{:S(2)}) copy-start(f32[4,3,3,64,64]{4,3,2,1,0:T(8,128)} %param.13) | copy-start | bytes 1769476
  14.4 0.7 %copy-start.7 = (f32[4,64]{1,0:T(4,128)S(1)}, f32[4,64]{1,0:T(4,128)}, u32[]{:S(2)}) copy-start(f32[4,64]{1,0:T(4,128)} %biases.1) | copy-start | bytes 3076
  21.3 5.3 %collective-permute-start.4 = (f32[210,128]{1,0:T(8,128)S(1)}, f32[210,128]{1,0:T(8,128)S(1)}, u32[]{:S(2)}, u32[]{:S(2)}) collective-permute-start(f32[210,128]{1,0:T(8,128)S(1)} %get-tuple-element.47), channel_id=1, source_target_pairs={{1,2},{2,1},{5,6},{6,5},{9,10},{10,9},{13,14},{14,13},{17,18},{18,... | collective-permute-start | bytes 322568 | tf_op jit(solution)/shard_map/ppermute | solution.py:201
  22.0 4.7 %collective-permute-start.5 = (f32[210,128]{1,0:T(8,128)S(1)}, f32[210,128]{1,0:T(8,128)S(1)}, u32[]{:S(2)}, u32[]{:S(2)}) collective-permute-start(f32[210,128]{1,0:T(8,128)S(1)} %get-tuple-element.48), channel_id=1, source_target_pairs={{0,1},{1,0},{2,3},{3,2},{4,5},{5,4},{6,7},{7,6},{8,9},{9,8},{10,11... | collective-permute-start | bytes 322568 | tf_op jit(solution)/shard_map/ppermute | solution.py:201
  26.7 14.5 %copy-start.6 = (f32[3]{0:T(128)S(1)}, f32[3]{0:T(128)}, u32[]{:S(2)}) copy-start(f32[3]{0:T(128)} %steps.5) | copy-start | bytes 40

commit v14 on v13

--- a/solution.py
+++ b/solution.py
@@ -22,6 +22,8 @@
 ROWS_SENT = (5, 5, 5, 4, 4, 4, 2, 3, 3)
 ROW_START = tuple(sum(ROWS_SENT[:m]) for m in range(9))
 SENT = sum(ROWS_SENT)
+OUTER = 3 * WIDE
+CORNER = (0, OUTER, OUTER + SENT, OUTER + 2 * SENT, OUTER + 3 * SENT, OUTER + 4 * SENT, 2 * OUTER + 4 * SENT)
 WINDOW = 4 * CH
 
 VMEM = pl.BlockSpec(memory_space=pltpu.VMEM)
@@ -29,9 +31,9 @@
 HBM = pl.BlockSpec(memory_space=pltpu.HBM)
 
 
-def call(body, outs, scratch, operands, flops, mem=20, scalars=(), far=(), scalar_outs=(), far_outs=()):
+def call(body, outs, scratch, operands, flops, mem=20, scalars=(), far=(), scalar_outs=()):
     specs = [SMEM if j in scalars else HBM if j in far else VMEM for j in range(len(operands))]
-    out_specs = tuple(SMEM if j in scalar_outs else HBM if j in far_outs else VMEM for j in range(len(outs)))
+    out_specs = tuple(SMEM if j in scalar_outs else VMEM for j in range(len(outs)))
     return pl.pallas_call(
         body,
         out_shape=outs,
@@ -111,29 +113,27 @@
     ]
 
 
-def ends_body(objective, center, radius, lower, upper, *rest):
+def ends_body(objective, center, radius, lower, upper, far_rows, near_rows, far_cols, near_cols, *rest):
     rows, cols = objective.shape
-    outs, held, made, sem = rest[:4], rest[4:9], rest[9:13], rest[13]
-    arrivals = copies(list(zip((objective, center, radius, lower, upper), held)), sem)
-    finish(arrivals)
+    held, sem = rest[:5], rest[5]
+    finish(copies(list(zip((objective, center, radius, lower, upper), held)), sem))
     strip = HALO_PAIRS * LANES
-    for q in range(cols // LANES):
-        values = [read(pl.ds(q * LANES, LANES)) for read in sources(*held)]
-        ends_of(values, made[0], made[1], q * SENT)
-    leaving = copies(list(zip(made[:2], outs[:2])), sem)
     for m, read in enumerate(sources(*held)):
         here = pl.ds(m * rows, rows)
         sorted_strips(
-            "col", read(pl.ds(0, strip)), read(pl.ds(cols - strip, strip)), made[2].at[here], made[3].at[here]
+            "col", read(pl.ds(0, strip)), read(pl.ds(cols - strip, strip)), far_cols.at[here], near_cols.at[here]
         )
-    finish(leaving + copies(list(zip(made[2:], outs[2:])), sem.at[2:4]))
+    for q in range(cols // LANES):
+        values = [read(pl.ds(q * LANES, LANES)) for read in sources(*held)]
+        ends_of(values, far_rows, near_rows, q * SENT)
 
 
 def ends_of(values, far, near, start):
     rows = values[0].shape[0]
     row = lax.broadcasted_iota(jnp.int32, (rows, LANES), 0)
     outer = (row >= 2) & (row < rows - 2)
-    values[3] = jnp.where(outer, values[3] - values[6], values[3])
+    if len(values) > 3:
+        values[3] = jnp.where(outer, values[3] - values[6], values[3])
     for m, value in enumerate(values):
         here = pl.ds(start + ROW_START[m], ROWS_SENT[m])
         sorted_strips("row", value[: ROWS_SENT[m]], value[rows - ROWS_SENT[m] :], far.at[here], near.at[here])
@@ -164,13 +164,14 @@
     return Side(axis, far, near, False), Side(axis, far, near, True)
 
 
-def corners_body(far_rows, near_rows, after, far, near):
-    del after
-    count = HALO_PAIRS * SENT
-    size = far_rows.shape[0]
-    for part, source in enumerate(sides("row", far_rows, near_rows)):
-        here = pl.ds(part * count, count)
-        sorted_strips("col", source[0:count, :], source[size - count : size, :], far.at[here], near.at[here])
+def corners_body(far_cols, near_cols, far, near):
+    rows = far_cols.shape[0] // 9
+    left, right = sides("col", far_cols, near_cols)
+    for j in range(2 * HALO_PAIRS):
+        strip, q = (left, j) if j < HALO_PAIRS else (right, j - HALO_PAIRS)
+        maps = 3 if j in (0, 2 * HALO_PAIRS - 1) else 9
+        values = [strip[pl.ds(m * rows, rows), pl.ds(q * LANES, LANES)] for m in range(maps)]
+        ends_of(values, far, near, CORNER[j])
 
 
 def column(reads, left, right, rows, pairs, m, q):
@@ -182,14 +183,12 @@
     return reads[m](pl.ds((q - HALO_PAIRS) * LANES, LANES))
 
 
-def halo(middle, left, right, part, pairs, q, m):
-    if q < HALO_PAIRS:
-        source, at = left, part * HALO_PAIRS + q
-    elif q >= HALO_PAIRS + pairs:
-        source, at = right, part * HALO_PAIRS + q - HALO_PAIRS - pairs
+def halo(middle, corner, pairs, q, m):
+    if HALO_PAIRS <= q < HALO_PAIRS + pairs:
+        source, start = middle, (q - HALO_PAIRS) * SENT
     else:
-        source, at = middle, q - HALO_PAIRS
-    return source[pl.ds(at * SENT + ROW_START[m], ROWS_SENT[m]), :]
+        source, start = corner, CORNER[q if q < HALO_PAIRS else q - pairs]
+    return source[pl.ds(start + ROW_START[m], ROWS_SENT[m]), :]
 
 
 def partners(far, near, axis):
@@ -309,9 +308,9 @@
                 if at:
                     dest[0:EDGE, :] = blank
                     dest[EDGE + rows : frame, :] = blank
-            dest[at : at + sent, :] = halo(above, *corners, 0, pairs, q, m)
+            dest[at : at + sent, :] = halo(above, corners[0], pairs, q, m)
             dest[edge : edge + rows, :] = column(reads, left, right, rows, pairs, m, q)
-            dest[edge + rows : edge + rows + sent, :] = halo(below, *corners, 1, pairs, q, m)
+            dest[edge + rows : edge + rows + sent, :] = halo(below, corners[1], pairs, q, m)
     count = len(slots)
     spare = raw.shape[2] - rows - 2 * WIDE
     raw[:, :, rows + 2 * WIDE :, :] = jnp.zeros((3, count, spare, LANES), F32)
@@ -386,7 +385,7 @@
     reads = sources(objective, center, radius, lower, upper)
     above, below = sides("row", far_rows, near_rows)
     left, right = sides("col", far_cols, near_cols)
-    corners = sides("col", far_corner, near_corner)
+    corners = sides("row", far_corner, near_corner)
     slots = list(range(5)) + list(range(wide - 3, wide + 2))
     assemble(reads, above, below, left, right, corners, slots, rows, pairs, raw, gaps, target)
     start_convs(raw, target, store, sums, fwd, bwd, frame)
@@ -555,22 +554,15 @@
     stats(stat, [folded(squares), start, middle + fixed, folded(worth) + own_rows(framed) + fixed])
 
 
-def last_body(
-    total, steps, duals, multipliers, slope, mult, duals_far, mult_far, bounds,
-    duals_out, mult_out, sem, *, cells,
-):
+def last_body(total, steps, duals, multipliers, slope, mult, duals_out, mult_out, bounds, *, cells):
     scale = scale_of(total, steps[2], cells, duals.shape[1:])
-    leaving = []
     for k in range(LAYERS - 1):
         duals_out[k] = duals[k] + scale * slope[k]
         mult_out[k] = multipliers[k] + scale * mult[k]
-        moves = [(duals_out.at[k], duals_far.at[k]), (mult_out.at[k], mult_far.at[k])]
-        leaving += copies(moves, sem.at[2 * k : 2 * k + 2])
     values = summed(total) / cells
     lane = lax.broadcasted_iota(jnp.int32, (1, LANES), 1)
     for j in range(ITERS):
         bounds[j] = jnp.sum(jnp.where(lane == j + 1, values, 0.0))
-    finish(leaving)
 
 
 def everyone(partial):
@@ -595,19 +587,18 @@
     far_rows, near_rows, far_cols, near_cols = call(
         ends_body,
         made,
-        [pltpu.VMEM(one.shape, one.dtype) for one in inputs + made] + [pltpu.SemaphoreType.DMA((5,))],
+        [pltpu.VMEM(one.shape, one.dtype) for one in inputs] + [pltpu.SemaphoreType.DMA((5,))],
         inputs,
         1 << 20,
         mem=58,
         far=range(5),
-        far_outs=range(4),
     )
     far_rows, near_rows = partners(far_rows, near_rows, "row")
     far_cols, near_cols = partners(far_cols, near_cols, "col")
     fwd, bwd, bias = weights(kernels, biases)
-    corner = shape(2 * HALO_PAIRS * SENT, LANES)
-    far_corner, near_corner = call(corners_body, (corner, corner), [], (far_rows, near_rows, bias), 1 << 20)
-    far_corner, near_corner = partners(far_corner, near_corner, "col")
+    corner = shape(CORNER[-1], LANES)
+    far_corner, near_corner = call(corners_body, (corner, corner), [], (far_cols, near_cols), 1 << 20)
+    far_corner, near_corner = partners(far_corner, near_corner, "row")
 
     def start_scratch(count):
         return [
@@ -686,11 +677,10 @@
     final_duals, final_multipliers, bounds = call(
         functools.partial(last_body, cells=cells),
         (out, out, shape(ITERS)),
-        [pltpu.VMEM(out.shape, F32), pltpu.VMEM(out.shape, F32), pltpu.SemaphoreType.DMA((6,))],
+        [],
         (total2, steps, duals, multipliers, slope2, mult2),
         1 << 20,
         scalar_outs=(2,),
-        far_outs=(0, 1),
         scalars=(1,),
     )
     return bounds, final_duals, final_multipliers

time: 68.2 us -> 65.4 us (0.959)
  waiting for transfers between devices: 5.33 us -> 2.3 us
  starting transfers between devices: 13.7 us -> 15.1 us
    ppermute x3, waiting for transfers between devices: 5.32 us -> 2.29 us  [partners(): lax.ppermute(near, axis, pairs(0))]
    ppermute x3, starting transfers between devices: 11.7 us -> 13.1 us  [partners(): lax.ppermute(near, axis, pairs(0))]
  transfers between devices with their start and end apart: 6 -> 6, of which waited for: 1 -> 2; matrix products, arithmetic and copies ran while one was open for 0% -> 0% of each run, Pallas kernels for 4% -> 4%
where the time goes in v14:
time: 65.4 us; the launch traced here: 65.1 us
  blocking collectives  30.5 us (47%)
  starting transfers between devices  15.1 us (23%)
  Pallas kernels  14.5 us (22%)
  waiting for transfers between devices  2.3 us (4%)
  local copies, waits for them, and re-layouts  1.98 us (3%)
  between operations  0.76 us (1%)
    all_to_all x3, blocking collectives, everyone(): return lax.all_to_all(partial, ('row', 'col'), 0, 0, tiled=True)  30.5 us
    pallas_call x8, Pallas kernels, call(): pl.pallas_call(body, out_shape=outs, in_specs=specs, out_specs=out_specs,...  14.5 us
    ppermute x3, starting transfers between devices, partners(): lax.ppermute(near, axis, pairs(0))  13.1 us
    ppermute x3, waiting for transfers between devices, partners(): lax.ppermute(near, axis, pairs(0))  2.29 us
    ppermute x3, starting transfers between devices, partners(): lax.ppermute(far, axis, pairs(1))  2.01 us
    unnamed x16, local copies, waits for them, and re-layouts  1.98 us
  transfers between devices with their start and end apart: 6, of which 2 were waited for; matrix products, arithmetic and copies ran while one was open for 0% of the time, Pallas kernels for 4%

profile of v14, /device:TPU:0, one launch (start us, length us, event | category | flops | bytes accessed | tf_op | source)
XLA Modules:
  0.0 65.1 jit_solution(2071778691946956007)
XLA Ops:
  0.7 2.3 %shard_map.103 = (f32[560,128]{1,0:T(8,128)}, f32[560,128]{1,0:T(8,128)}, f32[144,384]{1,0:T(8,128)}, f32[144,384]{1,0:T(8,128)}) custom-call(f32[16,2048]{1,0:T(8,128)} %objective.5, bf16[16,2048]{1,0:T(8,128)(2,1)} %center.5, bf16[16,2048]{1,0:T(8,128)(2,1)} %radius.5, bf16[3,16,2048]{2,1,0:T(8,128)(2,1)} %lower.7, bf16[3,16,2048]{2,1,0:T(8,128)(2,1)} %upper.7), custom_call_target="tpu_custom_call" | custom-call | flops 1048576 | bytes 4194304 | tf_op jit(solution)/shard_map/pallas_call | solution.py:37
  3.0 0.7 %collective-permute-start.2 = (f32[560,128]{1,0:T(8,128)}, f32[560,128]{1,0:T(8,128)S(1)}, u32[]{:S(2)}, u32[]{:S(2)}) collective-permute-start(f32[560,128]{1,0:T(8,128)} %get-tuple-element.44), channel_id=1, source_target_pairs={{4,8},{8,4},{12,16},{16,12},{20,24},{24,20},{5,9},{9,5},{13,17},{1... | collective-permute-start | bytes 860168 | tf_op jit(solution)/shard_map/ppermute | solution.py:200
  3.7 5.8 %collective-permute-start.3 = (f32[560,128]{1,0:T(8,128)}, f32[560,128]{1,0:T(8,128)S(1)}, u32[]{:S(2)}, u32[]{:S(2)}) collective-permute-start(f32[560,128]{1,0:T(8,128)} %get-tuple-element.45), channel_id=1, source_target_pairs={{0,4},{4,0},{8,12},{12,8},{16,20},{20,16},{24,28},{28,24},{1,5},{5... | collective-permute-start | bytes 860168 | tf_op jit(solution)/shard_map/ppermute | solution.py:200
  9.5 0.7 %collective-permute-start = (f32[144,384]{1,0:T(8,128)}, f32[144,384]{1,0:T(8,128)S(1)}, u32[]{:S(2)}, u32[]{:S(2)}) collective-permute-start(f32[144,384]{1,0:T(8,128)} %get-tuple-element.42), channel_id=1, source_target_pairs={{1,2},{2,1},{5,6},{6,5},{9,10},{10,9},{13,14},{14,13},{17,18},{18,... | collective-permute-start | bytes 663560 | tf_op jit(solution)/shard_map/ppermute | solution.py:200
  10.2 2.9 %collective-permute-start.1 = (f32[144,384]{1,0:T(8,128)}, f32[144,384]{1,0:T(8,128)S(1)}, u32[]{:S(2)}, u32[]{:S(2)}) collective-permute-start(f32[144,384]{1,0:T(8,128)} %get-tuple-element.43), channel_id=1, source_target_pairs={{0,1},{1,0},{2,3},{3,2},{4,5},{5,4},{6,7},{7,6},{8,9},{9,8},{10,11... | collective-permute-start | bytes 663560 | tf_op jit(solution)/shard_map/ppermute | solution.py:200
  13.1 0.0 collective-permute-done.far_cols
  13.1 1.3 %collective-permute-done.1.near_cols = f32[144,384]{1,0:T(8,128)S(1)} collective-permute-done((f32[144,384]{1,0:T(8,128)}, f32[144,384]{1,0:T(8,128)S(1)}, u32[]{:S(2)}, u32[]{:S(2)}) %collective-permute-start.1) | collective-permute-done | bytes 221216 | tf_op jit(solution)/shard_map/ppermute | solution.py:200
  14.4 0.1 shard_map.104
  14.5 0.7 %collective-permute-start.4 = (f32[170,128]{1,0:T(8,128)S(1)}, f32[170,128]{1,0:T(8,128)S(1)}, u32[]{:S(2)}, u32[]{:S(2)}) collective-permute-start(f32[170,128]{1,0:T(8,128)S(1)} %get-tuple-element.46), channel_id=1, source_target_pairs={{4,8},{8,4},{12,16},{16,12},{20,24},{24,20},{5,9},{9,5},{13,17},{1... | collective-permute-start | bytes 261128 | tf_op jit(solution)/shard_map/ppermute | solution.py:200
  15.2 4.3 %collective-permute-start.5 = (f32[170,128]{1,0:T(8,128)S(1)}, f32[170,128]{1,0:T(8,128)S(1)}, u32[]{:S(2)}, u32[]{:S(2)}) collective-permute-start(f32[170,128]{1,0:T(8,128)S(1)} %get-tuple-element.47), channel_id=1, source_target_pairs={{0,4},{4,0},{8,12},{12,8},{16,20},{20,16},{24,28},{28,24},{1,5},{5... | collective-permute-start | bytes 261128 | tf_op jit(solution)/shard_map/ppermute | solution.py:200
  19.5 1.3 %copy-done.2 = f32[4,3,3,64,64]{4,3,2,1,0:T(8,128)S(1)} copy-done((f32[4,3,3,64,64]{4,3,2,1,0:T(8,128)S(1)}, f32[4,3,3,64,64]{4,3,2,1,0:T(8,128)}, u32[]{:S(2)}) %copy-start.2) | copy-done | bytes 589848
  20.8 0.7 %copy-done.7 = f32[4,64]{1,0:T(4,128)S(1)} copy-done((f32[4,64]{1,0:T(4,128)S(1)}, f32[4,64]{1,0:T(4,128)}, u32[]{:S(2)}) %copy-start.7) | copy-done | bytes 1048
  21.5 0.9 %shard_map.105 = (bf16[3,768,384]{2,1,0:T(8,128)(2,1)S(1)}, bf16[4,768,384]{2,1,0:T(8,128)(2,1)S(1)}, f32[8,128]{1,0:T(8,128)S(1)}) custom-call(f32[36,64,64]{2,1,0:T(8,128)S(1)} %bitcast.13, f32[4,64]{1,0:T(4,128)S(1)} %copy-done.7), custom_call_target="tpu_custom_call" | custom-call | flops 4194304 | bytes 4194304 | tf_op jit(solution)/shard_map/pallas_call | solution.py:37
  22.4 0.9 %collective-permute-done.3.near_rows = f32[560,128]{1,0:T(8,128)S(1)} collective-permute-done((f32[560,128]{1,0:T(8,128)}, f32[560,128]{1,0:T(8,128)S(1)}, u32[]{:S(2)}, u32[]{:S(2)}) %collective-permute-start.3) | collective-permute-done | bytes 286752 | tf_op jit(solution)/shard_map/ppermute | solution.py:200
  23.4 1.7 %shard_map.106 = (bf16[4,14,24,128]{3,2,1,0:T(8,128)(2,1)S(1)}, bf16[4,14,24,128]{3,2,1,0:T(8,128)(2,1)S(1)}, f32[14,24,128]{2,1,0:T(8,128)S(1)}, f32[3,14,24,12...) custom-call(f32[16,2048]{1,0:T(8,128)S(1)} %copy-done.3, bf16[16,2048]{1,0:T(8,128)(2,1)S(1)} %copy-done.4, ...), custom_call_target="tpu_custom_call" | custom-call | flops 849346560 | bytes 4194304 | tf_op jit(solution)/shard_map/pallas_call | solution.py:37
  25.0 0.0 collective-permute-done.4.far_corner
  25.0 0.0 collective-permute-done.5.near_corner
  25.1 1.0 %shard_map.107 = (bf16[4,20,24,128]{3,2,1,0:T(8,128)(2,1)S(1)}, bf16[4,20,24,128]{3,2,1,0:T(8,128)(2,1)S(1)}, f32[20,24,128]{2,1,0:T(8,128)S(1)}, f32[3,20,24,12...) custom-call(f32[16,2048]{1,0:T(8,128)S(1)} %copy-done.3, ...), custom_call_target="tpu_custom_call" | custom-call | flops 849346560 | bytes 4194304 | tf_op jit(solution)/shard_map/pallas_call | solution.py:37
  26.1 12.9 %all_to_all.33 = f32[32,1,128]{2,1,0:T(1,128)S(1)} all-to-all(f32[32,1,128]{2,1,0:T(1,128)S(1)} %bitcast.17), channel_id=1, replica_groups=mesh['row'=8,'col'=4] {'row','col'}, dimensions={0} | all-to-all | bytes 32768 | tf_op jit(solution)/shard_map/all_to_all | solution.py:569
  39.0 3.8 %shard_map.108 = (f32[3,20,24,128]{3,2,1,0:T(8,128)S(1)}, f32[3,18,24,128]{3,2,1,0:T(8,128)S(1)}, f32[2,18,24,128]{3,2,1,0:T(8,128)S(1)}, f32[3,18,16,128]{3,2,1...) custom-call(f32[32,128]{1,0:T(8,128)S(1)} %bitcast.15, ...), custom_call_target="tpu_custom_call" | custom-call | flops 1698693120 | bytes 4194304 | tf_op jit(solution)/shard_map/pallas_call | solution.py:37
  42.8 8.8 %all_to_all.34 = f32[32,1,128]{2,1,0:T(1,128)S(1)} all-to-all(f32[32,1,128]{2,1,0:T(1,128)S(1)} %bitcast.19), channel_id=1, replica_groups=mesh['row'=8,'col'=4] {'row','col'}, dimensions={0} | all-to-all | bytes 32768 | tf_op jit(solution)/shard_map/all_to_all | solution.py:569
  51.7 3.1 %shard_map.109 = (f32[3,16,2048]{2,1,0:T(8,128)S(1)}, f32[3,16,2048]{2,1,0:T(8,128)S(1)}, f32[3,16,2048]{2,1,0:T(8,128)S(1)}, f32[3,16,2048]{2,1,0:T(8,128)S(1)}, f32[32,128]{1,0:T(8,128)S(1)}) custom-call(f32[32,128]{1,0:T(8,128)S(1)} %bitcast.14, f32[3]{0:T(128)S(1)} %copy-done.6, bf16[4,20,24,128]{3,2,1,0:T(8,128)(2,1)S(1)} %get-tuple-element.58.near_box, ...), custom_call_target="tpu_custom_call" | custom-call | flops 1698693120 | bytes 4194304 | tf_op jit(solution)/shard_map/pallas_call | solution.py:37
  54.7 8.8 %all_to_all.35 = f32[32,1,128]{2,1,0:T(1,128)S(1)} all-to-all(f32[32,1,128]{2,1,0:T(1,128)S(1)} %bitcast.18), channel_id=1, replica_groups=mesh['row'=8,'col'=4] {'row','col'}, dimensions={0} | all-to-all | bytes 32768 | tf_op jit(solution)/shard_map/all_to_all | solution.py:569
  63.5 1.6 %shard_map.110 = (f32[3,16,2048]{2,1,0:T(8,128)}, f32[3,16,2048]{2,1,0:T(8,128)}, f32[3]{0:T(128)}) custom-call(f32[32,128]{1,0:T(8,128)S(1)} %bitcast.16, f32[3]{0:T(128)S(1)} %copy-done.6, f32[3,16,2048]{2,1,0:T(8,128)S(1)} %get-tuple-element.74.duals, f32[3,16,2048]{2,1,0:T(8,128)S(1)} %get-tuple-element.75.multipliers, ...), custom_call_target="tpu_custom_call" | custom-call | flops 1048576 | bytes 4194304 | tf_op jit(solution)/shard_map/pallas_call | solution.py:37
  (15 shorter events, 0.0 us)
Async XLA Ops:
  0.6 22.7 %copy-start.1 = (bf16[3,16,2048]{2,1,0:T(8,128)(2,1)S(1)}, bf16[3,16,2048]{2,1,0:T(8,128)(2,1)}, u32[]{:S(2)}) copy-start(bf16[3,16,2048]{2,1,0:T(8,128)(2,1)} %upper.7) | copy-start | bytes 589828
  0.6 22.7 %copy-start = (bf16[3,16,2048]{2,1,0:T(8,128)(2,1)S(1)}, bf16[3,16,2048]{2,1,0:T(8,128)(2,1)}, u32[]{:S(2)}) copy-start(bf16[3,16,2048]{2,1,0:T(8,128)(2,1)} %lower.7) | copy-start | bytes 589828
  0.7 22.7 %copy-start.5 = (bf16[16,2048]{1,0:T(8,128)(2,1)S(1)}, bf16[16,2048]{1,0:T(8,128)(2,1)}, u32[]{:S(2)}) copy-start(bf16[16,2048]{1,0:T(8,128)(2,1)} %radius.5) | copy-start | bytes 196612
  0.7 22.7 %copy-start.4 = (bf16[16,2048]{1,0:T(8,128)(2,1)S(1)}, bf16[16,2048]{1,0:T(8,128)(2,1)}, u32[]{:S(2)}) copy-start(bf16[16,2048]{1,0:T(8,128)(2,1)} %center.5) | copy-start | bytes 196612
  0.7 22.7 %copy-start.3 = (f32[16,2048]{1,0:T(8,128)S(1)}, f32[16,2048]{1,0:T(8,128)}, u32[]{:S(2)}) copy-start(f32[16,2048]{1,0:T(8,128)} %objective.5) | copy-start | bytes 393220
  3.0 19.4 %collective-permute-start.2 = (f32[560,128]{1,0:T(8,128)}, f32[560,128]{1,0:T(8,128)S(1)}, u32[]{:S(2)}, u32[]{:S(2)}) collective-permute-start(f32[560,128]{1,0:T(8,128)} %get-tuple-element.44), channel_id=1, source_target_pairs={{4,8},{8,4},{12,16},{16,12},{20,24},{24,20},{5,9},{9,5},{13,17},{1... | collective-permute-start | bytes 860168 | tf_op jit(solution)/shard_map/ppermute | solution.py:200
  3.7 19.6 %collective-permute-start.3 = (f32[560,128]{1,0:T(8,128)}, f32[560,128]{1,0:T(8,128)S(1)}, u32[]{:S(2)}, u32[]{:S(2)}) collective-permute-start(f32[560,128]{1,0:T(8,128)} %get-tuple-element.45), channel_id=1, source_target_pairs={{0,4},{4,0},{8,12},{12,8},{16,20},{20,16},{24,28},{28,24},{1,5},{5... | collective-permute-start | bytes 860168 | tf_op jit(solution)/shard_map/ppermute | solution.py:200
  9.5 3.6 %collective-permute-start = (f32[144,384]{1,0:T(8,128)}, f32[144,384]{1,0:T(8,128)S(1)}, u32[]{:S(2)}, u32[]{:S(2)}) collective-permute-start(f32[144,384]{1,0:T(8,128)} %get-tuple-element.42), channel_id=1, source_target_pairs={{1,2},{2,1},{5,6},{6,5},{9,10},{10,9},{13,14},{14,13},{17,18},{18,... | collective-permute-start | bytes 663560 | tf_op jit(solution)/shard_map/ppermute | solution.py:200
  10.2 4.2 %collective-permute-start.1 = (f32[144,384]{1,0:T(8,128)}, f32[144,384]{1,0:T(8,128)S(1)}, u32[]{:S(2)}, u32[]{:S(2)}) collective-permute-start(f32[144,384]{1,0:T(8,128)} %get-tuple-element.43), channel_id=1, source_target_pairs={{0,1},{1,0},{2,3},{3,2},{4,5},{5,4},{6,7},{7,6},{8,9},{9,8},{10,11... | collective-permute-start | bytes 663560 | tf_op jit(solution)/shard_map/ppermute | solution.py:200
  14.5 10.5 %collective-permute-start.4 = (f32[170,128]{1,0:T(8,128)S(1)}, f32[170,128]{1,0:T(8,128)S(1)}, u32[]{:S(2)}, u32[]{:S(2)}) collective-permute-start(f32[170,128]{1,0:T(8,128)S(1)} %get-tuple-element.46), channel_id=1, source_target_pairs={{4,8},{8,4},{12,16},{16,12},{20,24},{24,20},{5,9},{9,5},{13,17},{1... | collective-permute-start | bytes 261128 | tf_op jit(solution)/shard_map/ppermute | solution.py:200
  15.2 9.9 %collective-permute-start.5 = (f32[170,128]{1,0:T(8,128)S(1)}, f32[170,128]{1,0:T(8,128)S(1)}, u32[]{:S(2)}, u32[]{:S(2)}) collective-permute-start(f32[170,128]{1,0:T(8,128)S(1)} %get-tuple-element.47), channel_id=1, source_target_pairs={{0,4},{4,0},{8,12},{12,8},{16,20},{20,16},{24,28},{28,24},{1,5},{5... | collective-permute-start | bytes 261128 | tf_op jit(solution)/shard_map/ppermute | solution.py:200
  19.5 1.3 %copy-start.2 = (f32[4,3,3,64,64]{4,3,2,1,0:T(8,128)S(1)}, f32[4,3,3,64,64]{4,3,2,1,0:T(8,128)}, u32[]{:S(2)}) copy-start(f32[4,3,3,64,64]{4,3,2,1,0:T(8,128)} %param.13) | copy-start | bytes 1769476
  20.8 0.7 %copy-start.7 = (f32[4,64]{1,0:T(4,128)S(1)}, f32[4,64]{1,0:T(4,128)}, u32[]{:S(2)}) copy-start(f32[4,64]{1,0:T(4,128)} %biases.1) | copy-start | bytes 3076
  25.1 13.9 %copy-start.6 = (f32[3]{0:T(128)S(1)}, f32[3]{0:T(128)}, u32[]{:S(2)}) copy-start(f32[3]{0:T(128)} %steps.5) | copy-start | bytes 40

commit v15 on v14

--- a/solution.py
+++ b/solution.py
@@ -113,16 +113,27 @@
     ]
 
 
+def pairs_of(m):
+    return HALO_PAIRS if m < 3 else HALO_PAIRS - 1
+
+
+def block_of(m, j):
+    return sum(pairs_of(n) for n in range(m)) + j
+
+
+BLOCKS = block_of(9, 0)
+
+
 def ends_body(objective, center, radius, lower, upper, far_rows, near_rows, far_cols, near_cols, *rest):
     rows, cols = objective.shape
     held, sem = rest[:5], rest[5]
     finish(copies(list(zip((objective, center, radius, lower, upper), held)), sem))
-    strip = HALO_PAIRS * LANES
     for m, read in enumerate(sources(*held)):
-        here = pl.ds(m * rows, rows)
-        sorted_strips(
-            "col", read(pl.ds(0, strip)), read(pl.ds(cols - strip, strip)), far_cols.at[here], near_cols.at[here]
-        )
+        for j in range(pairs_of(m)):
+            here = pl.ds(block_of(m, j) * rows, rows)
+            first = read(pl.ds(j * LANES, LANES))
+            last = read(pl.ds(cols - (pairs_of(m) - j) * LANES, LANES))
+            sorted_strips("col", first, last, far_cols.at[here], near_cols.at[here])
     for q in range(cols // LANES):
         values = [read(pl.ds(q * LANES, LANES)) for read in sources(*held)]
         ends_of(values, far_rows, near_rows, q * SENT)
@@ -164,22 +175,23 @@
     return Side(axis, far, near, False), Side(axis, far, near, True)
 
 
-def corners_body(far_cols, near_cols, far, near):
-    rows = far_cols.shape[0] // 9
+def corners_body(far_cols, near_cols, after, far, near):
+    del after
+    rows = far_cols.shape[0] // BLOCKS
     left, right = sides("col", far_cols, near_cols)
     for j in range(2 * HALO_PAIRS):
-        strip, q = (left, j) if j < HALO_PAIRS else (right, j - HALO_PAIRS)
         maps = 3 if j in (0, 2 * HALO_PAIRS - 1) else 9
-        values = [strip[pl.ds(m * rows, rows), pl.ds(q * LANES, LANES)] for m in range(maps)]
+        values = [column(None, left, right, rows, 0, m, j) for m in range(maps)]
         ends_of(values, far, near, CORNER[j])
 
 
 def column(reads, left, right, rows, pairs, m, q):
     if q < HALO_PAIRS:
-        return left[m * rows : (m + 1) * rows, q * LANES : (q + 1) * LANES]
+        at = block_of(m, q - HALO_PAIRS + pairs_of(m)) * rows
+        return left[at : at + rows, :]
     if q >= HALO_PAIRS + pairs:
-        q -= HALO_PAIRS + pairs
-        return right[m * rows : (m + 1) * rows, q * LANES : (q + 1) * LANES]
+        at = block_of(m, q - HALO_PAIRS - pairs) * rows
+        return right[at : at + rows, :]
     return reads[m](pl.ds((q - HALO_PAIRS) * LANES, LANES))
 
 
@@ -209,13 +221,12 @@
     early = lax.broadcasted_iota(jnp.int32, (rows, LANES), 1) < CH
     zero = jnp.zeros((rows, LANES), F32)
 
-    def step(q, carry):
+    last = (zero,) * maps
+    for q in range(count):
         fresh = [pltpu.roll(value, CH, 1) for value in produce(q)]
         for k in range(maps):
-            store[k, q] = jnp.where(early, carry[k], fresh[k])
-        return tuple(fresh)
-
-    last = lax.fori_loop(0, count, step, (zero,) * maps, unroll=True)
+            store[k, q] = jnp.where(early, last[k], fresh[k])
+        last = fresh
     for k in range(maps):
         store[k, count] = jnp.where(early, last[k], zero)
 
@@ -258,16 +269,22 @@
 
 
 class Bound:
-    def __init__(self, start):
+    def __init__(self, start, counted=True):
         self.linear = start
         self.factor = None
+        self.counted = counted
 
     def add(self, t):
         bend = jnp.tanh(t)
-        self.linear = self.linear + (jnp.minimum(t, 0.0) - 0.5 * math.log(2.0))
-        factor = 1.0 + jnp.abs(bend)
-        self.factor = factor if self.factor is None else self.factor * factor
+        if self.counted:
+            self.linear = self.linear + (jnp.minimum(t, 0.0) - 0.5 * math.log(2.0))
+            factor = 1.0 + jnp.abs(bend)
+            self.factor = factor if self.factor is None else self.factor * factor
         return bend
+
+    def less(self, term):
+        if self.counted:
+            self.linear = self.linear - term
 
     def total(self):
         return self.linear + 0.5 * jnp.log(self.factor)
@@ -422,7 +439,7 @@
         center, radius = near_box[0, q].astype(F32), near_box[3, q].astype(F32)
         g = -(scale * gathered(sums, 0, q))
         base[0, q] = g
-        bound = Bound(g * (center - radius))
+        bound = Bound(g * (center - radius), 2 <= q < wide - 2)
         outs = [center - radius * bound.add(2.0 * radius * g)]
         for k in (1, 2):
             gap = near_box[k, q].astype(F32)
@@ -431,18 +448,20 @@
             x = soft(gap, bound.add(g * gap))
             points[k - 1, q] = x
             outs.append(x)
-        worths[q] = bound.total()
+        if bound.counted:
+            worths[q] = bound.total()
         return outs
 
     slide(3, wide, store, produce)
     for k in range(3):
         multiply(store, k, 1, wide - 2, fwd, k, sums)
 
-    def step(j, carry):
-        squares, worth = carry
+    squares = worth = zero
+    for j in range(wide - 2):
         q = j + 1
+        own = 2 <= q < wide - 2
         new = zero
-        bound = Bound(worths[q])
+        bound = Bound(worths[q] if own else None, own)
         for k in range(3):
             gap = (near_box[1 + k, q] if k < 2 else far_box[0, q]).astype(F32)
             low = far_box[1 + k, q].astype(F32)
@@ -457,7 +476,7 @@
                 tp = (lam - mu) * gap
             positive = soft(gap, bound.add(tp))
             negative = soft(low, bound.add(-lam * low))
-            bound.linear = bound.linear - lam * bias[k : k + 1, :]
+            bound.less(lam * bias[k : k + 1, :])
             dl = positive - negative - gathered(sums, k, j) - bias[k : k + 1, :]
             dl = jnp.where(gap > 0.0, dl, 0.0)
             dm = x - positive
@@ -470,10 +489,9 @@
                 last_slope[j] = dm[inside]
                 last_pull[j] = g[inside]
             new = new + dl * dl + dm * dm
-        own = (q >= 2) & (q < wide - 2)
-        return squares + jnp.where(own, new, 0.0), worth + jnp.where(own, bound.total(), 0.0)
-
-    squares, worth = lax.fori_loop(0, wide - 2, step, (zero, zero), unroll=True)
+        if own:
+            squares = squares + new
+            worth = worth + bound.total()
     stats(stat, [own_rows(squares)])
     stats(value, [own_rows(worth)])
 
@@ -494,11 +512,14 @@
         multiply(store, k, 0, wide - 2, bwd, k, sums)
     early = lax.broadcasted_iota(jnp.int32, (frame, LANES), 1) < CH
 
-    def point(j, carry):
+    framed = zero
+    before = (zero,) * 3
+    for j in range(wide - 2):
         q = j + 1
+        own = 2 <= q < wide - 2
         center, radius = near_box[0, q].astype(F32), near_box[3, q].astype(F32)
         g = base[0, q] - scale * gathered(sums, 0, j)
-        bound = Bound(g * (center - radius))
+        bound = Bound(g * (center - radius), own)
         outs = [center - radius * bound.add(2.0 * radius * g)]
         for k in (1, 2):
             gap = near_box[k, q].astype(F32)
@@ -506,28 +527,28 @@
             x = soft(gap, bound.add(t))
             points[k - 1, j] = x
             outs.append(x)
-        own = (q >= 2) & (q < wide - 2)
         fresh = [pltpu.roll(value, CH, 1) for value in outs]
         for k in range(3):
-            store[k, j] = jnp.where(early, carry[k], fresh[k])
-        return tuple(fresh) + (carry[3] + jnp.where(own, bound.total(), 0.0),)
-
-    framed = lax.fori_loop(0, wide - 2, point, (zero,) * 4, unroll=True)[3]
+            store[k, j] = jnp.where(early, before[k], fresh[k])
+        before = fresh
+        if own:
+            framed = framed + bound.total()
+
     for k in range(3):
         multiply(store, k, 1, wide - 4, fwd, k, sums)
 
     scale = scale[:rows]
 
-    def step(i, carry):
-        squares, worth = carry
+    squares = worth = jnp.zeros((rows, LANES), F32)
+    for i in range(wide - 4):
         j = i + 1
-        here = pl.ds(pl.multiple_of(i * LANES, LANES), LANES)
+        here = pl.ds(i * LANES, LANES)
         bound = Bound(jnp.zeros((rows, LANES), F32))
         for k in range(3):
             gap = upper[k, :, here].astype(F32)
             low = lower[k, :, here].astype(F32)
             lam = duals1[k, j] + scale * slope[k, j, inside, :]
-            bound.linear = bound.linear - lam * bias[k : k + 1, :]
+            bound.less(lam * bias[k : k + 1, :])
             if k < 2:
                 x = points[k, j, inside, :]
                 mu = scale * mult[k, j, inside, :]
@@ -544,10 +565,8 @@
             slope_out[k, :, here] = dl
             mult_out[k, :, here] = dm
             squares = squares + dl * dl + dm * dm
-        return squares, worth + bound.total()
-
-    zero = jnp.zeros((rows, LANES), F32)
-    squares, worth = lax.fori_loop(0, wide - 4, step, (zero, zero), unroll=True)
+        worth = worth + bound.total()
+
     lane = lax.broadcasted_iota(jnp.int32, (1, LANES), 1)
     start, fixed = (jnp.where(lane == j, value0[0:1, :], 0.0) for j in range(2))
     middle = jnp.where(lane == 0, value1[0:1, :], 0.0)
@@ -582,7 +601,7 @@
     small = shape(8, LANES)
 
     ends = shape(pairs * SENT, LANES)
-    strip = shape(9 * rows, HALO_PAIRS * LANES)
+    strip = shape(BLOCKS * rows, LANES)
     made = (ends, ends, strip, strip)
     far_rows, near_rows, far_cols, near_cols = call(
         ends_body,
@@ -597,7 +616,7 @@
     far_cols, near_cols = partners(far_cols, near_cols, "col")
     fwd, bwd, bias = weights(kernels, biases)
     corner = shape(CORNER[-1], LANES)
-    far_corner, near_corner = call(corners_body, (corner, corner), [], (far_cols, near_cols), 1 << 20)
+    far_corner, near_corner = call(corners_body, (corner, corner), [], (far_cols, near_cols, bias), 1 << 20)
     far_corner, near_corner = partners(far_corner, near_corner, "row")
 
     def start_scratch(count):

time: 65.4 us -> 65.4 us (level)
  transfers between devices with their start and end apart: 6 -> 6, of which waited for: 2 -> 1; matrix products, arithmetic and copies ran while one was open for 0% -> 0% of each run, Pallas kernels for 4% -> 4%
where the time goes in v15:
time: 65.4 us; the launch traced here: 65.1 us
  blocking collectives  30.5 us (47%)
  starting transfers between devices  15.1 us (23%)
  Pallas kernels  14.5 us (22%)
  waiting for transfers between devices  2.28 us (3%)
  local copies, waits for them, and re-layouts  1.98 us (3%)
  between operations  0.78 us (1%)
    all_to_all x3, blocking collectives, everyone(): return lax.all_to_all(partial, ('row', 'col'), 0, 0, tiled=True)  30.5 us
    pallas_call x8, Pallas kernels, call(): pl.pallas_call(body, out_shape=outs, in_specs=specs, out_specs=out_specs,...  14.5 us
    ppermute x3, starting transfers between devices, partners(): lax.ppermute(near, axis, pairs(0))  13.1 us
    ppermute x3, waiting for transfers between devices, partners(): lax.ppermute(near, axis, pairs(0))  2.28 us
    ppermute x3, starting transfers between devices, partners(): lax.ppermute(far, axis, pairs(1))  2 us
    unnamed x16, local copies, waits for them, and re-layouts  1.98 us
  transfers between devices with their start and end apart: 6, of which 1 were waited for; matrix products, arithmetic and copies ran while one was open for 0% of the time, Pallas kernels for 4%

profile of v15, /device:TPU:0, one launch (start us, length us, event | category | flops | bytes accessed | tf_op | source)
XLA Modules:
  0.0 65.1 jit_solution(15154329023337632913)
XLA Ops:
  0.7 2.3 %shard_map.103 = (f32[560,128]{1,0:T(8,128)}, f32[560,128]{1,0:T(8,128)}, f32[336,128]{1,0:T(8,128)}, f32[336,128]{1,0:T(8,128)}) custom-call(f32[16,2048]{1,0:T(8,128)} %objective.5, bf16[16,2048]{1,0:T(8,128)(2,1)} %center.5, bf16[16,2048]{1,0:T(8,128)(2,1)} %radius.5, bf16[3,16,2048]{2,1,0:T(8,128)(2,1)} %lower.7, bf16[3,16,2048]{2,1,0:T(8,128)(2,1)} %upper.7), custom_call_target="tpu_custom_call" | custom-call | flops 1048576 | bytes 4194304 | tf_op jit(solution)/shard_map/pallas_call | solution.py:37
  3.0 0.7 %collective-permute-start.2 = (f32[560,128]{1,0:T(8,128)}, f32[560,128]{1,0:T(8,128)S(1)}, u32[]{:S(2)}, u32[]{:S(2)}) collective-permute-start(f32[560,128]{1,0:T(8,128)} %get-tuple-element.44), channel_id=1, source_target_pairs={{4,8},{8,4},{12,16},{16,12},{20,24},{24,20},{5,9},{9,5},{13,17},{1... | collective-permute-start | bytes 860168 | tf_op jit(solution)/shard_map/ppermute | solution.py:212
  3.7 5.8 %collective-permute-start.3 = (f32[560,128]{1,0:T(8,128)}, f32[560,128]{1,0:T(8,128)S(1)}, u32[]{:S(2)}, u32[]{:S(2)}) collective-permute-start(f32[560,128]{1,0:T(8,128)} %get-tuple-element.45), channel_id=1, source_target_pairs={{0,4},{4,0},{8,12},{12,8},{16,20},{20,16},{24,28},{28,24},{1,5},{5... | collective-permute-start | bytes 860168 | tf_op jit(solution)/shard_map/ppermute | solution.py:212
  9.5 0.7 %collective-permute-start = (f32[336,128]{1,0:T(8,128)}, f32[336,128]{1,0:T(8,128)S(1)}, u32[]{:S(2)}, u32[]{:S(2)}) collective-permute-start(f32[336,128]{1,0:T(8,128)} %get-tuple-element.42), channel_id=1, source_target_pairs={{1,2},{2,1},{5,6},{6,5},{9,10},{10,9},{13,14},{14,13},{17,18},{18,... | collective-permute-start | bytes 516104 | tf_op jit(solution)/shard_map/ppermute | solution.py:212
  10.1 2.9 %collective-permute-start.1 = (f32[336,128]{1,0:T(8,128)}, f32[336,128]{1,0:T(8,128)S(1)}, u32[]{:S(2)}, u32[]{:S(2)}) collective-permute-start(f32[336,128]{1,0:T(8,128)} %get-tuple-element.43), channel_id=1, source_target_pairs={{0,1},{1,0},{2,3},{3,2},{4,5},{5,4},{6,7},{7,6},{8,9},{9,8},{10,11... | collective-permute-start | bytes 516104 | tf_op jit(solution)/shard_map/ppermute | solution.py:212
  13.1 1.3 %copy-done.3 = f32[4,3,3,64,64]{4,3,2,1,0:T(8,128)S(1)} copy-done((f32[4,3,3,64,64]{4,3,2,1,0:T(8,128)S(1)}, f32[4,3,3,64,64]{4,3,2,1,0:T(8,128)}, u32[]{:S(2)}) %copy-start.3) | copy-done | bytes 589848
  14.3 0.7 %copy-done.7 = f32[4,64]{1,0:T(4,128)S(1)} copy-done((f32[4,64]{1,0:T(4,128)S(1)}, f32[4,64]{1,0:T(4,128)}, u32[]{:S(2)}) %copy-start.7) | copy-done | bytes 1048
  15.0 0.9 %shard_map.104 = (bf16[3,768,384]{2,1,0:T(8,128)(2,1)S(1)}, bf16[4,768,384]{2,1,0:T(8,128)(2,1)S(1)}, f32[8,128]{1,0:T(8,128)S(1)}) custom-call(f32[36,64,64]{2,1,0:T(8,128)S(1)} %bitcast.13, f32[4,64]{1,0:T(4,128)S(1)} %copy-done.7), custom_call_target="tpu_custom_call" | custom-call | flops 4194304 | bytes 4194304 | tf_op jit(solution)/shard_map/pallas_call | solution.py:37
  16.0 0.0 collective-permute-done.far_cols
  16.0 0.0 collective-permute-done.1.near_cols
  16.0 0.1 shard_map.105
  16.0 0.7 %collective-permute-start.4 = (f32[170,128]{1,0:T(8,128)S(1)}, f32[170,128]{1,0:T(8,128)S(1)}, u32[]{:S(2)}, u32[]{:S(2)}) collective-permute-start(f32[170,128]{1,0:T(8,128)S(1)} %get-tuple-element.47), channel_id=1, source_target_pairs={{4,8},{8,4},{12,16},{16,12},{20,24},{24,20},{5,9},{9,5},{13,17},{1... | collective-permute-start | bytes 261128 | tf_op jit(solution)/shard_map/ppermute | solution.py:212
  16.7 4.3 %collective-permute-start.5 = (f32[170,128]{1,0:T(8,128)S(1)}, f32[170,128]{1,0:T(8,128)S(1)}, u32[]{:S(2)}, u32[]{:S(2)}) collective-permute-start(f32[170,128]{1,0:T(8,128)S(1)} %get-tuple-element.48), channel_id=1, source_target_pairs={{0,4},{4,0},{8,12},{12,8},{16,20},{20,16},{24,28},{28,24},{1,5},{5... | collective-permute-start | bytes 261128 | tf_op jit(solution)/shard_map/ppermute | solution.py:212
  21.1 0.0 collective-permute-done.2.far_rows
  21.1 2.2 %collective-permute-done.3.near_rows = f32[560,128]{1,0:T(8,128)S(1)} collective-permute-done((f32[560,128]{1,0:T(8,128)}, f32[560,128]{1,0:T(8,128)S(1)}, u32[]{:S(2)}, u32[]{:S(2)}) %collective-permute-start.3) | collective-permute-done | bytes 286752 | tf_op jit(solution)/shard_map/ppermute | solution.py:212
  23.3 1.7 %shard_map.106 = (bf16[4,14,24,128]{3,2,1,0:T(8,128)(2,1)S(1)}, bf16[4,14,24,128]{3,2,1,0:T(8,128)(2,1)S(1)}, f32[14,24,128]{2,1,0:T(8,128)S(1)}, f32[3,14,24,12...) custom-call(f32[16,2048]{1,0:T(8,128)S(1)} %copy-done.2, bf16[16,2048]{1,0:T(8,128)(2,1)S(1)} %copy-done.4, ...), custom_call_target="tpu_custom_call" | custom-call | flops 849346560 | bytes 4194304 | tf_op jit(solution)/shard_map/pallas_call | solution.py:37
  25.0 0.0 collective-permute-done.5.near_corner
  25.0 1.0 %shard_map.107 = (bf16[4,20,24,128]{3,2,1,0:T(8,128)(2,1)S(1)}, bf16[4,20,24,128]{3,2,1,0:T(8,128)(2,1)S(1)}, f32[20,24,128]{2,1,0:T(8,128)S(1)}, f32[3,20,24,12...) custom-call(f32[16,2048]{1,0:T(8,128)S(1)} %copy-done.2, ...), custom_call_target="tpu_custom_call" | custom-call | flops 849346560 | bytes 4194304 | tf_op jit(solution)/shard_map/pallas_call | solution.py:37
  26.1 12.9 %all_to_all.33 = f32[32,1,128]{2,1,0:T(1,128)S(1)} all-to-all(f32[32,1,128]{2,1,0:T(1,128)S(1)} %bitcast.17), channel_id=1, replica_groups=mesh['row'=8,'col'=4] {'row','col'}, dimensions={0} | all-to-all | bytes 32768 | tf_op jit(solution)/shard_map/all_to_all | solution.py:588
  38.9 3.9 %shard_map.108 = (f32[3,20,24,128]{3,2,1,0:T(8,128)S(1)}, f32[3,18,24,128]{3,2,1,0:T(8,128)S(1)}, f32[2,18,24,128]{3,2,1,0:T(8,128)S(1)}, f32[3,18,16,128]{3,2,1...) custom-call(f32[32,128]{1,0:T(8,128)S(1)} %bitcast.15, ...), custom_call_target="tpu_custom_call" | custom-call | flops 1698693120 | bytes 4194304 | tf_op jit(solution)/shard_map/pallas_call | solution.py:37
  42.8 8.8 %all_to_all.34 = f32[32,1,128]{2,1,0:T(1,128)S(1)} all-to-all(f32[32,1,128]{2,1,0:T(1,128)S(1)} %bitcast.19), channel_id=1, replica_groups=mesh['row'=8,'col'=4] {'row','col'}, dimensions={0} | all-to-all | bytes 32768 | tf_op jit(solution)/shard_map/all_to_all | solution.py:588
  51.6 3.1 %shard_map.109 = (f32[3,16,2048]{2,1,0:T(8,128)S(1)}, f32[3,16,2048]{2,1,0:T(8,128)S(1)}, f32[3,16,2048]{2,1,0:T(8,128)S(1)}, f32[3,16,2048]{2,1,0:T(8,128)S(1)}, f32[32,128]{1,0:T(8,128)S(1)}) custom-call(f32[32,128]{1,0:T(8,128)S(1)} %bitcast.14, f32[3]{0:T(128)S(1)} %copy-done.6, bf16[4,20,24,128]{3,2,1,0:T(8,128)(2,1)S(1)} %get-tuple-element.58.near_box, ...), custom_call_target="tpu_custom_call" | custom-call | flops 1698693120 | bytes 4194304 | tf_op jit(solution)/shard_map/pallas_call | solution.py:37
  54.7 8.8 %all_to_all.35 = f32[32,1,128]{2,1,0:T(1,128)S(1)} all-to-all(f32[32,1,128]{2,1,0:T(1,128)S(1)} %bitcast.18), channel_id=1, replica_groups=mesh['row'=8,'col'=4] {'row','col'}, dimensions={0} | all-to-all | bytes 32768 | tf_op jit(solution)/shard_map/all_to_all | solution.py:588
  63.5 1.6 %shard_map.110 = (f32[3,16,2048]{2,1,0:T(8,128)}, f32[3,16,2048]{2,1,0:T(8,128)}, f32[3]{0:T(128)}) custom-call(f32[32,128]{1,0:T(8,128)S(1)} %bitcast.16, f32[3]{0:T(128)S(1)} %copy-done.6, f32[3,16,2048]{2,1,0:T(8,128)S(1)} %get-tuple-element.74.duals, f32[3,16,2048]{2,1,0:T(8,128)S(1)} %get-tuple-element.75.multipliers, ...), custom_call_target="tpu_custom_call" | custom-call | flops 1048576 | bytes 4194304 | tf_op jit(solution)/shard_map/pallas_call | solution.py:37
  (15 shorter events, 0.0 us)
Async XLA Ops:
  0.6 22.7 %copy-start.1 = (bf16[3,16,2048]{2,1,0:T(8,128)(2,1)S(1)}, bf16[3,16,2048]{2,1,0:T(8,128)(2,1)}, u32[]{:S(2)}) copy-start(bf16[3,16,2048]{2,1,0:T(8,128)(2,1)} %upper.7) | copy-start | bytes 589828
  0.6 22.7 %copy-start = (bf16[3,16,2048]{2,1,0:T(8,128)(2,1)S(1)}, bf16[3,16,2048]{2,1,0:T(8,128)(2,1)}, u32[]{:S(2)}) copy-start(bf16[3,16,2048]{2,1,0:T(8,128)(2,1)} %lower.7) | copy-start | bytes 589828
  0.7 22.7 %copy-start.5 = (bf16[16,2048]{1,0:T(8,128)(2,1)S(1)}, bf16[16,2048]{1,0:T(8,128)(2,1)}, u32[]{:S(2)}) copy-start(bf16[16,2048]{1,0:T(8,128)(2,1)} %radius.5) | copy-start | bytes 196612
  0.7 22.7 %copy-start.4 = (bf16[16,2048]{1,0:T(8,128)(2,1)S(1)}, bf16[16,2048]{1,0:T(8,128)(2,1)}, u32[]{:S(2)}) copy-start(bf16[16,2048]{1,0:T(8,128)(2,1)} %center.5) | copy-start | bytes 196612
  0.7 22.7 %copy-start.2 = (f32[16,2048]{1,0:T(8,128)S(1)}, f32[16,2048]{1,0:T(8,128)}, u32[]{:S(2)}) copy-start(f32[16,2048]{1,0:T(8,128)} %objective.5) | copy-start | bytes 393220
  3.0 18.1 %collective-permute-start.2 = (f32[560,128]{1,0:T(8,128)}, f32[560,128]{1,0:T(8,128)S(1)}, u32[]{:S(2)}, u32[]{:S(2)}) collective-permute-start(f32[560,128]{1,0:T(8,128)} %get-tuple-element.44), channel_id=1, source_target_pairs={{4,8},{8,4},{12,16},{16,12},{20,24},{24,20},{5,9},{9,5},{13,17},{1... | collective-permute-start | bytes 860168 | tf_op jit(solution)/shard_map/ppermute | solution.py:212
  3.7 19.6 %collective-permute-start.3 = (f32[560,128]{1,0:T(8,128)}, f32[560,128]{1,0:T(8,128)S(1)}, u32[]{:S(2)}, u32[]{:S(2)}) collective-permute-start(f32[560,128]{1,0:T(8,128)} %get-tuple-element.45), channel_id=1, source_target_pairs={{0,4},{4,0},{8,12},{12,8},{16,20},{20,16},{24,28},{28,24},{1,5},{5... | collective-permute-start | bytes 860168 | tf_op jit(solution)/shard_map/ppermute | solution.py:212
  9.5 6.5 %collective-permute-start = (f32[336,128]{1,0:T(8,128)}, f32[336,128]{1,0:T(8,128)S(1)}, u32[]{:S(2)}, u32[]{:S(2)}) collective-permute-start(f32[336,128]{1,0:T(8,128)} %get-tuple-element.42), channel_id=1, source_target_pairs={{1,2},{2,1},{5,6},{6,5},{9,10},{10,9},{13,14},{14,13},{17,18},{18,... | collective-permute-start | bytes 516104 | tf_op jit(solution)/shard_map/ppermute | solution.py:212
  10.1 5.8 %collective-permute-start.1 = (f32[336,128]{1,0:T(8,128)}, f32[336,128]{1,0:T(8,128)S(1)}, u32[]{:S(2)}, u32[]{:S(2)}) collective-permute-start(f32[336,128]{1,0:T(8,128)} %get-tuple-element.43), channel_id=1, source_target_pairs={{0,1},{1,0},{2,3},{3,2},{4,5},{5,4},{6,7},{7,6},{8,9},{9,8},{10,11... | collective-permute-start | bytes 516104 | tf_op jit(solution)/shard_map/ppermute | solution.py:212
  13.1 1.3 %copy-start.3 = (f32[4,3,3,64,64]{4,3,2,1,0:T(8,128)S(1)}, f32[4,3,3,64,64]{4,3,2,1,0:T(8,128)}, u32[]{:S(2)}) copy-start(f32[4,3,3,64,64]{4,3,2,1,0:T(8,128)} %param.13) | copy-start | bytes 1769476
  14.3 0.7 %copy-start.7 = (f32[4,64]{1,0:T(4,128)S(1)}, f32[4,64]{1,0:T(4,128)}, u32[]{:S(2)}) copy-start(f32[4,64]{1,0:T(4,128)} %biases.1) | copy-start | bytes 3076
  16.0 8.9 %collective-permute-start.4 = (f32[170,128]{1,0:T(8,128)S(1)}, f32[170,128]{1,0:T(8,128)S(1)}, u32[]{:S(2)}, u32[]{:S(2)}) collective-permute-start(f32[170,128]{1,0:T(8,128)S(1)} %get-tuple-element.47), channel_id=1, source_target_pairs={{4,8},{8,4},{12,16},{16,12},{20,24},{24,20},{5,9},{9,5},{13,17},{1... | collective-permute-start | bytes 261128 | tf_op jit(solution)/shard_map/ppermute | solution.py:212
  16.7 8.3 %collective-permute-start.5 = (f32[170,128]{1,0:T(8,128)S(1)}, f32[170,128]{1,0:T(8,128)S(1)}, u32[]{:S(2)}, u32[]{:S(2)}) collective-permute-start(f32[170,128]{1,0:T(8,128)S(1)} %get-tuple-element.48), channel_id=1, source_target_pairs={{0,4},{4,0},{8,12},{12,8},{16,20},{20,16},{24,28},{28,24},{1,5},{5... | collective-permute-start | bytes 261128 | tf_op jit(solution)/shard_map/ppermute | solution.py:212
  25.0 13.9 %copy-start.6 = (f32[3]{0:T(128)S(1)}, f32[3]{0:T(128)}, u32[]{:S(2)}) copy-start(f32[3]{0:T(128)} %steps.5) | copy-start | bytes 40

commit v16 on v15

--- a/solution.py
+++ b/solution.py
@@ -259,8 +259,9 @@
     return jnp.sum(total[...], axis=0, keepdims=True)
 
 
-def scale_of(total, step, cells, dims):
-    squares = summed(total)[:, 0:1]
+def scale_of(total, step, cells, dims, packed=False):
+    squares = summed(total)
+    squares = squares[:, 0:1] if packed else jnp.sum(squares, axis=1, keepdims=True)
     return jnp.broadcast_to(step / jnp.sqrt(squares / (2 * (LAYERS - 1) * cells) + EPS), dims)
 
 
@@ -306,6 +307,22 @@
     for j, row in enumerate(rows):
         packed = jnp.where(lane == j, jnp.sum(row, axis=1, keepdims=True), packed)
     out[...] = jnp.broadcast_to(packed, out.shape)
+
+
+def lanes(out, rows):
+    out[...] = jnp.concatenate(rows + [jnp.zeros((8 - len(rows), LANES), F32)], axis=0)
+
+
+class Joined:
+    def __init__(self, middle, ends):
+        self.middle, self.ends = middle, ends
+        self.count = middle.shape[-3]
+
+    def __getitem__(self, index):
+        *lead, q = index if isinstance(index, tuple) else (index,)
+        inner_pair = 3 <= q < 3 + self.count
+        source, at = (self.middle, q - 3) if inner_pair else (self.ends, q if q < 3 else q - self.count)
+        return source[tuple(lead) + (at,)]
 
 
 def assemble(reads, above, below, left, right, corners, slots, rows, pairs, raw, gaps, target):
@@ -391,7 +408,7 @@
 
 def first_body(
     objective, center, radius, lower, upper, far_cols, near_cols, far_rows, near_rows, far_corner, near_corner, fwd, bwd, bias,
-    near_in, far_in, back_in, slope_in, mult_in, totals,
+    totals,
     near_box, far_box, back, slope, mult, stat, value,
     raw, gaps, target, store, sums,
 ):
@@ -406,28 +423,29 @@
     slots = list(range(5)) + list(range(wide - 3, wide + 2))
     assemble(reads, above, below, left, right, corners, slots, rows, pairs, raw, gaps, target)
     start_convs(raw, target, store, sums, fwd, bwd, frame)
-    here = slice(3, wide - 3)
-    near_box[:, here] = near_in[...]
-    far_box[:, here] = far_in[...]
-    back[here] = back_in[...]
-    slope[:, here] = slope_in[...]
-    mult[here] = mult_in[...]
     sizes = [totals[j] for j in range(3)]
-    for slot, q in ((1, 0), (2, 1), (3, 2), (6, wide - 3), (7, wide - 2), (8, wide - 1)):
-        new = start_step(slot, q, raw, gaps, target, sums, bias, near_box, far_box, back, slope, mult)
-        if 2 <= q < wide - 2:
+    for out, slot in enumerate((1, 2, 3, 6, 7, 8)):
+        new = start_step(slot, out, raw, gaps, target, sums, bias, near_box, far_box, back, slope, mult)
+        if out in (2, 3):
             sizes = [old + one for old, one in zip(sizes, new)]
     squares, worth, fixed = (own_rows(one) for one in sizes)
-    stats(stat, [squares])
-    stats(value, [worth + fixed, fixed])
+    stat[...] = jnp.broadcast_to(squares, stat.shape)
+    lanes(value, [worth + fixed, fixed])
 
 
 def second_body(
+    total, steps, *rest, cells,
+):
+    start, rest = rest[:10], rest[10:]
+    second_joined(total, steps, *(Joined(*two) for two in zip(start[:5], start[5:])), *rest, cells=cells)
+
+
+def second_joined(
     total, steps, near_box, far_box, back, slope, mult, fwd, bwd, bias,
     base, slope_out, mult_out, duals, last_mult, last_slope, last_pull, stat, value,
     points, worths, store, sums, *, cells,
 ):
-    wide, frame = near_box.shape[1:3]
+    wide, frame = base.shape[1:3]
     inside = slice(EDGE, frame - EDGE)
     scale = scale_of(total, steps[0], cells, (frame, LANES))
     zero = jnp.zeros((frame, LANES), F32)
@@ -492,17 +510,18 @@
         if own:
             squares = squares + new
             worth = worth + bound.total()
-    stats(stat, [own_rows(squares)])
-    stats(value, [own_rows(worth)])
+    stat[...] = jnp.broadcast_to(own_rows(squares), stat.shape)
+    lanes(value, [own_rows(worth)])
 
 
 def third_body(
-    total, steps, near_box, base, mult, slope, duals1, last_mult, last_slope, last_pull,
+    total, steps, near_middle, near_ends, base, mult, slope, duals1, last_mult, last_slope, last_pull,
     fwd, bwd, lower, upper, bias, value0, value1,
     duals, multipliers, slope_out, mult_out, stat,
     points, store, sums, *, cells,
 ):
-    wide, frame = near_box.shape[1:3]
+    near_box = Joined(near_middle, near_ends)
+    wide, frame = base.shape[1:3]
     rows = frame - 2 * EDGE
     inside = slice(EDGE, frame - EDGE)
     scale = scale_of(total, steps[1], cells, (frame, LANES))
@@ -567,14 +586,12 @@
             squares = squares + dl * dl + dm * dm
         worth = worth + bound.total()
 
-    lane = lax.broadcasted_iota(jnp.int32, (1, LANES), 1)
-    start, fixed = (jnp.where(lane == j, value0[0:1, :], 0.0) for j in range(2))
-    middle = jnp.where(lane == 0, value1[0:1, :], 0.0)
-    stats(stat, [folded(squares), start, middle + fixed, folded(worth) + own_rows(framed) + fixed])
+    start, fixed = value0[0:1, :], value0[1:2, :]
+    stats(stat, [folded(squares), start, value1[0:1, :] + fixed, folded(worth) + own_rows(framed) + fixed])
 
 
 def last_body(total, steps, duals, multipliers, slope, mult, duals_out, mult_out, bounds, *, cells):
-    scale = scale_of(total, steps[2], cells, duals.shape[1:])
+    scale = scale_of(total, steps[2], cells, duals.shape[1:], packed=True)
     for k in range(LAYERS - 1):
         duals_out[k] = duals[k] + scale * slope[k]
         mult_out[k] = multipliers[k] + scale * mult[k]
@@ -633,20 +650,20 @@
         full = shape(count, frame, LANES)
         return box, box, full, shape(3, count, frame, LANES), full
 
-    middle = call(
+    *middle, totals = call(
         middle_body,
         start_shapes(pairs - 2) + (shape(3, frame, LANES),),
         start_scratch(pairs),
         inputs + (far_rows, near_rows, fwd, bwd, bias),
         flops,
     )
-    near_box, far_box, back, slope0, mult0, stat0, value0 = call(
+    *ends, stat0, value0 = call(
         first_body,
-        start_shapes(wide) + (spread, small),
+        start_shapes(6) + (spread, small),
         start_scratch(10),
         inputs
         + (far_cols, near_cols, far_rows, near_rows, far_corner, near_corner, fwd, bwd, bias)
-        + tuple(middle),
+        + (totals,),
         flops,
     )
 
@@ -671,7 +688,7 @@
             pltpu.VMEM((3, wide + 1, frame, LANES), F32),
             pltpu.VMEM((3, 3, wide, frame, LANES), F32),
         ],
-        (total0, steps, near_box, far_box, back, slope0, mult0, fwd, bwd, bias),
+        (total0, steps, *middle, *ends, fwd, bwd, bias),
         2 * flops,
         scalars=(1,),
     )
@@ -686,7 +703,7 @@
             pltpu.VMEM((3, 3, wide - 2, frame, LANES), F32),
         ],
         (
-            total1, steps, near_box, base, mult1, slope1, duals1, last_mult, last_slope, last_pull,
+            total1, steps, middle[0], ends[0], base, mult1, slope1, duals1, last_mult, last_slope, last_pull,
             fwd, bwd, lower, upper, bias, value0, value1,
         ),
         2 * flops,

time: 65.4 us -> 65.3 us (level)
  no operation moved by 1% of the time
where the time goes in v16:
time: 65.3 us; the launch traced here: 65.1 us
  blocking collectives  30.5 us (47%)
  starting transfers between devices  15.1 us (23%)
  Pallas kernels  14.4 us (22%)
  waiting for transfers between devices  2.29 us (4%)
  local copies, waits for them, and re-layouts  1.98 us (3%)
  between operations  0.78 us (1%)
    all_to_all x3, blocking collectives, everyone(): return lax.all_to_all(partial, ('row', 'col'), 0, 0, tiled=True)  30.5 us
    pallas_call x8, Pallas kernels, call(): pl.pallas_call(body, out_shape=outs, in_specs=specs, out_specs=out_specs,...  14.4 us
    ppermute x3, starting transfers between devices, partners(): lax.ppermute(near, axis, pairs(0))  13.1 us
    ppermute x3, waiting for transfers between devices, partners(): lax.ppermute(near, axis, pairs(0))  2.28 us
    ppermute x3, starting transfers between devices, partners(): lax.ppermute(far, axis, pairs(1))  2 us
    unnamed x16, local copies, waits for them, and re-layouts  1.98 us
  transfers between devices with their start and end apart: 6, of which 1 were waited for; matrix products, arithmetic and copies ran while one was open for 0% of the time, Pallas kernels for 4%

profile of v16, /device:TPU:0, one launch (start us, length us, event | category | flops | bytes accessed | tf_op | source)
XLA Modules:
  0.0 65.1 jit_solution(6581470077168262415)
XLA Ops:
  0.7 2.3 %shard_map.103 = (f32[560,128]{1,0:T(8,128)}, f32[560,128]{1,0:T(8,128)}, f32[336,128]{1,0:T(8,128)}, f32[336,128]{1,0:T(8,128)}) custom-call(f32[16,2048]{1,0:T(8,128)} %objective.5, bf16[16,2048]{1,0:T(8,128)(2,1)} %center.5, bf16[16,2048]{1,0:T(8,128)(2,1)} %radius.5, bf16[3,16,2048]{2,1,0:T(8,128)(2,1)} %lower.7, bf16[3,16,2048]{2,1,0:T(8,128)(2,1)} %upper.7), custom_call_target="tpu_custom_call" | custom-call | flops 1048576 | bytes 4194304 | tf_op jit(solution)/shard_map/pallas_call | solution.py:37
  3.0 0.7 %collective-permute-start.2 = (f32[560,128]{1,0:T(8,128)}, f32[560,128]{1,0:T(8,128)S(1)}, u32[]{:S(2)}, u32[]{:S(2)}) collective-permute-start(f32[560,128]{1,0:T(8,128)} %get-tuple-element.44), channel_id=1, source_target_pairs={{4,8},{8,4},{12,16},{16,12},{20,24},{24,20},{5,9},{9,5},{13,17},{1... | collective-permute-start | bytes 860168 | tf_op jit(solution)/shard_map/ppermute | solution.py:212
  3.7 5.8 %collective-permute-start.3 = (f32[560,128]{1,0:T(8,128)}, f32[560,128]{1,0:T(8,128)S(1)}, u32[]{:S(2)}, u32[]{:S(2)}) collective-permute-start(f32[560,128]{1,0:T(8,128)} %get-tuple-element.45), channel_id=1, source_target_pairs={{0,4},{4,0},{8,12},{12,8},{16,20},{20,16},{24,28},{28,24},{1,5},{5... | collective-permute-start | bytes 860168 | tf_op jit(solution)/shard_map/ppermute | solution.py:212
  9.5 0.7 %collective-permute-start = (f32[336,128]{1,0:T(8,128)}, f32[336,128]{1,0:T(8,128)S(1)}, u32[]{:S(2)}, u32[]{:S(2)}) collective-permute-start(f32[336,128]{1,0:T(8,128)} %get-tuple-element.42), channel_id=1, source_target_pairs={{1,2},{2,1},{5,6},{6,5},{9,10},{10,9},{13,14},{14,13},{17,18},{18,... | collective-permute-start | bytes 516104 | tf_op jit(solution)/shard_map/ppermute | solution.py:212
  10.1 2.9 %collective-permute-start.1 = (f32[336,128]{1,0:T(8,128)}, f32[336,128]{1,0:T(8,128)S(1)}, u32[]{:S(2)}, u32[]{:S(2)}) collective-permute-start(f32[336,128]{1,0:T(8,128)} %get-tuple-element.43), channel_id=1, source_target_pairs={{0,1},{1,0},{2,3},{3,2},{4,5},{5,4},{6,7},{7,6},{8,9},{9,8},{10,11... | collective-permute-start | bytes 516104 | tf_op jit(solution)/shard_map/ppermute | solution.py:212
  13.1 1.3 %copy-done.3 = f32[4,3,3,64,64]{4,3,2,1,0:T(8,128)S(1)} copy-done((f32[4,3,3,64,64]{4,3,2,1,0:T(8,128)S(1)}, f32[4,3,3,64,64]{4,3,2,1,0:T(8,128)}, u32[]{:S(2)}) %copy-start.3) | copy-done | bytes 589848
  14.3 0.7 %copy-done.7 = f32[4,64]{1,0:T(4,128)S(1)} copy-done((f32[4,64]{1,0:T(4,128)S(1)}, f32[4,64]{1,0:T(4,128)}, u32[]{:S(2)}) %copy-start.7) | copy-done | bytes 1048
  15.0 0.9 %shard_map.104 = (bf16[3,768,384]{2,1,0:T(8,128)(2,1)S(1)}, bf16[4,768,384]{2,1,0:T(8,128)(2,1)S(1)}, f32[8,128]{1,0:T(8,128)S(1)}) custom-call(f32[36,64,64]{2,1,0:T(8,128)S(1)} %bitcast.13, f32[4,64]{1,0:T(4,128)S(1)} %copy-done.7), custom_call_target="tpu_custom_call" | custom-call | flops 4194304 | bytes 4194304 | tf_op jit(solution)/shard_map/pallas_call | solution.py:37
  16.0 0.0 collective-permute-done.1.near_cols
  16.0 0.1 shard_map.105
  16.0 0.7 %collective-permute-start.4 = (f32[170,128]{1,0:T(8,128)S(1)}, f32[170,128]{1,0:T(8,128)S(1)}, u32[]{:S(2)}, u32[]{:S(2)}) collective-permute-start(f32[170,128]{1,0:T(8,128)S(1)} %get-tuple-element.47), channel_id=1, source_target_pairs={{4,8},{8,4},{12,16},{16,12},{20,24},{24,20},{5,9},{9,5},{13,17},{1... | collective-permute-start | bytes 261128 | tf_op jit(solution)/shard_map/ppermute | solution.py:212
  16.7 4.3 %collective-permute-start.5 = (f32[170,128]{1,0:T(8,128)S(1)}, f32[170,128]{1,0:T(8,128)S(1)}, u32[]{:S(2)}, u32[]{:S(2)}) collective-permute-start(f32[170,128]{1,0:T(8,128)S(1)} %get-tuple-element.48), channel_id=1, source_target_pairs={{0,4},{4,0},{8,12},{12,8},{16,20},{20,16},{24,28},{28,24},{1,5},{5... | collective-permute-start | bytes 261128 | tf_op jit(solution)/shard_map/ppermute | solution.py:212
  21.1 0.0 collective-permute-done.2.far_rows
  21.1 2.2 %collective-permute-done.3.near_rows = f32[560,128]{1,0:T(8,128)S(1)} collective-permute-done((f32[560,128]{1,0:T(8,128)}, f32[560,128]{1,0:T(8,128)S(1)}, u32[]{:S(2)}, u32[]{:S(2)}) %collective-permute-start.3) | collective-permute-done | bytes 286752 | tf_op jit(solution)/shard_map/ppermute | solution.py:212
  23.3 1.7 %shard_map.106 = (bf16[4,14,24,128]{3,2,1,0:T(8,128)(2,1)S(1)}, bf16[4,14,24,128]{3,2,1,0:T(8,128)(2,1)S(1)}, f32[14,24,128]{2,1,0:T(8,128)S(1)}, f32[3,14,24,12...) custom-call(f32[16,2048]{1,0:T(8,128)S(1)} %copy-done.2, bf16[16,2048]{1,0:T(8,128)(2,1)S(1)} %copy-done.4, ...), custom_call_target="tpu_custom_call" | custom-call | flops 849346560 | bytes 4194304 | tf_op jit(solution)/shard_map/pallas_call | solution.py:37
  25.0 0.0 collective-permute-done.4.far_corner
  25.0 0.0 collective-permute-done.5.near_corner
  25.0 0.9 %shard_map.107 = (bf16[4,6,24,128]{3,2,1,0:T(8,128)(2,1)S(1)}, bf16[4,6,24,128]{3,2,1,0:T(8,128)(2,1)S(1)}, f32[6,24,128]{2,1,0:T(8,128)S(1)}, f32[3,6,24,128]{3...) custom-call(f32[16,2048]{1,0:T(8,128)S(1)} %copy-done.2, ...), custom_call_target="tpu_custom_call" | custom-call | flops 849346560 | bytes 4194304 | tf_op jit(solution)/shard_map/pallas_call | solution.py:37
  26.0 12.9 %all_to_all.33 = f32[32,1,128]{2,1,0:T(1,128)S(1)} all-to-all(f32[32,1,128]{2,1,0:T(1,128)S(1)} %bitcast.19), channel_id=1, replica_groups=mesh['row'=8,'col'=4] {'row','col'}, dimensions={0} | all-to-all | bytes 32768 | tf_op jit(solution)/shard_map/all_to_all | solution.py:605
  38.9 3.5 %shard_map.108 = (f32[3,20,24,128]{3,2,1,0:T(8,128)S(1)}, f32[3,18,24,128]{3,2,1,0:T(8,128)S(1)}, f32[2,18,24,128]{3,2,1,0:T(8,128)S(1)}, f32[3,18,16,128]{3,2,1...) custom-call(f32[32,128]{1,0:T(8,128)S(1)} %bitcast.15, ...), custom_call_target="tpu_custom_call" | custom-call | flops 1698693120 | bytes 4194304 | tf_op jit(solution)/shard_map/pallas_call | solution.py:37
  42.4 8.8 %all_to_all.34 = f32[32,1,128]{2,1,0:T(1,128)S(1)} all-to-all(f32[32,1,128]{2,1,0:T(1,128)S(1)} %bitcast.18), channel_id=1, replica_groups=mesh['row'=8,'col'=4] {'row','col'}, dimensions={0} | all-to-all | bytes 32768 | tf_op jit(solution)/shard_map/all_to_all | solution.py:605
  51.2 3.4 %shard_map.109 = (f32[3,16,2048]{2,1,0:T(8,128)S(1)}, f32[3,16,2048]{2,1,0:T(8,128)S(1)}, f32[3,16,2048]{2,1,0:T(8,128)S(1)}, f32[3,16,2048]{2,1,0:T(8,128)S(1)}, f32[32,128]{1,0:T(8,128)S(1)}) custom-call(f32[32,128]{1,0:T(8,128)S(1)} %bitcast.14, f32[3]{0:T(128)S(1)} %copy-done.6, bf16[4,14,24,128]{3,2,1,0:T(8,128)(2,1)S(1)} %get-tuple-element.53.rest_0_.near_middle, ...), custom_call_target="tpu_custom_call" | custom-call | flops 1698693120 | bytes 4194304 | tf_op jit(solution)/shard_map/pallas_call | solution.py:37
  54.6 8.8 %all_to_all.35 = f32[32,1,128]{2,1,0:T(1,128)S(1)} all-to-all(f32[32,1,128]{2,1,0:T(1,128)S(1)} %bitcast.17), channel_id=1, replica_groups=mesh['row'=8,'col'=4] {'row','col'}, dimensions={0} | all-to-all | bytes 32768 | tf_op jit(solution)/shard_map/all_to_all | solution.py:605
  63.5 1.6 %shard_map.110 = (f32[3,16,2048]{2,1,0:T(8,128)}, f32[3,16,2048]{2,1,0:T(8,128)}, f32[3]{0:T(128)}) custom-call(f32[32,128]{1,0:T(8,128)S(1)} %bitcast.16, f32[3]{0:T(128)S(1)} %copy-done.6, f32[3,16,2048]{2,1,0:T(8,128)S(1)} %get-tuple-element.74.duals, f32[3,16,2048]{2,1,0:T(8,128)S(1)} %get-tuple-element.75.multipliers, ...), custom_call_target="tpu_custom_call" | custom-call | flops 1048576 | bytes 4194304 | tf_op jit(solution)/shard_map/pallas_call | solution.py:37
  (15 shorter events, 0.0 us)
Async XLA Ops:
  0.6 22.7 %copy-start.1 = (bf16[3,16,2048]{2,1,0:T(8,128)(2,1)S(1)}, bf16[3,16,2048]{2,1,0:T(8,128)(2,1)}, u32[]{:S(2)}) copy-start(bf16[3,16,2048]{2,1,0:T(8,128)(2,1)} %upper.7) | copy-start | bytes 589828
  0.6 22.7 %copy-start = (bf16[3,16,2048]{2,1,0:T(8,128)(2,1)S(1)}, bf16[3,16,2048]{2,1,0:T(8,128)(2,1)}, u32[]{:S(2)}) copy-start(bf16[3,16,2048]{2,1,0:T(8,128)(2,1)} %lower.7) | copy-start | bytes 589828
  0.7 22.7 %copy-start.5 = (bf16[16,2048]{1,0:T(8,128)(2,1)S(1)}, bf16[16,2048]{1,0:T(8,128)(2,1)}, u32[]{:S(2)}) copy-start(bf16[16,2048]{1,0:T(8,128)(2,1)} %radius.5) | copy-start | bytes 196612
  0.7 22.7 %copy-start.4 = (bf16[16,2048]{1,0:T(8,128)(2,1)S(1)}, bf16[16,2048]{1,0:T(8,128)(2,1)}, u32[]{:S(2)}) copy-start(bf16[16,2048]{1,0:T(8,128)(2,1)} %center.5) | copy-start | bytes 196612
  0.7 22.7 %copy-start.2 = (f32[16,2048]{1,0:T(8,128)S(1)}, f32[16,2048]{1,0:T(8,128)}, u32[]{:S(2)}) copy-start(f32[16,2048]{1,0:T(8,128)} %objective.5) | copy-start | bytes 393220
  3.0 18.1 %collective-permute-start.2 = (f32[560,128]{1,0:T(8,128)}, f32[560,128]{1,0:T(8,128)S(1)}, u32[]{:S(2)}, u32[]{:S(2)}) collective-permute-start(f32[560,128]{1,0:T(8,128)} %get-tuple-element.44), channel_id=1, source_target_pairs={{4,8},{8,4},{12,16},{16,12},{20,24},{24,20},{5,9},{9,5},{13,17},{1... | collective-permute-start | bytes 860168 | tf_op jit(solution)/shard_map/ppermute | solution.py:212
  3.7 19.6 %collective-permute-start.3 = (f32[560,128]{1,0:T(8,128)}, f32[560,128]{1,0:T(8,128)S(1)}, u32[]{:S(2)}, u32[]{:S(2)}) collective-permute-start(f32[560,128]{1,0:T(8,128)} %get-tuple-element.45), channel_id=1, source_target_pairs={{0,4},{4,0},{8,12},{12,8},{16,20},{20,16},{24,28},{28,24},{1,5},{5... | collective-permute-start | bytes 860168 | tf_op jit(solution)/shard_map/ppermute | solution.py:212
  9.5 6.5 %collective-permute-start = (f32[336,128]{1,0:T(8,128)}, f32[336,128]{1,0:T(8,128)S(1)}, u32[]{:S(2)}, u32[]{:S(2)}) collective-permute-start(f32[336,128]{1,0:T(8,128)} %get-tuple-element.42), channel_id=1, source_target_pairs={{1,2},{2,1},{5,6},{6,5},{9,10},{10,9},{13,14},{14,13},{17,18},{18,... | collective-permute-start | bytes 516104 | tf_op jit(solution)/shard_map/ppermute | solution.py:212
  10.1 5.8 %collective-permute-start.1 = (f32[336,128]{1,0:T(8,128)}, f32[336,128]{1,0:T(8,128)S(1)}, u32[]{:S(2)}, u32[]{:S(2)}) collective-permute-start(f32[336,128]{1,0:T(8,128)} %get-tuple-element.43), channel_id=1, source_target_pairs={{0,1},{1,0},{2,3},{3,2},{4,5},{5,4},{6,7},{7,6},{8,9},{9,8},{10,11... | collective-permute-start | bytes 516104 | tf_op jit(solution)/shard_map/ppermute | solution.py:212
  13.1 1.3 %copy-start.3 = (f32[4,3,3,64,64]{4,3,2,1,0:T(8,128)S(1)}, f32[4,3,3,64,64]{4,3,2,1,0:T(8,128)}, u32[]{:S(2)}) copy-start(f32[4,3,3,64,64]{4,3,2,1,0:T(8,128)} %param.13) | copy-start | bytes 1769476
  14.3 0.7 %copy-start.7 = (f32[4,64]{1,0:T(4,128)S(1)}, f32[4,64]{1,0:T(4,128)}, u32[]{:S(2)}) copy-start(f32[4,64]{1,0:T(4,128)} %biases.1) | copy-start | bytes 3076
  16.0 8.9 %collective-permute-start.4 = (f32[170,128]{1,0:T(8,128)S(1)}, f32[170,128]{1,0:T(8,128)S(1)}, u32[]{:S(2)}, u32[]{:S(2)}) collective-permute-start(f32[170,128]{1,0:T(8,128)S(1)} %get-tuple-element.47), channel_id=1, source_target_pairs={{4,8},{8,4},{12,16},{16,12},{20,24},{24,20},{5,9},{9,5},{13,17},{1... | collective-permute-start | bytes 261128 | tf_op jit(solution)/shard_map/ppermute | solution.py:212
  16.7 8.3 %collective-permute-start.5 = (f32[170,128]{1,0:T(8,128)S(1)}, f32[170,128]{1,0:T(8,128)S(1)}, u32[]{:S(2)}, u32[]{:S(2)}) collective-permute-start(f32[170,128]{1,0:T(8,128)S(1)} %get-tuple-element.48), channel_id=1, source_target_pairs={{0,4},{4,0},{8,12},{12,8},{16,20},{20,16},{24,28},{28,24},{1,5},{5... | collective-permute-start | bytes 261128 | tf_op jit(solution)/shard_map/ppermute | solution.py:212
  25.0 13.8 %copy-start.6 = (f32[3]{0:T(128)S(1)}, f32[3]{0:T(128)}, u32[]{:S(2)}) copy-start(f32[3]{0:T(128)} %steps.5) | copy-start | bytes 40

commit v17 on v16

--- a/solution.py
+++ b/solution.py
@@ -309,8 +309,12 @@
     out[...] = jnp.broadcast_to(packed, out.shape)
 
 
-def lanes(out, rows):
-    out[...] = jnp.concatenate(rows + [jnp.zeros((8 - len(rows), LANES), F32)], axis=0)
+class At:
+    def __init__(self, box, pairs):
+        self.box, self.pairs = box, pairs
+
+    def __setitem__(self, index, value):
+        self.box[index[0], self.pairs[index[1]]] = value
 
 
 class Joined:
@@ -408,7 +412,7 @@
 
 def first_body(
     objective, center, radius, lower, upper, far_cols, near_cols, far_rows, near_rows, far_corner, near_corner, fwd, bwd, bias,
-    totals,
+    totals, near_in,
     near_box, far_box, back, slope, mult, stat, value,
     raw, gaps, target, store, sums,
 ):
@@ -423,21 +427,24 @@
     slots = list(range(5)) + list(range(wide - 3, wide + 2))
     assemble(reads, above, below, left, right, corners, slots, rows, pairs, raw, gaps, target)
     start_convs(raw, target, store, sums, fwd, bwd, frame)
+    near_box[:, 3 : wide - 3] = near_in[...]
+    ends_box = At(near_box, (0, 1, 2, wide - 3, wide - 2, wide - 1))
     sizes = [totals[j] for j in range(3)]
     for out, slot in enumerate((1, 2, 3, 6, 7, 8)):
-        new = start_step(slot, out, raw, gaps, target, sums, bias, near_box, far_box, back, slope, mult)
+        new = start_step(slot, out, raw, gaps, target, sums, bias, ends_box, far_box, back, slope, mult)
         if out in (2, 3):
             sizes = [old + one for old, one in zip(sizes, new)]
     squares, worth, fixed = (own_rows(one) for one in sizes)
     stat[...] = jnp.broadcast_to(squares, stat.shape)
-    lanes(value, [worth + fixed, fixed])
+    stats(value, [worth + fixed, fixed])
 
 
 def second_body(
     total, steps, *rest, cells,
 ):
-    start, rest = rest[:10], rest[10:]
-    second_joined(total, steps, *(Joined(*two) for two in zip(start[:5], start[5:])), *rest, cells=cells)
+    start, rest = rest[:9], rest[9:]
+    joined = [Joined(*two) for two in zip(start[1:5], start[5:])]
+    second_joined(total, steps, start[0], *joined, *rest, cells=cells)
 
 
 def second_joined(
@@ -510,21 +517,20 @@
         if own:
             squares = squares + new
             worth = worth + bound.total()
-    stat[...] = jnp.broadcast_to(own_rows(squares), stat.shape)
-    lanes(value, [own_rows(worth)])
+    stats(stat, [own_rows(squares)])
+    stats(value, [own_rows(worth)])
 
 
 def third_body(
-    total, steps, near_middle, near_ends, base, mult, slope, duals1, last_mult, last_slope, last_pull,
+    total, steps, near_box, base, mult, slope, duals1, last_mult, last_slope, last_pull,
     fwd, bwd, lower, upper, bias, value0, value1,
     duals, multipliers, slope_out, mult_out, stat,
     points, store, sums, *, cells,
 ):
-    near_box = Joined(near_middle, near_ends)
-    wide, frame = base.shape[1:3]
+    wide, frame = near_box.shape[1:3]
     rows = frame - 2 * EDGE
     inside = slice(EDGE, frame - EDGE)
-    scale = scale_of(total, steps[1], cells, (frame, LANES))
+    scale = scale_of(total, steps[1], cells, (frame, LANES), packed=True)
     zero = jnp.zeros((frame, LANES), F32)
     slide(3, wide - 2, store, lambda j: [slope[k, j] for k in range(3)])
     for k in range(3):
@@ -586,8 +592,10 @@
             squares = squares + dl * dl + dm * dm
         worth = worth + bound.total()
 
-    start, fixed = value0[0:1, :], value0[1:2, :]
-    stats(stat, [folded(squares), start, value1[0:1, :] + fixed, folded(worth) + own_rows(framed) + fixed])
+    lane = lax.broadcasted_iota(jnp.int32, (1, LANES), 1)
+    start, fixed = (jnp.where(lane == j, value0[0:1, :], 0.0) for j in range(2))
+    middle = jnp.where(lane == 0, value1[0:1, :], 0.0)
+    stats(stat, [folded(squares), start, middle + fixed, folded(worth) + own_rows(framed) + fixed])
 
 
 def last_body(total, steps, duals, multipliers, slope, mult, duals_out, mult_out, bounds, *, cells):
@@ -657,13 +665,13 @@
         inputs + (far_rows, near_rows, fwd, bwd, bias),
         flops,
     )
-    *ends, stat0, value0 = call(
+    near_box, *ends, stat0, value0 = call(
         first_body,
-        start_shapes(6) + (spread, small),
+        start_shapes(wide)[:1] + start_shapes(6)[1:] + (spread, small),
         start_scratch(10),
         inputs
         + (far_cols, near_cols, far_rows, near_rows, far_corner, near_corner, fwd, bwd, bias)
-        + (totals,),
+        + (totals, middle[0]),
         flops,
     )
 
@@ -688,7 +696,7 @@
             pltpu.VMEM((3, wide + 1, frame, LANES), F32),
             pltpu.VMEM((3, 3, wide, frame, LANES), F32),
         ],
-        (total0, steps, *middle, *ends, fwd, bwd, bias),
+        (total0, steps, near_box, *middle[1:], *ends, fwd, bwd, bias),
         2 * flops,
         scalars=(1,),
     )
@@ -703,7 +711,7 @@
             pltpu.VMEM((3, 3, wide - 2, frame, LANES), F32),
         ],
         (
-            total1, steps, middle[0], ends[0], base, mult1, slope1, duals1, last_mult, last_slope, last_pull,
+            total1, steps, near_box, base, mult1, slope1, duals1, last_mult, last_slope, last_pull,
             fwd, bwd, lower, upper, bias, value0, value1,
         ),
         2 * flops,

time: 65.3 us -> 65.4 us (level)
  no operation moved by 1% of the time
where the time goes in v17:
time: 65.4 us; the launch traced here: 65.1 us
  blocking collectives  30.5 us (47%)
  starting transfers between devices  15.1 us (23%)
  Pallas kernels  14.4 us (22%)
  waiting for transfers between devices  2.27 us (3%)
  local copies, waits for them, and re-layouts  1.98 us (3%)
  between operations  0.77 us (1%)
    all_to_all x3, blocking collectives, everyone(): return lax.all_to_all(partial, ('row', 'col'), 0, 0, tiled=True)  30.5 us
    pallas_call x8, Pallas kernels, call(): pl.pallas_call(body, out_shape=outs, in_specs=specs, out_specs=out_specs,...  14.4 us
    ppermute x3, starting transfers between devices, partners(): lax.ppermute(near, axis, pairs(0))  13.1 us
    ppermute x3, waiting for transfers between devices, partners(): lax.ppermute(near, axis, pairs(0))  2.27 us
    ppermute x3, starting transfers between devices, partners(): lax.ppermute(far, axis, pairs(1))  2 us
    unnamed x16, local copies, waits for them, and re-layouts  1.98 us
  transfers between devices with their start and end apart: 6, of which 1 were waited for; matrix products, arithmetic and copies ran while one was open for 0% of the time, Pallas kernels for 4%

profile of v17, /device:TPU:0, one launch (start us, length us, event | category | flops | bytes accessed | tf_op | source)
XLA Modules:
  0.0 65.1 jit_solution(17114108721694529270)
XLA Ops:
  0.7 2.3 %shard_map.103 = (f32[560,128]{1,0:T(8,128)}, f32[560,128]{1,0:T(8,128)}, f32[336,128]{1,0:T(8,128)}, f32[336,128]{1,0:T(8,128)}) custom-call(f32[16,2048]{1,0:T(8,128)} %objective.5, bf16[16,2048]{1,0:T(8,128)(2,1)} %center.5, bf16[16,2048]{1,0:T(8,128)(2,1)} %radius.5, bf16[3,16,2048]{2,1,0:T(8,128)(2,1)} %lower.7, bf16[3,16,2048]{2,1,0:T(8,128)(2,1)} %upper.7), custom_call_target="tpu_custom_call" | custom-call | flops 1048576 | bytes 4194304 | tf_op jit(solution)/shard_map/pallas_call | solution.py:37
  3.0 0.7 %collective-permute-start.2 = (f32[560,128]{1,0:T(8,128)}, f32[560,128]{1,0:T(8,128)S(1)}, u32[]{:S(2)}, u32[]{:S(2)}) collective-permute-start(f32[560,128]{1,0:T(8,128)} %get-tuple-element.44), channel_id=1, source_target_pairs={{4,8},{8,4},{12,16},{16,12},{20,24},{24,20},{5,9},{9,5},{13,17},{1... | collective-permute-start | bytes 860168 | tf_op jit(solution)/shard_map/ppermute | solution.py:212
  3.7 5.8 %collective-permute-start.3 = (f32[560,128]{1,0:T(8,128)}, f32[560,128]{1,0:T(8,128)S(1)}, u32[]{:S(2)}, u32[]{:S(2)}) collective-permute-start(f32[560,128]{1,0:T(8,128)} %get-tuple-element.45), channel_id=1, source_target_pairs={{0,4},{4,0},{8,12},{12,8},{16,20},{20,16},{24,28},{28,24},{1,5},{5... | collective-permute-start | bytes 860168 | tf_op jit(solution)/shard_map/ppermute | solution.py:212
  9.5 0.7 %collective-permute-start = (f32[336,128]{1,0:T(8,128)}, f32[336,128]{1,0:T(8,128)S(1)}, u32[]{:S(2)}, u32[]{:S(2)}) collective-permute-start(f32[336,128]{1,0:T(8,128)} %get-tuple-element.42), channel_id=1, source_target_pairs={{1,2},{2,1},{5,6},{6,5},{9,10},{10,9},{13,14},{14,13},{17,18},{18,... | collective-permute-start | bytes 516104 | tf_op jit(solution)/shard_map/ppermute | solution.py:212
  10.1 2.9 %collective-permute-start.1 = (f32[336,128]{1,0:T(8,128)}, f32[336,128]{1,0:T(8,128)S(1)}, u32[]{:S(2)}, u32[]{:S(2)}) collective-permute-start(f32[336,128]{1,0:T(8,128)} %get-tuple-element.43), channel_id=1, source_target_pairs={{0,1},{1,0},{2,3},{3,2},{4,5},{5,4},{6,7},{7,6},{8,9},{9,8},{10,11... | collective-permute-start | bytes 516104 | tf_op jit(solution)/shard_map/ppermute | solution.py:212
  13.1 1.3 %copy-done.3 = f32[4,3,3,64,64]{4,3,2,1,0:T(8,128)S(1)} copy-done((f32[4,3,3,64,64]{4,3,2,1,0:T(8,128)S(1)}, f32[4,3,3,64,64]{4,3,2,1,0:T(8,128)}, u32[]{:S(2)}) %copy-start.3) | copy-done | bytes 589848
  14.3 0.7 %copy-done.7 = f32[4,64]{1,0:T(4,128)S(1)} copy-done((f32[4,64]{1,0:T(4,128)S(1)}, f32[4,64]{1,0:T(4,128)}, u32[]{:S(2)}) %copy-start.7) | copy-done | bytes 1048
  15.0 0.9 %shard_map.104 = (bf16[3,768,384]{2,1,0:T(8,128)(2,1)S(1)}, bf16[4,768,384]{2,1,0:T(8,128)(2,1)S(1)}, f32[8,128]{1,0:T(8,128)S(1)}) custom-call(f32[36,64,64]{2,1,0:T(8,128)S(1)} %bitcast.13, f32[4,64]{1,0:T(4,128)S(1)} %copy-done.7), custom_call_target="tpu_custom_call" | custom-call | flops 4194304 | bytes 4194304 | tf_op jit(solution)/shard_map/pallas_call | solution.py:37
  16.0 0.0 collective-permute-done.1.near_cols
  16.0 0.1 shard_map.105
  16.0 0.7 %collective-permute-start.4 = (f32[170,128]{1,0:T(8,128)S(1)}, f32[170,128]{1,0:T(8,128)S(1)}, u32[]{:S(2)}, u32[]{:S(2)}) collective-permute-start(f32[170,128]{1,0:T(8,128)S(1)} %get-tuple-element.47), channel_id=1, source_target_pairs={{4,8},{8,4},{12,16},{16,12},{20,24},{24,20},{5,9},{9,5},{13,17},{1... | collective-permute-start | bytes 261128 | tf_op jit(solution)/shard_map/ppermute | solution.py:212
  16.7 4.3 %collective-permute-start.5 = (f32[170,128]{1,0:T(8,128)S(1)}, f32[170,128]{1,0:T(8,128)S(1)}, u32[]{:S(2)}, u32[]{:S(2)}) collective-permute-start(f32[170,128]{1,0:T(8,128)S(1)} %get-tuple-element.48), channel_id=1, source_target_pairs={{0,4},{4,0},{8,12},{12,8},{16,20},{20,16},{24,28},{28,24},{1,5},{5... | collective-permute-start | bytes 261128 | tf_op jit(solution)/shard_map/ppermute | solution.py:212
  21.1 0.0 collective-permute-done.2.far_rows
  21.1 2.2 %collective-permute-done.3.near_rows = f32[560,128]{1,0:T(8,128)S(1)} collective-permute-done((f32[560,128]{1,0:T(8,128)}, f32[560,128]{1,0:T(8,128)S(1)}, u32[]{:S(2)}, u32[]{:S(2)}) %collective-permute-start.3) | collective-permute-done | bytes 286752 | tf_op jit(solution)/shard_map/ppermute | solution.py:212
  23.3 1.7 %shard_map.106 = (bf16[4,14,24,128]{3,2,1,0:T(8,128)(2,1)S(1)}, bf16[4,14,24,128]{3,2,1,0:T(8,128)(2,1)S(1)}, f32[14,24,128]{2,1,0:T(8,128)S(1)}, f32[3,14,24,12...) custom-call(f32[16,2048]{1,0:T(8,128)S(1)} %copy-done.2, bf16[16,2048]{1,0:T(8,128)(2,1)S(1)} %copy-done.4, ...), custom_call_target="tpu_custom_call" | custom-call | flops 849346560 | bytes 4194304 | tf_op jit(solution)/shard_map/pallas_call | solution.py:37
  25.0 0.0 collective-permute-done.4.far_corner
  25.0 0.0 collective-permute-done.5.near_corner
  25.0 1.0 %shard_map.107 = (bf16[4,20,24,128]{3,2,1,0:T(8,128)(2,1)S(1)}, bf16[4,6,24,128]{3,2,1,0:T(8,128)(2,1)S(1)}, f32[6,24,128]{2,1,0:T(8,128)S(1)}, f32[3,6,24,128]{...) custom-call(f32[16,2048]{1,0:T(8,128)S(1)} %copy-done.2, ...), custom_call_target="tpu_custom_call" | custom-call | flops 849346560 | bytes 4194304 | tf_op jit(solution)/shard_map/pallas_call | solution.py:37
  26.0 12.9 %all_to_all.33 = f32[32,1,128]{2,1,0:T(1,128)S(1)} all-to-all(f32[32,1,128]{2,1,0:T(1,128)S(1)} %bitcast.19), channel_id=1, replica_groups=mesh['row'=8,'col'=4] {'row','col'}, dimensions={0} | all-to-all | bytes 32768 | tf_op jit(solution)/shard_map/all_to_all | solution.py:613
  38.9 3.8 %shard_map.108 = (f32[3,20,24,128]{3,2,1,0:T(8,128)S(1)}, f32[3,18,24,128]{3,2,1,0:T(8,128)S(1)}, f32[2,18,24,128]{3,2,1,0:T(8,128)S(1)}, f32[3,18,16,128]{3,2,1...) custom-call(f32[32,128]{1,0:T(8,128)S(1)} %bitcast.15, ...), custom_call_target="tpu_custom_call" | custom-call | flops 1698693120 | bytes 4194304 | tf_op jit(solution)/shard_map/pallas_call | solution.py:37
  42.7 8.8 %all_to_all.34 = f32[32,1,128]{2,1,0:T(1,128)S(1)} all-to-all(f32[32,1,128]{2,1,0:T(1,128)S(1)} %bitcast.18), channel_id=1, replica_groups=mesh['row'=8,'col'=4] {'row','col'}, dimensions={0} | all-to-all | bytes 32768 | tf_op jit(solution)/shard_map/all_to_all | solution.py:613
  51.6 3.1 %shard_map.109 = (f32[3,16,2048]{2,1,0:T(8,128)S(1)}, f32[3,16,2048]{2,1,0:T(8,128)S(1)}, f32[3,16,2048]{2,1,0:T(8,128)S(1)}, f32[3,16,2048]{2,1,0:T(8,128)S(1)}, f32[32,128]{1,0:T(8,128)S(1)}) custom-call(f32[32,128]{1,0:T(8,128)S(1)} %bitcast.14, f32[3]{0:T(128)S(1)} %copy-done.6, bf16[4,20,24,128]{3,2,1,0:T(8,128)(2,1)S(1)} %get-tuple-element.54.rest_0_.near_box, ...), custom_call_target="tpu_custom_call" | custom-call | flops 1698693120 | bytes 4194304 | tf_op jit(solution)/shard_map/pallas_call | solution.py:37
  54.7 8.8 %all_to_all.35 = f32[32,1,128]{2,1,0:T(1,128)S(1)} all-to-all(f32[32,1,128]{2,1,0:T(1,128)S(1)} %bitcast.17), channel_id=1, replica_groups=mesh['row'=8,'col'=4] {'row','col'}, dimensions={0} | all-to-all | bytes 32768 | tf_op jit(solution)/shard_map/all_to_all | solution.py:613
  63.5 1.6 %shard_map.110 = (f32[3,16,2048]{2,1,0:T(8,128)}, f32[3,16,2048]{2,1,0:T(8,128)}, f32[3]{0:T(128)}) custom-call(f32[32,128]{1,0:T(8,128)S(1)} %bitcast.16, f32[3]{0:T(128)S(1)} %copy-done.6, f32[3,16,2048]{2,1,0:T(8,128)S(1)} %get-tuple-element.74.duals, f32[3,16,2048]{2,1,0:T(8,128)S(1)} %get-tuple-element.75.multipliers, ...), custom_call_target="tpu_custom_call" | custom-call | flops 1048576 | bytes 4194304 | tf_op jit(solution)/shard_map/pallas_call | solution.py:37
  (15 shorter events, 0.0 us)
Async XLA Ops:
  0.6 22.7 %copy-start.1 = (bf16[3,16,2048]{2,1,0:T(8,128)(2,1)S(1)}, bf16[3,16,2048]{2,1,0:T(8,128)(2,1)}, u32[]{:S(2)}) copy-start(bf16[3,16,2048]{2,1,0:T(8,128)(2,1)} %upper.7) | copy-start | bytes 589828
  0.6 22.7 %copy-start = (bf16[3,16,2048]{2,1,0:T(8,128)(2,1)S(1)}, bf16[3,16,2048]{2,1,0:T(8,128)(2,1)}, u32[]{:S(2)}) copy-start(bf16[3,16,2048]{2,1,0:T(8,128)(2,1)} %lower.7) | copy-start | bytes 589828
  0.7 22.7 %copy-start.5 = (bf16[16,2048]{1,0:T(8,128)(2,1)S(1)}, bf16[16,2048]{1,0:T(8,128)(2,1)}, u32[]{:S(2)}) copy-start(bf16[16,2048]{1,0:T(8,128)(2,1)} %radius.5) | copy-start | bytes 196612
  0.7 22.7 %copy-start.4 = (bf16[16,2048]{1,0:T(8,128)(2,1)S(1)}, bf16[16,2048]{1,0:T(8,128)(2,1)}, u32[]{:S(2)}) copy-start(bf16[16,2048]{1,0:T(8,128)(2,1)} %center.5) | copy-start | bytes 196612
  0.7 22.7 %copy-start.2 = (f32[16,2048]{1,0:T(8,128)S(1)}, f32[16,2048]{1,0:T(8,128)}, u32[]{:S(2)}) copy-start(f32[16,2048]{1,0:T(8,128)} %objective.5) | copy-start | bytes 393220
  3.0 18.1 %collective-permute-start.2 = (f32[560,128]{1,0:T(8,128)}, f32[560,128]{1,0:T(8,128)S(1)}, u32[]{:S(2)}, u32[]{:S(2)}) collective-permute-start(f32[560,128]{1,0:T(8,128)} %get-tuple-element.44), channel_id=1, source_target_pairs={{4,8},{8,4},{12,16},{16,12},{20,24},{24,20},{5,9},{9,5},{13,17},{1... | collective-permute-start | bytes 860168 | tf_op jit(solution)/shard_map/ppermute | solution.py:212
  3.7 19.6 %collective-permute-start.3 = (f32[560,128]{1,0:T(8,128)}, f32[560,128]{1,0:T(8,128)S(1)}, u32[]{:S(2)}, u32[]{:S(2)}) collective-permute-start(f32[560,128]{1,0:T(8,128)} %get-tuple-element.45), channel_id=1, source_target_pairs={{0,4},{4,0},{8,12},{12,8},{16,20},{20,16},{24,28},{28,24},{1,5},{5... | collective-permute-start | bytes 860168 | tf_op jit(solution)/shard_map/ppermute | solution.py:212
  9.5 6.5 %collective-permute-start = (f32[336,128]{1,0:T(8,128)}, f32[336,128]{1,0:T(8,128)S(1)}, u32[]{:S(2)}, u32[]{:S(2)}) collective-permute-start(f32[336,128]{1,0:T(8,128)} %get-tuple-element.42), channel_id=1, source_target_pairs={{1,2},{2,1},{5,6},{6,5},{9,10},{10,9},{13,14},{14,13},{17,18},{18,... | collective-permute-start | bytes 516104 | tf_op jit(solution)/shard_map/ppermute | solution.py:212
  10.1 5.8 %collective-permute-start.1 = (f32[336,128]{1,0:T(8,128)}, f32[336,128]{1,0:T(8,128)S(1)}, u32[]{:S(2)}, u32[]{:S(2)}) collective-permute-start(f32[336,128]{1,0:T(8,128)} %get-tuple-element.43), channel_id=1, source_target_pairs={{0,1},{1,0},{2,3},{3,2},{4,5},{5,4},{6,7},{7,6},{8,9},{9,8},{10,11... | collective-permute-start | bytes 516104 | tf_op jit(solution)/shard_map/ppermute | solution.py:212
  13.1 1.3 %copy-start.3 = (f32[4,3,3,64,64]{4,3,2,1,0:T(8,128)S(1)}, f32[4,3,3,64,64]{4,3,2,1,0:T(8,128)}, u32[]{:S(2)}) copy-start(f32[4,3,3,64,64]{4,3,2,1,0:T(8,128)} %param.13) | copy-start | bytes 1769476
  14.3 0.7 %copy-start.7 = (f32[4,64]{1,0:T(4,128)S(1)}, f32[4,64]{1,0:T(4,128)}, u32[]{:S(2)}) copy-start(f32[4,64]{1,0:T(4,128)} %biases.1) | copy-start | bytes 3076
  16.0 9.0 %collective-permute-start.4 = (f32[170,128]{1,0:T(8,128)S(1)}, f32[170,128]{1,0:T(8,128)S(1)}, u32[]{:S(2)}, u32[]{:S(2)}) collective-permute-start(f32[170,128]{1,0:T(8,128)S(1)} %get-tuple-element.47), channel_id=1, source_target_pairs={{4,8},{8,4},{12,16},{16,12},{20,24},{24,20},{5,9},{9,5},{13,17},{1... | collective-permute-start | bytes 261128 | tf_op jit(solution)/shard_map/ppermute | solution.py:212
  16.7 8.3 %collective-permute-start.5 = (f32[170,128]{1,0:T(8,128)S(1)}, f32[170,128]{1,0:T(8,128)S(1)}, u32[]{:S(2)}, u32[]{:S(2)}) collective-permute-start(f32[170,128]{1,0:T(8,128)S(1)} %get-tuple-element.48), channel_id=1, source_target_pairs={{0,4},{4,0},{8,12},{12,8},{16,20},{20,16},{24,28},{28,24},{1,5},{5... | collective-permute-start | bytes 261128 | tf_op jit(solution)/shard_map/ppermute | solution.py:212
  25.0 13.9 %copy-start.6 = (f32[3]{0:T(128)S(1)}, f32[3]{0:T(128)}, u32[]{:S(2)}) copy-start(f32[3]{0:T(128)} %steps.5) | copy-start | bytes 40

commit v18 on v17

--- a/solution.py
+++ b/solution.py
@@ -517,7 +517,7 @@
         if own:
             squares = squares + new
             worth = worth + bound.total()
-    stats(stat, [own_rows(squares)])
+    stat[...] = jnp.broadcast_to(own_rows(squares), stat.shape)
     stats(value, [own_rows(worth)])
 
 
@@ -530,7 +530,7 @@
     wide, frame = near_box.shape[1:3]
     rows = frame - 2 * EDGE
     inside = slice(EDGE, frame - EDGE)
-    scale = scale_of(total, steps[1], cells, (frame, LANES), packed=True)
+    scale = scale_of(total, steps[1], cells, (frame, LANES))
     zero = jnp.zeros((frame, LANES), F32)
     slide(3, wide - 2, store, lambda j: [slope[k, j] for k in range(3)])
     for k in range(3):

time: 65.4 us -> 65.6 us (level)
  no operation moved by 1% of the time
where the time goes in v18:
time: 65.6 us; the launch traced here: 65.3 us
  blocking collectives  30.5 us (46%)
  starting transfers between devices  15.1 us (23%)
  Pallas kernels  14.7 us (22%)
  waiting for transfers between devices  2.27 us (3%)
  local copies, waits for them, and re-layouts  1.98 us (3%)
  between operations  0.77 us (1%)
    all_to_all x3, blocking collectives, everyone(): return lax.all_to_all(partial, ('row', 'col'), 0, 0, tiled=True)  30.5 us
    pallas_call x8, Pallas kernels, call(): pl.pallas_call(body, out_shape=outs, in_specs=specs, out_specs=out_specs,...  14.7 us
    ppermute x3, starting transfers between devices, partners(): lax.ppermute(near, axis, pairs(0))  13.1 us
    ppermute x3, waiting for transfers between devices, partners(): lax.ppermute(near, axis, pairs(0))  2.27 us
    ppermute x3, starting transfers between devices, partners(): lax.ppermute(far, axis, pairs(1))  2 us
    unnamed x16, local copies, waits for them, and re-layouts  1.98 us
  transfers between devices with their start and end apart: 6, of which 1 were waited for; matrix products, arithmetic and copies ran while one was open for 0% of the time, Pallas kernels for 4%

profile of v18, /device:TPU:0, one launch (start us, length us, event | category | flops | bytes accessed | tf_op | source)
XLA Modules:
  0.0 65.3 jit_solution(14121862807298851177)
XLA Ops:
  0.7 2.3 %shard_map.103 = (f32[560,128]{1,0:T(8,128)}, f32[560,128]{1,0:T(8,128)}, f32[336,128]{1,0:T(8,128)}, f32[336,128]{1,0:T(8,128)}) custom-call(f32[16,2048]{1,0:T(8,128)} %objective.5, bf16[16,2048]{1,0:T(8,128)(2,1)} %center.5, bf16[16,2048]{1,0:T(8,128)(2,1)} %radius.5, bf16[3,16,2048]{2,1,0:T(8,128)(2,1)} %lower.7, bf16[3,16,2048]{2,1,0:T(8,128)(2,1)} %upper.7), custom_call_target="tpu_custom_call" | custom-call | flops 1048576 | bytes 4194304 | tf_op jit(solution)/shard_map/pallas_call | solution.py:37
  3.0 0.7 %collective-permute-start.2 = (f32[560,128]{1,0:T(8,128)}, f32[560,128]{1,0:T(8,128)S(1)}, u32[]{:S(2)}, u32[]{:S(2)}) collective-permute-start(f32[560,128]{1,0:T(8,128)} %get-tuple-element.44), channel_id=1, source_target_pairs={{4,8},{8,4},{12,16},{16,12},{20,24},{24,20},{5,9},{9,5},{13,17},{1... | collective-permute-start | bytes 860168 | tf_op jit(solution)/shard_map/ppermute | solution.py:212
  3.7 5.8 %collective-permute-start.3 = (f32[560,128]{1,0:T(8,128)}, f32[560,128]{1,0:T(8,128)S(1)}, u32[]{:S(2)}, u32[]{:S(2)}) collective-permute-start(f32[560,128]{1,0:T(8,128)} %get-tuple-element.45), channel_id=1, source_target_pairs={{0,4},{4,0},{8,12},{12,8},{16,20},{20,16},{24,28},{28,24},{1,5},{5... | collective-permute-start | bytes 860168 | tf_op jit(solution)/shard_map/ppermute | solution.py:212
  9.5 0.7 %collective-permute-start = (f32[336,128]{1,0:T(8,128)}, f32[336,128]{1,0:T(8,128)S(1)}, u32[]{:S(2)}, u32[]{:S(2)}) collective-permute-start(f32[336,128]{1,0:T(8,128)} %get-tuple-element.42), channel_id=1, source_target_pairs={{1,2},{2,1},{5,6},{6,5},{9,10},{10,9},{13,14},{14,13},{17,18},{18,... | collective-permute-start | bytes 516104 | tf_op jit(solution)/shard_map/ppermute | solution.py:212
  10.1 2.9 %collective-permute-start.1 = (f32[336,128]{1,0:T(8,128)}, f32[336,128]{1,0:T(8,128)S(1)}, u32[]{:S(2)}, u32[]{:S(2)}) collective-permute-start(f32[336,128]{1,0:T(8,128)} %get-tuple-element.43), channel_id=1, source_target_pairs={{0,1},{1,0},{2,3},{3,2},{4,5},{5,4},{6,7},{7,6},{8,9},{9,8},{10,11... | collective-permute-start | bytes 516104 | tf_op jit(solution)/shard_map/ppermute | solution.py:212
  13.1 1.3 %copy-done.3 = f32[4,3,3,64,64]{4,3,2,1,0:T(8,128)S(1)} copy-done((f32[4,3,3,64,64]{4,3,2,1,0:T(8,128)S(1)}, f32[4,3,3,64,64]{4,3,2,1,0:T(8,128)}, u32[]{:S(2)}) %copy-start.3) | copy-done | bytes 589848
  14.3 0.7 %copy-done.7 = f32[4,64]{1,0:T(4,128)S(1)} copy-done((f32[4,64]{1,0:T(4,128)S(1)}, f32[4,64]{1,0:T(4,128)}, u32[]{:S(2)}) %copy-start.7) | copy-done | bytes 1048
  15.0 0.9 %shard_map.104 = (bf16[3,768,384]{2,1,0:T(8,128)(2,1)S(1)}, bf16[4,768,384]{2,1,0:T(8,128)(2,1)S(1)}, f32[8,128]{1,0:T(8,128)S(1)}) custom-call(f32[36,64,64]{2,1,0:T(8,128)S(1)} %bitcast.13, f32[4,64]{1,0:T(4,128)S(1)} %copy-done.7), custom_call_target="tpu_custom_call" | custom-call | flops 4194304 | bytes 4194304 | tf_op jit(solution)/shard_map/pallas_call | solution.py:37
  16.0 0.0 collective-permute-done.1.near_cols
  16.0 0.1 shard_map.105
  16.0 0.7 %collective-permute-start.4 = (f32[170,128]{1,0:T(8,128)S(1)}, f32[170,128]{1,0:T(8,128)S(1)}, u32[]{:S(2)}, u32[]{:S(2)}) collective-permute-start(f32[170,128]{1,0:T(8,128)S(1)} %get-tuple-element.47), channel_id=1, source_target_pairs={{4,8},{8,4},{12,16},{16,12},{20,24},{24,20},{5,9},{9,5},{13,17},{1... | collective-permute-start | bytes 261128 | tf_op jit(solution)/shard_map/ppermute | solution.py:212
  16.7 4.3 %collective-permute-start.5 = (f32[170,128]{1,0:T(8,128)S(1)}, f32[170,128]{1,0:T(8,128)S(1)}, u32[]{:S(2)}, u32[]{:S(2)}) collective-permute-start(f32[170,128]{1,0:T(8,128)S(1)} %get-tuple-element.48), channel_id=1, source_target_pairs={{0,4},{4,0},{8,12},{12,8},{16,20},{20,16},{24,28},{28,24},{1,5},{5... | collective-permute-start | bytes 261128 | tf_op jit(solution)/shard_map/ppermute | solution.py:212
  21.1 0.0 collective-permute-done.2.far_rows
  21.1 2.2 %collective-permute-done.3.near_rows = f32[560,128]{1,0:T(8,128)S(1)} collective-permute-done((f32[560,128]{1,0:T(8,128)}, f32[560,128]{1,0:T(8,128)S(1)}, u32[]{:S(2)}, u32[]{:S(2)}) %collective-permute-start.3) | collective-permute-done | bytes 286752 | tf_op jit(solution)/shard_map/ppermute | solution.py:212
  23.3 1.7 %shard_map.106 = (bf16[4,14,24,128]{3,2,1,0:T(8,128)(2,1)S(1)}, bf16[4,14,24,128]{3,2,1,0:T(8,128)(2,1)S(1)}, f32[14,24,128]{2,1,0:T(8,128)S(1)}, f32[3,14,24,12...) custom-call(f32[16,2048]{1,0:T(8,128)S(1)} %copy-done.2, bf16[16,2048]{1,0:T(8,128)(2,1)S(1)} %copy-done.4, ...), custom_call_target="tpu_custom_call" | custom-call | flops 849346560 | bytes 4194304 | tf_op jit(solution)/shard_map/pallas_call | solution.py:37
  25.0 0.0 collective-permute-done.4.far_corner
  25.0 0.0 collective-permute-done.5.near_corner
  25.0 1.0 %shard_map.107 = (bf16[4,20,24,128]{3,2,1,0:T(8,128)(2,1)S(1)}, bf16[4,6,24,128]{3,2,1,0:T(8,128)(2,1)S(1)}, f32[6,24,128]{2,1,0:T(8,128)S(1)}, f32[3,6,24,128]{...) custom-call(f32[16,2048]{1,0:T(8,128)S(1)} %copy-done.2, ...), custom_call_target="tpu_custom_call" | custom-call | flops 849346560 | bytes 4194304 | tf_op jit(solution)/shard_map/pallas_call | solution.py:37
  26.0 12.9 %all_to_all.33 = f32[32,1,128]{2,1,0:T(1,128)S(1)} all-to-all(f32[32,1,128]{2,1,0:T(1,128)S(1)} %bitcast.19), channel_id=1, replica_groups=mesh['row'=8,'col'=4] {'row','col'}, dimensions={0} | all-to-all | bytes 32768 | tf_op jit(solution)/shard_map/all_to_all | solution.py:613
  38.9 3.8 %shard_map.108 = (f32[3,20,24,128]{3,2,1,0:T(8,128)S(1)}, f32[3,18,24,128]{3,2,1,0:T(8,128)S(1)}, f32[2,18,24,128]{3,2,1,0:T(8,128)S(1)}, f32[3,18,16,128]{3,2,1...) custom-call(f32[32,128]{1,0:T(8,128)S(1)} %bitcast.15, ...), custom_call_target="tpu_custom_call" | custom-call | flops 1698693120 | bytes 4194304 | tf_op jit(solution)/shard_map/pallas_call | solution.py:37
  42.7 8.8 %all_to_all.34 = f32[32,1,128]{2,1,0:T(1,128)S(1)} all-to-all(f32[32,1,128]{2,1,0:T(1,128)S(1)} %bitcast.18), channel_id=1, replica_groups=mesh['row'=8,'col'=4] {'row','col'}, dimensions={0} | all-to-all | bytes 32768 | tf_op jit(solution)/shard_map/all_to_all | solution.py:613
  51.5 3.4 %shard_map.109 = (f32[3,16,2048]{2,1,0:T(8,128)S(1)}, f32[3,16,2048]{2,1,0:T(8,128)S(1)}, f32[3,16,2048]{2,1,0:T(8,128)S(1)}, f32[3,16,2048]{2,1,0:T(8,128)S(1)}, f32[32,128]{1,0:T(8,128)S(1)}) custom-call(f32[32,128]{1,0:T(8,128)S(1)} %bitcast.14, f32[3]{0:T(128)S(1)} %copy-done.6, bf16[4,20,24,128]{3,2,1,0:T(8,128)(2,1)S(1)} %get-tuple-element.54.rest_0_.near_box, ...), custom_call_target="tpu_custom_call" | custom-call | flops 1698693120 | bytes 4194304 | tf_op jit(solution)/shard_map/pallas_call | solution.py:37
  54.9 8.8 %all_to_all.35 = f32[32,1,128]{2,1,0:T(1,128)S(1)} all-to-all(f32[32,1,128]{2,1,0:T(1,128)S(1)} %bitcast.17), channel_id=1, replica_groups=mesh['row'=8,'col'=4] {'row','col'}, dimensions={0} | all-to-all | bytes 32768 | tf_op jit(solution)/shard_map/all_to_all | solution.py:613
  63.8 1.6 %shard_map.110 = (f32[3,16,2048]{2,1,0:T(8,128)}, f32[3,16,2048]{2,1,0:T(8,128)}, f32[3]{0:T(128)}) custom-call(f32[32,128]{1,0:T(8,128)S(1)} %bitcast.16, f32[3]{0:T(128)S(1)} %copy-done.6, f32[3,16,2048]{2,1,0:T(8,128)S(1)} %get-tuple-element.74.duals, f32[3,16,2048]{2,1,0:T(8,128)S(1)} %get-tuple-element.75.multipliers, ...), custom_call_target="tpu_custom_call" | custom-call | flops 1048576 | bytes 4194304 | tf_op jit(solution)/shard_map/pallas_call | solution.py:37
  (15 shorter events, 0.0 us)
Async XLA Ops:
  0.6 22.7 %copy-start.1 = (bf16[3,16,2048]{2,1,0:T(8,128)(2,1)S(1)}, bf16[3,16,2048]{2,1,0:T(8,128)(2,1)}, u32[]{:S(2)}) copy-start(bf16[3,16,2048]{2,1,0:T(8,128)(2,1)} %upper.7) | copy-start | bytes 589828
  0.6 22.7 %copy-start = (bf16[3,16,2048]{2,1,0:T(8,128)(2,1)S(1)}, bf16[3,16,2048]{2,1,0:T(8,128)(2,1)}, u32[]{:S(2)}) copy-start(bf16[3,16,2048]{2,1,0:T(8,128)(2,1)} %lower.7) | copy-start | bytes 589828
  0.7 22.7 %copy-start.5 = (bf16[16,2048]{1,0:T(8,128)(2,1)S(1)}, bf16[16,2048]{1,0:T(8,128)(2,1)}, u32[]{:S(2)}) copy-start(bf16[16,2048]{1,0:T(8,128)(2,1)} %radius.5) | copy-start | bytes 196612
  0.7 22.7 %copy-start.4 = (bf16[16,2048]{1,0:T(8,128)(2,1)S(1)}, bf16[16,2048]{1,0:T(8,128)(2,1)}, u32[]{:S(2)}) copy-start(bf16[16,2048]{1,0:T(8,128)(2,1)} %center.5) | copy-start | bytes 196612
  0.7 22.7 %copy-start.2 = (f32[16,2048]{1,0:T(8,128)S(1)}, f32[16,2048]{1,0:T(8,128)}, u32[]{:S(2)}) copy-start(f32[16,2048]{1,0:T(8,128)} %objective.5) | copy-start | bytes 393220
  3.0 18.1 %collective-permute-start.2 = (f32[560,128]{1,0:T(8,128)}, f32[560,128]{1,0:T(8,128)S(1)}, u32[]{:S(2)}, u32[]{:S(2)}) collective-permute-start(f32[560,128]{1,0:T(8,128)} %get-tuple-element.44), channel_id=1, source_target_pairs={{4,8},{8,4},{12,16},{16,12},{20,24},{24,20},{5,9},{9,5},{13,17},{1... | collective-permute-start | bytes 860168 | tf_op jit(solution)/shard_map/ppermute | solution.py:212
  3.7 19.6 %collective-permute-start.3 = (f32[560,128]{1,0:T(8,128)}, f32[560,128]{1,0:T(8,128)S(1)}, u32[]{:S(2)}, u32[]{:S(2)}) collective-permute-start(f32[560,128]{1,0:T(8,128)} %get-tuple-element.45), channel_id=1, source_target_pairs={{0,4},{4,0},{8,12},{12,8},{16,20},{20,16},{24,28},{28,24},{1,5},{5... | collective-permute-start | bytes 860168 | tf_op jit(solution)/shard_map/ppermute | solution.py:212
  9.5 6.5 %collective-permute-start = (f32[336,128]{1,0:T(8,128)}, f32[336,128]{1,0:T(8,128)S(1)}, u32[]{:S(2)}, u32[]{:S(2)}) collective-permute-start(f32[336,128]{1,0:T(8,128)} %get-tuple-element.42), channel_id=1, source_target_pairs={{1,2},{2,1},{5,6},{6,5},{9,10},{10,9},{13,14},{14,13},{17,18},{18,... | collective-permute-start | bytes 516104 | tf_op jit(solution)/shard_map/ppermute | solution.py:212
  10.1 5.8 %collective-permute-start.1 = (f32[336,128]{1,0:T(8,128)}, f32[336,128]{1,0:T(8,128)S(1)}, u32[]{:S(2)}, u32[]{:S(2)}) collective-permute-start(f32[336,128]{1,0:T(8,128)} %get-tuple-element.43), channel_id=1, source_target_pairs={{0,1},{1,0},{2,3},{3,2},{4,5},{5,4},{6,7},{7,6},{8,9},{9,8},{10,11... | collective-permute-start | bytes 516104 | tf_op jit(solution)/shard_map/ppermute | solution.py:212
  13.1 1.3 %copy-start.3 = (f32[4,3,3,64,64]{4,3,2,1,0:T(8,128)S(1)}, f32[4,3,3,64,64]{4,3,2,1,0:T(8,128)}, u32[]{:S(2)}) copy-start(f32[4,3,3,64,64]{4,3,2,1,0:T(8,128)} %param.13) | copy-start | bytes 1769476
  14.3 0.7 %copy-start.7 = (f32[4,64]{1,0:T(4,128)S(1)}, f32[4,64]{1,0:T(4,128)}, u32[]{:S(2)}) copy-start(f32[4,64]{1,0:T(4,128)} %biases.1) | copy-start | bytes 3076
  16.0 9.0 %collective-permute-start.4 = (f32[170,128]{1,0:T(8,128)S(1)}, f32[170,128]{1,0:T(8,128)S(1)}, u32[]{:S(2)}, u32[]{:S(2)}) collective-permute-start(f32[170,128]{1,0:T(8,128)S(1)} %get-tuple-element.47), channel_id=1, source_target_pairs={{4,8},{8,4},{12,16},{16,12},{20,24},{24,20},{5,9},{9,5},{13,17},{1... | collective-permute-start | bytes 261128 | tf_op jit(solution)/shard_map/ppermute | solution.py:212
  16.7 8.3 %collective-permute-start.5 = (f32[170,128]{1,0:T(8,128)S(1)}, f32[170,128]{1,0:T(8,128)S(1)}, u32[]{:S(2)}, u32[]{:S(2)}) collective-permute-start(f32[170,128]{1,0:T(8,128)S(1)} %get-tuple-element.48), channel_id=1, source_target_pairs={{0,4},{4,0},{8,12},{12,8},{16,20},{20,16},{24,28},{28,24},{1,5},{5... | collective-permute-start | bytes 261128 | tf_op jit(solution)/shard_map/ppermute | solution.py:212
  25.0 13.9 %copy-start.6 = (f32[3]{0:T(128)S(1)}, f32[3]{0:T(128)}, u32[]{:S(2)}) copy-start(f32[3]{0:T(128)} %steps.5) | copy-start | bytes 40
